TPU v7x, 32 devices: a whole 2x2x4 slice. The times are simulated.
32 devices in a mesh: dp: 4 (over z), trow: 2 (over y), tcol: 4 (over x, core).
Axes of the slice: x: 2, y: 2, z: 4, core: 2. Of those that a mesh axis runs over, the one named last changes fastest.
Arguments:
- embeddings: bfloat16 [1024, 4, 2, 768], P('dp', 'tcol', 'trow'), may hold values from -21.5 to 21.5
- targets: bfloat16 [1024, 256], P('dp'), may hold values from -384 to 384
- gram_prior: float32 [4, 2, 4, 192, 6144], P(None, 'trow', 'dp', None, 'tcol'), may hold values from -0.2 to 4.2, as said below
- penalty: float32 [4, 2, 4, 192], P('tcol', 'trow', 'dp'), may hold values from 0.3 to 3
Outputs:
- gram: float32 [4, 2, 4, 192, 6144], P(None, 'trow', 'dp', None, 'tcol')
- weights: float32 [4, 2, 4, 192, 256], P('tcol', 'trow', 'dp')
- residual: float32 [4, 2, 4, 192, 256], P('tcol', 'trow', 'dp')
Inputs may be any that keep to these rules, and one draw needn't show every extreme that they name: `gram_prior`: symmetric and positive definite as a 6144 x 6144 matrix.
All inputs are finite; a program needn't handle non-finite values.
Results may differ from a plain program's by a relative error of at most 0.0003.
Values may be sent and summed in bfloat16 or wider, within the bound.
No kernel may reach another device: no remote copies, remote signals or barrier semaphores. Data moves between devices by JAX's collectives and lax.ppermute only.
A program may use at most 64 MiB of HBM per device.

v0:
```python
import jax
import jax.numpy as jnp
from jax import lax
from jax.sharding import PartitionSpec as P

ITERS = 2


def column_sums(first_value, second_value):
    return jnp.sum(first_value * second_value, axis=0)


def shards(embeddings, targets, gram_prior, penalty):
    row_count = embeddings.shape[0]
    block_width = embeddings.shape[3]
    head_count = targets.shape[1]
    data_count = lax.axis_size("dp")
    trow_count = lax.axis_size("trow")
    tcol_count = lax.axis_size("tcol")
    piece_rows = block_width // data_count
    total_rows = row_count * data_count
    tile_rows = tcol_count * piece_rows
    contract = (((0,), (0,)), ((), ()))
    own_columns = embeddings.reshape(row_count, block_width)
    columns = lax.all_gather(embeddings, "trow", axis=2, tiled=True).reshape(
        row_count, trow_count * block_width
    )
    sliced = own_columns.reshape(row_count, data_count, piece_rows)
    own_slices = lax.all_to_all(sliced, "dp", split_axis=1, concat_axis=0, tiled=True)
    all_panel = lax.all_gather(own_slices, "tcol", axis=1, tiled=True).reshape(
        total_rows, tile_rows
    )
    summed = lax.dot_general(
        all_panel,
        lax.all_gather(columns, "dp", axis=0, tiled=True),
        contract,
        preferred_element_type=jnp.float32,
    )
    gram_new = gram_prior + (summed / total_rows).reshape(gram_prior.shape)
    right_side = (
        lax.psum_scatter(
            lax.dot_general(own_columns, targets, contract, preferred_element_type=jnp.float32),
            "dp",
            scatter_dimension=0,
            tiled=True,
        )
        / total_rows
    )
    gram_tile = gram_new.reshape(tile_rows, trow_count, data_count, piece_rows)
    penalty_rows = penalty.reshape(piece_rows, 1)

    def squared_norm(vector):
        return lax.psum(column_sums(vector, vector), ("dp", "trow", "tcol"))

    weights = jnp.zeros_like(right_side)
    residual = right_side
    direction = right_side
    norm_now = squared_norm(residual)
    for iteration in range(ITERS):
        shared = lax.all_gather(
            direction.reshape(1, piece_rows, head_count), ("dp", "trow"), axis=0, tiled=True
        )
        shared = shared.reshape(data_count, trow_count, piece_rows, head_count)
        contribution = jnp.einsum(
            "ktdr,dtrh->kh", gram_tile, shared, precision=lax.Precision.HIGHEST
        )
        applied = lax.psum_scatter(contribution, "tcol", scatter_dimension=0, tiled=True)
        applied = applied + penalty_rows * direction
        curvature = lax.psum(column_sums(direction, applied), ("dp", "trow", "tcol"))
        step_size = norm_now / curvature
        weights = weights + step_size * direction
        residual = residual - step_size * applied
        if iteration + 1 < ITERS:
            norm_next = squared_norm(residual)
            direction = residual + norm_next / norm_now * direction
            norm_now = norm_next
    out_shape = (1, 1, 1, piece_rows, head_count)
    return (gram_new, weights.reshape(out_shape), residual.reshape(out_shape))


def solution(mesh):
    placed = (
        P("dp", "tcol", "trow", None),
        P("dp", None),
        P(None, "trow", "dp", None, "tcol"),
        P("tcol", "trow", "dp", None),
    )
    return jax.shard_map(
        shards,
        mesh=mesh,
        in_specs=placed,
        out_specs=(
            P(None, "trow", "dp", None, "tcol"),
            P("tcol", "trow", "dp", None, None),
            P("tcol", "trow", "dp", None, None),
        ),
        check_vma=False,
    )
```

profile of v0, /device:TPU:0, one launch (start us, length us, event | category | flops | bytes accessed | tf_op | source)
XLA Modules:
  0.0 411.1 jit_solution(10354952467919148368)
XLA Ops:
  8.1 0.8 copy-done
  8.9 2.2 fusion
  11.2 1.2 copy.16
  12.4 27.8 %all_to_all.18 = bf16[256,4,192]{0,2,1:T(8,128)(2,1)S(1)} all-to-all(bf16[256,4,192]{0,2,1:T(8,128)(2,1)S(1)} %bitcast.48), channel_id=1, replica_groups=mesh['dp'=4,'trow'=2,'tcol'=4] {'dp'}, dimensions={1} | all-to-all | bytes 786432 | tf_op jit(solution)/shard_map/all_to_all | solution.py:29
  40.2 0.8 copy.25
  41.0 0.0 all-gather.9.cloned.1.call-start
  41.1 8.5 %all_gather.16 = bf16[256,1,2,768]{3,0,1,2:T(8,128)(2,1)S(1)} all-gather(bf16[256,1,1,768]{3,0,1,2:T(8,128)(2,1)S(1)} %bitcast.42), channel_id=1, replica_groups=mesh['dp'=4,'trow'=2,'tcol'=4] {'trow'}, dimensions={2}, use_global_device_ids=true | all-gather | bytes 1179648 | tf_op jit(solution)/shard_map/all_gather | solution.py:25
  49.5 1.2 copy.19
  50.7 0.0 all-gather.11.cloned.1.call-start
  50.8 1.7 broadcast_multiply_fusion
  52.5 0.0 reduce-scatter.6.cloned.1.call-start
  52.6 6.7 %all-gather.7.cloned.1.call-done = bf16[1024,4,192]{0,2,1:T(8,128)(2,1)} async-done(((bf16[1024,1,192]{0,2,1:T(8,128)(2,1)}), bf16[1024,4,192]{0,2,1:T(8,128)(2,1)}) %all-gather.7.cloned.1.call-update) | async-done | bytes 1572880 | tf_op jit(solution)/shard_map/all_gather | solution.py:30
  59.2 65.3 %all-gather.9.cloned.1.call-done = bf16[1024,1536]{0,1:T(8,128)(2,1)} async-done(((bf16[256,1536]{0,1:T(8,128)(2,1)}), bf16[1024,1536]{0,1:T(8,128)(2,1)}) %all-gather.9.cloned.1.call-update) | async-done | bytes 3145744 | tf_op jit(solution)/shard_map/all_gather | solution.py:35
  124.5 5.1 %convolution_multiply_fusion = f32[768,1536]{1,0:T(8,128)S(1)} fusion(bf16[1024,768]{0,1:T(8,128)(2,1)} %bitcast.52, bf16[1024,1536]{0,1:T(8,128)(2,1)} %all-gather.9.cloned.1.call-done), kind=kOutput, calls=%fused_computation | convolution fusion | flops 2417098752 | bytes 9437184 | tf_op jit(solution)/shard_map/dot_general | solution.py:33
  129.7 3.2 add.29
  132.9 8.6 %reshape.48 = f32[768,2,4,192]{3,2,1,0:T(4,128)} reshape(f32[4,1,1,192,1536]{4,3,2,1,0:T(8,128)} %add.29) | data formatting | bytes 9437184 | tf_op jit(solution)/shard_map/reshape | solution.py:49
  141.4 7.2 %copy.21 = f32[768,2,4,192]{0,3,1,2:T(8,128)} copy(f32[768,2,4,192]{3,2,1,0:T(4,128)} %reshape.48) | data formatting | bytes 9437184 | tf_op jit(solution)/shard_map/reshape | solution.py:49
  148.7 20.9 %all-gather.11.cloned.1.call-done = f32[1536,256]{1,0:T(8,128)} async-done(((f32[192,256]{1,0:T(8,128)}), f32[1536,256]{1,0:T(8,128)}) %all-gather.11.cloned.1.call-update) | async-done | bytes 1572880 | tf_op jit(solution)/shard_map/all_gather | solution.py:60
  169.6 11.2 %convolution_bitcast_fusion.1 = f32[768,256]{1,0:T(8,128)} fusion(f32[768,2,4,192]{0,3,1,2:T(8,128)} %copy.21, f32[4,2,192,256]{3,2,1,0:T(8,128)} %bitcast.44), kind=kOutput, calls=%fused_computation.2 | convolution fusion | flops 3623878656 | bytes 7077888 | tf_op jit(solution)/shard_map/ktdr,dtrh->kh/dot_general | solution.py:64
  180.8 0.2 all-gather.13.cloned.1.call-start
  181.1 21.3 %reduce-scatter.6.cloned.1.call-done = f32[192,256]{1,0:T(8,128)} async-done(((f32[768,256]{1,0:T(8,128)}), f32[192,256]{1,0:T(8,128)}) %reduce-scatter.6.cloned.1.call-update) | async-done | bytes 196624 | tf_op jit(solution)/shard_map/reduce_scatter | solution.py:67
  202.4 1.0 multiply_reduce_fusion.2
  203.4 39.4 %all-reduce = (f32[256]{0:T(256)S(1)}, f32[256]{0:T(256)S(1)}) all-reduce(f32[256]{0:T(256)S(1)} %get-tuple-element.4, f32[256]{0:T(256)S(1)} %get-tuple-element.3), channel_id=1, replica_groups=mesh['dp'=4,'trow'=2,'tcol'=4] {'dp','trow','tcol'}, use_global_device_ids=true, to_apply=%region_2.0 | all-reduce | flops 512 | bytes 4096 | tf_op jit(solution)/shard_map/psum | solution.py:53
  242.8 0.1 multiply_reduce_fusion.1
  242.9 41.0 %psum.30 = f32[256]{0:T(256)S(1)} all-reduce(f32[256]{0:T(256)S(1)} %multiply_reduce_fusion.1), channel_id=1, replica_groups=mesh['dp'=4,'trow'=2,'tcol'=4] {'dp','trow','tcol'}, use_global_device_ids=true, to_apply=%region_7.0 | all-reduce | flops 256 | bytes 2048 | tf_op jit(solution)/shard_map/psum | solution.py:53
  283.9 0.7 multiply_add_fusion.1
  284.7 44.1 %all-gather.13.cloned.1.call-done = f32[1536,256]{1,0:T(8,128)} async-done(((f32[192,256]{1,0:T(8,128)}), f32[1536,256]{1,0:T(8,128)}) %all-gather.13.cloned.1.call-update) | async-done | bytes 1572880 | tf_op jit(solution)/shard_map/all_gather | solution.py:60
  328.7 11.2 %convolution_bitcast_fusion = f32[768,256]{1,0:T(8,128)} fusion(f32[768,2,4,192]{0,3,1,2:T(8,128)} %copy.21, f32[4,2,192,256]{3,2,1,0:T(8,128)} %bitcast.45), kind=kOutput, calls=%fused_computation.1 | convolution fusion | flops 3623878656 | bytes 7077888 | tf_op jit(solution)/shard_map/ktdr,dtrh->kh/dot_general | solution.py:64
  340.0 21.5 %reduce-scatter.8.cloned.1.call-done = f32[192,256]{1,0:T(8,128)} async-done(((f32[768,256]{1,0:T(8,128)}), f32[192,256]{1,0:T(8,128)}) %reduce-scatter.8.cloned.1.call-update) | async-done | bytes 196624 | tf_op jit(solution)/shard_map/reduce_scatter | solution.py:67
  361.6 1.0 multiply_reduce_fusion
  362.6 39.3 %psum.31 = f32[256]{0:T(256)S(1)} all-reduce(f32[256]{0:T(256)S(1)} %multiply_reduce_fusion), channel_id=1, replica_groups=mesh['dp'=4,'trow'=2,'tcol'=4] {'dp','trow','tcol'}, use_global_device_ids=true, to_apply=%region_10.0 | all-reduce | flops 256 | bytes 2048 | tf_op jit(solution)/shard_map/psum | solution.py:69
  401.9 1.7 subtract_bitcast_fusion
  (29 shorter events, 0.3 us)
Async XLA Ops:
  8.0 0.9 copy-start
  8.0 33.1 %copy-start.2 = (bf16[256,1,1,768]{3,0,2,1:T(8,128)(2,1)S(1)}, bf16[256,1,1,768]{3,0,2,1:T(8,128)(2,1)}, u32[]{:S(2)}) copy-start(bf16[256,1,1,768]{3,0,2,1:T(8,128)(2,1)} %param.4) | copy-start | bytes 1179652
  8.0 42.8 %reduce-scatter.4.cloned.1.call-start = ((), (), s32[]{:S(2)}) async-start(), calls=%async_computation.6 | async-start | bytes 983040 | tf_op jit(solution)/shard_map/reduce_scatter | solution.py:41
  11.1 48.1 %all-gather.7.cloned.1.call-start = ((), (), s32[]{:S(2)}) async-start(), calls=%async_computation.4 | async-start | bytes 1966080 | tf_op jit(solution)/shard_map/all_gather | solution.py:30
  41.0 83.5 %all-gather.9.cloned.1.call-start = ((), (), s32[]{:S(2)}) async-start(), calls=%async_computation.5 | async-start | bytes 3932160 | tf_op jit(solution)/shard_map/all_gather | solution.py:35
  50.7 118.9 %all-gather.11.cloned.1.call-start = ((), (), s32[]{:S(2)}) async-start(), calls=%async_computation.9 | async-start | bytes 1769472 | tf_op jit(solution)/shard_map/all_gather | solution.py:60
  50.8 78.9 %slice-start = ((s8[4718592]{0:T(1024)(128)(4,1)}), s8[524288]{0:T(1024)(128)(4,1)S(1)}, s32[]{:S(2)}) async-start(s8[4718592]{0:T(1024)(128)(4,1)} %bitcast.39), calls=%async_computation.11 | async-start | bytes 1048576
  52.5 149.9 %reduce-scatter.6.cloned.1.call-start = ((), (), s32[]{:S(2)}) async-start(), calls=%async_computation.7 | async-start | bytes 983040 | tf_op jit(solution)/shard_map/reduce_scatter | solution.py:67
  124.5 5.2 %slice-start.1 = ((s8[4718592]{0:T(1024)(128)(4,1)}), s8[4194304]{0:T(1024)(128)(4,1)S(1)}, s32[]{:S(2)}) async-start(s8[4718592]{0:T(1024)(128)(4,1)} %bitcast.39), calls=%async_computation.12 | async-start | bytes 8388608
  169.6 11.5 %copy-start.4 = (f32[1,1,1,192]{3,2,1,0:T(1,128)S(1)}, f32[1,1,1,192]{3,2,1,0:T(1,128)}, u32[]{:S(2)}) copy-start(f32[1,1,1,192]{3,2,1,0:T(1,128)} %param.7) | copy-start | bytes 2308
  169.6 32.8 %copy-start.1 = (f32[192,256]{1,0:T(8,128)S(1)}, f32[192,256]{1,0:T(8,128)}, u32[]{:S(2)}) copy-start(f32[192,256]{1,0:T(8,128)} %reduce-scatter.4.cloned.1.call-done) | copy-start | bytes 589828
  180.8 147.9 %all-gather.13.cloned.1.call-start = ((), (), s32[]{:S(2)}) async-start(), calls=%async_computation.10 | async-start | bytes 1769472 | tf_op jit(solution)/shard_map/all_gather | solution.py:60
  284.6 76.9 %reduce-scatter.8.cloned.1.call-start = ((), (), s32[]{:S(2)}) async-start(), calls=%async_computation.8 | async-start | bytes 983040 | tf_op jit(solution)/shard_map/reduce_scatter | solution.py:67
  328.7 32.8 %copy-start.3 = (f32[192,256]{1,0:T(8,128)S(1)}, f32[192,256]{1,0:T(8,128)}, u32[]{:S(2)}) copy-start(f32[192,256]{1,0:T(8,128)} %multiply_add_fusion.1) | copy-start | bytes 589828
Sparse Core Ops, SparseCore 0:
  11.3 32.2 reduce-scatter.3
Sparse Core Ops, SparseCore 1:
  41.1 18.1 all-gather.6
  61.2 63.2 all-gather.8
  127.1 42.4 all-gather.10
  180.9 21.4 reduce-scatter.5
  284.7 44.0 all-gather.12
  340.1 21.4 reduce-scatter.7
where the time goes:
time: 412 us; the launch traced here: 411 us
  waiting for transfers between devices  180 us (44%)
  blocking collectives  156 us (38%)
  matrix products  29.8 us (7%)
  local copies, waits for them, and re-layouts  19.8 us (5%)
  between operations  15.7 us (4%)
  other arithmetic  9.43 us (2%)
    psum x2, blocking collectives, squared_norm(): return lax.psum(column_sums(vector, vector), ('dp', 'trow', 'tcol'))  80.4 us
    all_gather x1, waiting for transfers between devices, shards(): lax.all_gather(columns, 'dp', axis=0, tiled=True)  65.3 us
    all_gather x2, waiting for transfers between devices, shards(): lax.all_gather(direction.reshape(1, piece_rows, head_count), ('dp', 'trow...  65 us
    reduce_scatter x2, waiting for transfers between devices, shards(): lax.psum_scatter(contribution, 'tcol', scatter_dimension=0, tiled=True)  42.8 us
    psum x1, blocking collectives, shards(): lax.psum(column_sums(direction, applied), ('dp', 'trow', 'tcol'))  39.3 us
    all_to_all x1, blocking collectives, shards(): lax.all_to_all(sliced, 'dp', split_axis=1, concat_axis=0, tiled=True)  27.8 us
    dot_general x2, matrix products, shards(): jnp.einsum('ktdr,dtrh->kh', gram_tile, shared, precision=lax.Precision.HI...  22.5 us
    reshape x2, local copies, waits for them, and re-layouts, shards(): gram_tile = gram_new.reshape(tile_rows, trow_count, data_count, piece_rows)  15.8 us
  transfers between devices with their start and end apart: 7, of which 6 were waited for; matrix products, arithmetic and copies ran while one was open for 7% of the time, Pallas kernels for 0%

commit v1 on v0

v1 whole, which is shorter than its diff:
```python
import jax
import jax.numpy as jnp
from jax import lax
from jax.sharding import PartitionSpec as P

ITERS = 2
NT = (((1,), (1,)), ((), ()))


def turn(count, shift):
    return [(place, (place + shift) % count) for place in range(count)]


def swap(count, bit):
    return [(place, place ^ bit) for place in range(count)]


def all_sum(value, axis_names):
    count = 1
    for name in axis_names:
        count *= lax.axis_size(name)
    spread = jnp.broadcast_to(value[None], (count,) + value.shape)
    return jnp.sum(lax.all_to_all(spread, axis_names, split_axis=0, concat_axis=0, tiled=True), axis=0)


def pair_order(own, other, upper):
    first = jnp.where(upper, other, own)
    second = jnp.where(upper, own, other)
    return jnp.concatenate([first, second], axis=0)


def gather_pairs(value, axis, count):
    place = lax.axis_index(axis)
    bit = count // 2
    held = value[None]
    bits = []
    while bit >= 1:
        other = lax.ppermute(held, axis, swap(count, bit))
        upper = (place & bit) != 0
        first = jnp.where(upper, other, held)
        second = jnp.where(upper, held, other)
        held = jnp.stack([first, second], axis=1).reshape((2 * held.shape[0],) + held.shape[1:])
        bits.append(bit)
        bit //= 2
    return held


def sum_pairs(value, axis, count):
    if count == 1:
        return value
    place = lax.axis_index(axis)
    upper = (place & 1) != 0
    half = value.shape[0] // 2
    low, high = value[:half], value[half:]
    kept = jnp.where(upper, high, low)
    held = kept + lax.ppermute(jnp.where(upper, low, high), axis, swap(count, 1))
    bit = 2
    while bit < count:
        held = held + lax.ppermute(held, axis, swap(count, bit))
        bit *= 2
    other = lax.ppermute(held, axis, swap(count, 1))
    return pair_order(held, other, upper)


def scatter_sum(value, axis, count):
    place = lax.axis_index(axis)
    total = lax.dynamic_index_in_dim(value, place, 0, keepdims=False)
    for shift in range(1, count):
        target = lax.rem(place + shift, count)
        part = lax.dynamic_index_in_dim(value, target, 0, keepdims=False)
        total = total + lax.ppermute(part, axis, turn(count, shift))
    return total


def shards(embeddings, targets, gram_prior, penalty):
    row_count = embeddings.shape[0]
    block_width = embeddings.shape[3]
    head_count = targets.shape[1]
    data_count = lax.axis_size("dp")
    trow_count = lax.axis_size("trow")
    tcol_count = lax.axis_size("tcol")
    piece_rows = block_width // data_count
    total_rows = row_count * data_count
    tile_rows = tcol_count * piece_rows
    data_place = lax.axis_index("dp")
    trow_place = lax.axis_index("trow")
    tcol_place = lax.axis_index("tcol")
    upper = (tcol_place & 1) != 0
    head_half = head_count // 2

    own = embeddings.reshape(row_count, block_width).T
    heads = targets.T
    head_part = jnp.where(upper, heads[head_half:], heads[:head_half])
    carried = jnp.concatenate([own, head_part], axis=0)
    groups = [carried]
    for _ in range(1, data_count):
        groups.append(lax.ppermute(groups[-1], "dp", turn(data_count, 1)))
    own_groups = [group[:block_width] for group in groups]
    blocks = [jnp.concatenate(own_groups, axis=1)]
    for shift in range(1, trow_count):
        blocks.append(
            jnp.concatenate(
                [lax.ppermute(group, "trow", turn(trow_count, shift)) for group in own_groups], axis=1
            )
        )
    head_own = jnp.concatenate([group[block_width:] for group in groups], axis=1)
    head_other = lax.ppermute(head_own, "tcol", swap(tcol_count, 1))
    all_heads = pair_order(head_own, head_other, upper)
    stacked = jnp.stack(blocks)
    order = lax.rem(trow_place - jnp.arange(trow_count) + trow_count, trow_count)
    columns = jnp.take(stacked, order, axis=0).reshape(trow_count * block_width, total_rows)
    piece = lax.dynamic_slice_in_dim(blocks[0], data_place * piece_rows, piece_rows, axis=0)
    panel = gather_pairs(piece, "tcol", tcol_count).reshape(tile_rows, total_rows)

    summed = lax.dot_general(panel, columns, NT, preferred_element_type=jnp.float32)
    gram_tile = gram_prior.reshape(tile_rows, trow_count * block_width) + summed / total_rows
    right_columns = lax.dot_general(columns, all_heads, NT, preferred_element_type=jnp.float32) / total_rows
    right_rows = lax.dot_general(panel, all_heads, NT, preferred_element_type=jnp.float32) / total_rows

    def own_rows(value):
        return lax.dynamic_slice_in_dim(value, tcol_place * piece_rows, piece_rows, axis=0)

    penalty_rows = penalty.reshape(piece_rows, 1)
    start = own_rows(right_rows)
    rows_part = jnp.dot(gram_tile, right_columns, precision=lax.Precision.HIGH)
    rows_part = lax.dynamic_update_slice_in_dim(
        rows_part, own_rows(rows_part) + penalty_rows * start, tcol_place * piece_rows, axis=0
    )
    image_rows = sum_pairs(rows_part, "tcol", tcol_count)
    image = own_rows(image_rows)
    partial = lax.dot_general(
        gram_tile, image_rows, (((0,), (0,)), ((), ())), precision=lax.Precision.HIGH
    )
    partial = partial.reshape(trow_count, data_count * piece_rows, head_count)
    second = scatter_sum(partial, "trow", trow_count).reshape(data_count, piece_rows, head_count)
    second = scatter_sum(second, "dp", data_count) + penalty_rows * image

    def sums(*pairs):
        return jnp.stack([jnp.sum(a * b, axis=0) for a, b in pairs])

    early = all_sum(sums((start, start), (start, image)), ("dp", "trow", "tcol"))
    norm, curvature = early[0], early[1]
    step = norm / curvature
    residual = start - step * image
    applied = image - step * second
    late = all_sum(sums((residual, residual), (residual, applied), (residual, image)), ("dp", "trow", "tcol"))
    ratio = late[0] / norm
    direction = residual + ratio * start
    moved = applied + ratio * image
    next_step = late[0] / (late[1] + ratio * late[2])
    weights = step * start + next_step * direction
    residual = residual - next_step * moved
    out_shape = (1, 1, 1, piece_rows, head_count)
    return (gram_tile.reshape(gram_prior.shape), weights.reshape(out_shape), residual.reshape(out_shape))


def solution(mesh):
    placed = (
        P("dp", "tcol", "trow", None),
        P("dp", None),
        P(None, "trow", "dp", None, "tcol"),
        P("tcol", "trow", "dp", None),
    )
    return jax.shard_map(
        shards,
        mesh=mesh,
        in_specs=placed,
        out_specs=(
            P(None, "trow", "dp", None, "tcol"),
            P("tcol", "trow", "dp", None, None),
            P("tcol", "trow", "dp", None, None),
        ),
        check_vma=False,
    )
```

time: 412 us -> 169 us (0.41)
  blocking collectives: 156 us -> 13.3 us
  waiting for transfers between devices: 180 us -> 99.1 us
  starting transfers between devices: 0.48 us -> 18.2 us
  matrix products: 29.8 us -> 12.6 us
  between operations: 15.7 us -> 1.17 us
  local copies, waits for them, and re-layouts: 19.8 us -> 7.42 us
  other arithmetic: 9.43 us -> 16.3 us
    all_gather x4 -> x0, waiting for transfers between devices: 137 us -> none  [the longest x1 65.3 us: shards(): lax.all_gather(columns, 'dp', axis=0, tiled=True)]
    psum x3 -> x0, blocking collectives: 120 us -> none  [the longest x2 80.4 us: squared_norm(): return lax.psum(column_sums(vector, vector), ('dp', 'trow', 'tcol'))]
    ppermute x0 -> x17, waiting for transfers between devices: none -> 84.6 us  [the longest x3 37.2 us: shards(): groups.append(lax.ppermute(groups[-1], 'dp', turn(data_count, 1)))]
    reduce_scatter x3 -> x0, waiting for transfers between devices: 42.8 us -> none  [the longest x2 42.8 us: shards(): lax.psum_scatter(contribution, 'tcol', scatter_dimension=0, tiled=True)]
    dot_general x4 -> x5, matrix products: 29.8 us -> 12.6 us  [the longest x1 6.24 us: shards(): lax.dot_general(gram_tile, image_rows, (((0,), (0,)), ((), ())), precisio...]
    reshape x2 -> x0, local copies, waits for them, and re-layouts: 15.8 us -> none  [shards(): gram_tile = gram_new.reshape(tile_rows, trow_count, data_count, piece_rows)]
    ppermute x0 -> x17, starting transfers between devices: none -> 15.7 us  [the longest x4 5.45 us: scatter_sum(): total = total + lax.ppermute(part, axis, turn(count, shift))]
    all_to_all x1, blocking collectives: 27.8 us -> 13.3 us  [all_sum(): lax.all_to_all(spread, axis_names, split_axis=0, concat_axis=0, tiled=True)]
  transfers between devices with their start and end apart: 7 -> 18, of which waited for: 6 -> 12; matrix products, arithmetic and copies ran while one was open for 7% -> 10% of each run, Pallas kernels for 0% -> 0%
where the time goes in v1:
time: 169 us; the launch traced here: 168 us
  waiting for transfers between devices  99.1 us (59%)
  starting transfers between devices  18.2 us (11%)
  other arithmetic  16.3 us (10%)
  blocking collectives  13.3 us (8%)
  matrix products  12.6 us (7%)
  local copies, waits for them, and re-layouts  7.42 us (4%)
    ppermute x3, waiting for transfers between devices, shards(): groups.append(lax.ppermute(groups[-1], 'dp', turn(data_count, 1)))  37.2 us
    ppermute x4, waiting for transfers between devices, shards(): lax.ppermute(group, 'trow', turn(trow_count, shift))  15.4 us
    all_to_all x1, waiting for transfers between devices, all_sum(): lax.all_to_all(spread, axis_names, split_axis=0, concat_axis=0, tiled=True)  14.5 us
    ppermute x4, waiting for transfers between devices, scatter_sum(): total = total + lax.ppermute(part, axis, turn(count, shift))  13.4 us
    all_to_all x1, blocking collectives, all_sum(): lax.all_to_all(spread, axis_names, split_axis=0, concat_axis=0, tiled=True)  13.3 us
    ppermute x1, waiting for transfers between devices, sum_pairs(): held = held + lax.ppermute(held, axis, swap(count, bit))  10.1 us
    dot_general x1, matrix products, shards(): lax.dot_general(gram_tile, image_rows, (((0,), (0,)), ((), ())), precisio...  6.24 us
    ppermute x4, starting transfers between devices, scatter_sum(): total = total + lax.ppermute(part, axis, turn(count, shift))  5.45 us
  transfers between devices with their start and end apart: 18, of which 12 were waited for; matrix products, arithmetic and copies ran while one was open for 10% of the time, Pallas kernels for 0%

profile of v1, /device:TPU:0, one launch (start us, length us, event | category | flops | bytes accessed | tf_op | source)
XLA Modules:
  0.0 168.2 jit_solution(5443675975227339757)
XLA Ops:
  1.6 1.2 copy.19
  2.9 3.1 %collective-permute-start = (bf16[896,256]{1,0:T(8,128)(2,1)S(1)}, bf16[896,256]{1,0:T(8,128)(2,1)S(1)}, u32[]{:S(2)}, u32[]{:S(2)}) collective-permute-start(bf16[896,256]{1,0:T(8,128)(2,1)S(1)} %pad_maximum_fusion.6), channel_id=1, source_target_pairs={{0,8},{8,16},{16,24},{24,0},{1,9},{9,17},{17,25},{25,1},{2,10},{10... | collective-permute-start | bytes 1376264 | tf_op jit(solution)/shard_map/ppermute | solution.py:97
  6.0 12.5 %collective-permute-done = bf16[896,256]{1,0:T(8,128)(2,1)S(1)} collective-permute-done((bf16[896,256]{1,0:T(8,128)(2,1)S(1)}, bf16[896,256]{1,0:T(8,128)(2,1)S(1)}, u32[]{:S(2)}, u32[]{:S(2)}) %collective-permute-start) | collective-permute-done | bytes 458784 | tf_op jit(solution)/shard_map/ppermute | solution.py:97
  18.5 13.5 %collective-permute-done.1 = bf16[896,256]{1,0:T(8,128)(2,1)S(1)} collective-permute-done((bf16[896,256]{1,0:T(8,128)(2,1)S(1)}, bf16[896,256]{1,0:T(8,128)(2,1)S(1)}, u32[]{:S(2)}, u32[]{:S(2)}) %collective-permute-start.1) | collective-permute-done | bytes 458784 | tf_op jit(solution)/shard_map/ppermute | solution.py:97
  32.0 1.3 collective-permute-start.5
  33.4 11.2 %collective-permute-done.2 = bf16[896,256]{1,0:T(8,128)(2,1)S(1)} collective-permute-done((bf16[896,256]{1,0:T(8,128)(2,1)S(1)}, bf16[896,256]{1,0:T(8,128)(2,1)S(1)}, u32[]{:S(2)}, u32[]{:S(2)}) %collective-permute-start.2) | collective-permute-done | bytes 458784 | tf_op jit(solution)/shard_map/ppermute | solution.py:97
  47.8 1.6 collective-permute-start.6
  49.8 1.5 collective-permute-start.8
  51.4 1.9 %broadcast_select_fusion.2 = (bf16[128,1024]{1,0:T(8,128)(2,1)}, bf16[128,1024]{1,0:T(8,128)(2,1)}) fusion(bf16[128,1024]{1,0:T(8,128)(2,1)} %collective-permute-done.9, pred[]{:T(512)S(6)} %ne.8, bf16[128,256]{1,0:T(8,128)(2,1)} %copy-done.12, bf16[128,256]{1,0:T(8,128)(2,1)} %copy-done.11, bf16[128,256]{1,0:T(8,128)(2,1)} %copy-done.10, ...), kind=kLoop, calls=%fused_computation.28 | loop fusion | flops 1310720 | bytes 1048577 | tf_op jit(solution)/shard_map/jit(_where)/select_n | solution.py:27
  53.3 5.2 %collective-permute-done.3 = bf16[1,192,1024]{2,1,0:T(8,128)(2,1)} collective-permute-done((bf16[1,192,1024]{2,1,0:T(8,128)(2,1)}, bf16[1,192,1024]{2,1,0:T(8,128)(2,1)}, u32[]{:S(2)}, u32[]{:S(2)}) %collective-permute-start.3) | collective-permute-done | bytes 393248 | tf_op jit(solution)/shard_map/ppermute | solution.py:38
  58.5 1.2 select_bitcast_fusion.3
  60.7 7.7 %collective-permute-done.7 = bf16[768,256]{1,0:T(8,128)(2,1)S(1)} collective-permute-done((bf16[768,256]{1,0:T(8,128)(2,1)}, bf16[768,256]{1,0:T(8,128)(2,1)S(1)}, u32[]{:S(2)}, u32[]{:S(2)}) %collective-permute-start.7) | collective-permute-done | bytes 393248 | tf_op jit(solution)/shard_map/ppermute | solution.py:103
  68.4 7.7 %collective-permute-done.8 = bf16[768,256]{1,0:T(8,128)(2,1)S(1)} collective-permute-done((bf16[768,256]{1,0:T(8,128)(2,1)}, bf16[768,256]{1,0:T(8,128)(2,1)S(1)}, u32[]{:S(2)}, u32[]{:S(2)}) %collective-permute-start.8) | collective-permute-done | bytes 393248 | tf_op jit(solution)/shard_map/ppermute | solution.py:103
  76.1 1.2 maximum_bitcast_fusion
  77.3 1.9 %pad_maximum_fusion = bf16[2,768,1024]{2,1,0:T(8,128)(2,1)} fusion(bf16[1,768,1024]{2,1,0:T(8,128)(2,1)S(1)} %maximum_bitcast_fusion, bf16[1,768,1024]{2,1,0:T(8,128)(2,1)S(1)} %get-tuple-element.28), kind=kLoop, calls=%fused_computation.2 | loop fusion | flops 1572864 | bytes 6291456 | tf_op jit(solution)/shard_map/stack | solution.py:109
  79.3 2.6 %gather_fusion = bf16[2,768,1024]{2,1,0:T(8,128)(2,1)S(1)} fusion(bf16[2,768,1024]{2,1,0:T(8,128)(2,1)} %pad_maximum_fusion, s32[1024]{0:T(1024)S(1)} %pad_clamp_fusion), kind=kCustom, calls=%fused_computation | custom fusion | bytes 6291464 | tf_op jit(solution)/shard_map/jit(_take)/gather | solution.py:111
  81.9 1.1 bitcast_select_fusion
  85.2 1.8 %select_bitcast_fusion.1 = (bf16[2,1,192,1024]{3,2,1,0:T(8,128)(2,1)S(1)}, bf16[2,1,192,1024]{3,2,1,0:T(8,128)(2,1)S(1)}) fusion(bf16[2,192,1024]{2,1,0:T(8,128)(2,1)} %collective-permute-done.4, pred[]{:T(512)S(6)} %ne.8, bf16[1,1,192,1024]{3,2,1,0:T(8,128)(2,1)S(1)} %copy-done.4, bf16[1,1,192,1024]{3,2,1,0:T(8,128)(2,1)S(1)} %copy-done.2), kind=kLoop, calls=%fused_computation.17 | loop fusion | flops 1179648 | bytes 3145729 | tf_op jit(solution)/shard_map/stack | solution.py:42
  87.8 2.7 %bitcast_add_fusion = f32[768,1536]{1,0:T(8,128)S(1)} fusion(f32[4,1,1,192,1536]{4,3,2,1,0:T(8,128)S(1)} %bitcast.108, bf16[768,1024]{1,0:T(8,128)(2,1)S(1)} %bitcast.94, bf16[1536,1024]{1,0:T(8,128)(2,1)S(1)} %bitcast.92), kind=kOutput, calls=%fused_computation.1 | convolution fusion | flops 2418278400 | bytes 14155776 | tf_op jit(solution)/shard_map/dot_general | solution.py:115
  90.5 2.1 %fusion.19 = f32[768,256]{1,0:T(8,128)S(1)} fusion(f32[768,1536]{1,0:T(8,128)S(1)} %bitcast_add_fusion, f32[1536,256]{1,0:T(8,128)S(1)} %convolution_multiply_fusion), kind=kOutput, calls=%fused_computation.74 | convolution fusion | flops 1811939328 | bytes 7077888 | tf_op jit(solution)/shard_map/dot_general | solution.py:125
  92.9 1.7 %collective-permute-done.10 = f32[384,256]{1,0:T(8,128)S(1)} collective-permute-done((f32[384,256]{1,0:T(8,128)S(1)}, f32[384,256]{1,0:T(8,128)S(1)}, u32[]{:S(2)}, u32[]{:S(2)}) %collective-permute-start.10) | collective-permute-done | bytes 393248 | tf_op jit(solution)/shard_map/ppermute | solution.py:56
  95.8 10.1 %collective-permute-done.11 = f32[384,256]{1,0:T(8,128)S(1)} collective-permute-done((f32[384,256]{1,0:T(8,128)S(1)}, f32[384,256]{1,0:T(8,128)S(1)}, u32[]{:S(2)}, u32[]{:S(2)}) %collective-permute-start.11) | collective-permute-done | bytes 393248 | tf_op jit(solution)/shard_map/ppermute | solution.py:59
  106.1 1.7 %collective-permute-done.12 = f32[384,256]{1,0:T(8,128)S(1)} collective-permute-done((f32[384,256]{1,0:T(8,128)S(1)}, f32[384,256]{1,0:T(8,128)S(1)}, u32[]{:S(2)}, u32[]{:S(2)}) %collective-permute-start.12) | collective-permute-done | bytes 393248 | tf_op jit(solution)/shard_map/ppermute | solution.py:61
  107.8 6.2 %fusion = f32[1536,256]{1,0:T(8,128)S(1)} fusion(f32[768,1536]{1,0:T(8,128)} %copy-done, f32[384,256]{1,0:T(8,128)S(1)} %get-tuple-element.36, f32[384,256]{1,0:T(8,128)S(1)} %get-tuple-element.35), kind=kOutput, calls=%fused_computation.12 | convolution fusion | flops 1812135936 | bytes 7077888 | tf_op jit(solution)/shard_map/dot_general | solution.py:131
  114.2 1.6 collective-permute-start.13
  117.4 2.6 %all-to-all-start = ((f32[32,2,256]{2,1,0:T(2,128)}), f32[32,2,256]{2,1,0:T(2,128)S(1)}, u32[]{:S(2)}, u32[]{:S(2)}) async-start(f32[32,2,256]{2,1,0:T(2,128)} %broadcast_in_dim.47), calls=%async_computation | async-start | bytes 131072 | tf_op jit(solution)/shard_map/all_to_all | solution.py:23
  120.0 14.5 %all-to-all-done = f32[32,2,256]{2,1,0:T(2,128)S(1)} async-done(((f32[32,2,256]{2,1,0:T(2,128)}), f32[32,2,256]{2,1,0:T(2,128)S(1)}, u32[]{:S(2)}, u32[]{:S(2)}) %all-to-all-start) | async-done | bytes 65568 | tf_op jit(solution)/shard_map/all_to_all | solution.py:23
  134.9 3.7 %collective-permute-start.16 = (f32[192,256]{1,0:T(8,128)S(1)}, f32[192,256]{1,0:T(8,128)S(1)}, u32[]{:S(2)}, u32[]{:S(2)}) collective-permute-start(f32[192,256]{1,0:T(8,128)S(1)} %get-tuple-element.33), channel_id=1, source_target_pairs={{0,24},{8,0},{16,8},{24,16},{1,25},{9,1},{17,9},{25,17},{2,26},{10... | collective-permute-start | bytes 589832 | tf_op jit(solution)/shard_map/ppermute | solution.py:71
  138.6 5.9 %collective-permute-done.14 = f32[192,256]{1,0:T(8,128)S(1)} collective-permute-done((f32[192,256]{1,0:T(8,128)S(1)}, f32[192,256]{1,0:T(8,128)S(1)}, u32[]{:S(2)}, u32[]{:S(2)}) %collective-permute-start.14) | collective-permute-done | bytes 196640 | tf_op jit(solution)/shard_map/ppermute | solution.py:71
  144.5 7.5 %collective-permute-done.15 = f32[192,256]{1,0:T(8,128)S(1)} collective-permute-done((f32[192,256]{1,0:T(8,128)S(1)}, f32[192,256]{1,0:T(8,128)S(1)}, u32[]{:S(2)}, u32[]{:S(2)}) %collective-permute-start.15) | collective-permute-done | bytes 196640 | tf_op jit(solution)/shard_map/ppermute | solution.py:71
  153.1 13.3 %all_to_all.10 = f32[32,3,256]{2,1,0:T(4,128)S(1)} all-to-all(f32[32,3,256]{2,1,0:T(4,128)S(1)} %broadcast_in_dim.48), channel_id=1, replica_groups=mesh['dp'=4,'trow'=2,'tcol'=4] {'dp','trow','tcol'}, dimensions={0} | all-to-all | bytes 196608 | tf_op jit(solution)/shard_map/all_to_all | solution.py:23
  166.4 1.7 %subtract_bitcast_fusion = (f32[1,1,1,192,256]{4,3,2,1,0:T(8,128)}, f32[1,1,1,192,256]{4,3,2,1,0:T(8,128)}) fusion(f32[192,256]{1,0:T(8,128)S(1)} %get-tuple-element.26, f32[192,256]{1,0:T(8,128)S(1)} %get-tuple-element.25, f32[192,256]{1,0:T(8,128)S(1)} %get-tuple-element.27, f32[256]{0:T(256)S(1)} %bitcast.104, f32[256]{0:T(256)S(1)} %bitcast.103, ...), kind=kLoop, calls=%fused_computation.37 | loop fusion | flops 491520 | bytes 1182724 | tf_op jit(solution)/shard_map/reshape | solution.py:154
  (94 shorter events, 13.6 us)
Async XLA Ops:
  2.8 42.5 %copy-start.8 = (bf16[128,256]{1,0:T(8,128)(2,1)}, bf16[128,256]{1,0:T(8,128)(2,1)S(1)}, u32[]{:S(2)}) copy-start(bf16[128,256]{1,0:T(8,128)(2,1)S(1)} %slice_select_fusion.1) | copy-start | bytes 196612
  2.9 15.6 %collective-permute-start = (bf16[896,256]{1,0:T(8,128)(2,1)S(1)}, bf16[896,256]{1,0:T(8,128)(2,1)S(1)}, u32[]{:S(2)}, u32[]{:S(2)}) collective-permute-start(bf16[896,256]{1,0:T(8,128)(2,1)S(1)} %pad_maximum_fusion.6), channel_id=1, source_target_pairs={{0,8},{8,16},{16,24},{24,0},{1,9},{9,17},{17,25},{25,1},{2,10},{10... | collective-permute-start | bytes 1376264 | tf_op jit(solution)/shard_map/ppermute | solution.py:97
  18.5 13.5 %collective-permute-start.1 = (bf16[896,256]{1,0:T(8,128)(2,1)S(1)}, bf16[896,256]{1,0:T(8,128)(2,1)S(1)}, u32[]{:S(2)}, u32[]{:S(2)}) collective-permute-start(bf16[896,256]{1,0:T(8,128)(2,1)S(1)} %collective-permute-done), channel_id=1, source_target_pairs={{0,8},{8,16},{16,24},{24,0},{1,9},{9,17},{17,25},{25,1},{2,10},{10... | collective-permute-start | bytes 1376264 | tf_op jit(solution)/shard_map/ppermute | solution.py:97
  32.0 12.6 %collective-permute-start.2 = (bf16[896,256]{1,0:T(8,128)(2,1)S(1)}, bf16[896,256]{1,0:T(8,128)(2,1)S(1)}, u32[]{:S(2)}, u32[]{:S(2)}) collective-permute-start(bf16[896,256]{1,0:T(8,128)(2,1)S(1)} %collective-permute-done.1), channel_id=1, source_target_pairs={{0,8},{8,16},{16,24},{24,0},{1,9},{9,17},{17,25},{25,1},{2,10},{10... | collective-permute-start | bytes 1376264 | tf_op jit(solution)/shard_map/ppermute | solution.py:97
  32.0 28.7 %collective-permute-start.5 = (bf16[768,256]{1,0:T(8,128)(2,1)S(1)}, bf16[768,256]{1,0:T(8,128)(2,1)}, u32[]{:S(2)}, u32[]{:S(2)}) collective-permute-start(bf16[768,256]{1,0:T(8,128)(2,1)S(1)} %bitcast.88), channel_id=1, source_target_pairs={{0,4},{4,0},{1,5},{5,1},{2,6},{6,2},{3,7},{7,3},{8,12},{12,8},{9,1... | collective-permute-start | bytes 1179656 | tf_op jit(solution)/shard_map/ppermute | solution.py:103
  33.3 12.0 %copy-start.10 = (bf16[128,256]{1,0:T(8,128)(2,1)}, bf16[128,256]{1,0:T(8,128)(2,1)S(1)}, u32[]{:S(2)}) copy-start(bf16[128,256]{1,0:T(8,128)(2,1)S(1)} %slice.68) | copy-start | bytes 196612
  33.4 12.5 %copy-start.6 = (bf16[768,256]{1,0:T(8,128)(2,1)}, bf16[768,256]{1,0:T(8,128)(2,1)S(1)}, u32[]{:S(2)}) copy-start(bf16[768,256]{1,0:T(8,128)(2,1)S(1)} %slice.65) | copy-start | bytes 1179652
  33.4 12.0 %copy-start.11 = (bf16[128,256]{1,0:T(8,128)(2,1)}, bf16[128,256]{1,0:T(8,128)(2,1)S(1)}, u32[]{:S(2)}) copy-start(bf16[128,256]{1,0:T(8,128)(2,1)S(1)} %slice.69) | copy-start | bytes 196612
  33.4 13.2 %copy-start.5 = (bf16[768,256]{1,0:T(8,128)(2,1)}, bf16[768,256]{1,0:T(8,128)(2,1)S(1)}, u32[]{:S(2)}) copy-start(bf16[768,256]{1,0:T(8,128)(2,1)S(1)} %slice.66) | copy-start | bytes 1179652
  45.3 4.5 %collective-permute-start.9 = (bf16[128,1024]{1,0:T(8,128)(2,1)}, bf16[128,1024]{1,0:T(8,128)(2,1)}, u32[]{:S(2)}, u32[]{:S(2)}) collective-permute-start(bf16[128,1024]{1,0:T(8,128)(2,1)} %pad_maximum_fusion.9), channel_id=1, source_target_pairs={{0,1},{1,0},{2,3},{3,2},{4,5},{5,4},{6,7},{7,6},{8,9},{9,8},{10,11... | collective-permute-start | bytes 786440 | tf_op jit(solution)/shard_map/ppermute | solution.py:107
  45.4 2.2 %copy-start.7 = (bf16[768,256]{1,0:T(8,128)(2,1)}, bf16[768,256]{1,0:T(8,128)(2,1)S(1)}, u32[]{:S(2)}) copy-start(bf16[768,256]{1,0:T(8,128)(2,1)S(1)} %slice.67) | copy-start | bytes 1179652
  46.6 11.8 %collective-permute-start.3 = (bf16[1,192,1024]{2,1,0:T(8,128)(2,1)}, bf16[1,192,1024]{2,1,0:T(8,128)(2,1)}, u32[]{:S(2)}, u32[]{:S(2)}) collective-permute-start(bf16[1,192,1024]{2,1,0:T(8,128)(2,1)} %dynamic-slice_bitcast_fusion.1), channel_id=1, source_target_pairs={{0,2},{1,3},{2,0},{3,1},{4,6},{5,7},{6,4},{7,5},{8,10},{9,11},{10,... | collective-permute-start | bytes 1179656 | tf_op jit(solution)/shard_map/ppermute | solution.py:38
  47.8 13.0 %collective-permute-start.6 = (bf16[768,256]{1,0:T(8,128)(2,1)}, bf16[768,256]{1,0:T(8,128)(2,1)S(1)}, u32[]{:S(2)}, u32[]{:S(2)}) collective-permute-start(bf16[768,256]{1,0:T(8,128)(2,1)} %copy-done.6), channel_id=1, source_target_pairs={{0,4},{4,0},{1,5},{5,1},{2,6},{6,2},{3,7},{7,3},{8,12},{12,8},{9,1... | collective-permute-start | bytes 1179656 | tf_op jit(solution)/shard_map/ppermute | solution.py:103
  49.3 19.1 %collective-permute-start.7 = (bf16[768,256]{1,0:T(8,128)(2,1)}, bf16[768,256]{1,0:T(8,128)(2,1)S(1)}, u32[]{:S(2)}, u32[]{:S(2)}) collective-permute-start(bf16[768,256]{1,0:T(8,128)(2,1)} %copy-done.5), channel_id=1, source_target_pairs={{0,4},{4,0},{1,5},{5,1},{2,6},{6,2},{3,7},{7,3},{8,12},{12,8},{9,1... | collective-permute-start | bytes 1179656 | tf_op jit(solution)/shard_map/ppermute | solution.py:103
  49.8 26.3 %collective-permute-start.8 = (bf16[768,256]{1,0:T(8,128)(2,1)}, bf16[768,256]{1,0:T(8,128)(2,1)S(1)}, u32[]{:S(2)}, u32[]{:S(2)}) collective-permute-start(bf16[768,256]{1,0:T(8,128)(2,1)} %copy-done.7), channel_id=1, source_target_pairs={{0,4},{4,0},{1,5},{5,1},{2,6},{6,2},{3,7},{7,3},{8,12},{12,8},{9,1... | collective-permute-start | bytes 1179656 | tf_op jit(solution)/shard_map/ppermute | solution.py:103
  59.6 8.8 %copy-start.1 = (bf16[1,1,192,1024]{3,2,1,0:T(8,128)(2,1)}, bf16[1,1,192,1024]{3,2,1,0:T(8,128)(2,1)S(1)}, u32[]{:S(2)}) copy-start(bf16[1,1,192,1024]{3,2,1,0:T(8,128)(2,1)S(1)} %get-tuple-element.37) | copy-start | bytes 1179652
  59.7 8.8 %copy-start.3 = (bf16[1,1,192,1024]{3,2,1,0:T(8,128)(2,1)}, bf16[1,1,192,1024]{3,2,1,0:T(8,128)(2,1)S(1)}, u32[]{:S(2)}) copy-start(bf16[1,1,192,1024]{3,2,1,0:T(8,128)(2,1)S(1)} %get-tuple-element.38) | copy-start | bytes 1179652
  60.7 23.8 %collective-permute-start.4 = (bf16[2,192,1024]{2,1,0:T(8,128)(2,1)}, bf16[2,192,1024]{2,1,0:T(8,128)(2,1)}, u32[]{:S(2)}, u32[]{:S(2)}) collective-permute-start(bf16[2,192,1024]{2,1,0:T(8,128)(2,1)} %maximum_bitcast_fusion.1), channel_id=1, source_target_pairs={{0,1},{1,0},{2,3},{3,2},{4,5},{5,4},{6,7},{7,6},{8,9},{9,8},{10,11... | collective-permute-start | bytes 2359304 | tf_op jit(solution)/shard_map/ppermute | solution.py:38
  81.9 1.2 copy-start.13
  84.2 3.7 %slice-start = ((s8[4718592]{0:T(1024)(128)(4,1)}), s8[4194304]{0:T(1024)(128)(4,1)S(1)}, s32[]{:S(2)}) async-start(s8[4718592]{0:T(1024)(128)(4,1)} %bitcast.107), calls=%async_computation.2 | async-start | bytes 8388608
  84.5 3.3 %slice-start.1 = ((s8[4718592]{0:T(1024)(128)(4,1)}), s8[524288]{0:T(1024)(128)(4,1)S(1)}, s32[]{:S(2)}) async-start(s8[4718592]{0:T(1024)(128)(4,1)} %bitcast.107), calls=%async_computation.3 | async-start | bytes 1048576
  87.8 4.9 %copy-start.9 = (f32[768,256]{1,0:T(8,128)}, f32[768,256]{1,0:T(8,128)S(1)}, u32[]{:S(2)}) copy-start(f32[768,256]{1,0:T(8,128)S(1)} %fusion.1) | copy-start | bytes 2359300
  90.5 2.2 %copy-start = (f32[768,1536]{1,0:T(8,128)}, f32[768,1536]{1,0:T(8,128)S(1)}, u32[]{:S(2)}) copy-start(f32[768,1536]{1,0:T(8,128)S(1)} %bitcast_add_fusion) | copy-start | bytes 14155780
  90.5 2.2 %copy-start.15 = (f32[1,1,1,192]{3,2,1,0:T(1,128)S(1)}, f32[1,1,1,192]{3,2,1,0:T(1,128)}, u32[]{:S(2)}) copy-start(f32[1,1,1,192]{3,2,1,0:T(1,128)} %param.7) | copy-start | bytes 2308
  92.9 1.8 %collective-permute-start.10 = (f32[384,256]{1,0:T(8,128)S(1)}, f32[384,256]{1,0:T(8,128)S(1)}, u32[]{:S(2)}, u32[]{:S(2)}) collective-permute-start(f32[384,256]{1,0:T(8,128)S(1)} %slice_select_fusion), channel_id=1, source_target_pairs={{0,1},{1,0},{2,3},{3,2},{4,5},{5,4},{6,7},{7,6},{8,9},{9,8},{10,11... | collective-permute-start | bytes 1179656 | tf_op jit(solution)/shard_map/ppermute | solution.py:56
  94.7 11.2 %collective-permute-start.11 = (f32[384,256]{1,0:T(8,128)S(1)}, f32[384,256]{1,0:T(8,128)S(1)}, u32[]{:S(2)}, u32[]{:S(2)}) collective-permute-start(f32[384,256]{1,0:T(8,128)S(1)} %select_add_fusion), channel_id=1, source_target_pairs={{0,2},{1,3},{2,0},{3,1},{4,6},{5,7},{6,4},{7,5},{8,10},{9,11},{10,... | collective-permute-start | bytes 1179656 | tf_op jit(solution)/shard_map/ppermute | solution.py:59
  106.0 1.8 %collective-permute-start.12 = (f32[384,256]{1,0:T(8,128)S(1)}, f32[384,256]{1,0:T(8,128)S(1)}, u32[]{:S(2)}, u32[]{:S(2)}) collective-permute-start(f32[384,256]{1,0:T(8,128)S(1)} %add.119), channel_id=1, source_target_pairs={{0,1},{1,0},{2,3},{3,2},{4,5},{5,4},{6,7},{7,6},{8,9},{9,8},{10,11... | collective-permute-start | bytes 1179656 | tf_op jit(solution)/shard_map/ppermute | solution.py:61
  114.2 20.4 %collective-permute-start.13 = (f32[768,256]{1,0:T(8,128)S(1)}, f32[768,256]{1,0:T(8,128)S(1)}, u32[]{:S(2)}, u32[]{:S(2)}) collective-permute-start(f32[768,256]{1,0:T(8,128)S(1)} %dynamic-slice_bitcast_fusion), channel_id=1, source_target_pairs={{0,4},{4,0},{1,5},{5,1},{2,6},{6,2},{3,7},{7,3},{8,12},{12,8},{9,1... | collective-permute-start | bytes 2359304 | tf_op jit(solution)/shard_map/ppermute | solution.py:71
  117.4 17.1 %all-to-all-start = ((f32[32,2,256]{2,1,0:T(2,128)}), f32[32,2,256]{2,1,0:T(2,128)S(1)}, u32[]{:S(2)}, u32[]{:S(2)}) async-start(f32[32,2,256]{2,1,0:T(2,128)} %broadcast_in_dim.47), calls=%async_computation | async-start | bytes 131072 | tf_op jit(solution)/shard_map/all_to_all | solution.py:23
  134.7 9.8 %collective-permute-start.14 = (f32[192,256]{1,0:T(8,128)S(1)}, f32[192,256]{1,0:T(8,128)S(1)}, u32[]{:S(2)}, u32[]{:S(2)}) collective-permute-start(f32[192,256]{1,0:T(8,128)S(1)} %get-tuple-element.32), channel_id=1, source_target_pairs={{0,8},{8,16},{16,24},{24,0},{1,9},{9,17},{17,25},{25,1},{2,10},{10... | collective-permute-start | bytes 589832 | tf_op jit(solution)/shard_map/ppermute | solution.py:71
  134.8 17.2 %collective-permute-start.15 = (f32[192,256]{1,0:T(8,128)S(1)}, f32[192,256]{1,0:T(8,128)S(1)}, u32[]{:S(2)}, u32[]{:S(2)}) collective-permute-start(f32[192,256]{1,0:T(8,128)S(1)} %get-tuple-element.34), channel_id=1, source_target_pairs={{0,16},{8,24},{16,0},{24,8},{1,17},{9,25},{17,1},{25,9},{2,18},{10... | collective-permute-start | bytes 589832 | tf_op jit(solution)/shard_map/ppermute | solution.py:71
  134.9 17.1 %collective-permute-start.16 = (f32[192,256]{1,0:T(8,128)S(1)}, f32[192,256]{1,0:T(8,128)S(1)}, u32[]{:S(2)}, u32[]{:S(2)}) collective-permute-start(f32[192,256]{1,0:T(8,128)S(1)} %get-tuple-element.33), channel_id=1, source_target_pairs={{0,24},{8,0},{16,8},{24,16},{1,25},{9,1},{17,9},{25,17},{2,26},{10... | collective-permute-start | bytes 589832 | tf_op jit(solution)/shard_map/ppermute | solution.py:71
  (4 other events, 4.0 us)

commit v2 on v0

v2 whole, which is shorter than its diff:
```python
import functools

import jax
import jax.numpy as jnp
import numpy as np
from jax import lax
from jax.experimental import pallas as pl
from jax.experimental.pallas import tpu as pltpu
from jax.sharding import PartitionSpec as P

NT = (((1,), (1,)), ((), ()))
NN = (((1,), (0,)), ((), ()))
VMEM = pl.BlockSpec(memory_space=pltpu.VMEM)
VMEM_BYTES = 40 * 2**20


def swap(count, bit):
    return [(place, place ^ bit) for place in range(count)]


class Ring:
    def __init__(self, data_count, trow_count):
        self.data_count = data_count
        self.count = data_count * trow_count
        self.cells = []
        for trow in range(trow_count):
            along = range(data_count) if trow % 2 == 0 else reversed(range(data_count))
            self.cells += [(data, trow) for data in along]
        flat = [data * trow_count + trow for data, trow in self.cells]
        self.ahead = [(flat[i], flat[(i + 1) % self.count]) for i in range(self.count)]
        self.back = [(target, source) for source, target in self.ahead]
        self.far = self.count // 2
        self.offsets = [0]
        for distance in range(1, self.far):
            self.offsets += [-distance, distance]
        self.offsets.append(self.far)
        self.place = np.zeros((data_count, trow_count), np.int32)
        for position, (data, trow) in enumerate(self.cells):
            self.place[data, trow] = position
        self.rounds = np.zeros((self.count, data_count), np.int32)
        self.row_chunk = np.zeros((self.count, self.count), np.int32)
        self.row_trow = np.zeros((self.count, self.count), np.int32)
        self.row_data = np.zeros((self.count, self.count), np.int32)
        for position, (data, trow) in enumerate(self.cells):
            first = trow * data_count
            near = sorted(range(first, first + data_count), key=lambda q: (abs(q - position), q))
            chunk_of = {}
            for turn, other in enumerate(near):
                self.rounds[position, turn] = self.offsets.index(other - position)
                chunk_of[self.cells[other][0]] = turn
            for index, offset in enumerate(self.offsets):
                other_data, other_trow = self.cells[(position + offset) % self.count]
                self.row_chunk[position, index] = chunk_of[other_data]
                self.row_trow[position, index] = other_trow
                self.row_data[position, index] = other_data

    def gather(self, value, split_rows):
        ahead = back = value
        shards = [value]
        for _ in range(1, self.far):
            ahead = lax.ppermute(ahead, ("dp", "trow"), self.ahead)
            back = lax.ppermute(back, ("dp", "trow"), self.back)
            shards += [ahead, back]
        half = (split_rows // 2 + 15) // 16 * 16
        low = lax.ppermute(ahead[:half], ("dp", "trow"), self.ahead)
        high = lax.ppermute(back[half:split_rows], ("dp", "trow"), self.back)
        return shards + [low, high]


def split(value):
    high = value.astype(jnp.bfloat16)
    return high, (value - high.astype(jnp.float32)).astype(jnp.bfloat16)


def dot(a, b, dims):
    return lax.dot_general(a, b, dims, preferred_element_type=jnp.float32)


def product(a, b):
    (a_high, a_low), (b_high, b_low) = a, b
    return dot(a_high, b_high, NN) + (dot(a_high, b_low, NN) + dot(a_low, b_high, NN))


def gram_kernel(sizes, meta, *refs):
    n, data_count, trow_count, tcol_count, piece, width, head_part, block, total_rows, groups = sizes
    heads = head_part * tcol_count
    shard_refs = refs[: n + 1]
    round_refs = refs[n + 1 : n + 1 + 3 * groups]
    prior_ref, gram_ref, right_ref, image_ref, columns, rows, target = refs[n + 1 + 3 * groups :]
    step = pl.program_id(0)
    me = meta[2 * n]

    @pl.when(step == 0)
    def _():
        for index in range(n):
            chunk = meta[index]
            base = pl.multiple_of(meta[n + index] * width, 16)
            if index < n - 1:
                columns[chunk, pl.ds(base, width), :] = shard_refs[index][:width, :]
            else:
                half = shard_refs[n - 1].shape[0]
                columns[chunk, pl.ds(base, half), :] = shard_refs[n - 1][...]
                columns[chunk, pl.ds(pl.multiple_of(base + half, 16), width - half), :] = shard_refs[n][...]
        turn = 0
        for group in range(groups):
            own, far, near = round_refs[3 * group : 3 * group + 3]
            for inner in range(own.shape[0]):
                parts = [own[inner]]
                if tcol_count > 1:
                    parts = [own[inner], near[0, inner], far[inner], near[1, inner]]
                for j, part in enumerate(parts):
                    at = pl.multiple_of(jnp.bitwise_xor(me, j) * head_part, 16)
                    target[turn, pl.ds(at, head_part), :] = part[:head_part, :]
                rows[turn] = jnp.concatenate([part[head_part:, :] for part in parts], axis=0)
                turn += 1
        right = dot(rows[0, :piece, :], target[0], NT)
        for chunk in range(1, data_count):
            right += dot(rows[chunk, :piece, :], target[chunk], NT)
        right_ref[...] = right * (1.0 / total_rows)
        image_ref[...] = jnp.zeros_like(image_ref)

    at = pl.ds(pl.multiple_of(step * block, 128), block)
    column_side = dot(columns[0, at, :], target[0], NT)
    summed = dot(rows[0], columns[0, at, :], NT)
    for chunk in range(1, data_count):
        column_side += dot(columns[chunk, at, :], target[chunk], NT)
        summed += dot(rows[chunk], columns[chunk, at, :], NT)
    side = split(column_side * (1.0 / total_rows))
    summed = summed * (1.0 / total_rows)
    tile = []
    for j in range(tcol_count):
        place = pl.ds(pl.multiple_of(jnp.bitwise_xor(me, j) * piece, 8), piece)
        part = prior_ref[place, :] + summed[j * piece : (j + 1) * piece]
        gram_ref[place, :] = part
        tile.append(part)
    image_ref[...] += product(split(jnp.concatenate(tile, axis=0)), side)


def image_kernel(sizes, meta, *refs):
    n, data_count, tcol_count, piece, block = sizes
    shard_refs = refs[: n + 1]
    gram_ref, start_ref, near_ref, far_ref, penalty_ref, out_ref, sums_ref, high, low, total = refs[n + 1 :]
    step = pl.program_id(0)
    me = meta[2 * n]

    @pl.when(step == 0)
    def _():
        for index in range(n):
            base = pl.multiple_of((meta[n + index] * data_count + meta[index]) * piece, 8)
            if index < n - 1:
                parts = [(base, shard_refs[index][...])]
            else:
                half = shard_refs[n - 1].shape[0]
                parts = [(base, shard_refs[n - 1][...]), (base + half, shard_refs[n][...])]
            for start, value in parts:
                place = pl.ds(pl.multiple_of(start, 8), value.shape[0])
                high[place, :] = value.astype(jnp.bfloat16).astype(jnp.float32)
                low[place, :] = value - high[place, :]
        total[...] = jnp.zeros_like(total)

    at = pl.ds(pl.multiple_of(step * block, 128), block)
    side = high[at, :].astype(jnp.bfloat16), low[at, :].astype(jnp.bfloat16)
    total[...] += product(split(gram_ref[...]), side)

    @pl.when(step == pl.num_programs(0) - 1)
    def _():
        own = shard_refs[0][...]
        others = [own, near_ref[0], far_ref[...], near_ref[1]]
        late = jnp.zeros((1, own.shape[1]), jnp.float32)
        for j in range(tcol_count):
            place = pl.ds(pl.multiple_of(jnp.bitwise_xor(me, j) * piece, 8), piece)
            value = total[place, :]
            if j == 0:
                value = value + penalty_ref[...] * own
            out_ref[j] = value
            late = late + jnp.sum(value * others[j], axis=0, keepdims=True)
        start = start_ref[...]
        early = [jnp.sum(a * b, axis=0, keepdims=True) for a, b in ((start, start), (start, own), (own, own))]
        sums_ref[...] = jnp.concatenate(early + [late], axis=0)


def call(body, meta, inputs, grid, in_specs, out_specs, out_shape, scratch, flops, read):
    return pl.pallas_call(
        body,
        grid_spec=pltpu.PrefetchScalarGridSpec(
            num_scalar_prefetch=1,
            grid=(grid,),
            in_specs=in_specs,
            out_specs=out_specs,
            scratch_shapes=scratch,
        ),
        out_shape=out_shape,
        compiler_params=pltpu.CompilerParams(vmem_limit_bytes=VMEM_BYTES),
        cost_estimate=pl.CostEstimate(flops=flops, bytes_accessed=read, transcendentals=0),
    )(meta, *inputs)


def all_sum(value, axis_names):
    count = 1
    for name in axis_names:
        count *= lax.axis_size(name)
    spread = jnp.broadcast_to(value[None], (count,) + value.shape)
    return jnp.sum(lax.all_to_all(spread, axis_names, split_axis=0, concat_axis=0, tiled=True), axis=0)


def shards(embeddings, targets, gram_prior, penalty):
    row_count = embeddings.shape[0]
    width = embeddings.shape[3]
    heads = targets.shape[1]
    data_count = lax.axis_size("dp")
    trow_count = lax.axis_size("trow")
    tcol_count = lax.axis_size("tcol")
    piece = width // data_count
    total_rows = row_count * data_count
    tile_rows = tcol_count * piece
    tile_columns = trow_count * width
    head_part = heads // tcol_count
    data_place = lax.axis_index("dp")
    me = lax.axis_index("tcol")
    ring = Ring(data_count, trow_count)
    n = ring.count
    position = jnp.asarray(ring.place)[data_place, lax.axis_index("trow")]
    chunk_meta = jnp.asarray(ring.row_chunk)[position]
    trow_meta = jnp.asarray(ring.row_trow)[position]
    data_meta = jnp.asarray(ring.row_data)[position]
    rounds = jnp.asarray(ring.rounds)[position]
    me_meta = jnp.reshape(me, (1,)).astype(jnp.int32)

    own = embeddings.reshape(row_count, width).T
    head_rows = lax.dynamic_slice_in_dim(targets, me * head_part, head_part, axis=1).T
    gathered = ring.gather(jnp.concatenate([own, head_rows], axis=0), width)

    def piece_of(shard):
        features = lax.dynamic_slice_in_dim(shard, data_place * piece, piece, axis=0)
        return jnp.concatenate([shard[width:], features], axis=0)

    def round_piece(turn):
        choices = sorted(set(ring.rounds[:, turn].tolist()))
        value = piece_of(gathered[choices[0]])
        for choice in choices[1:]:
            value = jnp.where(rounds[turn] == choice, piece_of(gathered[choice]), value)
        return value

    split_turns = [[0], list(range(1, data_count - 1)), [data_count - 1]]
    groups = []
    for turns in split_turns:
        mine = jnp.stack([round_piece(turn) for turn in turns])
        far = lax.ppermute(mine, "tcol", swap(tcol_count, 2))
        near = lax.ppermute(jnp.stack([mine, far]), "tcol", swap(tcol_count, 1))
        groups += [mine, far, near]

    block = 384 if tile_columns % 384 == 0 else 128
    grid = tile_columns // block
    tile = pl.BlockSpec((tile_rows, block), lambda i, meta: (0, i))

    def whole(*shape):
        return pl.BlockSpec(shape, lambda i, meta: (0,) * len(shape))

    f32, bf16 = jnp.float32, jnp.bfloat16
    gram, start, partial = call(
        functools.partial(
            gram_kernel,
            (n, data_count, trow_count, tcol_count, piece, width, head_part, block, total_rows, len(split_turns)),
        ),
        jnp.concatenate([chunk_meta, trow_meta, me_meta]),
        [*gathered, *groups, gram_prior.reshape(tile_rows, tile_columns)],
        grid,
        [VMEM] * (n + 1 + len(groups)) + [tile],
        [tile, whole(piece, heads), whole(tile_rows, heads)],
        [
            jax.ShapeDtypeStruct((tile_rows, tile_columns), f32),
            jax.ShapeDtypeStruct((piece, heads), f32),
            jax.ShapeDtypeStruct((tile_rows, heads), f32),
        ],
        [
            pltpu.VMEM((data_count, tile_columns, row_count), bf16),
            pltpu.VMEM((data_count, tile_rows, row_count), bf16),
            pltpu.VMEM((data_count, heads, row_count), bf16),
        ],
        2 * tile_rows * tile_columns * (total_rows + 3 * heads),
        8 * tile_rows * tile_columns,
    )
    penalty_rows = penalty.reshape(piece, 1)

    def owner_sum(value):
        kept = [value[j] for j in range(tcol_count)]
        received = lax.ppermute(jnp.stack(kept[1::2]), "tcol", swap(tcol_count, 1))
        kept = [a + received[i] for i, a in enumerate(kept[0::2])]
        return kept[0] + lax.ppermute(kept[1], "tcol", swap(tcol_count, 2))

    image = owner_sum(partial.reshape(tcol_count, piece, heads)) + penalty_rows * start
    far_image = lax.ppermute(image, "tcol", swap(tcol_count, 2))
    near_images = lax.ppermute(jnp.stack([image, far_image]), "tcol", swap(tcol_count, 1))
    images = ring.gather(image, piece)
    second, sums = call(
        functools.partial(image_kernel, (n, data_count, tcol_count, piece, block)),
        jnp.concatenate([data_meta, trow_meta, me_meta]),
        [*images, gram, start, near_images, far_image, penalty_rows],
        grid,
        [VMEM] * (n + 1) + [tile] + [VMEM] * 4,
        [whole(tcol_count, piece, heads), whole(4, heads)],
        [jax.ShapeDtypeStruct((tcol_count, piece, heads), f32), jax.ShapeDtypeStruct((4, heads), f32)],
        [
            pltpu.VMEM((tile_columns, heads), f32),
            pltpu.VMEM((tile_columns, heads), f32),
            pltpu.VMEM((tile_rows, heads), f32),
        ],
        6 * tile_rows * tile_columns * heads,
        4 * tile_rows * tile_columns,
    )
    sums = all_sum(sums, ("dp", "trow", "tcol"))
    second = owner_sum(second)

    norm, curvature, image_norm, image_curvature = sums[0], sums[1], sums[2], sums[3]
    step = norm / curvature
    norm_next = step * step * image_norm - norm
    ratio = norm_next / norm
    moved_curvature = step * (step * image_curvature - (1.0 + ratio) * image_norm)
    next_step = norm_next / moved_curvature
    residual = start - step * image
    direction = residual + ratio * start
    weights = step * start + next_step * direction
    residual = residual - next_step * ((1.0 + ratio) * image - step * second)
    out_shape = (1, 1, 1, piece, heads)
    return (gram.reshape(gram_prior.shape), weights.reshape(out_shape), residual.reshape(out_shape))


def solution(mesh):
    placed = (
        P("dp", "tcol", "trow", None),
        P("dp", None),
        P(None, "trow", "dp", None, "tcol"),
        P("tcol", "trow", "dp", None),
    )
    return jax.shard_map(
        shards,
        mesh=mesh,
        in_specs=placed,
        out_specs=(
            P(None, "trow", "dp", None, "tcol"),
            P("tcol", "trow", "dp", None, None),
            P("tcol", "trow", "dp", None, None),
        ),
        check_vma=False,
    )
```

time: 412 us -> 137 us (0.33)
  blocking collectives: 156 us -> 0 us
  waiting for transfers between devices: 180 us -> 71.2 us
  matrix products: 29.8 us -> 0 us
  starting transfers between devices: 0.48 us -> 29.1 us
  Pallas kernels: 0 us -> 18 us
  local copies, waits for them, and re-layouts: 19.8 us -> 9.61 us
  between operations: 15.7 us -> 6.99 us
  other arithmetic: 9.43 us -> 1.76 us
    all_gather x4 -> x0, waiting for transfers between devices: 137 us -> none  [the longest x1 65.3 us: shards(): lax.all_gather(columns, 'dp', axis=0, tiled=True)]
    psum x3 -> x0, blocking collectives: 120 us -> none  [the longest x2 80.4 us: squared_norm(): return lax.psum(column_sums(vector, vector), ('dp', 'trow', 'tcol'))]
    ppermute x0 -> x28, waiting for transfers between devices: none -> 63.3 us  [the longest x6 28.3 us: gather(): ahead = lax.ppermute(ahead, ('dp', 'trow'), self.ahead)]
    reduce_scatter x3 -> x0, waiting for transfers between devices: 42.8 us -> none  [the longest x2 42.8 us: shards(): lax.psum_scatter(contribution, 'tcol', scatter_dimension=0, tiled=True)]
    dot_general x4 -> x0, matrix products: 29.8 us -> none  [the longest x2 22.5 us: shards(): jnp.einsum('ktdr,dtrh->kh', gram_tile, shared, precision=lax.Precision.HI...]
    all_to_all x1 -> x0, blocking collectives: 27.8 us -> none  [shards(): lax.all_to_all(sliced, 'dp', split_axis=1, concat_axis=0, tiled=True)]
    ppermute x0 -> x28, starting transfers between devices: none -> 25.2 us  [the longest x6 7.47 us: gather(): back = lax.ppermute(back, ('dp', 'trow'), self.back)]
    pallas_call x0 -> x2, Pallas kernels: none -> 18 us  [call(): pl.pallas_call(body, grid_spec=pltpu.PrefetchScalarGridSpec(num_scalar_pr...]
  transfers between devices with their start and end apart: 7 -> 29, of which waited for: 6 -> 17; matrix products, arithmetic and copies ran while one was open for 7% -> 4% of each run, Pallas kernels for 0% -> 0%
where the time goes in v2:
time: 137 us
  waiting for transfers between devices  71.2 us (52%)
  starting transfers between devices  29.1 us (21%)
  Pallas kernels  18 us (13%)
  local copies, waits for them, and re-layouts  9.61 us (7%)
  between operations  6.99 us (5%)
  other arithmetic  1.76 us (1%)
    ppermute x6, waiting for transfers between devices, gather(): ahead = lax.ppermute(ahead, ('dp', 'trow'), self.ahead)  28.3 us
    pallas_call x2, Pallas kernels, call(): pl.pallas_call(body, grid_spec=pltpu.PrefetchScalarGridSpec(num_scalar_pr...  18 us
    ppermute x2, waiting for transfers between devices, owner_sum(): return kept[0] + lax.ppermute(kept[1], 'tcol', swap(tcol_count, 2))  12 us
    ppermute x3, waiting for transfers between devices, shards(): far = lax.ppermute(mine, 'tcol', swap(tcol_count, 2))  10.4 us
    all_to_all x1, waiting for transfers between devices, all_sum(): lax.all_to_all(spread, axis_names, split_axis=0, concat_axis=0, tiled=True)  7.84 us
    ppermute x6, starting transfers between devices, gather(): back = lax.ppermute(back, ('dp', 'trow'), self.back)  7.47 us
    ppermute x2, waiting for transfers between devices, gather(): low = lax.ppermute(ahead[:half], ('dp', 'trow'), self.ahead)  6.82 us
    ppermute x6, starting transfers between devices, gather(): ahead = lax.ppermute(ahead, ('dp', 'trow'), self.ahead)  5.96 us
  transfers between devices with their start and end apart: 29, of which 17 were waited for; matrix products, arithmetic and copies ran while one was open for 4% of the time, Pallas kernels for 0%

profile of v2, /device:TPU:0, one launch (start us, length us, event | category | flops | bytes accessed | tf_op | source)
XLA Modules:
  0.0 136.6 jit_solution(8070152420976069214)
XLA Ops:
  1.7 1.2 copy.23
  2.9 3.0 %collective-permute-start.1 = (bf16[832,256]{1,0:T(8,128)(2,1)S(1)}, bf16[832,256]{1,0:T(8,128)(2,1)S(1)}, u32[]{:S(2)}, u32[]{:S(2)}) collective-permute-start(bf16[832,256]{1,0:T(8,128)(2,1)S(1)} %pad_maximum_fusion.refs_0_), channel_id=1, source_target_pairs={{8,0},{16,8},{24,16},{28,24},{20,28},{12,20},{4,12},{0,4},{9,1},{1... | collective-permute-start | bytes 1277960 | tf_op jit(solution)/shard_map/ppermute | solution.py:62
  6.1 1.3 dynamic_slice.42
  15.8 1.7 %collective-permute-start.3 = (bf16[832,256]{1,0:T(8,128)(2,1)S(1)}, bf16[832,256]{1,0:T(8,128)(2,1)S(1)}, u32[]{:S(2)}, u32[]{:S(2)}) collective-permute-start(bf16[832,256]{1,0:T(8,128)(2,1)S(1)} %collective-permute-done.1.refs_2_), channel_id=1, source_target_pairs={{8,0},{16,8},{24,16},{28,24},{20,28},{12,20},{4,12},{0,4},{9,1},{1... | collective-permute-start | bytes 1277960 | tf_op jit(solution)/shard_map/ppermute | solution.py:62
  18.0 10.0 %collective-permute-done.2.refs_3_ = bf16[832,256]{1,0:T(8,128)(2,1)S(1)} collective-permute-done((bf16[832,256]{1,0:T(8,128)(2,1)S(1)}, bf16[832,256]{1,0:T(8,128)(2,1)S(1)}, u32[]{:S(2)}, u32[]{:S(2)}) %collective-permute-start.2) | collective-permute-done | bytes 426016 | tf_op jit(solution)/shard_map/ppermute | solution.py:61
  28.7 1.4 %collective-permute-start.5 = (bf16[832,256]{1,0:T(8,128)(2,1)S(1)}, bf16[832,256]{1,0:T(8,128)(2,1)S(1)}, u32[]{:S(2)}, u32[]{:S(2)}) collective-permute-start(bf16[832,256]{1,0:T(8,128)(2,1)S(1)} %collective-permute-done.3.refs_4_), channel_id=1, source_target_pairs={{8,0},{16,8},{24,16},{28,24},{20,28},{12,20},{4,12},{0,4},{9,1},{1... | collective-permute-start | bytes 1277960 | tf_op jit(solution)/shard_map/ppermute | solution.py:62
  30.2 7.3 %collective-permute-done.4.refs_5_ = bf16[832,256]{1,0:T(8,128)(2,1)S(1)} collective-permute-done((bf16[832,256]{1,0:T(8,128)(2,1)S(1)}, bf16[832,256]{1,0:T(8,128)(2,1)S(1)}, u32[]{:S(2)}, u32[]{:S(2)}) %collective-permute-start.4) | collective-permute-done | bytes 426016 | tf_op jit(solution)/shard_map/ppermute | solution.py:61
  38.4 1.1 collective-permute-start.10
  39.5 1.1 collective-permute-start.8
  40.6 5.8 %collective-permute-done.8.refs_10_ = bf16[1,256,256]{2,1,0:T(8,128)(2,1)S(1)} collective-permute-done((bf16[1,256,256]{2,1,0:T(8,128)(2,1)S(1)}, bf16[1,256,256]{2,1,0:T(8,128)(2,1)S(1)}, u32[]{:S(2)}, u32[]{:S(2)}) %collective-permute-start.8) | collective-permute-done | bytes 131104 | tf_op jit(solution)/shard_map/ppermute | solution.py:248
  47.8 4.6 %collective-permute-done.12.refs_16_ = bf16[1,256,256]{2,1,0:T(8,128)(2,1)S(1)} collective-permute-done((bf16[1,256,256]{2,1,0:T(8,128)(2,1)S(1)}, bf16[1,256,256]{2,1,0:T(8,128)(2,1)S(1)}, u32[]{:S(2)}, u32[]{:S(2)}) %collective-permute-start.12) | collective-permute-done | bytes 131104 | tf_op jit(solution)/shard_map/ppermute | solution.py:248
  54.3 1.1 collective-permute-start.7
  56.2 4.4 %collective-permute-done.6.refs_7_ = bf16[384,256]{1,0:T(8,128)(2,1)S(1)} collective-permute-done((bf16[384,256]{1,0:T(8,128)(2,1)S(1)}, bf16[384,256]{1,0:T(8,128)(2,1)S(1)}, u32[]{:S(2)}, u32[]{:S(2)}) %collective-permute-start.6) | collective-permute-done | bytes 196640 | tf_op jit(solution)/shard_map/ppermute | solution.py:65
  61.4 13.5 %shard_map.112 = (f32[768,1536]{1,0:T(8,128)}, f32[192,256]{1,0:T(8,128)S(1)}, f32[768,256]{1,0:T(8,128)S(1)}) custom-call(s32[17]{0:T(128)S(1)} %get-tuple-element.57.meta, bf16[832,256]{1,0:T(8,128)(2,1)S(1)} %pad_maximum_fusion.refs_0_, bf16[832,256]{1,0:T(8,128)(2,1)S(1)} %collective-permute-done.refs_1_, ...), custom_call_target="tpu_custom_call" | custom-call | flops 4227858432 | bytes 9437184 | tf_op jit(solution)/shard_map/pallas_call | solution.py:183
  75.0 1.7 %collective-permute-done.14 = f32[2,192,256]{2,1,0:T(8,128)S(1)} collective-permute-done((f32[2,192,256]{2,1,0:T(8,128)S(1)}, f32[2,192,256]{2,1,0:T(8,128)S(1)}, u32[]{:S(2)}, u32[]{:S(2)}) %collective-permute-start.14) | collective-permute-done | bytes 393248 | tf_op jit(solution)/shard_map/ppermute | solution.py:287
  76.8 1.6 %collective-permute-start.15 = (f32[192,256]{1,0:T(8,128)S(1)}, f32[192,256]{1,0:T(8,128)S(1)}, u32[]{:S(2)}, u32[]{:S(2)}) collective-permute-start(f32[192,256]{1,0:T(8,128)S(1)} %fusion.8), channel_id=1, source_target_pairs={{0,2},{1,3},{2,0},{3,1},{4,6},{5,7},{6,4},{7,5},{8,10},{9,11},{10,... | collective-permute-start | bytes 589832 | tf_op jit(solution)/shard_map/ppermute | solution.py:289
  78.3 5.5 %collective-permute-done.15 = f32[192,256]{1,0:T(8,128)S(1)} collective-permute-done((f32[192,256]{1,0:T(8,128)S(1)}, f32[192,256]{1,0:T(8,128)S(1)}, u32[]{:S(2)}, u32[]{:S(2)}) %collective-permute-start.15) | collective-permute-done | bytes 196640 | tf_op jit(solution)/shard_map/ppermute | solution.py:289
  83.9 1.6 %collective-permute-start.16 = (f32[192,256]{1,0:T(8,128)S(1)}, f32[192,256]{1,0:T(8,128)S(1)}, u32[]{:S(2)}, u32[]{:S(2)}) collective-permute-start(f32[192,256]{1,0:T(8,128)S(1)} %fusion.11.refs_0_), channel_id=1, source_target_pairs={{0,8},{8,16},{16,24},{24,28},{28,20},{20,12},{12,4},{4,0},{1,9},{9... | collective-permute-start | bytes 589832 | tf_op jit(solution)/shard_map/ppermute | solution.py:61
  86.0 1.5 %collective-permute-start.24 = (f32[192,256]{1,0:T(8,128)S(1)}, f32[192,256]{1,0:T(8,128)S(1)}, u32[]{:S(2)}, u32[]{:S(2)}) collective-permute-start(f32[192,256]{1,0:T(8,128)S(1)} %fusion.11.refs_0_), channel_id=1, source_target_pairs={{0,2},{1,3},{2,0},{3,1},{4,6},{5,7},{6,4},{7,5},{8,10},{9,11},{10,... | collective-permute-start | bytes 589832 | tf_op jit(solution)/shard_map/ppermute | solution.py:292
  87.5 2.6 %collective-permute-done.16.refs_1_ = f32[192,256]{1,0:T(8,128)S(1)} collective-permute-done((f32[192,256]{1,0:T(8,128)S(1)}, f32[192,256]{1,0:T(8,128)S(1)}, u32[]{:S(2)}, u32[]{:S(2)}) %collective-permute-start.16) | collective-permute-done | bytes 196640 | tf_op jit(solution)/shard_map/ppermute | solution.py:61
  90.1 1.6 %collective-permute-start.18 = (f32[192,256]{1,0:T(8,128)S(1)}, f32[192,256]{1,0:T(8,128)S(1)}, u32[]{:S(2)}, u32[]{:S(2)}) collective-permute-start(f32[192,256]{1,0:T(8,128)S(1)} %collective-permute-done.16.refs_1_), channel_id=1, source_target_pairs={{0,8},{8,16},{16,24},{24,28},{28,20},{20,12},{12,4},{4,0},{1,9},{9... | collective-permute-start | bytes 589832 | tf_op jit(solution)/shard_map/ppermute | solution.py:61
  92.2 3.6 %collective-permute-done.18.refs_3_ = f32[192,256]{1,0:T(8,128)S(1)} collective-permute-done((f32[192,256]{1,0:T(8,128)S(1)}, f32[192,256]{1,0:T(8,128)S(1)}, u32[]{:S(2)}, u32[]{:S(2)}) %collective-permute-start.18) | collective-permute-done | bytes 196640 | tf_op jit(solution)/shard_map/ppermute | solution.py:61
  95.8 1.6 %collective-permute-start.20 = (f32[192,256]{1,0:T(8,128)S(1)}, f32[192,256]{1,0:T(8,128)S(1)}, u32[]{:S(2)}, u32[]{:S(2)}) collective-permute-start(f32[192,256]{1,0:T(8,128)S(1)} %collective-permute-done.18.refs_3_), channel_id=1, source_target_pairs={{0,8},{8,16},{16,24},{24,28},{28,20},{20,12},{12,4},{4,0},{1,9},{9... | collective-permute-start | bytes 589832 | tf_op jit(solution)/shard_map/ppermute | solution.py:61
  97.9 4.7 %collective-permute-done.20.refs_5_ = f32[192,256]{1,0:T(8,128)S(1)} collective-permute-done((f32[192,256]{1,0:T(8,128)S(1)}, f32[192,256]{1,0:T(8,128)S(1)}, u32[]{:S(2)}, u32[]{:S(2)}) %collective-permute-start.20) | collective-permute-done | bytes 196640 | tf_op jit(solution)/shard_map/ppermute | solution.py:61
  102.6 1.6 %collective-permute-start.22 = (f32[96,256]{1,0:T(8,128)S(1)}, f32[96,256]{1,0:T(8,128)S(1)}, u32[]{:S(2)}, u32[]{:S(2)}) collective-permute-start(f32[96,256]{1,0:T(8,128)S(1)} %slice.145), channel_id=1, source_target_pairs={{0,8},{8,16},{16,24},{24,28},{28,20},{20,12},{12,4},{4,0},{1,9},{9... | collective-permute-start | bytes 294920 | tf_op jit(solution)/shard_map/ppermute | solution.py:65
  104.8 2.4 %collective-permute-done.22.refs_7_ = f32[96,256]{1,0:T(8,128)S(1)} collective-permute-done((f32[96,256]{1,0:T(8,128)S(1)}, f32[96,256]{1,0:T(8,128)S(1)}, u32[]{:S(2)}, u32[]{:S(2)}) %collective-permute-start.22) | collective-permute-done | bytes 98336 | tf_op jit(solution)/shard_map/ppermute | solution.py:65
  107.2 1.6 %collective-permute-done.23.refs_8_ = f32[96,256]{1,0:T(8,128)S(1)} collective-permute-done((f32[96,256]{1,0:T(8,128)S(1)}, f32[96,256]{1,0:T(8,128)S(1)}, u32[]{:S(2)}, u32[]{:S(2)}) %collective-permute-start.23) | collective-permute-done | bytes 98336 | tf_op jit(solution)/shard_map/ppermute | solution.py:66
  108.9 2.3 %copy-done.1 = f32[768,1536]{1,0:T(8,128)S(1)} copy-done((f32[768,1536]{1,0:T(8,128)S(1)}, f32[768,1536]{1,0:T(8,128)}, u32[]{:S(2)}) %copy-start.1) | copy-done | bytes 4718616
  111.2 4.5 %shard_map.113 = (f32[4,192,256]{2,1,0:T(8,128)S(1)}, f32[4,256]{1,0:T(4,128)S(1)}) custom-call(s32[17]{0:T(128)S(1)} %get-tuple-element.56.meta, f32[192,256]{1,0:T(8,128)S(1)} %fusion.11.refs_0_, f32[192,256]{1,0:T(8,128)S(1)} %collective-permute-done.16.refs_1_, f32[192,256]{1,0:T(8,128)S(1)} %collective-permute-done.17.refs_2_, ...), custom_call_target="tpu_custom_call" | custom-call | flops 1811939328 | bytes 4718592 | tf_op jit(solution)/shard_map/pallas_call | solution.py:183
  116.4 3.9 %all-to-all-start = ((f32[32,4,256]{2,1,0:T(4,128)}), f32[32,4,256]{2,1,0:T(4,128)S(1)}, u32[]{:S(2)}, u32[]{:S(2)}) async-start(f32[32,4,256]{2,1,0:T(4,128)} %broadcast_in_dim.2), calls=%async_computation | async-start | bytes 262144 | tf_op jit(solution)/shard_map/all_to_all | solution.py:203
  120.7 7.8 %all-to-all-done = f32[32,4,256]{2,1,0:T(4,128)S(1)} async-done(((f32[32,4,256]{2,1,0:T(4,128)}), f32[32,4,256]{2,1,0:T(4,128)S(1)}, u32[]{:S(2)}, u32[]{:S(2)}) %all-to-all-start) | async-done | bytes 131104 | tf_op jit(solution)/shard_map/all_to_all | solution.py:203
  129.2 6.6 %collective-permute-done.27 = f32[192,256]{1,0:T(8,128)S(1)} collective-permute-done((f32[192,256]{1,0:T(8,128)S(1)}, f32[192,256]{1,0:T(8,128)S(1)}, u32[]{:S(2)}, u32[]{:S(2)}) %collective-permute-start.27) | collective-permute-done | bytes 196640 | tf_op jit(solution)/shard_map/ppermute | solution.py:289
  (85 shorter events, 15.5 us)
Async XLA Ops:
  2.9 12.9 %collective-permute-start.1 = (bf16[832,256]{1,0:T(8,128)(2,1)S(1)}, bf16[832,256]{1,0:T(8,128)(2,1)S(1)}, u32[]{:S(2)}, u32[]{:S(2)}) collective-permute-start(bf16[832,256]{1,0:T(8,128)(2,1)S(1)} %pad_maximum_fusion.refs_0_), channel_id=1, source_target_pairs={{8,0},{16,8},{24,16},{28,24},{20,28},{12,20},{4,12},{0,4},{9,1},{1... | collective-permute-start | bytes 1277960 | tf_op jit(solution)/shard_map/ppermute | solution.py:62
  6.0 11.6 %collective-permute-start = (bf16[832,256]{1,0:T(8,128)(2,1)S(1)}, bf16[832,256]{1,0:T(8,128)(2,1)S(1)}, u32[]{:S(2)}, u32[]{:S(2)}) collective-permute-start(bf16[832,256]{1,0:T(8,128)(2,1)S(1)} %pad_maximum_fusion.refs_0_), channel_id=1, source_target_pairs={{0,8},{8,16},{16,24},{24,28},{28,20},{20,12},{12,4},{4,0},{1,9},{9... | collective-permute-start | bytes 1277960 | tf_op jit(solution)/shard_map/ppermute | solution.py:61
  13.9 47.5 %copy-start.2 = (f32[4,1,1,192,1536]{4,3,2,1,0:T(8,128)S(1)}, f32[4,1,1,192,1536]{4,3,2,1,0:T(8,128)}, u32[]{:S(2)}) copy-start(f32[4,1,1,192,1536]{4,3,2,1,0:T(8,128)} %param.11) | copy-start | bytes 14155780
  15.8 12.8 %collective-permute-start.3 = (bf16[832,256]{1,0:T(8,128)(2,1)S(1)}, bf16[832,256]{1,0:T(8,128)(2,1)S(1)}, u32[]{:S(2)}, u32[]{:S(2)}) collective-permute-start(bf16[832,256]{1,0:T(8,128)(2,1)S(1)} %collective-permute-done.1.refs_2_), channel_id=1, source_target_pairs={{8,0},{16,8},{24,16},{28,24},{20,28},{12,20},{4,12},{0,4},{9,1},{1... | collective-permute-start | bytes 1277960 | tf_op jit(solution)/shard_map/ppermute | solution.py:62
  17.5 10.5 %collective-permute-start.2 = (bf16[832,256]{1,0:T(8,128)(2,1)S(1)}, bf16[832,256]{1,0:T(8,128)(2,1)S(1)}, u32[]{:S(2)}, u32[]{:S(2)}) collective-permute-start(bf16[832,256]{1,0:T(8,128)(2,1)S(1)} %collective-permute-done.refs_1_), channel_id=1, source_target_pairs={{0,8},{8,16},{16,24},{24,28},{28,20},{20,12},{12,4},{4,0},{1,9},{9... | collective-permute-start | bytes 1277960 | tf_op jit(solution)/shard_map/ppermute | solution.py:61
  28.0 9.5 %collective-permute-start.4 = (bf16[832,256]{1,0:T(8,128)(2,1)S(1)}, bf16[832,256]{1,0:T(8,128)(2,1)S(1)}, u32[]{:S(2)}, u32[]{:S(2)}) collective-permute-start(bf16[832,256]{1,0:T(8,128)(2,1)S(1)} %collective-permute-done.2.refs_3_), channel_id=1, source_target_pairs={{0,8},{8,16},{16,24},{24,28},{28,20},{20,12},{12,4},{4,0},{1,9},{9... | collective-permute-start | bytes 1277960 | tf_op jit(solution)/shard_map/ppermute | solution.py:61
  28.7 9.6 %collective-permute-start.5 = (bf16[832,256]{1,0:T(8,128)(2,1)S(1)}, bf16[832,256]{1,0:T(8,128)(2,1)S(1)}, u32[]{:S(2)}, u32[]{:S(2)}) collective-permute-start(bf16[832,256]{1,0:T(8,128)(2,1)S(1)} %collective-permute-done.3.refs_4_), channel_id=1, source_target_pairs={{8,0},{16,8},{24,16},{28,24},{20,28},{12,20},{4,12},{0,4},{9,1},{1... | collective-permute-start | bytes 1277960 | tf_op jit(solution)/shard_map/ppermute | solution.py:62
  38.4 9.0 %collective-permute-start.10 = (bf16[2,256,256]{2,1,0:T(8,128)(2,1)S(1)}, bf16[2,256,256]{2,1,0:T(8,128)(2,1)S(1)}, u32[]{:S(2)}, u32[]{:S(2)}) collective-permute-start(bf16[2,256,256]{2,1,0:T(8,128)(2,1)S(1)} %get-tuple-element.53.refs_12_), channel_id=1, source_target_pairs={{0,2},{1,3},{2,0},{3,1},{4,6},{5,7},{6,4},{7,5},{8,10},{9,11},{10,... | collective-permute-start | bytes 786440 | tf_op jit(solution)/shard_map/ppermute | solution.py:248
  39.5 6.9 %collective-permute-start.8 = (bf16[1,256,256]{2,1,0:T(8,128)(2,1)S(1)}, bf16[1,256,256]{2,1,0:T(8,128)(2,1)S(1)}, u32[]{:S(2)}, u32[]{:S(2)}) collective-permute-start(bf16[1,256,256]{2,1,0:T(8,128)(2,1)S(1)} %get-tuple-element.55.refs_9_), channel_id=1, source_target_pairs={{0,2},{1,3},{2,0},{3,1},{4,6},{5,7},{6,4},{7,5},{8,10},{9,11},{10,... | collective-permute-start | bytes 393224 | tf_op jit(solution)/shard_map/ppermute | solution.py:248
  46.4 9.8 %collective-permute-start.9 = (bf16[2,1,256,256]{3,2,1,0:T(8,128)(2,1)S(1)}, bf16[2,1,256,256]{3,2,1,0:T(8,128)(2,1)S(1)}, u32[]{:S(2)}, u32[]{:S(2)}) collective-permute-start(bf16[2,1,256,256]{3,2,1,0:T(8,128)(2,1)S(1)} %pad_maximum_fusion.5), channel_id=1, source_target_pairs={{0,1},{1,0},{2,3},{3,2},{4,5},{5,4},{6,7},{7,6},{8,9},{9,8},{10,11... | collective-permute-start | bytes 786440 | tf_op jit(solution)/shard_map/ppermute | solution.py:249
  46.5 5.9 %collective-permute-start.12 = (bf16[1,256,256]{2,1,0:T(8,128)(2,1)S(1)}, bf16[1,256,256]{2,1,0:T(8,128)(2,1)S(1)}, u32[]{:S(2)}, u32[]{:S(2)}) collective-permute-start(bf16[1,256,256]{2,1,0:T(8,128)(2,1)S(1)} %get-tuple-element.50.refs_15_), channel_id=1, source_target_pairs={{0,2},{1,3},{2,0},{3,1},{4,6},{5,7},{6,4},{7,5},{8,10},{9,11},{10,... | collective-permute-start | bytes 393224 | tf_op jit(solution)/shard_map/ppermute | solution.py:248
  47.5 13.9 %collective-permute-start.11 = (bf16[2,2,256,256]{3,2,1,0:T(8,128)(2,1)S(1)}, bf16[2,2,256,256]{3,2,1,0:T(8,128)(2,1)S(1)}, u32[]{:S(2)}, u32[]{:S(2)}) collective-permute-start(bf16[2,2,256,256]{3,2,1,0:T(8,128)(2,1)S(1)} %pad_maximum_fusion.1), channel_id=1, source_target_pairs={{0,1},{1,0},{2,3},{3,2},{4,5},{5,4},{6,7},{7,6},{8,9},{9,8},{10,11... | collective-permute-start | bytes 1572872 | tf_op jit(solution)/shard_map/ppermute | solution.py:249
  52.5 8.9 %collective-permute-start.13 = (bf16[2,1,256,256]{3,2,1,0:T(8,128)(2,1)S(1)}, bf16[2,1,256,256]{3,2,1,0:T(8,128)(2,1)S(1)}, u32[]{:S(2)}, u32[]{:S(2)}) collective-permute-start(bf16[2,1,256,256]{3,2,1,0:T(8,128)(2,1)S(1)} %pad_maximum_fusion.7), channel_id=1, source_target_pairs={{0,1},{1,0},{2,3},{3,2},{4,5},{5,4},{6,7},{7,6},{8,9},{9,8},{10,11... | collective-permute-start | bytes 786440 | tf_op jit(solution)/shard_map/ppermute | solution.py:249
  53.3 7.3 %collective-permute-start.6 = (bf16[384,256]{1,0:T(8,128)(2,1)S(1)}, bf16[384,256]{1,0:T(8,128)(2,1)S(1)}, u32[]{:S(2)}, u32[]{:S(2)}) collective-permute-start(bf16[384,256]{1,0:T(8,128)(2,1)S(1)} %slice.135), channel_id=1, source_target_pairs={{0,8},{8,16},{16,24},{24,28},{28,20},{20,12},{12,4},{4,0},{1,9},{9... | collective-permute-start | bytes 589832 | tf_op jit(solution)/shard_map/ppermute | solution.py:65
  54.3 7.1 %collective-permute-start.7 = (bf16[384,256]{1,0:T(8,128)(2,1)S(1)}, bf16[384,256]{1,0:T(8,128)(2,1)S(1)}, u32[]{:S(2)}, u32[]{:S(2)}) collective-permute-start(bf16[384,256]{1,0:T(8,128)(2,1)S(1)} %slice.136), channel_id=1, source_target_pairs={{8,0},{16,8},{24,16},{28,24},{20,28},{12,20},{4,12},{0,4},{9,1},{1... | collective-permute-start | bytes 589832 | tf_op jit(solution)/shard_map/ppermute | solution.py:66
  61.4 22.4 %copy-start.3 = (f32[1,1,1,192]{3,2,1,0:T(1,128)S(1)}, f32[1,1,1,192]{3,2,1,0:T(1,128)}, u32[]{:S(2)}) copy-start(f32[1,1,1,192]{3,2,1,0:T(1,128)} %param.12) | copy-start | bytes 2308
  75.0 1.8 %collective-permute-start.14 = (f32[2,192,256]{2,1,0:T(8,128)S(1)}, f32[2,192,256]{2,1,0:T(8,128)S(1)}, u32[]{:S(2)}, u32[]{:S(2)}) collective-permute-start(f32[2,192,256]{2,1,0:T(8,128)S(1)} %pad_maximum_fusion.2), channel_id=1, source_target_pairs={{0,1},{1,0},{2,3},{3,2},{4,5},{5,4},{6,7},{7,6},{8,9},{9,8},{10,11... | collective-permute-start | bytes 1179656 | tf_op jit(solution)/shard_map/ppermute | solution.py:287
  76.8 7.0 %collective-permute-start.15 = (f32[192,256]{1,0:T(8,128)S(1)}, f32[192,256]{1,0:T(8,128)S(1)}, u32[]{:S(2)}, u32[]{:S(2)}) collective-permute-start(f32[192,256]{1,0:T(8,128)S(1)} %fusion.8), channel_id=1, source_target_pairs={{0,2},{1,3},{2,0},{3,1},{4,6},{5,7},{6,4},{7,5},{8,10},{9,11},{10,... | collective-permute-start | bytes 589832 | tf_op jit(solution)/shard_map/ppermute | solution.py:289
  83.9 6.2 %collective-permute-start.16 = (f32[192,256]{1,0:T(8,128)S(1)}, f32[192,256]{1,0:T(8,128)S(1)}, u32[]{:S(2)}, u32[]{:S(2)}) collective-permute-start(f32[192,256]{1,0:T(8,128)S(1)} %fusion.11.refs_0_), channel_id=1, source_target_pairs={{0,8},{8,16},{16,24},{24,28},{28,20},{20,12},{12,4},{4,0},{1,9},{9... | collective-permute-start | bytes 589832 | tf_op jit(solution)/shard_map/ppermute | solution.py:61
  85.5 6.1 %collective-permute-start.17 = (f32[192,256]{1,0:T(8,128)S(1)}, f32[192,256]{1,0:T(8,128)S(1)}, u32[]{:S(2)}, u32[]{:S(2)}) collective-permute-start(f32[192,256]{1,0:T(8,128)S(1)} %fusion.11.refs_0_), channel_id=1, source_target_pairs={{8,0},{16,8},{24,16},{28,24},{20,28},{12,20},{4,12},{0,4},{9,1},{1... | collective-permute-start | bytes 589832 | tf_op jit(solution)/shard_map/ppermute | solution.py:62
  86.0 6.1 %collective-permute-start.24 = (f32[192,256]{1,0:T(8,128)S(1)}, f32[192,256]{1,0:T(8,128)S(1)}, u32[]{:S(2)}, u32[]{:S(2)}) collective-permute-start(f32[192,256]{1,0:T(8,128)S(1)} %fusion.11.refs_0_), channel_id=1, source_target_pairs={{0,2},{1,3},{2,0},{3,1},{4,6},{5,7},{6,4},{7,5},{8,10},{9,11},{10,... | collective-permute-start | bytes 589832 | tf_op jit(solution)/shard_map/ppermute | solution.py:292
  90.1 5.8 %collective-permute-start.18 = (f32[192,256]{1,0:T(8,128)S(1)}, f32[192,256]{1,0:T(8,128)S(1)}, u32[]{:S(2)}, u32[]{:S(2)}) collective-permute-start(f32[192,256]{1,0:T(8,128)S(1)} %collective-permute-done.16.refs_1_), channel_id=1, source_target_pairs={{0,8},{8,16},{16,24},{24,28},{28,20},{20,12},{12,4},{4,0},{1,9},{9... | collective-permute-start | bytes 589832 | tf_op jit(solution)/shard_map/ppermute | solution.py:61
  91.6 5.8 %collective-permute-start.19 = (f32[192,256]{1,0:T(8,128)S(1)}, f32[192,256]{1,0:T(8,128)S(1)}, u32[]{:S(2)}, u32[]{:S(2)}) collective-permute-start(f32[192,256]{1,0:T(8,128)S(1)} %collective-permute-done.17.refs_2_), channel_id=1, source_target_pairs={{8,0},{16,8},{24,16},{28,24},{20,28},{12,20},{4,12},{0,4},{9,1},{1... | collective-permute-start | bytes 589832 | tf_op jit(solution)/shard_map/ppermute | solution.py:62
  92.1 12.7 %collective-permute-start.25 = (f32[2,192,256]{2,1,0:T(8,128)S(1)}, f32[2,192,256]{2,1,0:T(8,128)S(1)}, u32[]{:S(2)}, u32[]{:S(2)}) collective-permute-start(f32[2,192,256]{2,1,0:T(8,128)S(1)} %pad_maximum_fusion.3), channel_id=1, source_target_pairs={{0,1},{1,0},{2,3},{3,2},{4,5},{5,4},{6,7},{7,6},{8,9},{9,8},{10,11... | collective-permute-start | bytes 1179656 | tf_op jit(solution)/shard_map/ppermute | solution.py:293
  95.8 6.7 %collective-permute-start.20 = (f32[192,256]{1,0:T(8,128)S(1)}, f32[192,256]{1,0:T(8,128)S(1)}, u32[]{:S(2)}, u32[]{:S(2)}) collective-permute-start(f32[192,256]{1,0:T(8,128)S(1)} %collective-permute-done.18.refs_3_), channel_id=1, source_target_pairs={{0,8},{8,16},{16,24},{24,28},{28,20},{20,12},{12,4},{4,0},{1,9},{9... | collective-permute-start | bytes 589832 | tf_op jit(solution)/shard_map/ppermute | solution.py:61
  97.4 6.8 %collective-permute-start.21 = (f32[192,256]{1,0:T(8,128)S(1)}, f32[192,256]{1,0:T(8,128)S(1)}, u32[]{:S(2)}, u32[]{:S(2)}) collective-permute-start(f32[192,256]{1,0:T(8,128)S(1)} %collective-permute-done.19.refs_4_), channel_id=1, source_target_pairs={{8,0},{16,8},{24,16},{28,24},{20,28},{12,20},{4,12},{0,4},{9,1},{1... | collective-permute-start | bytes 589832 | tf_op jit(solution)/shard_map/ppermute | solution.py:62
  102.6 4.7 %collective-permute-start.22 = (f32[96,256]{1,0:T(8,128)S(1)}, f32[96,256]{1,0:T(8,128)S(1)}, u32[]{:S(2)}, u32[]{:S(2)}) collective-permute-start(f32[96,256]{1,0:T(8,128)S(1)} %slice.145), channel_id=1, source_target_pairs={{0,8},{8,16},{16,24},{24,28},{28,20},{20,12},{12,4},{4,0},{1,9},{9... | collective-permute-start | bytes 294920 | tf_op jit(solution)/shard_map/ppermute | solution.py:65
  104.2 4.7 %collective-permute-start.23 = (f32[96,256]{1,0:T(8,128)S(1)}, f32[96,256]{1,0:T(8,128)S(1)}, u32[]{:S(2)}, u32[]{:S(2)}) collective-permute-start(f32[96,256]{1,0:T(8,128)S(1)} %slice.146), channel_id=1, source_target_pairs={{8,0},{16,8},{24,16},{28,24},{20,28},{12,20},{4,12},{0,4},{9,1},{1... | collective-permute-start | bytes 294920 | tf_op jit(solution)/shard_map/ppermute | solution.py:66
  108.9 2.3 %copy-start.1 = (f32[768,1536]{1,0:T(8,128)S(1)}, f32[768,1536]{1,0:T(8,128)}, u32[]{:S(2)}) copy-start(f32[768,1536]{1,0:T(8,128)} %get-tuple-element.8.refs_9_) | copy-start | bytes 14155780
  116.4 12.2 %all-to-all-start = ((f32[32,4,256]{2,1,0:T(4,128)}), f32[32,4,256]{2,1,0:T(4,128)S(1)}, u32[]{:S(2)}, u32[]{:S(2)}) async-start(f32[32,4,256]{2,1,0:T(4,128)} %broadcast_in_dim.2), calls=%async_computation | async-start | bytes 262144 | tf_op jit(solution)/shard_map/all_to_all | solution.py:203
  120.4 8.2 %collective-permute-start.26 = (f32[2,192,256]{2,1,0:T(8,128)S(1)}, f32[2,192,256]{2,1,0:T(8,128)S(1)}, u32[]{:S(2)}, u32[]{:S(2)}) collective-permute-start(f32[2,192,256]{2,1,0:T(8,128)S(1)} %pad_maximum_fusion.4), channel_id=1, source_target_pairs={{0,1},{1,0},{2,3},{3,2},{4,5},{5,4},{6,7},{7,6},{8,9},{9,8},{10,11... | collective-permute-start | bytes 1179656 | tf_op jit(solution)/shard_map/ppermute | solution.py:287
  128.7 7.1 %collective-permute-start.27 = (f32[192,256]{1,0:T(8,128)S(1)}, f32[192,256]{1,0:T(8,128)S(1)}, u32[]{:S(2)}, u32[]{:S(2)}) collective-permute-start(f32[192,256]{1,0:T(8,128)S(1)} %fusion), channel_id=1, source_target_pairs={{0,2},{1,3},{2,0},{3,1},{4,6},{5,7},{6,4},{7,5},{8,10},{9,11},{10,... | collective-permute-start | bytes 589832 | tf_op jit(solution)/shard_map/ppermute | solution.py:289
  (1 other events, 0.9 us)

commit v3 on v2

v3 whole, which is shorter than its diff:
```python
import functools

import jax
import jax.numpy as jnp
import numpy as np
from jax import lax
from jax.experimental import pallas as pl
from jax.experimental.pallas import tpu as pltpu
from jax.sharding import PartitionSpec as P

NT = (((1,), (1,)), ((), ()))
NN = (((1,), (0,)), ((), ()))
VMEM = pl.BlockSpec(memory_space=pltpu.VMEM)
HBM = pl.BlockSpec(memory_space=pltpu.HBM)
GRAM_BYTES = 24 * 2**20
IMAGE_BYTES = 20 * 2**20


def swap(count, bit):
    return [(place, place ^ bit) for place in range(count)]


class Ring:
    def __init__(self, data_count, trow_count):
        self.data_count = data_count
        self.count = data_count * trow_count
        self.cells = []
        for trow in range(trow_count):
            along = range(data_count) if trow % 2 == 0 else reversed(range(data_count))
            self.cells += [(data, trow) for data in along]
        flat = [data * trow_count + trow for data, trow in self.cells]
        self.ahead = [(flat[i], flat[(i + 1) % self.count]) for i in range(self.count)]
        self.back = [(target, source) for source, target in self.ahead]
        self.far = self.count // 2
        self.offsets = [0]
        for distance in range(1, self.far):
            self.offsets += [-distance, distance]
        self.offsets.append(self.far)
        self.place = np.zeros((data_count, trow_count), np.int32)
        for position, (data, trow) in enumerate(self.cells):
            self.place[data, trow] = position
        self.rounds = np.zeros((self.count, data_count), np.int32)
        self.chunk, self.trow, self.data = (np.zeros((self.count, self.count), np.int32) for _ in range(3))
        for position, (data, trow) in enumerate(self.cells):
            first = trow * data_count
            near = sorted(range(first, first + data_count), key=lambda q: (abs(q - position), q))
            chunk_of = {}
            for turn, other in enumerate(near):
                self.rounds[position, turn] = self.offsets.index(other - position)
                chunk_of[self.cells[other][0]] = turn
            for index, offset in enumerate(self.offsets):
                other_data, other_trow = self.cells[(position + offset) % self.count]
                self.chunk[position, index] = chunk_of[other_data]
                self.trow[position, index] = other_trow
                self.data[position, index] = other_data

    def steps(self, value, split_rows):
        ahead = back = value
        for _ in range(1, self.far):
            ahead = lax.ppermute(ahead, ("dp", "trow"), self.ahead)
            back = lax.ppermute(back, ("dp", "trow"), self.back)
            yield ahead, back
        half = (split_rows // 2 + 15) // 16 * 16
        low = lax.ppermute(ahead[:half], ("dp", "trow"), self.ahead)
        high = lax.ppermute(back[half:split_rows], ("dp", "trow"), self.back)
        yield low, high


def split(value):
    high = value.astype(jnp.bfloat16)
    return high, (value - high.astype(jnp.float32)).astype(jnp.bfloat16)


def dot(a, b, dims):
    return lax.dot_general(a, b, dims, preferred_element_type=jnp.float32)


def product(a, b):
    (a_high, a_low), (b_high, b_low) = a, b
    return dot(a_high, b_high, NN) + (dot(a_high, b_low, NN) + dot(a_low, b_high, NN))


def tile_copies(whole_ref, tile_ref, me, piece, block, semaphores, outward=False):
    copies = []
    for start in range(0, tile_ref.shape[1], block):
        lanes = pl.ds(start, block)
        for j in range(tile_ref.shape[0] // piece):
            place = pl.ds(pl.multiple_of(jnp.bitwise_xor(me, j) * piece, 8), piece)
            pair = whole_ref.at[place, lanes], tile_ref.at[pl.ds(j * piece, piece), lanes]
            if outward:
                pair = pair[::-1]
            copies.append(pltpu.make_async_copy(*pair, semaphores.at[len(copies)]))
    return copies


def fetch_kernel(sizes, meta, gram_ref, tile_ref, come):
    piece, block = sizes
    loads = tile_copies(gram_ref, tile_ref, meta[0], piece, block, come)
    for load in loads:
        load.start()
    for load in loads:
        load.wait()


def gram_kernel(sizes, meta, *refs):
    n, tcol_count, piece, width, head_part, block, groups = sizes
    shard_refs = refs[: n + 1]
    round_refs = refs[n + 1 : n + 1 + 3 * groups]
    prior_ref, gram_ref, right_ref, image_ref, columns, rows, target, tile_ref, sent = refs[n + 1 + 3 * groups :]
    me = meta[2 * n]
    total_rows = rows.shape[1]
    count = shard_refs[0].shape[1]
    for index in range(n):
        lanes = pl.ds(pl.multiple_of(meta[index] * count, 128), count)
        base = pl.multiple_of(meta[n + index] * width, 16)
        if index < n - 1:
            columns[pl.ds(base, width), lanes] = shard_refs[index][:width, :]
        else:
            half = shard_refs[n - 1].shape[0]
            columns[pl.ds(base, half), lanes] = shard_refs[n - 1][...]
            columns[pl.ds(pl.multiple_of(base + half, 16), width - half), lanes] = shard_refs[n][...]
    turn = 0
    for group in range(groups):
        own, far, near = round_refs[3 * group : 3 * group + 3]
        for inner in range(own.shape[0]):
            lanes = slice(turn * count, (turn + 1) * count)
            parts = [own[inner], near[0, inner], far[inner], near[1, inner]]
            for j, part in enumerate(parts):
                at = pl.multiple_of(jnp.bitwise_xor(me, j) * head_part, 16)
                target[pl.ds(at, head_part), lanes] = part[:head_part, :]
            rows[:, lanes] = jnp.concatenate([part[head_part:, :] for part in parts], axis=0)
            turn += 1
    scale = 1.0 / total_rows
    stores = tile_copies(gram_ref, tile_ref, me, piece, block, sent, outward=True)
    sides = []
    for step in range(columns.shape[0] // block):
        lanes = slice(step * block, (step + 1) * block)
        column = columns[lanes, :]
        summed = dot(rows[...], column, NT)
        tile_ref[:, lanes] = prior_ref[:, lanes] + summed * scale
        for index in range(step * tcol_count, (step + 1) * tcol_count):
            stores[index].start()
        sides.append(split(dot(column, target[...], NT) * scale))
    right_ref[...] = dot(rows[:piece, :], target[...], NT) * scale
    side = [jnp.concatenate(part, axis=0) for part in zip(*sides)]
    image_ref[...] = product(split(tile_ref[...]), side)
    for store in stores:
        store.wait()


def image_kernel(sizes, meta, *refs):
    n, data_count, tcol_count, piece = sizes
    shard_refs = refs[: n + 1]
    tile_ref, start_ref, near_ref, far_ref, penalty_ref, out_ref, sums_ref, side = refs[n + 1 :]
    for index in range(n):
        base = pl.multiple_of((meta[n + index] * data_count + meta[index]) * piece, 8)
        if index < n - 1:
            side[pl.ds(base, piece), :] = shard_refs[index][...]
        else:
            half = shard_refs[n - 1].shape[0]
            side[pl.ds(base, half), :] = shard_refs[n - 1][...]
            side[pl.ds(pl.multiple_of(base + half, 8), piece - half), :] = shard_refs[n][...]
    total = product(split(tile_ref[...]), split(side[...]))
    own = shard_refs[0][...]
    others = [own, near_ref[0], far_ref[...], near_ref[1]]
    late = jnp.zeros((1, own.shape[1]), jnp.float32)
    for j in range(tcol_count):
        value = total[j * piece : (j + 1) * piece]
        if j == 0:
            value = value + penalty_ref[...] * own
        out_ref[j] = value
        late = late + jnp.sum(value * others[j], axis=0, keepdims=True)
    start = start_ref[...]
    early = [jnp.sum(a * b, axis=0, keepdims=True) for a, b in ((start, start), (start, own), (own, own))]
    sums_ref[...] = jnp.concatenate(early + [late], axis=0)


def call(body, meta, inputs, in_specs, out_specs, out_shape, scratch, vmem, flops, read):
    return pl.pallas_call(
        body,
        grid_spec=pltpu.PrefetchScalarGridSpec(
            num_scalar_prefetch=1,
            grid=(1,),
            in_specs=in_specs,
            out_specs=out_specs,
            scratch_shapes=scratch,
        ),
        out_shape=out_shape,
        compiler_params=pltpu.CompilerParams(vmem_limit_bytes=vmem),
        cost_estimate=pl.CostEstimate(flops=flops, bytes_accessed=read, transcendentals=0),
    )(meta, *inputs)


def all_sum(value, axis_names):
    count = 1
    for name in axis_names:
        count *= lax.axis_size(name)
    spread = jnp.broadcast_to(value[None], (count,) + value.shape)
    return jnp.sum(lax.all_to_all(spread, axis_names, split_axis=0, concat_axis=0, tiled=True), axis=0)


def shards(embeddings, targets, gram_prior, penalty):
    row_count = embeddings.shape[0]
    width = embeddings.shape[3]
    heads = targets.shape[1]
    data_count = lax.axis_size("dp")
    trow_count = lax.axis_size("trow")
    tcol_count = lax.axis_size("tcol")
    piece = width // data_count
    total_rows = row_count * data_count
    tile_rows = tcol_count * piece
    tile_columns = trow_count * width
    head_part = heads // tcol_count
    data_place = lax.axis_index("dp")
    me = lax.axis_index("tcol")
    ring = Ring(data_count, trow_count)
    n = ring.count
    position = jnp.asarray(ring.place)[data_place, lax.axis_index("trow")]
    lookup = np.concatenate([ring.rounds, ring.chunk, ring.trow, ring.data, ring.trow], axis=1)
    lookup = jnp.asarray(lookup)[position]
    rounds = [lookup[turn] for turn in range(data_count)]
    me_meta = jnp.reshape(me, (1,)).astype(jnp.int32)
    gram_meta = jnp.concatenate([lookup[data_count : data_count + 2 * n], me_meta])
    image_meta = jnp.concatenate([lookup[data_count + 2 * n :], me_meta])

    own = embeddings.reshape(row_count, width).T
    head_rows = lax.dynamic_slice_in_dim(targets, me * head_part, head_part, axis=1).T
    payload = jnp.concatenate([own, head_rows], axis=0)

    def piece_of(shard):
        features = lax.dynamic_slice_in_dim(shard, data_place * piece, piece, axis=0)
        return jnp.concatenate([shard[width:], features], axis=0)

    def round_piece(turn):
        choices = sorted(set(ring.rounds[:, turn].tolist()))
        value = piece_of(gathered[choices[0]])
        for choice in choices[1:]:
            value = jnp.where(rounds[turn] == choice, piece_of(gathered[choice]), value)
        return value

    split_turns = [[0], list(range(1, data_count - 1)), [data_count - 1]]
    ready = [int(np.abs(np.asarray(ring.offsets)[ring.rounds[:, turns]]).max()) for turns in split_turns]
    gathered, groups, waiting = [payload], [], []

    def near_of(mine, far, *after):
        mine, far, *after = lax.optimization_barrier((mine, far, *after))
        groups.extend([mine, far, lax.ppermute(jnp.stack([mine, far]), "tcol", swap(tcol_count, 1))])
        return after

    def open_groups(step):
        for turns, when in zip(split_turns, ready):
            if when == step:
                mine = jnp.stack([round_piece(turn) for turn in turns])
                waiting.append((mine, lax.ppermute(mine, "tcol", swap(tcol_count, 2))))

    block = 384 if tile_columns % 384 == 0 else 128
    f32, bf16 = jnp.float32, jnp.bfloat16
    tile_semaphores = pltpu.SemaphoreType.DMA((tcol_count * (tile_columns // block),))

    def fetch(whole):
        return call(
            functools.partial(fetch_kernel, (piece, block)),
            me_meta,
            [whole],
            [HBM],
            VMEM,
            jax.ShapeDtypeStruct((tile_rows, tile_columns), f32),
            [tile_semaphores],
            2**20,
            0,
            8 * tile_rows * tile_columns,
        )

    prior = gram_prior.reshape(tile_rows, tile_columns)
    open_groups(0)
    for step, arrived in enumerate(ring.steps(payload, width), 1):
        arrived = list(arrived)
        if step == 1:
            gram_meta, image_meta, rounds, arrived = lax.optimization_barrier(
                (gram_meta, image_meta, rounds, arrived)
            )
        if step == ring.far - 2:
            prior, *arrived = lax.optimization_barrier((prior, *arrived))
            prior = fetch(prior)
        if step == ring.far - 1:
            prior, *arrived = lax.optimization_barrier((prior, *arrived))
        while waiting:
            arrived = near_of(*waiting.pop(), *arrived)
        gathered += arrived
        open_groups(step)

    gram, start, partial = call(
        functools.partial(
            gram_kernel, (n, tcol_count, piece, width, head_part, block, len(split_turns))
        ),
        gram_meta,
        [*gathered, *groups, prior],
        [VMEM] * (n + 2 + len(groups)),
        [HBM] + [VMEM] * 2,
        [
            jax.ShapeDtypeStruct((tile_rows, tile_columns), f32),
            jax.ShapeDtypeStruct((piece, heads), f32),
            jax.ShapeDtypeStruct((tile_rows, heads), f32),
        ],
        [
            pltpu.VMEM((tile_columns, total_rows), bf16),
            pltpu.VMEM((tile_rows, total_rows), bf16),
            pltpu.VMEM((heads, total_rows), bf16),
            pltpu.VMEM((tile_rows, tile_columns), f32),
            tile_semaphores,
        ],
        GRAM_BYTES,
        2 * tile_rows * tile_columns * (total_rows + 3 * heads),
        12 * tile_rows * tile_columns,
    )
    penalty_rows = penalty.reshape(piece, 1)

    def owner_sum(value, beside=None):
        kept = [value[j] for j in range(tcol_count)]
        received = lax.ppermute(jnp.stack(kept[1::2]), "tcol", swap(tcol_count, 1))
        if beside is not None:
            received, beside = lax.optimization_barrier((received, beside))
        kept = [a + received[i] for i, a in enumerate(kept[0::2])]
        return kept[0] + lax.ppermute(kept[1], "tcol", swap(tcol_count, 2)), beside

    image = owner_sum(partial.reshape(tcol_count, piece, heads))[0] + penalty_rows * start
    far_image = lax.ppermute(image, "tcol", swap(tcol_count, 2))
    near_images = lax.ppermute(jnp.stack([image, far_image]), "tcol", swap(tcol_count, 1))
    images = [image]
    for step, arrived in enumerate(ring.steps(image, piece), 1):
        if step == ring.far - 1:
            arrived = lax.optimization_barrier((*arrived, gram))
            gram = arrived[2]
            tile = fetch(gram)
        images += arrived[:2]
    second, sums = call(
        functools.partial(image_kernel, (n, data_count, tcol_count, piece)),
        image_meta,
        [*images, tile, start, near_images, far_image, penalty_rows],
        [VMEM] * (n + 6),
        [VMEM] * 2,
        [jax.ShapeDtypeStruct((tcol_count, piece, heads), f32), jax.ShapeDtypeStruct((4, heads), f32)],
        [pltpu.VMEM((tile_columns, heads), f32)],
        IMAGE_BYTES,
        6 * tile_rows * tile_columns * heads,
        4 * tile_rows * tile_columns,
    )
    second, sums = owner_sum(second, sums)
    sums = all_sum(sums, ("dp", "trow", "tcol"))

    norm, curvature, image_norm, image_curvature = sums[0], sums[1], sums[2], sums[3]
    step = norm / curvature
    norm_next = step * step * image_norm - norm
    ratio = norm_next / norm
    moved_curvature = step * (step * image_curvature - (1.0 + ratio) * image_norm)
    next_step = norm_next / moved_curvature
    residual = start - step * image
    direction = residual + ratio * start
    weights = step * start + next_step * direction
    residual = residual - next_step * ((1.0 + ratio) * image - step * second)
    out_shape = (1, 1, 1, piece, heads)
    return (gram.reshape(gram_prior.shape), weights.reshape(out_shape), residual.reshape(out_shape))


def solution(mesh):
    placed = (
        P("dp", "tcol", "trow", None),
        P("dp", None),
        P(None, "trow", "dp", None, "tcol"),
        P("tcol", "trow", "dp", None),
    )
    return jax.shard_map(
        shards,
        mesh=mesh,
        in_specs=placed,
        out_specs=(
            P(None, "trow", "dp", None, "tcol"),
            P("tcol", "trow", "dp", None, None),
            P("tcol", "trow", "dp", None, None),
        ),
        check_vma=False,
    )
```

time: 137 us -> 117 us (0.85)
  waiting for transfers between devices: 71.2 us -> 50.3 us
  Pallas kernels: 18 us -> 14.7 us
  local copies, waits for them, and re-layouts: 9.61 us -> 12.3 us
  starting transfers between devices: 29.1 us -> 31 us
    ppermute x24, waiting for transfers between devices: 61.6 us -> 40.5 us  [the longest x6 23.2 us: steps(): ahead = lax.ppermute(ahead, ('dp', 'trow'), self.ahead)]
    ppermute x24, starting transfers between devices: 23.2 us -> 26.5 us  [the longest x6 10.9 us: steps(): ahead = lax.ppermute(ahead, ('dp', 'trow'), self.ahead)]
    pallas_call x2 -> x4, Pallas kernels: 18 us -> 14.7 us  [call(): pl.pallas_call(body, grid_spec=pltpu.PrefetchScalarGridSpec(num_scalar_pr...]
    unnamed x10, local copies, waits for them, and re-layouts: 4.5 us -> 6.83 us
    concatenate x12 -> x10, local copies, waits for them, and re-layouts: 0.11 us -> 1.8 us  [piece_of(): return jnp.concatenate([shard[width:], features], axis=0)]
    ppermute x2, waiting for transfers between devices: 1.71 us -> 3.3 us  [owner_sum(): received = lax.ppermute(jnp.stack(kept[1::2]), 'tcol', swap(tcol_count, 1))]
    squeeze x2 -> x0, local copies, waits for them, and re-layouts: 1.41 us -> none  [the longest x1 0.72 us: shards(): chunk_meta = jnp.asarray(ring.row_chunk)[position]]
  transfers between devices with their start and end apart: 29 -> 29, of which waited for: 17 -> 16; matrix products, arithmetic and copies ran while one was open for 4% -> 3% of each run, Pallas kernels for 0% -> 1%
where the time goes in v3:
time: 117 us
  waiting for transfers between devices  50.3 us (43%)
  starting transfers between devices  31 us (26%)
  Pallas kernels  14.7 us (13%)
  local copies, waits for them, and re-layouts  12.3 us (11%)
  between operations  6.81 us (6%)
  other arithmetic  1.67 us (1%)
    ppermute x6, waiting for transfers between devices, steps(): ahead = lax.ppermute(ahead, ('dp', 'trow'), self.ahead)  23.2 us
    pallas_call x4, Pallas kernels, call(): pl.pallas_call(body, grid_spec=pltpu.PrefetchScalarGridSpec(num_scalar_pr...  14.7 us
    ppermute x6, starting transfers between devices, steps(): ahead = lax.ppermute(ahead, ('dp', 'trow'), self.ahead)  10.9 us
    unnamed x10, local copies, waits for them, and re-layouts  6.83 us
    all_to_all x1, waiting for transfers between devices, all_sum(): lax.all_to_all(spread, axis_names, split_axis=0, concat_axis=0, tiled=True)  6.5 us
    ppermute x2, waiting for transfers between devices, owner_sum(): lax.ppermute(kept[1], 'tcol', swap(tcol_count, 2))  5.48 us
    ppermute x3, starting transfers between devices, open_groups(): waiting.append((mine, lax.ppermute(mine, 'tcol', swap(tcol_count, 2))))  5.11 us
    ppermute x6, waiting for transfers between devices, steps(): back = lax.ppermute(back, ('dp', 'trow'), self.back)  5.08 us
  transfers between devices with their start and end apart: 29, of which 16 were waited for; matrix products, arithmetic and copies ran while one was open for 3% of the time, Pallas kernels for 1%

profile of v3, /device:TPU:0, one launch (start us, length us, event | category | flops | bytes accessed | tf_op | source)
XLA Modules:
  0.0 116.6 jit_solution(3264272604912808211)
XLA Ops:
  2.9 3.1 %collective-permute-start = (bf16[832,256]{1,0:T(8,128)(2,1)S(1)}, bf16[832,256]{1,0:T(8,128)(2,1)S(1)}, u32[]{:S(2)}, u32[]{:S(2)}) collective-permute-start(bf16[832,256]{1,0:T(8,128)(2,1)S(1)} %pad_maximum_fusion.refs_0_), channel_id=1, source_target_pairs={{0,8},{8,16},{16,24},{24,28},{28,20},{20,12},{12,4},{4,0},{1,9},{9... | collective-permute-start | bytes 1277960 | tf_op jit(solution)/shard_map/ppermute | solution.py:60
  6.2 2.0 %collective-permute-start.2 = (bf16[1,256,256]{2,1,0:T(8,128)(2,1)S(1)}, bf16[1,256,256]{2,1,0:T(8,128)(2,1)S(1)}, u32[]{:S(2)}, u32[]{:S(2)}) collective-permute-start(bf16[1,256,256]{2,1,0:T(8,128)(2,1)S(1)} %maximum_bitcast_fusion.refs_9_), channel_id=1, source_target_pairs={{0,2},{1,3},{2,0},{3,1},{4,6},{5,7},{6,4},{7,5},{8,10},{9,11},{10,... | collective-permute-start | bytes 393224 | tf_op jit(solution)/shard_map/ppermute | solution.py:254
  12.9 2.9 %collective-permute-done.refs_1_ = bf16[832,256]{1,0:T(8,128)(2,1)S(1)} collective-permute-done((bf16[832,256]{1,0:T(8,128)(2,1)S(1)}, bf16[832,256]{1,0:T(8,128)(2,1)S(1)}, u32[]{:S(2)}, u32[]{:S(2)}) %collective-permute-start) | collective-permute-done | bytes 426016 | tf_op jit(solution)/shard_map/ppermute | solution.py:60
  15.8 1.5 %collective-permute-done.1.refs_2_ = bf16[832,256]{1,0:T(8,128)(2,1)S(1)} collective-permute-done((bf16[832,256]{1,0:T(8,128)(2,1)S(1)}, bf16[832,256]{1,0:T(8,128)(2,1)S(1)}, u32[]{:S(2)}, u32[]{:S(2)}) %collective-permute-start.1) | collective-permute-done | bytes 426016 | tf_op jit(solution)/shard_map/ppermute | solution.py:61
  19.3 1.6 %collective-permute-start.3 = (bf16[832,256]{1,0:T(8,128)(2,1)S(1)}, bf16[832,256]{1,0:T(8,128)(2,1)}, u32[]{:S(2)}, u32[]{:S(2)}) collective-permute-start(bf16[832,256]{1,0:T(8,128)(2,1)S(1)} %collective-permute-done.refs_1_), channel_id=1, source_target_pairs={{0,8},{8,16},{16,24},{24,28},{28,20},{20,12},{12,4},{4,0},{1,9},{9... | collective-permute-start | bytes 1277960 | tf_op jit(solution)/shard_map/ppermute | solution.py:60
  21.3 8.4 %collective-permute-done.3.refs_3_ = bf16[832,256]{1,0:T(8,128)(2,1)} collective-permute-done((bf16[832,256]{1,0:T(8,128)(2,1)S(1)}, bf16[832,256]{1,0:T(8,128)(2,1)}, u32[]{:S(2)}, u32[]{:S(2)}) %collective-permute-start.3) | collective-permute-done | bytes 426016 | tf_op jit(solution)/shard_map/ppermute | solution.py:60
  32.8 1.6 %collective-permute-start.6 = (bf16[832,256]{1,0:T(8,128)(2,1)}, bf16[832,256]{1,0:T(8,128)(2,1)S(1)}, u32[]{:S(2)}, u32[]{:S(2)}) collective-permute-start(bf16[832,256]{1,0:T(8,128)(2,1)} %collective-permute-done.3.refs_3_), channel_id=1, source_target_pairs={{0,8},{8,16},{16,24},{24,28},{28,20},{20,12},{12,4},{4,0},{1,9},{9... | collective-permute-start | bytes 1277960 | tf_op jit(solution)/shard_map/ppermute | solution.py:60
  35.0 1.6 %collective-permute-start.5 = (bf16[2,256,256]{2,1,0:T(8,128)(2,1)S(1)}, bf16[2,256,256]{2,1,0:T(8,128)(2,1)S(1)}, u32[]{:S(2)}, u32[]{:S(2)}) collective-permute-start(bf16[2,256,256]{2,1,0:T(8,128)(2,1)S(1)} %pad_maximum_fusion.5.refs_12_), channel_id=1, source_target_pairs={{0,2},{1,3},{2,0},{3,1},{4,6},{5,7},{6,4},{7,5},{8,10},{9,11},{10,... | collective-permute-start | bytes 786440 | tf_op jit(solution)/shard_map/ppermute | solution.py:254
  38.5 2.3 %copy-done.1 = f32[4,1,1,192,1536]{4,3,2,1,0:T(8,128)S(1)} copy-done((f32[4,1,1,192,1536]{4,3,2,1,0:T(8,128)S(1)}, f32[4,1,1,192,1536]{4,3,2,1,0:T(8,128)}, u32[]{:S(2)}) %copy-start.1) | copy-done | bytes 4718616
  42.2 2.3 %collective-permute-done.7.refs_6_ = bf16[832,256]{1,0:T(8,128)(2,1)S(1)} collective-permute-done((bf16[832,256]{1,0:T(8,128)(2,1)}, bf16[832,256]{1,0:T(8,128)(2,1)S(1)}, u32[]{:S(2)}, u32[]{:S(2)}) %collective-permute-start.7) | collective-permute-done | bytes 426016 | tf_op jit(solution)/shard_map/ppermute | solution.py:61
  45.1 1.6 %collective-permute-start.9 = (bf16[384,256]{1,0:T(8,128)(2,1)S(1)}, bf16[384,256]{1,0:T(8,128)(2,1)S(1)}, u32[]{:S(2)}, u32[]{:S(2)}) collective-permute-start(bf16[384,256]{1,0:T(8,128)(2,1)S(1)} %slice.150), channel_id=1, source_target_pairs={{0,8},{8,16},{16,24},{24,28},{28,20},{20,12},{12,4},{4,0},{1,9},{9... | collective-permute-start | bytes 589832 | tf_op jit(solution)/shard_map/ppermute | solution.py:64
  46.9 1.6 %collective-permute-start.8 = (bf16[1,256,256]{2,1,0:T(8,128)(2,1)S(1)}, bf16[1,256,256]{2,1,0:T(8,128)(2,1)S(1)}, u32[]{:S(2)}, u32[]{:S(2)}) collective-permute-start(bf16[1,256,256]{2,1,0:T(8,128)(2,1)S(1)} %maximum_select_fusion.1.refs_15_), channel_id=1, source_target_pairs={{0,2},{1,3},{2,0},{3,1},{4,6},{5,7},{6,4},{7,5},{8,10},{9,11},{10,... | collective-permute-start | bytes 393224 | tf_op jit(solution)/shard_map/ppermute | solution.py:254
  48.8 4.1 %collective-permute-done.8.refs_16_ = bf16[1,256,256]{2,1,0:T(8,128)(2,1)S(1)} collective-permute-done((bf16[1,256,256]{2,1,0:T(8,128)(2,1)S(1)}, bf16[1,256,256]{2,1,0:T(8,128)(2,1)S(1)}, u32[]{:S(2)}, u32[]{:S(2)}) %collective-permute-start.8) | collective-permute-done | bytes 131104 | tf_op jit(solution)/shard_map/ppermute | solution.py:254
  53.0 1.5 %collective-permute-done.13.refs_17_ = bf16[2,1,256,256]{3,2,1,0:T(8,128)(2,1)S(1)} collective-permute-done((bf16[2,1,256,256]{3,2,1,0:T(8,128)(2,1)S(1)}, bf16[2,1,256,256]{3,2,1,0:T(8,128)(2,1)S(1)}, u32[]{:S(2)}, u32[]{:S(2)}) %collective-permute-start.13) | collective-permute-done | bytes 262176 | tf_op jit(solution)/shard_map/ppermute | solution.py:247
  54.5 11.0 %shard_map.86 = (f32[768,1536]{1,0:T(8,128)}, f32[192,256]{1,0:T(8,128)S(1)}, f32[768,256]{1,0:T(8,128)S(1)}) custom-call(s32[17]{0:T(128)S(1)} %get-tuple-element.38.meta, bf16[832,256]{1,0:T(8,128)(2,1)S(1)} %pad_maximum_fusion.refs_0_, bf16[832,256]{1,0:T(8,128)(2,1)S(1)} %collective-permute-done.refs_1_, ...), custom_call_target="tpu_custom_call" | custom-call | flops 4227858432 | bytes 14155776 | tf_op jit(solution)/shard_map/pallas_call | solution.py:179
  65.8 1.6 %collective-permute-done.14 = f32[2,192,256]{2,1,0:T(8,128)S(1)} collective-permute-done((f32[2,192,256]{2,1,0:T(8,128)S(1)}, f32[2,192,256]{2,1,0:T(8,128)S(1)}, u32[]{:S(2)}, u32[]{:S(2)}) %collective-permute-start.14) | collective-permute-done | bytes 393248 | tf_op jit(solution)/shard_map/ppermute | solution.py:320
  67.5 1.6 %collective-permute-start.15 = (f32[192,256]{1,0:T(8,128)S(1)}, f32[192,256]{1,0:T(8,128)S(1)}, u32[]{:S(2)}, u32[]{:S(2)}) collective-permute-start(f32[192,256]{1,0:T(8,128)S(1)} %fusion), channel_id=1, source_target_pairs={{0,2},{1,3},{2,0},{3,1},{4,6},{5,7},{6,4},{7,5},{8,10},{9,11},{10,... | collective-permute-start | bytes 589832 | tf_op jit(solution)/shard_map/ppermute | solution.py:324
  69.0 5.5 %collective-permute-done.15 = f32[192,256]{1,0:T(8,128)S(1)} collective-permute-done((f32[192,256]{1,0:T(8,128)S(1)}, f32[192,256]{1,0:T(8,128)S(1)}, u32[]{:S(2)}, u32[]{:S(2)}) %collective-permute-start.15) | collective-permute-done | bytes 196640 | tf_op jit(solution)/shard_map/ppermute | solution.py:324
  74.6 1.6 %collective-permute-start.16 = (f32[192,256]{1,0:T(8,128)S(1)}, f32[192,256]{1,0:T(8,128)S(1)}, u32[]{:S(2)}, u32[]{:S(2)}) collective-permute-start(f32[192,256]{1,0:T(8,128)S(1)} %fusion.3.refs_0_), channel_id=1, source_target_pairs={{0,8},{8,16},{16,24},{24,28},{28,20},{20,12},{12,4},{4,0},{1,9},{9... | collective-permute-start | bytes 589832 | tf_op jit(solution)/shard_map/ppermute | solution.py:60
  76.7 1.5 %collective-permute-start.24 = (f32[192,256]{1,0:T(8,128)S(1)}, f32[192,256]{1,0:T(8,128)S(1)}, u32[]{:S(2)}, u32[]{:S(2)}) collective-permute-start(f32[192,256]{1,0:T(8,128)S(1)} %fusion.3.refs_0_), channel_id=1, source_target_pairs={{0,2},{1,3},{2,0},{3,1},{4,6},{5,7},{6,4},{7,5},{8,10},{9,11},{10,... | collective-permute-start | bytes 589832 | tf_op jit(solution)/shard_map/ppermute | solution.py:327
  78.1 2.6 %collective-permute-done.16.refs_1_ = f32[192,256]{1,0:T(8,128)S(1)} collective-permute-done((f32[192,256]{1,0:T(8,128)S(1)}, f32[192,256]{1,0:T(8,128)S(1)}, u32[]{:S(2)}, u32[]{:S(2)}) %collective-permute-start.16) | collective-permute-done | bytes 196640 | tf_op jit(solution)/shard_map/ppermute | solution.py:60
  80.7 1.5 %collective-permute-start.17 = (f32[192,256]{1,0:T(8,128)S(1)}, f32[192,256]{1,0:T(8,128)S(1)}, u32[]{:S(2)}, u32[]{:S(2)}) collective-permute-start(f32[192,256]{1,0:T(8,128)S(1)} %collective-permute-done.16.refs_1_), channel_id=1, source_target_pairs={{0,8},{8,16},{16,24},{24,28},{28,20},{20,12},{12,4},{4,0},{1,9},{9... | collective-permute-start | bytes 589832 | tf_op jit(solution)/shard_map/ppermute | solution.py:60
  82.9 3.6 %collective-permute-done.17.refs_3_ = f32[192,256]{1,0:T(8,128)S(1)} collective-permute-done((f32[192,256]{1,0:T(8,128)S(1)}, f32[192,256]{1,0:T(8,128)S(1)}, u32[]{:S(2)}, u32[]{:S(2)}) %collective-permute-start.17) | collective-permute-done | bytes 196640 | tf_op jit(solution)/shard_map/ppermute | solution.py:60
  86.5 1.5 %collective-permute-start.18 = (f32[192,256]{1,0:T(8,128)S(1)}, f32[192,256]{1,0:T(8,128)S(1)}, u32[]{:S(2)}, u32[]{:S(2)}) collective-permute-start(f32[192,256]{1,0:T(8,128)S(1)} %collective-permute-done.17.refs_3_), channel_id=1, source_target_pairs={{0,8},{8,16},{16,24},{24,28},{28,20},{20,12},{12,4},{4,0},{1,9},{9... | collective-permute-start | bytes 589832 | tf_op jit(solution)/shard_map/ppermute | solution.py:60
  88.5 4.7 %collective-permute-done.18.refs_5_ = f32[192,256]{1,0:T(8,128)S(1)} collective-permute-done((f32[192,256]{1,0:T(8,128)S(1)}, f32[192,256]{1,0:T(8,128)S(1)}, u32[]{:S(2)}, u32[]{:S(2)}) %collective-permute-start.18) | collective-permute-done | bytes 196640 | tf_op jit(solution)/shard_map/ppermute | solution.py:60
  93.2 1.6 %collective-permute-start.22 = (f32[96,256]{1,0:T(8,128)S(1)}, f32[96,256]{1,0:T(8,128)S(1)}, u32[]{:S(2)}, u32[]{:S(2)}) collective-permute-start(f32[96,256]{1,0:T(8,128)S(1)} %slice.154), channel_id=1, source_target_pairs={{0,8},{8,16},{16,24},{24,28},{28,20},{20,12},{12,4},{4,0},{1,9},{9... | collective-permute-start | bytes 294920 | tf_op jit(solution)/shard_map/ppermute | solution.py:64
  95.7 2.3 %copy-done.2 = f32[768,1536]{1,0:T(8,128)S(1)} copy-done((f32[768,1536]{1,0:T(8,128)S(1)}, f32[768,1536]{1,0:T(8,128)}, u32[]{:S(2)}) %copy-start.2) | copy-done | bytes 4718616
  99.7 2.7 %shard_map.88 = (f32[4,192,256]{2,1,0:T(8,128)S(1)}, f32[4,256]{1,0:T(4,128)S(1)}) custom-call(s32[17]{0:T(128)S(1)} %get-tuple-element.66.meta, f32[192,256]{1,0:T(8,128)S(1)} %fusion.3.refs_0_, f32[192,256]{1,0:T(8,128)S(1)} %collective-permute-done.16.refs_1_, f32[192,256]{1,0:T(8,128)S(1)} %collective-permute-done.19.refs_2_, ...), custom_call_target="tpu_custom_call" | custom-call | flops 1811939328 | bytes 4718592 | tf_op jit(solution)/shard_map/pallas_call | solution.py:179
  102.5 1.7 %collective-permute-done.26 = f32[2,192,256]{2,1,0:T(8,128)S(1)} collective-permute-done((f32[2,192,256]{2,1,0:T(8,128)S(1)}, f32[2,192,256]{2,1,0:T(8,128)S(1)}, u32[]{:S(2)}, u32[]{:S(2)}) %collective-permute-start.26) | collective-permute-done | bytes 393248 | tf_op jit(solution)/shard_map/ppermute | solution.py:320
  104.9 2.6 %all-to-all-start = ((f32[32,4,256]{2,1,0:T(4,128)}), f32[32,4,256]{2,1,0:T(4,128)S(1)}, u32[]{:S(2)}, u32[]{:S(2)}) async-start(f32[32,4,256]{2,1,0:T(4,128)} %broadcast_in_dim.2), calls=%async_computation | async-start | bytes 262144 | tf_op jit(solution)/shard_map/all_to_all | solution.py:199
  107.5 1.7 %collective-permute-start.27 = (f32[192,256]{1,0:T(8,128)S(1)}, f32[192,256]{1,0:T(8,128)S(1)}, u32[]{:S(2)}, u32[]{:S(2)}) collective-permute-start(f32[192,256]{1,0:T(8,128)S(1)} %add_bitcast_fusion), channel_id=1, source_target_pairs={{0,2},{1,3},{2,0},{3,1},{4,6},{5,7},{6,4},{7,5},{8,10},{9,11},{10,... | collective-permute-start | bytes 589832 | tf_op jit(solution)/shard_map/ppermute | solution.py:324
  109.2 6.5 %all-to-all-done = f32[32,4,256]{2,1,0:T(4,128)S(1)} async-done(((f32[32,4,256]{2,1,0:T(4,128)}), f32[32,4,256]{2,1,0:T(4,128)S(1)}, u32[]{:S(2)}, u32[]{:S(2)}) %all-to-all-start) | async-done | bytes 131104 | tf_op jit(solution)/shard_map/all_to_all | solution.py:199
  (83 shorter events, 18.1 us)
Async XLA Ops:
  2.9 12.8 %collective-permute-start = (bf16[832,256]{1,0:T(8,128)(2,1)S(1)}, bf16[832,256]{1,0:T(8,128)(2,1)S(1)}, u32[]{:S(2)}, u32[]{:S(2)}) collective-permute-start(bf16[832,256]{1,0:T(8,128)(2,1)S(1)} %pad_maximum_fusion.refs_0_), channel_id=1, source_target_pairs={{0,8},{8,16},{16,24},{24,28},{28,20},{20,12},{12,4},{4,0},{1,9},{9... | collective-permute-start | bytes 1277960 | tf_op jit(solution)/shard_map/ppermute | solution.py:60
  6.0 11.3 %collective-permute-start.1 = (bf16[832,256]{1,0:T(8,128)(2,1)S(1)}, bf16[832,256]{1,0:T(8,128)(2,1)S(1)}, u32[]{:S(2)}, u32[]{:S(2)}) collective-permute-start(bf16[832,256]{1,0:T(8,128)(2,1)S(1)} %pad_maximum_fusion.refs_0_), channel_id=1, source_target_pairs={{8,0},{16,8},{24,16},{28,24},{20,28},{12,20},{4,12},{0,4},{9,1},{1... | collective-permute-start | bytes 1277960 | tf_op jit(solution)/shard_map/ppermute | solution.py:61
  6.2 11.1 %collective-permute-start.2 = (bf16[1,256,256]{2,1,0:T(8,128)(2,1)S(1)}, bf16[1,256,256]{2,1,0:T(8,128)(2,1)S(1)}, u32[]{:S(2)}, u32[]{:S(2)}) collective-permute-start(bf16[1,256,256]{2,1,0:T(8,128)(2,1)S(1)} %maximum_bitcast_fusion.refs_9_), channel_id=1, source_target_pairs={{0,2},{1,3},{2,0},{3,1},{4,6},{5,7},{6,4},{7,5},{8,10},{9,11},{10,... | collective-permute-start | bytes 393224 | tf_op jit(solution)/shard_map/ppermute | solution.py:254
  19.3 10.5 %collective-permute-start.3 = (bf16[832,256]{1,0:T(8,128)(2,1)S(1)}, bf16[832,256]{1,0:T(8,128)(2,1)}, u32[]{:S(2)}, u32[]{:S(2)}) collective-permute-start(bf16[832,256]{1,0:T(8,128)(2,1)S(1)} %collective-permute-done.refs_1_), channel_id=1, source_target_pairs={{0,8},{8,16},{16,24},{24,28},{28,20},{20,12},{12,4},{4,0},{1,9},{9... | collective-permute-start | bytes 1277960 | tf_op jit(solution)/shard_map/ppermute | solution.py:60
  20.9 10.2 %collective-permute-start.4 = (bf16[832,256]{1,0:T(8,128)(2,1)S(1)}, bf16[832,256]{1,0:T(8,128)(2,1)}, u32[]{:S(2)}, u32[]{:S(2)}) collective-permute-start(bf16[832,256]{1,0:T(8,128)(2,1)S(1)} %collective-permute-done.1.refs_2_), channel_id=1, source_target_pairs={{8,0},{16,8},{24,16},{28,24},{20,28},{12,20},{4,12},{0,4},{9,1},{1... | collective-permute-start | bytes 1277960 | tf_op jit(solution)/shard_map/ppermute | solution.py:61
  32.8 9.4 %collective-permute-start.6 = (bf16[832,256]{1,0:T(8,128)(2,1)}, bf16[832,256]{1,0:T(8,128)(2,1)S(1)}, u32[]{:S(2)}, u32[]{:S(2)}) collective-permute-start(bf16[832,256]{1,0:T(8,128)(2,1)} %collective-permute-done.3.refs_3_), channel_id=1, source_target_pairs={{0,8},{8,16},{16,24},{24,28},{28,20},{20,12},{12,4},{4,0},{1,9},{9... | collective-permute-start | bytes 1277960 | tf_op jit(solution)/shard_map/ppermute | solution.py:60
  34.4 10.1 %collective-permute-start.7 = (bf16[832,256]{1,0:T(8,128)(2,1)}, bf16[832,256]{1,0:T(8,128)(2,1)S(1)}, u32[]{:S(2)}, u32[]{:S(2)}) collective-permute-start(bf16[832,256]{1,0:T(8,128)(2,1)} %collective-permute-done.4.refs_4_), channel_id=1, source_target_pairs={{8,0},{16,8},{24,16},{28,24},{20,28},{12,20},{4,12},{0,4},{9,1},{1... | collective-permute-start | bytes 1277960 | tf_op jit(solution)/shard_map/ppermute | solution.py:61
  35.0 9.5 %collective-permute-start.5 = (bf16[2,256,256]{2,1,0:T(8,128)(2,1)S(1)}, bf16[2,256,256]{2,1,0:T(8,128)(2,1)S(1)}, u32[]{:S(2)}, u32[]{:S(2)}) collective-permute-start(bf16[2,256,256]{2,1,0:T(8,128)(2,1)S(1)} %pad_maximum_fusion.5.refs_12_), channel_id=1, source_target_pairs={{0,2},{1,3},{2,0},{3,1},{4,6},{5,7},{6,4},{7,5},{8,10},{9,11},{10,... | collective-permute-start | bytes 786440 | tf_op jit(solution)/shard_map/ppermute | solution.py:254
  38.5 2.3 %copy-start.1 = (f32[4,1,1,192,1536]{4,3,2,1,0:T(8,128)S(1)}, f32[4,1,1,192,1536]{4,3,2,1,0:T(8,128)}, u32[]{:S(2)}) copy-start(f32[4,1,1,192,1536]{4,3,2,1,0:T(8,128)} %param.8) | copy-start | bytes 14155780
  44.5 8.3 %collective-permute-start.10 = (bf16[384,256]{1,0:T(8,128)(2,1)S(1)}, bf16[384,256]{1,0:T(8,128)(2,1)S(1)}, u32[]{:S(2)}, u32[]{:S(2)}) collective-permute-start(bf16[384,256]{1,0:T(8,128)(2,1)S(1)} %slice.151), channel_id=1, source_target_pairs={{8,0},{16,8},{24,16},{28,24},{20,28},{12,20},{4,12},{0,4},{9,1},{1... | collective-permute-start | bytes 589832 | tf_op jit(solution)/shard_map/ppermute | solution.py:65
  45.1 7.8 %collective-permute-start.9 = (bf16[384,256]{1,0:T(8,128)(2,1)S(1)}, bf16[384,256]{1,0:T(8,128)(2,1)S(1)}, u32[]{:S(2)}, u32[]{:S(2)}) collective-permute-start(bf16[384,256]{1,0:T(8,128)(2,1)S(1)} %slice.150), channel_id=1, source_target_pairs={{0,8},{8,16},{16,24},{24,28},{28,20},{20,12},{12,4},{4,0},{1,9},{9... | collective-permute-start | bytes 589832 | tf_op jit(solution)/shard_map/ppermute | solution.py:64
  46.7 7.8 %collective-permute-start.12 = (bf16[2,2,256,256]{3,2,1,0:T(8,128)(2,1)S(1)}, bf16[2,2,256,256]{3,2,1,0:T(8,128)(2,1)S(1)}, u32[]{:S(2)}, u32[]{:S(2)}) collective-permute-start(bf16[2,2,256,256]{3,2,1,0:T(8,128)(2,1)S(1)} %pad_maximum_fusion.1), channel_id=1, source_target_pairs={{0,1},{1,0},{2,3},{3,2},{4,5},{5,4},{6,7},{7,6},{8,9},{9,8},{10,11... | collective-permute-start | bytes 1572872 | tf_op jit(solution)/shard_map/ppermute | solution.py:247
  46.9 6.0 %collective-permute-start.8 = (bf16[1,256,256]{2,1,0:T(8,128)(2,1)S(1)}, bf16[1,256,256]{2,1,0:T(8,128)(2,1)S(1)}, u32[]{:S(2)}, u32[]{:S(2)}) collective-permute-start(bf16[1,256,256]{2,1,0:T(8,128)(2,1)S(1)} %maximum_select_fusion.1.refs_15_), channel_id=1, source_target_pairs={{0,2},{1,3},{2,0},{3,1},{4,6},{5,7},{6,4},{7,5},{8,10},{9,11},{10,... | collective-permute-start | bytes 393224 | tf_op jit(solution)/shard_map/ppermute | solution.py:254
  48.5 4.5 %collective-permute-start.11 = (bf16[2,1,256,256]{3,2,1,0:T(8,128)(2,1)S(1)}, bf16[2,1,256,256]{3,2,1,0:T(8,128)(2,1)S(1)}, u32[]{:S(2)}, u32[]{:S(2)}) collective-permute-start(bf16[2,1,256,256]{3,2,1,0:T(8,128)(2,1)S(1)} %pad_maximum_fusion.6), channel_id=1, source_target_pairs={{0,1},{1,0},{2,3},{3,2},{4,5},{5,4},{6,7},{7,6},{8,9},{9,8},{10,11... | collective-permute-start | bytes 786440 | tf_op jit(solution)/shard_map/ppermute | solution.py:247
  52.9 21.6 %copy-start.3 = (f32[1,1,1,192]{3,2,1,0:T(1,128)S(1)}, f32[1,1,1,192]{3,2,1,0:T(1,128)}, u32[]{:S(2)}) copy-start(f32[1,1,1,192]{3,2,1,0:T(1,128)} %param.9) | copy-start | bytes 2308
  52.9 1.6 %collective-permute-start.13 = (bf16[2,1,256,256]{3,2,1,0:T(8,128)(2,1)S(1)}, bf16[2,1,256,256]{3,2,1,0:T(8,128)(2,1)S(1)}, u32[]{:S(2)}, u32[]{:S(2)}) collective-permute-start(bf16[2,1,256,256]{3,2,1,0:T(8,128)(2,1)S(1)} %pad_maximum_fusion.7), channel_id=1, source_target_pairs={{0,1},{1,0},{2,3},{3,2},{4,5},{5,4},{6,7},{7,6},{8,9},{9,8},{10,11... | collective-permute-start | bytes 786440 | tf_op jit(solution)/shard_map/ppermute | solution.py:247
  65.6 1.8 %collective-permute-start.14 = (f32[2,192,256]{2,1,0:T(8,128)S(1)}, f32[2,192,256]{2,1,0:T(8,128)S(1)}, u32[]{:S(2)}, u32[]{:S(2)}) collective-permute-start(f32[2,192,256]{2,1,0:T(8,128)S(1)} %pad_maximum_fusion.2), channel_id=1, source_target_pairs={{0,1},{1,0},{2,3},{3,2},{4,5},{5,4},{6,7},{7,6},{8,9},{9,8},{10,11... | collective-permute-start | bytes 1179656 | tf_op jit(solution)/shard_map/ppermute | solution.py:320
  67.5 7.0 %collective-permute-start.15 = (f32[192,256]{1,0:T(8,128)S(1)}, f32[192,256]{1,0:T(8,128)S(1)}, u32[]{:S(2)}, u32[]{:S(2)}) collective-permute-start(f32[192,256]{1,0:T(8,128)S(1)} %fusion), channel_id=1, source_target_pairs={{0,2},{1,3},{2,0},{3,1},{4,6},{5,7},{6,4},{7,5},{8,10},{9,11},{10,... | collective-permute-start | bytes 589832 | tf_op jit(solution)/shard_map/ppermute | solution.py:324
  74.6 6.2 %collective-permute-start.16 = (f32[192,256]{1,0:T(8,128)S(1)}, f32[192,256]{1,0:T(8,128)S(1)}, u32[]{:S(2)}, u32[]{:S(2)}) collective-permute-start(f32[192,256]{1,0:T(8,128)S(1)} %fusion.3.refs_0_), channel_id=1, source_target_pairs={{0,8},{8,16},{16,24},{24,28},{28,20},{20,12},{12,4},{4,0},{1,9},{9... | collective-permute-start | bytes 589832 | tf_op jit(solution)/shard_map/ppermute | solution.py:60
  76.1 6.1 %collective-permute-start.19 = (f32[192,256]{1,0:T(8,128)S(1)}, f32[192,256]{1,0:T(8,128)S(1)}, u32[]{:S(2)}, u32[]{:S(2)}) collective-permute-start(f32[192,256]{1,0:T(8,128)S(1)} %fusion.3.refs_0_), channel_id=1, source_target_pairs={{8,0},{16,8},{24,16},{28,24},{20,28},{12,20},{4,12},{0,4},{9,1},{1... | collective-permute-start | bytes 589832 | tf_op jit(solution)/shard_map/ppermute | solution.py:61
  76.7 6.1 %collective-permute-start.24 = (f32[192,256]{1,0:T(8,128)S(1)}, f32[192,256]{1,0:T(8,128)S(1)}, u32[]{:S(2)}, u32[]{:S(2)}) collective-permute-start(f32[192,256]{1,0:T(8,128)S(1)} %fusion.3.refs_0_), channel_id=1, source_target_pairs={{0,2},{1,3},{2,0},{3,1},{4,6},{5,7},{6,4},{7,5},{8,10},{9,11},{10,... | collective-permute-start | bytes 589832 | tf_op jit(solution)/shard_map/ppermute | solution.py:327
  80.7 5.8 %collective-permute-start.17 = (f32[192,256]{1,0:T(8,128)S(1)}, f32[192,256]{1,0:T(8,128)S(1)}, u32[]{:S(2)}, u32[]{:S(2)}) collective-permute-start(f32[192,256]{1,0:T(8,128)S(1)} %collective-permute-done.16.refs_1_), channel_id=1, source_target_pairs={{0,8},{8,16},{16,24},{24,28},{28,20},{20,12},{12,4},{4,0},{1,9},{9... | collective-permute-start | bytes 589832 | tf_op jit(solution)/shard_map/ppermute | solution.py:60
  82.3 5.8 %collective-permute-start.20 = (f32[192,256]{1,0:T(8,128)S(1)}, f32[192,256]{1,0:T(8,128)S(1)}, u32[]{:S(2)}, u32[]{:S(2)}) collective-permute-start(f32[192,256]{1,0:T(8,128)S(1)} %collective-permute-done.19.refs_2_), channel_id=1, source_target_pairs={{8,0},{16,8},{24,16},{28,24},{20,28},{12,20},{4,12},{0,4},{9,1},{1... | collective-permute-start | bytes 589832 | tf_op jit(solution)/shard_map/ppermute | solution.py:61
  82.8 15.7 %collective-permute-start.25 = (f32[2,192,256]{2,1,0:T(8,128)S(1)}, f32[2,192,256]{2,1,0:T(8,128)S(1)}, u32[]{:S(2)}, u32[]{:S(2)}) collective-permute-start(f32[2,192,256]{2,1,0:T(8,128)S(1)} %pad_maximum_fusion.3), channel_id=1, source_target_pairs={{0,1},{1,0},{2,3},{3,2},{4,5},{5,4},{6,7},{7,6},{8,9},{9,8},{10,11... | collective-permute-start | bytes 1179656 | tf_op jit(solution)/shard_map/ppermute | solution.py:328
  86.5 6.7 %collective-permute-start.18 = (f32[192,256]{1,0:T(8,128)S(1)}, f32[192,256]{1,0:T(8,128)S(1)}, u32[]{:S(2)}, u32[]{:S(2)}) collective-permute-start(f32[192,256]{1,0:T(8,128)S(1)} %collective-permute-done.17.refs_3_), channel_id=1, source_target_pairs={{0,8},{8,16},{16,24},{24,28},{28,20},{20,12},{12,4},{4,0},{1,9},{9... | collective-permute-start | bytes 589832 | tf_op jit(solution)/shard_map/ppermute | solution.py:60
  88.0 6.8 %collective-permute-start.21 = (f32[192,256]{1,0:T(8,128)S(1)}, f32[192,256]{1,0:T(8,128)S(1)}, u32[]{:S(2)}, u32[]{:S(2)}) collective-permute-start(f32[192,256]{1,0:T(8,128)S(1)} %collective-permute-done.20.refs_4_), channel_id=1, source_target_pairs={{8,0},{16,8},{24,16},{28,24},{20,28},{12,20},{4,12},{0,4},{9,1},{1... | collective-permute-start | bytes 589832 | tf_op jit(solution)/shard_map/ppermute | solution.py:61
  93.2 5.3 %collective-permute-start.22 = (f32[96,256]{1,0:T(8,128)S(1)}, f32[96,256]{1,0:T(8,128)S(1)}, u32[]{:S(2)}, u32[]{:S(2)}) collective-permute-start(f32[96,256]{1,0:T(8,128)S(1)} %slice.154), channel_id=1, source_target_pairs={{0,8},{8,16},{16,24},{24,28},{28,20},{20,12},{12,4},{4,0},{1,9},{9... | collective-permute-start | bytes 294920 | tf_op jit(solution)/shard_map/ppermute | solution.py:64
  94.8 4.8 %collective-permute-start.23 = (f32[96,256]{1,0:T(8,128)S(1)}, f32[96,256]{1,0:T(8,128)S(1)}, u32[]{:S(2)}, u32[]{:S(2)}) collective-permute-start(f32[96,256]{1,0:T(8,128)S(1)} %slice.155), channel_id=1, source_target_pairs={{8,0},{16,8},{24,16},{28,24},{20,28},{12,20},{4,12},{0,4},{9,1},{1... | collective-permute-start | bytes 294920 | tf_op jit(solution)/shard_map/ppermute | solution.py:65
  95.7 2.3 %copy-start.2 = (f32[768,1536]{1,0:T(8,128)S(1)}, f32[768,1536]{1,0:T(8,128)}, u32[]{:S(2)}) copy-start(f32[768,1536]{1,0:T(8,128)} %get-tuple-element.65.gram_ref) | copy-start | bytes 14155780
  102.4 1.8 %collective-permute-start.26 = (f32[2,192,256]{2,1,0:T(8,128)S(1)}, f32[2,192,256]{2,1,0:T(8,128)S(1)}, u32[]{:S(2)}, u32[]{:S(2)}) collective-permute-start(f32[2,192,256]{2,1,0:T(8,128)S(1)} %pad_maximum_fusion.4), channel_id=1, source_target_pairs={{0,1},{1,0},{2,3},{3,2},{4,5},{5,4},{6,7},{7,6},{8,9},{9,8},{10,11... | collective-permute-start | bytes 1179656 | tf_op jit(solution)/shard_map/ppermute | solution.py:320
  104.9 10.8 %all-to-all-start = ((f32[32,4,256]{2,1,0:T(4,128)}), f32[32,4,256]{2,1,0:T(4,128)S(1)}, u32[]{:S(2)}, u32[]{:S(2)}) async-start(f32[32,4,256]{2,1,0:T(4,128)} %broadcast_in_dim.2), calls=%async_computation | async-start | bytes 262144 | tf_op jit(solution)/shard_map/all_to_all | solution.py:199
  107.5 8.3 %collective-permute-start.27 = (f32[192,256]{1,0:T(8,128)S(1)}, f32[192,256]{1,0:T(8,128)S(1)}, u32[]{:S(2)}, u32[]{:S(2)}) collective-permute-start(f32[192,256]{1,0:T(8,128)S(1)} %add_bitcast_fusion), channel_id=1, source_target_pairs={{0,2},{1,3},{2,0},{3,1},{4,6},{5,7},{6,4},{7,5},{8,10},{9,11},{10,... | collective-permute-start | bytes 589832 | tf_op jit(solution)/shard_map/ppermute | solution.py:324
  (1 other events, 0.9 us)

commit v4 on v3

--- a/solution.py
+++ b/solution.py
@@ -12,6 +12,7 @@
 NN = (((1,), (0,)), ((), ()))
 VMEM = pl.BlockSpec(memory_space=pltpu.VMEM)
 HBM = pl.BlockSpec(memory_space=pltpu.HBM)
+EARLY_BYTES = 12 * 2**20
 GRAM_BYTES = 24 * 2**20
 IMAGE_BYTES = 20 * 2**20
 
@@ -43,7 +44,11 @@
         self.chunk, self.trow, self.data = (np.zeros((self.count, self.count), np.int32) for _ in range(3))
         for position, (data, trow) in enumerate(self.cells):
             first = trow * data_count
-            near = sorted(range(first, first + data_count), key=lambda q: (abs(q - position), q))
+            far_data = self.cells[(position + self.far) % self.count][0]
+            near = sorted(
+                range(first, first + data_count),
+                key=lambda q: (self.cells[q][0] == far_data, abs(q - position), q),
+            )
             chunk_of = {}
             for turn, other in enumerate(near):
                 self.rounds[position, turn] = self.offsets.index(other - position)
@@ -102,25 +107,29 @@
         load.wait()
 
 
-def gram_kernel(sizes, meta, *refs):
-    n, tcol_count, piece, width, head_part, block, groups = sizes
-    shard_refs = refs[: n + 1]
-    round_refs = refs[n + 1 : n + 1 + 3 * groups]
-    prior_ref, gram_ref, right_ref, image_ref, columns, rows, target, tile_ref, sent = refs[n + 1 + 3 * groups :]
-    me = meta[2 * n]
-    total_rows = rows.shape[1]
-    count = shard_refs[0].shape[1]
-    for index in range(n):
-        lanes = pl.ds(pl.multiple_of(meta[index] * count, 128), count)
-        base = pl.multiple_of(meta[n + index] * width, 16)
-        if index < n - 1:
-            columns[pl.ds(base, width), lanes] = shard_refs[index][:width, :]
-        else:
-            half = shard_refs[n - 1].shape[0]
-            columns[pl.ds(base, half), lanes] = shard_refs[n - 1][...]
-            columns[pl.ds(pl.multiple_of(base + half, 16), width - half), lanes] = shard_refs[n][...]
-    turn = 0
-    for group in range(groups):
+def pick_kernel(sizes, meta, *refs):
+    turns, choices, width, piece, data_count = sizes
+    *shard_refs, out_ref = refs
+    head_part = shard_refs[0].shape[0] - width
+    for index, turn in enumerate(turns):
+        for shard_ref, choice in zip(shard_refs, choices):
+
+            @pl.when(meta[turn] == choice)
+            def _():
+                out_ref[index, :head_part, :] = shard_ref[width:, :]
+                if piece % 16 == 0:
+                    place = pl.ds(pl.multiple_of(meta[data_count] * piece, 16), piece)
+                    out_ref[index, head_part:, :] = shard_ref[place, :]
+                else:
+                    for data in range(data_count):
+
+                        @pl.when(meta[data_count] == data)
+                        def _():
+                            out_ref[index, head_part:, :] = shard_ref[data * piece : (data + 1) * piece, :]
+
+
+def place_rows(round_refs, me, head_part, rows, target, turn, count):
+    for group in range(len(round_refs) // 3):
         own, far, near = round_refs[3 * group : 3 * group + 3]
         for inner in range(own.shape[0]):
             lanes = slice(turn * count, (turn + 1) * count)
@@ -130,18 +139,54 @@
                 target[pl.ds(at, head_part), lanes] = part[:head_part, :]
             rows[:, lanes] = jnp.concatenate([part[head_part:, :] for part in parts], axis=0)
             turn += 1
+
+
+def early_kernel(sizes, meta, *refs):
+    n, width, head_part, block, groups = sizes
+    shard_refs, refs = refs[: n - 1], refs[n - 1 :]
+    round_refs, refs = refs[: 3 * groups], refs[3 * groups :]
+    prior_ref, tile_ref, columns, rows, target = refs
+    count = shard_refs[0].shape[1]
+    for index in range(n - 1):
+        lanes = pl.ds(pl.multiple_of(meta[index] * count, 128), count)
+        base = pl.multiple_of(meta[n + index] * width, 16)
+        columns[pl.ds(base, width), lanes] = shard_refs[index][:width, :]
+    place_rows(round_refs, meta[2 * n], head_part, rows, target, 0, count)
+    done = columns.shape[1] - count
+    scale = 1.0 / columns.shape[1]
+    for start in range(0, columns.shape[0], block):
+        lanes = slice(start, start + block)
+        tile_ref[:, lanes] = prior_ref[:, lanes] + dot(rows[:, :done], columns[lanes, :done], NT) * scale
+
+
+def gram_kernel(sizes, meta, *refs):
+    n, tcol_count, piece, width, head_part, block = sizes
+    low_ref, high_ref, *round_refs = refs[:5]
+    early_ref, columns, rows, target, gram_ref, right_ref, image_ref = refs[5:12]
+    last_columns, last_rows, last_target, tile_ref, sent = refs[12:]
+    me = meta[2 * n]
+    total_rows = columns.shape[1]
+    count = last_rows.shape[1]
+    done = total_rows - count
+    last_columns[...] = columns[:, done:]
+    base = pl.multiple_of(meta[2 * n - 1] * width, 16)
+    half = low_ref.shape[0]
+    last_columns[pl.ds(base, half), :] = low_ref[...]
+    last_columns[pl.ds(pl.multiple_of(base + half, 16), width - half), :] = high_ref[...]
+    place_rows(round_refs, me, head_part, last_rows, last_target, 0, count)
     scale = 1.0 / total_rows
     stores = tile_copies(gram_ref, tile_ref, me, piece, block, sent, outward=True)
     sides = []
     for step in range(columns.shape[0] // block):
         lanes = slice(step * block, (step + 1) * block)
-        column = columns[lanes, :]
-        summed = dot(rows[...], column, NT)
-        tile_ref[:, lanes] = prior_ref[:, lanes] + summed * scale
+        last = last_columns[lanes, :]
+        tile_ref[:, lanes] = early_ref[:, lanes] + dot(last_rows[...], last, NT) * scale
         for index in range(step * tcol_count, (step + 1) * tcol_count):
             stores[index].start()
-        sides.append(split(dot(column, target[...], NT) * scale))
-    right_ref[...] = dot(rows[:piece, :], target[...], NT) * scale
+        side = dot(columns[lanes, :done], target[:, :done], NT) + dot(last, last_target[...], NT)
+        sides.append(split(side * scale))
+    right = dot(rows[:piece, :done], target[:, :done], NT) + dot(last_rows[:piece, :], last_target[...], NT)
+    right_ref[...] = right * scale
     side = [jnp.concatenate(part, axis=0) for part in zip(*sides)]
     image_ref[...] = product(split(tile_ref[...]), side)
     for store in stores:
@@ -218,7 +263,7 @@
     position = jnp.asarray(ring.place)[data_place, lax.axis_index("trow")]
     lookup = np.concatenate([ring.rounds, ring.chunk, ring.trow, ring.data, ring.trow], axis=1)
     lookup = jnp.asarray(lookup)[position]
-    rounds = [lookup[turn] for turn in range(data_count)]
+    pick_meta = jnp.concatenate([lookup[:data_count], jnp.reshape(data_place, (1,)).astype(jnp.int32)])
     me_meta = jnp.reshape(me, (1,)).astype(jnp.int32)
     gram_meta = jnp.concatenate([lookup[data_count : data_count + 2 * n], me_meta])
     image_meta = jnp.concatenate([lookup[data_count + 2 * n :], me_meta])
@@ -227,31 +272,36 @@
     head_rows = lax.dynamic_slice_in_dim(targets, me * head_part, head_part, axis=1).T
     payload = jnp.concatenate([own, head_rows], axis=0)
 
-    def piece_of(shard):
-        features = lax.dynamic_slice_in_dim(shard, data_place * piece, piece, axis=0)
-        return jnp.concatenate([shard[width:], features], axis=0)
-
-    def round_piece(turn):
-        choices = sorted(set(ring.rounds[:, turn].tolist()))
-        value = piece_of(gathered[choices[0]])
-        for choice in choices[1:]:
-            value = jnp.where(rounds[turn] == choice, piece_of(gathered[choice]), value)
-        return value
+    def pieces_of(turns):
+        if turns == [0]:
+            features = lax.dynamic_slice_in_dim(own, data_place * piece, piece, axis=0)
+            return jnp.concatenate([head_rows, features], axis=0)[None]
+        choices = sorted(set(ring.rounds[:, turns].ravel().tolist()))
+        return call(
+            functools.partial(pick_kernel, (turns, choices, width, piece, data_count)),
+            pick_meta,
+            [gathered[choice] for choice in choices],
+            [VMEM] * len(choices),
+            VMEM,
+            jax.ShapeDtypeStruct((len(turns), head_part + piece, row_count), payload.dtype),
+            [],
+            2**20,
+            0,
+            4 * len(turns) * (head_part + piece) * row_count,
+        )
 
     split_turns = [[0], list(range(1, data_count - 1)), [data_count - 1]]
     ready = [int(np.abs(np.asarray(ring.offsets)[ring.rounds[:, turns]]).max()) for turns in split_turns]
-    gathered, groups, waiting = [payload], [], []
-
-    def near_of(mine, far, *after):
-        mine, far, *after = lax.optimization_barrier((mine, far, *after))
-        groups.extend([mine, far, lax.ppermute(jnp.stack([mine, far]), "tcol", swap(tcol_count, 1))])
-        return after
+    gathered, groups, waiting = [payload], {}, []
+
+    def near_of(group, mine, far):
+        groups[group] = [mine, far, lax.ppermute(jnp.stack([mine, far]), "tcol", swap(tcol_count, 1))]
 
     def open_groups(step):
-        for turns, when in zip(split_turns, ready):
+        for group, (turns, when) in enumerate(zip(split_turns, ready)):
             if when == step:
-                mine = jnp.stack([round_piece(turn) for turn in turns])
-                waiting.append((mine, lax.ppermute(mine, "tcol", swap(tcol_count, 2))))
+                mine = pieces_of(turns)
+                waiting.append((group, mine, lax.ppermute(mine, "tcol", swap(tcol_count, 2))))
 
     block = 384 if tile_columns % 384 == 0 else 128
     f32, bf16 = jnp.float32, jnp.bfloat16
@@ -276,8 +326,8 @@
     for step, arrived in enumerate(ring.steps(payload, width), 1):
         arrived = list(arrived)
         if step == 1:
-            gram_meta, image_meta, rounds, arrived = lax.optimization_barrier(
-                (gram_meta, image_meta, rounds, arrived)
+            gram_meta, image_meta, pick_meta, *arrived = lax.optimization_barrier(
+                (gram_meta, image_meta, pick_meta, *arrived)
             )
         if step == ring.far - 2:
             prior, *arrived = lax.optimization_barrier((prior, *arrived))
@@ -285,17 +335,37 @@
         if step == ring.far - 1:
             prior, *arrived = lax.optimization_barrier((prior, *arrived))
         while waiting:
-            arrived = near_of(*waiting.pop(), *arrived)
+            group, mine, far = waiting.pop()
+            if step == ring.far:
+                early, mine, far, *arrived = lax.optimization_barrier((early, mine, far, *arrived))
+            else:
+                mine, far, *arrived = lax.optimization_barrier((mine, far, *arrived))
+            near_of(group, mine, far)
         gathered += arrived
         open_groups(step)
-
+        if step == ring.far - 1:
+            early, columns, rows, target = call(
+                functools.partial(early_kernel, (n, width, head_part, block, 2)),
+                gram_meta,
+                [*gathered, *groups[0], *groups[1], prior],
+                [VMEM] * (n + 6),
+                [VMEM] * 4,
+                [
+                    jax.ShapeDtypeStruct((tile_rows, tile_columns), f32),
+                    jax.ShapeDtypeStruct((tile_columns, total_rows), bf16),
+                    jax.ShapeDtypeStruct((tile_rows, total_rows), bf16),
+                    jax.ShapeDtypeStruct((heads, total_rows), bf16),
+                ],
+                [],
+                EARLY_BYTES,
+                2 * tile_rows * tile_columns * (total_rows - row_count),
+                8 * tile_rows * tile_columns,
+            )
     gram, start, partial = call(
-        functools.partial(
-            gram_kernel, (n, tcol_count, piece, width, head_part, block, len(split_turns))
-        ),
+        functools.partial(gram_kernel, (n, tcol_count, piece, width, head_part, block)),
         gram_meta,
-        [*gathered, *groups, prior],
-        [VMEM] * (n + 2 + len(groups)),
+        [*gathered[-2:], *groups[2], early, columns, rows, target],
+        [VMEM] * 9,
         [HBM] + [VMEM] * 2,
         [
             jax.ShapeDtypeStruct((tile_rows, tile_columns), f32),
@@ -303,9 +373,9 @@
             jax.ShapeDtypeStruct((tile_rows, heads), f32),
         ],
         [
-            pltpu.VMEM((tile_columns, total_rows), bf16),
-            pltpu.VMEM((tile_rows, total_rows), bf16),
-            pltpu.VMEM((heads, total_rows), bf16),
+            pltpu.VMEM((tile_columns, row_count), bf16),
+            pltpu.VMEM((tile_rows, row_count), bf16),
+            pltpu.VMEM((heads, row_count), bf16),
             pltpu.VMEM((tile_rows, tile_columns), f32),
             tile_semaphores,
         ],

time: 117 us -> 108 us (0.923)
  waiting for transfers between devices: 50.3 us -> 44.7 us
  between operations: 6.81 us -> 2.9 us
  local copies, waits for them, and re-layouts: 12.3 us -> 11 us
    ppermute x6, waiting for transfers between devices: 5.08 us -> 0.9 us  [steps(): back = lax.ppermute(back, ('dp', 'trow'), self.back)]
    ppermute x3, waiting for transfers between devices: 4.1 us -> 0.01 us  [open_groups(): lax.ppermute(mine, 'tcol', swap(tcol_count, 2))]
    ppermute x6, waiting for transfers between devices: 23.2 us -> 25.5 us  [steps(): ahead = lax.ppermute(ahead, ('dp', 'trow'), self.ahead)]
    concatenate x10 -> x0, local copies, waits for them, and re-layouts: 1.8 us -> none  [piece_of(): return jnp.concatenate([shard[width:], features], axis=0)]
    pallas_call x4 -> x7, Pallas kernels: 14.7 us -> 15.6 us  [call(): pl.pallas_call(body, grid_spec=pltpu.PrefetchScalarGridSpec(num_scalar_pr...]
  transfers between devices with their start and end apart: 29 -> 29, of which waited for: 16 -> 15; matrix products, arithmetic and copies ran while one was open for 3% -> 3% of each run, Pallas kernels for 1% -> 5%
where the time goes in v4:
time: 108 us
  waiting for transfers between devices  44.7 us (41%)
  starting transfers between devices  32.1 us (30%)
  Pallas kernels  15.6 us (14%)
  local copies, waits for them, and re-layouts  11 us (10%)
  between operations  2.9 us (3%)
  other arithmetic  1.44 us (1%)
    ppermute x6, waiting for transfers between devices, steps(): ahead = lax.ppermute(ahead, ('dp', 'trow'), self.ahead)  25.5 us
    pallas_call x7, Pallas kernels, call(): pl.pallas_call(body, grid_spec=pltpu.PrefetchScalarGridSpec(num_scalar_pr...  15.6 us
    ppermute x6, starting transfers between devices, steps(): ahead = lax.ppermute(ahead, ('dp', 'trow'), self.ahead)  11.1 us
    unnamed x10, local copies, waits for them, and re-layouts  6.83 us
    all_to_all x1, waiting for transfers between devices, all_sum(): lax.all_to_all(spread, axis_names, split_axis=0, concat_axis=0, tiled=True)  6.37 us
    ppermute x2, waiting for transfers between devices, owner_sum(): lax.ppermute(kept[1], 'tcol', swap(tcol_count, 2))  5.61 us
    ppermute x3, starting transfers between devices, open_groups(): lax.ppermute(mine, 'tcol', swap(tcol_count, 2))  5.01 us
    all_to_all x1, starting transfers between devices, all_sum(): lax.all_to_all(spread, axis_names, split_axis=0, concat_axis=0, tiled=True)  3.46 us
  transfers between devices with their start and end apart: 29, of which 15 were waited for; matrix products, arithmetic and copies ran while one was open for 3% of the time, Pallas kernels for 5%

profile of v4, /device:TPU:0, one launch (start us, length us, event | category | flops | bytes accessed | tf_op | source)
XLA Modules:
  0.0 107.7 jit_solution(5113736125578362154)
XLA Ops:
  2.9 3.1 %collective-permute-start = (bf16[832,256]{1,0:T(8,128)(2,1)S(1)}, bf16[832,256]{1,0:T(8,128)(2,1)S(1)}, u32[]{:S(2)}, u32[]{:S(2)}) collective-permute-start(bf16[832,256]{1,0:T(8,128)(2,1)S(1)} %pad_maximum_fusion.1.refs_0_), channel_id=1, source_target_pairs={{0,8},{8,16},{16,24},{24,28},{28,20},{20,12},{12,4},{4,0},{1,9},{9... | collective-permute-start | bytes 1277960 | tf_op jit(solution)/shard_map/ppermute | solution.py:65
  7.2 2.0 %collective-permute-start.2 = (bf16[1,256,256]{2,1,0:T(8,128)(2,1)S(1)}, bf16[1,256,256]{2,1,0:T(8,128)(2,1)S(1)}, u32[]{:S(2)}, u32[]{:S(2)}) collective-permute-start(bf16[1,256,256]{2,1,0:T(8,128)(2,1)S(1)} %maximum_bitcast_fusion.refs_7_), channel_id=1, source_target_pairs={{0,2},{1,3},{2,0},{3,1},{4,6},{5,7},{6,4},{7,5},{8,10},{9,11},{10,... | collective-permute-start | bytes 393224 | tf_op jit(solution)/shard_map/ppermute | solution.py:304
  9.2 1.3 %dynamic_slice.12 = s32[1,1]{1,0:T(1,128)} dynamic-slice(s32[4,2]{1,0:T(4,128)} %constant.37.clone, s32[]{:T(128)S(6)} %select_n.15, s32[]{:T(128)S(6)} %select_n.16), dynamic_slice_sizes={1,1} | dynamic-slice | bytes 12 | tf_op jit(solution)/shard_map/dynamic_slice | solution.py:263
  13.1 2.7 %collective-permute-done.refs_0_.refs_1_ = bf16[832,256]{1,0:T(8,128)(2,1)S(1)} collective-permute-done((bf16[832,256]{1,0:T(8,128)(2,1)S(1)}, bf16[832,256]{1,0:T(8,128)(2,1)S(1)}, u32[]{:S(2)}, u32[]{:S(2)}) %collective-permute-start) | collective-permute-done | bytes 426016 | tf_op jit(solution)/shard_map/ppermute | solution.py:65
  15.8 1.8 %collective-permute-start.3 = (bf16[832,256]{1,0:T(8,128)(2,1)S(1)}, bf16[832,256]{1,0:T(8,128)(2,1)S(1)}, u32[]{:S(2)}, u32[]{:S(2)}) collective-permute-start(bf16[832,256]{1,0:T(8,128)(2,1)S(1)} %collective-permute-done.refs_0_.refs_1_), channel_id=1, source_target_pairs={{0,8},{8,16},{16,24},{24,28},{28,20},{20,12},{12,4},{4,0},{1,9},{9... | collective-permute-start | bytes 1277960 | tf_op jit(solution)/shard_map/ppermute | solution.py:65
  17.9 8.9 %collective-permute-done.3.refs_2_.refs_3_ = bf16[832,256]{1,0:T(8,128)(2,1)S(1)} collective-permute-done((bf16[832,256]{1,0:T(8,128)(2,1)S(1)}, bf16[832,256]{1,0:T(8,128)(2,1)S(1)}, u32[]{:S(2)}, u32[]{:S(2)}) %collective-permute-start.3) | collective-permute-done | bytes 426016 | tf_op jit(solution)/shard_map/ppermute | solution.py:65
  26.8 1.5 %collective-permute-start.6 = (bf16[832,256]{1,0:T(8,128)(2,1)S(1)}, bf16[832,256]{1,0:T(8,128)(2,1)S(1)}, u32[]{:S(2)}, u32[]{:S(2)}) collective-permute-start(bf16[832,256]{1,0:T(8,128)(2,1)S(1)} %collective-permute-done.3.refs_2_.refs_3_), channel_id=1, source_target_pairs={{0,8},{8,16},{16,24},{24,28},{28,20},{20,12},{12,4},{4,0},{1,9},{9... | collective-permute-start | bytes 1277960 | tf_op jit(solution)/shard_map/ppermute | solution.py:65
  29.6 1.5 %collective-permute-start.5 = (bf16[2,256,256]{2,1,0:T(8,128)(2,1)S(1)}, bf16[2,256,256]{2,1,0:T(8,128)(2,1)S(1)}, u32[]{:S(2)}, u32[]{:S(2)}) collective-permute-start(bf16[2,256,256]{2,1,0:T(8,128)(2,1)S(1)} %shard_map.85.refs_10_), channel_id=1, source_target_pairs={{0,2},{1,3},{2,0},{3,1},{4,6},{5,7},{6,4},{7,5},{8,10},{9,11},{10,... | collective-permute-start | bytes 786440 | tf_op jit(solution)/shard_map/ppermute | solution.py:304
  31.1 2.3 %copy-done.1 = f32[4,1,1,192,1536]{4,3,2,1,0:T(8,128)S(1)} copy-done((f32[4,1,1,192,1536]{4,3,2,1,0:T(8,128)S(1)}, f32[4,1,1,192,1536]{4,3,2,1,0:T(8,128)}, u32[]{:S(2)}) %copy-start.1) | copy-done | bytes 4718616
  33.9 3.0 %collective-permute-done.6.refs_5_.refs_2_ = bf16[832,256]{1,0:T(8,128)(2,1)S(1)} collective-permute-done((bf16[832,256]{1,0:T(8,128)(2,1)S(1)}, bf16[832,256]{1,0:T(8,128)(2,1)S(1)}, u32[]{:S(2)}, u32[]{:S(2)}) %collective-permute-start.6) | collective-permute-done | bytes 426016 | tf_op jit(solution)/shard_map/ppermute | solution.py:65
  38.5 1.6 %collective-permute-start.11 = (bf16[384,256]{1,0:T(8,128)(2,1)S(1)}, bf16[384,256]{1,0:T(8,128)(2,1)S(1)}, u32[]{:S(2)}, u32[]{:S(2)}) collective-permute-start(bf16[384,256]{1,0:T(8,128)(2,1)S(1)} %slice.114), channel_id=1, source_target_pairs={{0,8},{8,16},{16,24},{24,28},{28,20},{20,12},{12,4},{4,0},{1,9},{9... | collective-permute-start | bytes 589832 | tf_op jit(solution)/shard_map/ppermute | solution.py:69
  41.2 1.6 %collective-permute-start.10 = (bf16[1,256,256]{2,1,0:T(8,128)(2,1)S(1)}, bf16[1,256,256]{2,1,0:T(8,128)(2,1)S(1)}, u32[]{:S(2)}, u32[]{:S(2)}) collective-permute-start(bf16[1,256,256]{2,1,0:T(8,128)(2,1)S(1)} %shard_map.88.refs_2_), channel_id=1, source_target_pairs={{0,2},{1,3},{2,0},{3,1},{4,6},{5,7},{6,4},{7,5},{8,10},{9,11},{10,... | collective-permute-start | bytes 393224 | tf_op jit(solution)/shard_map/ppermute | solution.py:304
  42.8 3.6 %shard_map.87 = (f32[768,1536]{1,0:T(8,128)S(1)}, bf16[1536,1024]{1,0:T(8,128)(2,1)S(1)}, bf16[768,1024]{1,0:T(8,128)(2,1)S(1)}, bf16[256,1024]{1,0:T(8,128)(2,1)S(1)}) custom-call(s32[17]{0:T(128)S(1)} %get-tuple-element.41.meta, bf16[832,256]{1,0:T(8,128)(2,1)S(1)} %pad_maximum_fusion.1.refs_0_, bf16[832,256]{1,0:T(8,128)(2,1)S(1)} %collective-permute-done.refs_0_.refs_1_, ...), custom_call_target="tpu_custom_call" | custom-call | flops 1811939328 | bytes 9437184 | tf_op jit(solution)/shard_map/pallas_call | solution.py:224
  46.8 1.5 %collective-permute-done.13.refs_4_ = bf16[2,1,256,256]{3,2,1,0:T(8,128)(2,1)S(1)} collective-permute-done((bf16[2,1,256,256]{3,2,1,0:T(8,128)(2,1)S(1)}, bf16[2,1,256,256]{3,2,1,0:T(8,128)(2,1)S(1)}, u32[]{:S(2)}, u32[]{:S(2)}) %collective-permute-start.13) | collective-permute-done | bytes 262176 | tf_op jit(solution)/shard_map/ppermute | solution.py:298
  48.4 7.2 %shard_map.89 = (f32[768,1536]{1,0:T(8,128)}, f32[192,256]{1,0:T(8,128)S(1)}, f32[768,256]{1,0:T(8,128)S(1)}) custom-call(s32[17]{0:T(128)S(1)} %get-tuple-element.41.meta, bf16[384,256]{1,0:T(8,128)(2,1)S(1)} %collective-permute-done.11.refs_0_, bf16[384,256]{1,0:T(8,128)(2,1)S(1)} %collective-permute-done.12.refs_1_, ...), custom_call_target="tpu_custom_call" | custom-call | flops 4227858432 | bytes 14155776 | tf_op jit(solution)/shard_map/pallas_call | solution.py:224
  55.8 1.6 %collective-permute-done.14 = f32[2,192,256]{2,1,0:T(8,128)S(1)} collective-permute-done((f32[2,192,256]{2,1,0:T(8,128)S(1)}, f32[2,192,256]{2,1,0:T(8,128)S(1)}, u32[]{:S(2)}, u32[]{:S(2)}) %collective-permute-start.14) | collective-permute-done | bytes 393248 | tf_op jit(solution)/shard_map/ppermute | solution.py:390
  57.4 1.6 %collective-permute-start.15 = (f32[192,256]{1,0:T(8,128)S(1)}, f32[192,256]{1,0:T(8,128)S(1)}, u32[]{:S(2)}, u32[]{:S(2)}) collective-permute-start(f32[192,256]{1,0:T(8,128)S(1)} %fusion), channel_id=1, source_target_pairs={{0,2},{1,3},{2,0},{3,1},{4,6},{5,7},{6,4},{7,5},{8,10},{9,11},{10,... | collective-permute-start | bytes 589832 | tf_op jit(solution)/shard_map/ppermute | solution.py:394
  59.0 5.5 %collective-permute-done.15 = f32[192,256]{1,0:T(8,128)S(1)} collective-permute-done((f32[192,256]{1,0:T(8,128)S(1)}, f32[192,256]{1,0:T(8,128)S(1)}, u32[]{:S(2)}, u32[]{:S(2)}) %collective-permute-start.15) | collective-permute-done | bytes 196640 | tf_op jit(solution)/shard_map/ppermute | solution.py:394
  64.6 1.6 %collective-permute-start.16 = (f32[192,256]{1,0:T(8,128)S(1)}, f32[192,256]{1,0:T(8,128)S(1)}, u32[]{:S(2)}, u32[]{:S(2)}) collective-permute-start(f32[192,256]{1,0:T(8,128)S(1)} %fusion.3.refs_0_), channel_id=1, source_target_pairs={{0,8},{8,16},{16,24},{24,28},{28,20},{20,12},{12,4},{4,0},{1,9},{9... | collective-permute-start | bytes 589832 | tf_op jit(solution)/shard_map/ppermute | solution.py:65
  66.6 1.5 %collective-permute-start.24 = (f32[192,256]{1,0:T(8,128)S(1)}, f32[192,256]{1,0:T(8,128)S(1)}, u32[]{:S(2)}, u32[]{:S(2)}) collective-permute-start(f32[192,256]{1,0:T(8,128)S(1)} %fusion.3.refs_0_), channel_id=1, source_target_pairs={{0,2},{1,3},{2,0},{3,1},{4,6},{5,7},{6,4},{7,5},{8,10},{9,11},{10,... | collective-permute-start | bytes 589832 | tf_op jit(solution)/shard_map/ppermute | solution.py:397
  68.1 2.6 %collective-permute-done.16.refs_1_ = f32[192,256]{1,0:T(8,128)S(1)} collective-permute-done((f32[192,256]{1,0:T(8,128)S(1)}, f32[192,256]{1,0:T(8,128)S(1)}, u32[]{:S(2)}, u32[]{:S(2)}) %collective-permute-start.16) | collective-permute-done | bytes 196640 | tf_op jit(solution)/shard_map/ppermute | solution.py:65
  70.7 1.6 %collective-permute-start.17 = (f32[192,256]{1,0:T(8,128)S(1)}, f32[192,256]{1,0:T(8,128)S(1)}, u32[]{:S(2)}, u32[]{:S(2)}) collective-permute-start(f32[192,256]{1,0:T(8,128)S(1)} %collective-permute-done.16.refs_1_), channel_id=1, source_target_pairs={{0,8},{8,16},{16,24},{24,28},{28,20},{20,12},{12,4},{4,0},{1,9},{9... | collective-permute-start | bytes 589832 | tf_op jit(solution)/shard_map/ppermute | solution.py:65
  72.9 3.6 %collective-permute-done.17.refs_3_ = f32[192,256]{1,0:T(8,128)S(1)} collective-permute-done((f32[192,256]{1,0:T(8,128)S(1)}, f32[192,256]{1,0:T(8,128)S(1)}, u32[]{:S(2)}, u32[]{:S(2)}) %collective-permute-start.17) | collective-permute-done | bytes 196640 | tf_op jit(solution)/shard_map/ppermute | solution.py:65
  76.5 1.6 %collective-permute-start.18 = (f32[192,256]{1,0:T(8,128)S(1)}, f32[192,256]{1,0:T(8,128)S(1)}, u32[]{:S(2)}, u32[]{:S(2)}) collective-permute-start(f32[192,256]{1,0:T(8,128)S(1)} %collective-permute-done.17.refs_3_), channel_id=1, source_target_pairs={{0,8},{8,16},{16,24},{24,28},{28,20},{20,12},{12,4},{4,0},{1,9},{9... | collective-permute-start | bytes 589832 | tf_op jit(solution)/shard_map/ppermute | solution.py:65
  78.5 4.7 %collective-permute-done.18.refs_5_ = f32[192,256]{1,0:T(8,128)S(1)} collective-permute-done((f32[192,256]{1,0:T(8,128)S(1)}, f32[192,256]{1,0:T(8,128)S(1)}, u32[]{:S(2)}, u32[]{:S(2)}) %collective-permute-start.18) | collective-permute-done | bytes 196640 | tf_op jit(solution)/shard_map/ppermute | solution.py:65
  83.2 1.6 %collective-permute-start.22 = (f32[96,256]{1,0:T(8,128)S(1)}, f32[96,256]{1,0:T(8,128)S(1)}, u32[]{:S(2)}, u32[]{:S(2)}) collective-permute-start(f32[96,256]{1,0:T(8,128)S(1)} %slice.118), channel_id=1, source_target_pairs={{0,8},{8,16},{16,24},{24,28},{28,20},{20,12},{12,4},{4,0},{1,9},{9... | collective-permute-start | bytes 294920 | tf_op jit(solution)/shard_map/ppermute | solution.py:69
  85.7 2.3 %copy-done.2 = f32[768,1536]{1,0:T(8,128)S(1)} copy-done((f32[768,1536]{1,0:T(8,128)S(1)}, f32[768,1536]{1,0:T(8,128)}, u32[]{:S(2)}) %copy-start.2) | copy-done | bytes 4718616
  89.7 2.7 %shard_map.91 = (f32[4,192,256]{2,1,0:T(8,128)S(1)}, f32[4,256]{1,0:T(4,128)S(1)}) custom-call(s32[17]{0:T(128)S(1)} %get-tuple-element.72.meta, f32[192,256]{1,0:T(8,128)S(1)} %fusion.3.refs_0_, f32[192,256]{1,0:T(8,128)S(1)} %collective-permute-done.16.refs_1_, f32[192,256]{1,0:T(8,128)S(1)} %collective-permute-done.19.refs_2_, ...), custom_call_target="tpu_custom_call" | custom-call | flops 1811939328 | bytes 4718592 | tf_op jit(solution)/shard_map/pallas_call | solution.py:224
  92.5 1.7 %collective-permute-done.26 = f32[2,192,256]{2,1,0:T(8,128)S(1)} collective-permute-done((f32[2,192,256]{2,1,0:T(8,128)S(1)}, f32[2,192,256]{2,1,0:T(8,128)S(1)}, u32[]{:S(2)}, u32[]{:S(2)}) %collective-permute-start.26) | collective-permute-done | bytes 393248 | tf_op jit(solution)/shard_map/ppermute | solution.py:390
  94.9 3.5 %all-to-all-start = ((f32[32,4,256]{2,1,0:T(4,128)}), f32[32,4,256]{2,1,0:T(4,128)S(1)}, u32[]{:S(2)}, u32[]{:S(2)}) async-start(f32[32,4,256]{2,1,0:T(4,128)} %broadcast_in_dim.5), calls=%async_computation | async-start | bytes 262144 | tf_op jit(solution)/shard_map/all_to_all | solution.py:244
  98.4 1.8 %collective-permute-start.27 = (f32[192,256]{1,0:T(8,128)S(1)}, f32[192,256]{1,0:T(8,128)S(1)}, u32[]{:S(2)}, u32[]{:S(2)}) collective-permute-start(f32[192,256]{1,0:T(8,128)S(1)} %add_bitcast_fusion), channel_id=1, source_target_pairs={{0,2},{1,3},{2,0},{3,1},{4,6},{5,7},{6,4},{7,5},{8,10},{9,11},{10,... | collective-permute-start | bytes 589832 | tf_op jit(solution)/shard_map/ppermute | solution.py:394
  100.3 6.4 %all-to-all-done = f32[32,4,256]{2,1,0:T(4,128)S(1)} async-done(((f32[32,4,256]{2,1,0:T(4,128)}), f32[32,4,256]{2,1,0:T(4,128)S(1)}, u32[]{:S(2)}, u32[]{:S(2)}) %all-to-all-start) | async-done | bytes 131104 | tf_op jit(solution)/shard_map/all_to_all | solution.py:244
  (75 shorter events, 15.6 us)
Async XLA Ops:
  2.9 12.8 %collective-permute-start = (bf16[832,256]{1,0:T(8,128)(2,1)S(1)}, bf16[832,256]{1,0:T(8,128)(2,1)S(1)}, u32[]{:S(2)}, u32[]{:S(2)}) collective-permute-start(bf16[832,256]{1,0:T(8,128)(2,1)S(1)} %pad_maximum_fusion.1.refs_0_), channel_id=1, source_target_pairs={{0,8},{8,16},{16,24},{24,28},{28,20},{20,12},{12,4},{4,0},{1,9},{9... | collective-permute-start | bytes 1277960 | tf_op jit(solution)/shard_map/ppermute | solution.py:65
  6.0 11.6 %collective-permute-start.1 = (bf16[832,256]{1,0:T(8,128)(2,1)S(1)}, bf16[832,256]{1,0:T(8,128)(2,1)S(1)}, u32[]{:S(2)}, u32[]{:S(2)}) collective-permute-start(bf16[832,256]{1,0:T(8,128)(2,1)S(1)} %pad_maximum_fusion.1.refs_0_), channel_id=1, source_target_pairs={{8,0},{16,8},{24,16},{28,24},{20,28},{12,20},{4,12},{0,4},{9,1},{1... | collective-permute-start | bytes 1277960 | tf_op jit(solution)/shard_map/ppermute | solution.py:66
  7.2 21.8 %collective-permute-start.2 = (bf16[1,256,256]{2,1,0:T(8,128)(2,1)S(1)}, bf16[1,256,256]{2,1,0:T(8,128)(2,1)S(1)}, u32[]{:S(2)}, u32[]{:S(2)}) collective-permute-start(bf16[1,256,256]{2,1,0:T(8,128)(2,1)S(1)} %maximum_bitcast_fusion.refs_7_), channel_id=1, source_target_pairs={{0,2},{1,3},{2,0},{3,1},{4,6},{5,7},{6,4},{7,5},{8,10},{9,11},{10,... | collective-permute-start | bytes 393224 | tf_op jit(solution)/shard_map/ppermute | solution.py:304
  15.8 11.0 %collective-permute-start.3 = (bf16[832,256]{1,0:T(8,128)(2,1)S(1)}, bf16[832,256]{1,0:T(8,128)(2,1)S(1)}, u32[]{:S(2)}, u32[]{:S(2)}) collective-permute-start(bf16[832,256]{1,0:T(8,128)(2,1)S(1)} %collective-permute-done.refs_0_.refs_1_), channel_id=1, source_target_pairs={{0,8},{8,16},{16,24},{24,28},{28,20},{20,12},{12,4},{4,0},{1,9},{9... | collective-permute-start | bytes 1277960 | tf_op jit(solution)/shard_map/ppermute | solution.py:65
  17.6 10.7 %collective-permute-start.4 = (bf16[832,256]{1,0:T(8,128)(2,1)S(1)}, bf16[832,256]{1,0:T(8,128)(2,1)S(1)}, u32[]{:S(2)}, u32[]{:S(2)}) collective-permute-start(bf16[832,256]{1,0:T(8,128)(2,1)S(1)} %collective-permute-done.1.refs_1_.refs_2_), channel_id=1, source_target_pairs={{8,0},{16,8},{24,16},{28,24},{20,28},{12,20},{4,12},{0,4},{9,1},{1... | collective-permute-start | bytes 1277960 | tf_op jit(solution)/shard_map/ppermute | solution.py:66
  26.8 10.1 %collective-permute-start.6 = (bf16[832,256]{1,0:T(8,128)(2,1)S(1)}, bf16[832,256]{1,0:T(8,128)(2,1)S(1)}, u32[]{:S(2)}, u32[]{:S(2)}) collective-permute-start(bf16[832,256]{1,0:T(8,128)(2,1)S(1)} %collective-permute-done.3.refs_2_.refs_3_), channel_id=1, source_target_pairs={{0,8},{8,16},{16,24},{24,28},{28,20},{20,12},{12,4},{4,0},{1,9},{9... | collective-permute-start | bytes 1277960 | tf_op jit(solution)/shard_map/ppermute | solution.py:65
  28.3 9.5 %collective-permute-start.7 = (bf16[832,256]{1,0:T(8,128)(2,1)S(1)}, bf16[832,256]{1,0:T(8,128)(2,1)S(1)}, u32[]{:S(2)}, u32[]{:S(2)}) collective-permute-start(bf16[832,256]{1,0:T(8,128)(2,1)S(1)} %collective-permute-done.4.refs_3_.refs_4_), channel_id=1, source_target_pairs={{8,0},{16,8},{24,16},{28,24},{20,28},{12,20},{4,12},{0,4},{9,1},{1... | collective-permute-start | bytes 1277960 | tf_op jit(solution)/shard_map/ppermute | solution.py:66
  29.6 8.2 %collective-permute-start.5 = (bf16[2,256,256]{2,1,0:T(8,128)(2,1)S(1)}, bf16[2,256,256]{2,1,0:T(8,128)(2,1)S(1)}, u32[]{:S(2)}, u32[]{:S(2)}) collective-permute-start(bf16[2,256,256]{2,1,0:T(8,128)(2,1)S(1)} %shard_map.85.refs_10_), channel_id=1, source_target_pairs={{0,2},{1,3},{2,0},{3,1},{4,6},{5,7},{6,4},{7,5},{8,10},{9,11},{10,... | collective-permute-start | bytes 786440 | tf_op jit(solution)/shard_map/ppermute | solution.py:304
  31.1 2.3 %copy-start.1 = (f32[4,1,1,192,1536]{4,3,2,1,0:T(8,128)S(1)}, f32[4,1,1,192,1536]{4,3,2,1,0:T(8,128)}, u32[]{:S(2)}) copy-start(f32[4,1,1,192,1536]{4,3,2,1,0:T(8,128)} %param.8) | copy-start | bytes 14155780
  37.8 5.0 %collective-permute-start.9 = (bf16[2,2,256,256]{3,2,1,0:T(8,128)(2,1)S(1)}, bf16[2,2,256,256]{3,2,1,0:T(8,128)(2,1)S(1)}, u32[]{:S(2)}, u32[]{:S(2)}) collective-permute-start(bf16[2,2,256,256]{3,2,1,0:T(8,128)(2,1)S(1)} %pad_maximum_fusion), channel_id=1, source_target_pairs={{0,1},{1,0},{2,3},{3,2},{4,5},{5,4},{6,7},{7,6},{8,9},{9,8},{10,11... | collective-permute-start | bytes 1572872 | tf_op jit(solution)/shard_map/ppermute | solution.py:298
  37.9 4.9 %collective-permute-start.8 = (bf16[2,1,256,256]{3,2,1,0:T(8,128)(2,1)S(1)}, bf16[2,1,256,256]{3,2,1,0:T(8,128)(2,1)S(1)}, u32[]{:S(2)}, u32[]{:S(2)}) collective-permute-start(bf16[2,1,256,256]{3,2,1,0:T(8,128)(2,1)S(1)} %pad_maximum_fusion.5), channel_id=1, source_target_pairs={{0,1},{1,0},{2,3},{3,2},{4,5},{5,4},{6,7},{7,6},{8,9},{9,8},{10,11... | collective-permute-start | bytes 786440 | tf_op jit(solution)/shard_map/ppermute | solution.py:298
  38.5 7.9 %collective-permute-start.11 = (bf16[384,256]{1,0:T(8,128)(2,1)S(1)}, bf16[384,256]{1,0:T(8,128)(2,1)S(1)}, u32[]{:S(2)}, u32[]{:S(2)}) collective-permute-start(bf16[384,256]{1,0:T(8,128)(2,1)S(1)} %slice.114), channel_id=1, source_target_pairs={{0,8},{8,16},{16,24},{24,28},{28,20},{20,12},{12,4},{4,0},{1,9},{9... | collective-permute-start | bytes 589832 | tf_op jit(solution)/shard_map/ppermute | solution.py:69
  40.1 6.6 %collective-permute-start.12 = (bf16[384,256]{1,0:T(8,128)(2,1)S(1)}, bf16[384,256]{1,0:T(8,128)(2,1)S(1)}, u32[]{:S(2)}, u32[]{:S(2)}) collective-permute-start(bf16[384,256]{1,0:T(8,128)(2,1)S(1)} %slice.115), channel_id=1, source_target_pairs={{8,0},{16,8},{24,16},{28,24},{20,28},{12,20},{4,12},{0,4},{9,1},{1... | collective-permute-start | bytes 589832 | tf_op jit(solution)/shard_map/ppermute | solution.py:70
  41.2 5.2 %collective-permute-start.10 = (bf16[1,256,256]{2,1,0:T(8,128)(2,1)S(1)}, bf16[1,256,256]{2,1,0:T(8,128)(2,1)S(1)}, u32[]{:S(2)}, u32[]{:S(2)}) collective-permute-start(bf16[1,256,256]{2,1,0:T(8,128)(2,1)S(1)} %shard_map.88.refs_2_), channel_id=1, source_target_pairs={{0,2},{1,3},{2,0},{3,1},{4,6},{5,7},{6,4},{7,5},{8,10},{9,11},{10,... | collective-permute-start | bytes 393224 | tf_op jit(solution)/shard_map/ppermute | solution.py:304
  46.8 1.6 %collective-permute-start.13 = (bf16[2,1,256,256]{3,2,1,0:T(8,128)(2,1)S(1)}, bf16[2,1,256,256]{3,2,1,0:T(8,128)(2,1)S(1)}, u32[]{:S(2)}, u32[]{:S(2)}) collective-permute-start(bf16[2,1,256,256]{3,2,1,0:T(8,128)(2,1)S(1)} %pad_maximum_fusion.6), channel_id=1, source_target_pairs={{0,1},{1,0},{2,3},{3,2},{4,5},{5,4},{6,7},{7,6},{8,9},{9,8},{10,11... | collective-permute-start | bytes 786440 | tf_op jit(solution)/shard_map/ppermute | solution.py:298
  48.4 16.1 %copy-start.3 = (f32[1,1,1,192]{3,2,1,0:T(1,128)S(1)}, f32[1,1,1,192]{3,2,1,0:T(1,128)}, u32[]{:S(2)}) copy-start(f32[1,1,1,192]{3,2,1,0:T(1,128)} %param.9) | copy-start | bytes 2308
  55.6 1.8 %collective-permute-start.14 = (f32[2,192,256]{2,1,0:T(8,128)S(1)}, f32[2,192,256]{2,1,0:T(8,128)S(1)}, u32[]{:S(2)}, u32[]{:S(2)}) collective-permute-start(f32[2,192,256]{2,1,0:T(8,128)S(1)} %pad_maximum_fusion.2), channel_id=1, source_target_pairs={{0,1},{1,0},{2,3},{3,2},{4,5},{5,4},{6,7},{7,6},{8,9},{9,8},{10,11... | collective-permute-start | bytes 1179656 | tf_op jit(solution)/shard_map/ppermute | solution.py:390
  57.4 7.0 %collective-permute-start.15 = (f32[192,256]{1,0:T(8,128)S(1)}, f32[192,256]{1,0:T(8,128)S(1)}, u32[]{:S(2)}, u32[]{:S(2)}) collective-permute-start(f32[192,256]{1,0:T(8,128)S(1)} %fusion), channel_id=1, source_target_pairs={{0,2},{1,3},{2,0},{3,1},{4,6},{5,7},{6,4},{7,5},{8,10},{9,11},{10,... | collective-permute-start | bytes 589832 | tf_op jit(solution)/shard_map/ppermute | solution.py:394
  64.6 6.2 %collective-permute-start.16 = (f32[192,256]{1,0:T(8,128)S(1)}, f32[192,256]{1,0:T(8,128)S(1)}, u32[]{:S(2)}, u32[]{:S(2)}) collective-permute-start(f32[192,256]{1,0:T(8,128)S(1)} %fusion.3.refs_0_), channel_id=1, source_target_pairs={{0,8},{8,16},{16,24},{24,28},{28,20},{20,12},{12,4},{4,0},{1,9},{9... | collective-permute-start | bytes 589832 | tf_op jit(solution)/shard_map/ppermute | solution.py:65
  66.2 6.1 %collective-permute-start.19 = (f32[192,256]{1,0:T(8,128)S(1)}, f32[192,256]{1,0:T(8,128)S(1)}, u32[]{:S(2)}, u32[]{:S(2)}) collective-permute-start(f32[192,256]{1,0:T(8,128)S(1)} %fusion.3.refs_0_), channel_id=1, source_target_pairs={{8,0},{16,8},{24,16},{28,24},{20,28},{12,20},{4,12},{0,4},{9,1},{1... | collective-permute-start | bytes 589832 | tf_op jit(solution)/shard_map/ppermute | solution.py:66
  66.6 6.1 %collective-permute-start.24 = (f32[192,256]{1,0:T(8,128)S(1)}, f32[192,256]{1,0:T(8,128)S(1)}, u32[]{:S(2)}, u32[]{:S(2)}) collective-permute-start(f32[192,256]{1,0:T(8,128)S(1)} %fusion.3.refs_0_), channel_id=1, source_target_pairs={{0,2},{1,3},{2,0},{3,1},{4,6},{5,7},{6,4},{7,5},{8,10},{9,11},{10,... | collective-permute-start | bytes 589832 | tf_op jit(solution)/shard_map/ppermute | solution.py:397
  70.7 5.8 %collective-permute-start.17 = (f32[192,256]{1,0:T(8,128)S(1)}, f32[192,256]{1,0:T(8,128)S(1)}, u32[]{:S(2)}, u32[]{:S(2)}) collective-permute-start(f32[192,256]{1,0:T(8,128)S(1)} %collective-permute-done.16.refs_1_), channel_id=1, source_target_pairs={{0,8},{8,16},{16,24},{24,28},{28,20},{20,12},{12,4},{4,0},{1,9},{9... | collective-permute-start | bytes 589832 | tf_op jit(solution)/shard_map/ppermute | solution.py:65
  72.3 5.8 %collective-permute-start.20 = (f32[192,256]{1,0:T(8,128)S(1)}, f32[192,256]{1,0:T(8,128)S(1)}, u32[]{:S(2)}, u32[]{:S(2)}) collective-permute-start(f32[192,256]{1,0:T(8,128)S(1)} %collective-permute-done.19.refs_2_), channel_id=1, source_target_pairs={{8,0},{16,8},{24,16},{28,24},{20,28},{12,20},{4,12},{0,4},{9,1},{1... | collective-permute-start | bytes 589832 | tf_op jit(solution)/shard_map/ppermute | solution.py:66
  72.8 15.7 %collective-permute-start.25 = (f32[2,192,256]{2,1,0:T(8,128)S(1)}, f32[2,192,256]{2,1,0:T(8,128)S(1)}, u32[]{:S(2)}, u32[]{:S(2)}) collective-permute-start(f32[2,192,256]{2,1,0:T(8,128)S(1)} %pad_maximum_fusion.3), channel_id=1, source_target_pairs={{0,1},{1,0},{2,3},{3,2},{4,5},{5,4},{6,7},{7,6},{8,9},{9,8},{10,11... | collective-permute-start | bytes 1179656 | tf_op jit(solution)/shard_map/ppermute | solution.py:398
  76.5 6.7 %collective-permute-start.18 = (f32[192,256]{1,0:T(8,128)S(1)}, f32[192,256]{1,0:T(8,128)S(1)}, u32[]{:S(2)}, u32[]{:S(2)}) collective-permute-start(f32[192,256]{1,0:T(8,128)S(1)} %collective-permute-done.17.refs_3_), channel_id=1, source_target_pairs={{0,8},{8,16},{16,24},{24,28},{28,20},{20,12},{12,4},{4,0},{1,9},{9... | collective-permute-start | bytes 589832 | tf_op jit(solution)/shard_map/ppermute | solution.py:65
  78.1 6.8 %collective-permute-start.21 = (f32[192,256]{1,0:T(8,128)S(1)}, f32[192,256]{1,0:T(8,128)S(1)}, u32[]{:S(2)}, u32[]{:S(2)}) collective-permute-start(f32[192,256]{1,0:T(8,128)S(1)} %collective-permute-done.20.refs_4_), channel_id=1, source_target_pairs={{8,0},{16,8},{24,16},{28,24},{20,28},{12,20},{4,12},{0,4},{9,1},{1... | collective-permute-start | bytes 589832 | tf_op jit(solution)/shard_map/ppermute | solution.py:66
  83.2 5.3 %collective-permute-start.22 = (f32[96,256]{1,0:T(8,128)S(1)}, f32[96,256]{1,0:T(8,128)S(1)}, u32[]{:S(2)}, u32[]{:S(2)}) collective-permute-start(f32[96,256]{1,0:T(8,128)S(1)} %slice.118), channel_id=1, source_target_pairs={{0,8},{8,16},{16,24},{24,28},{28,20},{20,12},{12,4},{4,0},{1,9},{9... | collective-permute-start | bytes 294920 | tf_op jit(solution)/shard_map/ppermute | solution.py:69
  84.9 4.8 %collective-permute-start.23 = (f32[96,256]{1,0:T(8,128)S(1)}, f32[96,256]{1,0:T(8,128)S(1)}, u32[]{:S(2)}, u32[]{:S(2)}) collective-permute-start(f32[96,256]{1,0:T(8,128)S(1)} %slice.119), channel_id=1, source_target_pairs={{8,0},{16,8},{24,16},{28,24},{20,28},{12,20},{4,12},{0,4},{9,1},{1... | collective-permute-start | bytes 294920 | tf_op jit(solution)/shard_map/ppermute | solution.py:70
  85.7 2.3 %copy-start.2 = (f32[768,1536]{1,0:T(8,128)S(1)}, f32[768,1536]{1,0:T(8,128)}, u32[]{:S(2)}) copy-start(f32[768,1536]{1,0:T(8,128)} %get-tuple-element.71.gram_ref) | copy-start | bytes 14155780
  92.5 1.8 %collective-permute-start.26 = (f32[2,192,256]{2,1,0:T(8,128)S(1)}, f32[2,192,256]{2,1,0:T(8,128)S(1)}, u32[]{:S(2)}, u32[]{:S(2)}) collective-permute-start(f32[2,192,256]{2,1,0:T(8,128)S(1)} %pad_maximum_fusion.4), channel_id=1, source_target_pairs={{0,1},{1,0},{2,3},{3,2},{4,5},{5,4},{6,7},{7,6},{8,9},{9,8},{10,11... | collective-permute-start | bytes 1179656 | tf_op jit(solution)/shard_map/ppermute | solution.py:390
  94.9 11.7 %all-to-all-start = ((f32[32,4,256]{2,1,0:T(4,128)}), f32[32,4,256]{2,1,0:T(4,128)S(1)}, u32[]{:S(2)}, u32[]{:S(2)}) async-start(f32[32,4,256]{2,1,0:T(4,128)} %broadcast_in_dim.5), calls=%async_computation | async-start | bytes 262144 | tf_op jit(solution)/shard_map/all_to_all | solution.py:244
  98.4 8.4 %collective-permute-start.27 = (f32[192,256]{1,0:T(8,128)S(1)}, f32[192,256]{1,0:T(8,128)S(1)}, u32[]{:S(2)}, u32[]{:S(2)}) collective-permute-start(f32[192,256]{1,0:T(8,128)S(1)} %add_bitcast_fusion), channel_id=1, source_target_pairs={{0,2},{1,3},{2,0},{3,1},{4,6},{5,7},{6,4},{7,5},{8,10},{9,11},{10,... | collective-permute-start | bytes 589832 | tf_op jit(solution)/shard_map/ppermute | solution.py:394
  (1 other events, 0.9 us)

commit v5 on v4

--- a/solution.py
+++ b/solution.py
@@ -71,6 +71,9 @@
         yield low, high
 
 
+ORDER = (1, 3, 0, 2)
+
+
 def split(value):
     high = value.astype(jnp.bfloat16)
     return high, (value - high.astype(jnp.float32)).astype(jnp.bfloat16)
@@ -89,9 +92,9 @@
     copies = []
     for start in range(0, tile_ref.shape[1], block):
         lanes = pl.ds(start, block)
-        for j in range(tile_ref.shape[0] // piece):
+        for index, j in enumerate(ORDER):
             place = pl.ds(pl.multiple_of(jnp.bitwise_xor(me, j) * piece, 8), piece)
-            pair = whole_ref.at[place, lanes], tile_ref.at[pl.ds(j * piece, piece), lanes]
+            pair = whole_ref.at[place, lanes], tile_ref.at[pl.ds(index * piece, piece), lanes]
             if outward:
                 pair = pair[::-1]
             copies.append(pltpu.make_async_copy(*pair, semaphores.at[len(copies)]))
@@ -133,8 +136,8 @@
         own, far, near = round_refs[3 * group : 3 * group + 3]
         for inner in range(own.shape[0]):
             lanes = slice(turn * count, (turn + 1) * count)
-            parts = [own[inner], near[0, inner], far[inner], near[1, inner]]
-            for j, part in enumerate(parts):
+            parts = [near[0, inner], near[1, inner], own[inner], far[inner]]
+            for j, part in zip(ORDER, parts):
                 at = pl.multiple_of(jnp.bitwise_xor(me, j) * head_part, 16)
                 target[pl.ds(at, head_part), lanes] = part[:head_part, :]
             rows[:, lanes] = jnp.concatenate([part[head_part:, :] for part in parts], axis=0)
@@ -162,8 +165,8 @@
 def gram_kernel(sizes, meta, *refs):
     n, tcol_count, piece, width, head_part, block = sizes
     low_ref, high_ref, *round_refs = refs[:5]
-    early_ref, columns, rows, target, gram_ref, right_ref, image_ref = refs[5:12]
-    last_columns, last_rows, last_target, tile_ref, sent = refs[12:]
+    early_ref, columns, rows, target, gram_ref, tile_ref, right_ref, side_high, side_low, image_ref = refs[5:15]
+    last_columns, last_rows, last_target, sent = refs[15:]
     me = meta[2 * n]
     total_rows = columns.shape[1]
     count = last_rows.shape[1]
@@ -176,7 +179,6 @@
     place_rows(round_refs, me, head_part, last_rows, last_target, 0, count)
     scale = 1.0 / total_rows
     stores = tile_copies(gram_ref, tile_ref, me, piece, block, sent, outward=True)
-    sides = []
     for step in range(columns.shape[0] // block):
         lanes = slice(step * block, (step + 1) * block)
         last = last_columns[lanes, :]
@@ -184,40 +186,59 @@
         for index in range(step * tcol_count, (step + 1) * tcol_count):
             stores[index].start()
         side = dot(columns[lanes, :done], target[:, :done], NT) + dot(last, last_target[...], NT)
-        sides.append(split(side * scale))
-    right = dot(rows[:piece, :done], target[:, :done], NT) + dot(last_rows[:piece, :], last_target[...], NT)
+        side_high[lanes, :], side_low[lanes, :] = split(side * scale)
+    own = slice(2 * piece, 3 * piece)
+    right = dot(rows[own, :done], target[:, :done], NT) + dot(last_rows[own, :], last_target[...], NT)
     right_ref[...] = right * scale
-    side = [jnp.concatenate(part, axis=0) for part in zip(*sides)]
-    image_ref[...] = product(split(tile_ref[...]), side)
+    value = product(split(tile_ref[: 2 * piece, :]), (side_high[...], side_low[...]))
+    image_ref[...] = value.reshape(image_ref.shape)
     for store in stores:
         store.wait()
 
 
+def kept_kernel(sizes, meta, tile_ref, side_high, side_low, image_ref):
+    value = product(split(tile_ref[2 * sizes :, :]), (side_high[...], side_low[...]))
+    image_ref[...] = value.reshape(image_ref.shape)
+
+
+def partial_kernel(sizes, meta, *refs):
+    n, data_count, piece = sizes
+    shard_refs = refs[: n - 1]
+    tile_ref, start_ref, total_ref, sums_ref, side = refs[n - 1 :]
+    for index in range(n - 1):
+        base = pl.multiple_of((meta[n + index] * data_count + meta[index]) * piece, 8)
+        side[pl.ds(base, piece), :] = shard_refs[index][...]
+    far = pl.multiple_of((meta[2 * n - 1] * data_count + meta[n - 1]) * piece, 8)
+    side[pl.ds(far, piece), :] = jnp.zeros((piece, side.shape[1]), jnp.float32)
+    total_ref[...] = product(split(tile_ref[...]), split(side[...]))
+    own, start = shard_refs[0][...], start_ref[...]
+    early = [jnp.sum(a * b, axis=0, keepdims=True) for a, b in ((start, start), (start, own), (own, own))]
+    sums_ref[...] = jnp.concatenate(early, axis=0)
+
+
 def image_kernel(sizes, meta, *refs):
-    n, data_count, tcol_count, piece = sizes
-    shard_refs = refs[: n + 1]
-    tile_ref, start_ref, near_ref, far_ref, penalty_ref, out_ref, sums_ref, side = refs[n + 1 :]
-    for index in range(n):
-        base = pl.multiple_of((meta[n + index] * data_count + meta[index]) * piece, 8)
-        if index < n - 1:
-            side[pl.ds(base, piece), :] = shard_refs[index][...]
-        else:
-            half = shard_refs[n - 1].shape[0]
-            side[pl.ds(base, half), :] = shard_refs[n - 1][...]
-            side[pl.ds(pl.multiple_of(base + half, 8), piece - half), :] = shard_refs[n][...]
-    total = product(split(tile_ref[...]), split(side[...]))
-    own = shard_refs[0][...]
-    others = [own, near_ref[0], far_ref[...], near_ref[1]]
+    n, data_count, piece, block = sizes
+    low_ref, high_ref, total_ref, tile_ref, early_ref = refs[:5]
+    own_ref, near_ref, far_ref, penalty_ref, out_ref, sums_ref, side = refs[5:]
+    base = (meta[2 * n - 1] * data_count + meta[n - 1]) * piece
+    lanes = pl.ds(pl.multiple_of(base // block * block, 128), block)
+    base = pl.multiple_of(base % block, 8)
+    half = low_ref.shape[0]
+    side[...] = jnp.zeros_like(side)
+    side[pl.ds(base, half), :] = low_ref[...]
+    side[pl.ds(pl.multiple_of(base + half, 8), piece - half), :] = high_ref[...]
+    total = total_ref[...] + product(split(tile_ref[:, lanes]), split(side[...]))
+    own = own_ref[...]
+    others = [near_ref[0], near_ref[1], own, far_ref[...]]
     late = jnp.zeros((1, own.shape[1]), jnp.float32)
-    for j in range(tcol_count):
-        value = total[j * piece : (j + 1) * piece]
+    for index, j in enumerate(ORDER):
+        value = total[index * piece : (index + 1) * piece]
         if j == 0:
             value = value + penalty_ref[...] * own
-        out_ref[j] = value
-        late = late + jnp.sum(value * others[j], axis=0, keepdims=True)
-    start = start_ref[...]
-    early = [jnp.sum(a * b, axis=0, keepdims=True) for a, b in ((start, start), (start, own), (own, own))]
-    sums_ref[...] = jnp.concatenate(early + [late], axis=0)
+        out_ref[index] = value
+        late = late + jnp.sum(value * others[index], axis=0, keepdims=True)
+    sums = jnp.concatenate([early_ref[...], late], axis=0)
+    sums_ref[...] = jnp.broadcast_to(sums[None], sums_ref.shape)
 
 
 def call(body, meta, inputs, in_specs, out_specs, out_shape, scratch, vmem, flops, read):
@@ -234,14 +255,6 @@
         compiler_params=pltpu.CompilerParams(vmem_limit_bytes=vmem),
         cost_estimate=pl.CostEstimate(flops=flops, bytes_accessed=read, transcendentals=0),
     )(meta, *inputs)
-
-
-def all_sum(value, axis_names):
-    count = 1
-    for name in axis_names:
-        count *= lax.axis_size(name)
-    spread = jnp.broadcast_to(value[None], (count,) + value.shape)
-    return jnp.sum(lax.all_to_all(spread, axis_names, split_axis=0, concat_axis=0, tiled=True), axis=0)
 
 
 def shards(embeddings, targets, gram_prior, penalty):
@@ -361,62 +374,92 @@
                 2 * tile_rows * tile_columns * (total_rows - row_count),
                 8 * tile_rows * tile_columns,
             )
-    gram, start, partial = call(
+    half_rows = (2, piece, heads)
+    gram, gram_tile, start, side_high, side_low, sent = call(
         functools.partial(gram_kernel, (n, tcol_count, piece, width, head_part, block)),
         gram_meta,
         [*gathered[-2:], *groups[2], early, columns, rows, target],
         [VMEM] * 9,
-        [HBM] + [VMEM] * 2,
+        [HBM] + [VMEM] * 5,
         [
             jax.ShapeDtypeStruct((tile_rows, tile_columns), f32),
+            jax.ShapeDtypeStruct((tile_rows, tile_columns), f32),
             jax.ShapeDtypeStruct((piece, heads), f32),
-            jax.ShapeDtypeStruct((tile_rows, heads), f32),
+            jax.ShapeDtypeStruct((tile_columns, heads), bf16),
+            jax.ShapeDtypeStruct((tile_columns, heads), bf16),
+            jax.ShapeDtypeStruct(half_rows, f32),
         ],
         [
             pltpu.VMEM((tile_columns, row_count), bf16),
             pltpu.VMEM((tile_rows, row_count), bf16),
             pltpu.VMEM((heads, row_count), bf16),
-            pltpu.VMEM((tile_rows, tile_columns), f32),
             tile_semaphores,
         ],
         GRAM_BYTES,
-        2 * tile_rows * tile_columns * (total_rows + 3 * heads),
+        2 * tile_rows * tile_columns * (row_count + 2 * heads),
         12 * tile_rows * tile_columns,
     )
     penalty_rows = penalty.reshape(piece, 1)
-
-    def owner_sum(value, beside=None):
-        kept = [value[j] for j in range(tcol_count)]
-        received = lax.ppermute(jnp.stack(kept[1::2]), "tcol", swap(tcol_count, 1))
-        if beside is not None:
-            received, beside = lax.optimization_barrier((received, beside))
-        kept = [a + received[i] for i, a in enumerate(kept[0::2])]
-        return kept[0] + lax.ppermute(kept[1], "tcol", swap(tcol_count, 2)), beside
-
-    image = owner_sum(partial.reshape(tcol_count, piece, heads))[0] + penalty_rows * start
+    received = lax.ppermute(sent, "tcol", swap(tcol_count, 1))
+    kept = call(
+        functools.partial(kept_kernel, piece),
+        me_meta,
+        [gram_tile, side_high, side_low],
+        [VMEM] * 3,
+        VMEM,
+        jax.ShapeDtypeStruct(half_rows, f32),
+        [],
+        IMAGE_BYTES,
+        3 * tile_rows * tile_columns * heads,
+        2 * tile_rows * tile_columns,
+    )
+    image = kept[0] + received[0] + lax.ppermute(kept[1] + received[1], "tcol", swap(tcol_count, 2))
+    image = image + penalty_rows * start
     far_image = lax.ppermute(image, "tcol", swap(tcol_count, 2))
     near_images = lax.ppermute(jnp.stack([image, far_image]), "tcol", swap(tcol_count, 1))
     images = [image]
     for step, arrived in enumerate(ring.steps(image, piece), 1):
+        if step == ring.far - 2:
+            *arrived, gram = lax.optimization_barrier((*arrived, gram))
+            tile = fetch(gram)
         if step == ring.far - 1:
-            arrived = lax.optimization_barrier((*arrived, gram))
-            gram = arrived[2]
-            tile = fetch(gram)
-        images += arrived[:2]
-    second, sums = call(
-        functools.partial(image_kernel, (n, data_count, tcol_count, piece)),
+            *arrived, tile = lax.optimization_barrier((*arrived, tile))
+        images += arrived
+    total, early_sums = call(
+        functools.partial(partial_kernel, (n, data_count, piece)),
         image_meta,
-        [*images, tile, start, near_images, far_image, penalty_rows],
-        [VMEM] * (n + 6),
+        [*images[:-2], tile, start],
+        [VMEM] * (n + 1),
         [VMEM] * 2,
-        [jax.ShapeDtypeStruct((tcol_count, piece, heads), f32), jax.ShapeDtypeStruct((4, heads), f32)],
+        [jax.ShapeDtypeStruct((tile_rows, heads), f32), jax.ShapeDtypeStruct((3, heads), f32)],
         [pltpu.VMEM((tile_columns, heads), f32)],
         IMAGE_BYTES,
         6 * tile_rows * tile_columns * heads,
         4 * tile_rows * tile_columns,
     )
-    second, sums = owner_sum(second, sums)
-    sums = all_sum(sums, ("dp", "trow", "tcol"))
+    axes = ("dp", "trow", "tcol")
+    second, sums = call(
+        functools.partial(image_kernel, (n, data_count, piece, block)),
+        image_meta,
+        [*images[-2:], total, tile, early_sums, image, near_images, far_image, penalty_rows],
+        [VMEM] * 9,
+        [VMEM] * 2,
+        [
+            jax.ShapeDtypeStruct((tcol_count, piece, heads), f32),
+            jax.ShapeDtypeStruct((n * tcol_count, 4, heads), f32),
+        ],
+        [pltpu.VMEM((block, heads), f32)],
+        IMAGE_BYTES,
+        6 * tile_rows * block * heads,
+        4 * tile_rows * block,
+    )
+    sums, second = lax.optimization_barrier((sums, second))
+    sums = lax.all_to_all(sums, axes, split_axis=0, concat_axis=0, tiled=True)
+    received = lax.ppermute(second[:2], "tcol", swap(tcol_count, 1))
+    far_second = lax.ppermute(second[3] + received[1], "tcol", swap(tcol_count, 2))
+    far_second, sums = lax.optimization_barrier((far_second, sums))
+    sums = jnp.sum(sums, axis=0)
+    second = second[2] + received[0] + far_second
 
     norm, curvature, image_norm, image_curvature = sums[0], sums[1], sums[2], sums[3]
     step = norm / curvature

time: 108 us -> 104 us (0.963)
  waiting for transfers between devices: 44.7 us -> 39.7 us
  Pallas kernels: 15.6 us -> 17.1 us
    ppermute x6, waiting for transfers between devices: 25.5 us -> 21.4 us  [steps(): ahead = lax.ppermute(ahead, ('dp', 'trow'), self.ahead)]
    ppermute x4, waiting for transfers between devices: 8.91 us -> 6.17 us  [the longest x1 5.45 us: shards(): lax.ppermute(kept[1] + received[1], 'tcol', swap(tcol_count, 2))]
    ppermute x6, waiting for transfers between devices: 0.9 us -> 2.48 us  [steps(): back = lax.ppermute(back, ('dp', 'trow'), self.back)]
    pallas_call x7 -> x9, Pallas kernels: 15.6 us -> 17.1 us  [call(): pl.pallas_call(body, grid_spec=pltpu.PrefetchScalarGridSpec(num_scalar_pr...]
  transfers between devices with their start and end apart: 29 -> 29, of which waited for: 15 -> 15; matrix products, arithmetic and copies ran while one was open for 3% -> 3% of each run, Pallas kernels for 5% -> 9%
where the time goes in v5:
time: 104 us
  waiting for transfers between devices  39.7 us (38%)
  starting transfers between devices  32.3 us (31%)
  Pallas kernels  17.1 us (16%)
  local copies, waits for them, and re-layouts  10.3 us (10%)
  between operations  2.89 us (3%)
  other arithmetic  1.39 us (1%)
    ppermute x6, waiting for transfers between devices, steps(): ahead = lax.ppermute(ahead, ('dp', 'trow'), self.ahead)  21.4 us
    pallas_call x9, Pallas kernels, call(): pl.pallas_call(body, grid_spec=pltpu.PrefetchScalarGridSpec(num_scalar_pr...  17.1 us
    ppermute x6, starting transfers between devices, steps(): ahead = lax.ppermute(ahead, ('dp', 'trow'), self.ahead)  11.1 us
    unnamed x10, local copies, waits for them, and re-layouts  6.83 us
    all_to_all x1, waiting for transfers between devices, shards(): sums = lax.all_to_all(sums, axes, split_axis=0, concat_axis=0, tiled=True)  6.35 us
    ppermute x1, waiting for transfers between devices, shards(): lax.ppermute(kept[1] + received[1], 'tcol', swap(tcol_count, 2))  5.45 us
    ppermute x3, starting transfers between devices, open_groups(): lax.ppermute(mine, 'tcol', swap(tcol_count, 2))  5.01 us
    all_to_all x1, starting transfers between devices, shards(): sums = lax.all_to_all(sums, axes, split_axis=0, concat_axis=0, tiled=True)  3.7 us
  transfers between devices with their start and end apart: 29, of which 15 were waited for; matrix products, arithmetic and copies ran while one was open for 3% of the time, Pallas kernels for 9%

profile of v5, /device:TPU:0, one launch (start us, length us, event | category | flops | bytes accessed | tf_op | source)
XLA Modules:
  0.0 103.6 jit_solution(10001390936809411936)
XLA Ops:
  2.9 3.1 %collective-permute-start = (bf16[832,256]{1,0:T(8,128)(2,1)S(1)}, bf16[832,256]{1,0:T(8,128)(2,1)S(1)}, u32[]{:S(2)}, u32[]{:S(2)}) collective-permute-start(bf16[832,256]{1,0:T(8,128)(2,1)S(1)} %pad_maximum_fusion.1.refs_0_), channel_id=1, source_target_pairs={{0,8},{8,16},{16,24},{24,28},{28,20},{20,12},{12,4},{4,0},{1,9},{9... | collective-permute-start | bytes 1277960 | tf_op jit(solution)/shard_map/ppermute | solution.py:65
  7.2 2.0 %collective-permute-start.2 = (bf16[1,256,256]{2,1,0:T(8,128)(2,1)S(1)}, bf16[1,256,256]{2,1,0:T(8,128)(2,1)S(1)}, u32[]{:S(2)}, u32[]{:S(2)}) collective-permute-start(bf16[1,256,256]{2,1,0:T(8,128)(2,1)S(1)} %maximum_bitcast_fusion.refs_7_), channel_id=1, source_target_pairs={{0,2},{1,3},{2,0},{3,1},{4,6},{5,7},{6,4},{7,5},{8,10},{9,11},{10,... | collective-permute-start | bytes 393224 | tf_op jit(solution)/shard_map/ppermute | solution.py:317
  9.2 1.3 %dynamic_slice.12 = s32[1,1]{1,0:T(1,128)} dynamic-slice(s32[4,2]{1,0:T(4,128)} %constant.37.clone, s32[]{:T(128)S(6)} %select_n.15, s32[]{:T(128)S(6)} %select_n.16), dynamic_slice_sizes={1,1} | dynamic-slice | bytes 12 | tf_op jit(solution)/shard_map/dynamic_slice | solution.py:276
  13.1 2.7 %collective-permute-done.refs_0_.refs_1_ = bf16[832,256]{1,0:T(8,128)(2,1)S(1)} collective-permute-done((bf16[832,256]{1,0:T(8,128)(2,1)S(1)}, bf16[832,256]{1,0:T(8,128)(2,1)S(1)}, u32[]{:S(2)}, u32[]{:S(2)}) %collective-permute-start) | collective-permute-done | bytes 426016 | tf_op jit(solution)/shard_map/ppermute | solution.py:65
  15.8 1.8 %collective-permute-start.3 = (bf16[832,256]{1,0:T(8,128)(2,1)S(1)}, bf16[832,256]{1,0:T(8,128)(2,1)S(1)}, u32[]{:S(2)}, u32[]{:S(2)}) collective-permute-start(bf16[832,256]{1,0:T(8,128)(2,1)S(1)} %collective-permute-done.refs_0_.refs_1_), channel_id=1, source_target_pairs={{0,8},{8,16},{16,24},{24,28},{28,20},{20,12},{12,4},{4,0},{1,9},{9... | collective-permute-start | bytes 1277960 | tf_op jit(solution)/shard_map/ppermute | solution.py:65
  17.9 8.9 %collective-permute-done.3.refs_2_.refs_3_ = bf16[832,256]{1,0:T(8,128)(2,1)S(1)} collective-permute-done((bf16[832,256]{1,0:T(8,128)(2,1)S(1)}, bf16[832,256]{1,0:T(8,128)(2,1)S(1)}, u32[]{:S(2)}, u32[]{:S(2)}) %collective-permute-start.3) | collective-permute-done | bytes 426016 | tf_op jit(solution)/shard_map/ppermute | solution.py:65
  26.8 1.5 %collective-permute-start.6 = (bf16[832,256]{1,0:T(8,128)(2,1)S(1)}, bf16[832,256]{1,0:T(8,128)(2,1)S(1)}, u32[]{:S(2)}, u32[]{:S(2)}) collective-permute-start(bf16[832,256]{1,0:T(8,128)(2,1)S(1)} %collective-permute-done.3.refs_2_.refs_3_), channel_id=1, source_target_pairs={{0,8},{8,16},{16,24},{24,28},{28,20},{20,12},{12,4},{4,0},{1,9},{9... | collective-permute-start | bytes 1277960 | tf_op jit(solution)/shard_map/ppermute | solution.py:65
  29.6 1.5 %collective-permute-start.5 = (bf16[2,256,256]{2,1,0:T(8,128)(2,1)S(1)}, bf16[2,256,256]{2,1,0:T(8,128)(2,1)S(1)}, u32[]{:S(2)}, u32[]{:S(2)}) collective-permute-start(bf16[2,256,256]{2,1,0:T(8,128)(2,1)S(1)} %shard_map.85.refs_10_), channel_id=1, source_target_pairs={{0,2},{1,3},{2,0},{3,1},{4,6},{5,7},{6,4},{7,5},{8,10},{9,11},{10,... | collective-permute-start | bytes 786440 | tf_op jit(solution)/shard_map/ppermute | solution.py:317
  31.1 2.3 %copy-done.1 = f32[4,1,1,192,1536]{4,3,2,1,0:T(8,128)S(1)} copy-done((f32[4,1,1,192,1536]{4,3,2,1,0:T(8,128)S(1)}, f32[4,1,1,192,1536]{4,3,2,1,0:T(8,128)}, u32[]{:S(2)}) %copy-start.1) | copy-done | bytes 4718616
  33.9 3.0 %collective-permute-done.6.refs_5_.refs_2_ = bf16[832,256]{1,0:T(8,128)(2,1)S(1)} collective-permute-done((bf16[832,256]{1,0:T(8,128)(2,1)S(1)}, bf16[832,256]{1,0:T(8,128)(2,1)S(1)}, u32[]{:S(2)}, u32[]{:S(2)}) %collective-permute-start.6) | collective-permute-done | bytes 426016 | tf_op jit(solution)/shard_map/ppermute | solution.py:65
  38.5 1.6 %collective-permute-start.11 = (bf16[384,256]{1,0:T(8,128)(2,1)S(1)}, bf16[384,256]{1,0:T(8,128)(2,1)S(1)}, u32[]{:S(2)}, u32[]{:S(2)}) collective-permute-start(bf16[384,256]{1,0:T(8,128)(2,1)S(1)} %slice.92), channel_id=1, source_target_pairs={{0,8},{8,16},{16,24},{24,28},{28,20},{20,12},{12,4},{4,0},{1,9},{9... | collective-permute-start | bytes 589832 | tf_op jit(solution)/shard_map/ppermute | solution.py:69
  41.2 1.6 %collective-permute-start.10 = (bf16[1,256,256]{2,1,0:T(8,128)(2,1)S(1)}, bf16[1,256,256]{2,1,0:T(8,128)(2,1)S(1)}, u32[]{:S(2)}, u32[]{:S(2)}) collective-permute-start(bf16[1,256,256]{2,1,0:T(8,128)(2,1)S(1)} %shard_map.88.refs_2_), channel_id=1, source_target_pairs={{0,2},{1,3},{2,0},{3,1},{4,6},{5,7},{6,4},{7,5},{8,10},{9,11},{10,... | collective-permute-start | bytes 393224 | tf_op jit(solution)/shard_map/ppermute | solution.py:317
  42.8 3.6 %shard_map.87 = (f32[768,1536]{1,0:T(8,128)S(1)}, bf16[1536,1024]{1,0:T(8,128)(2,1)S(1)}, bf16[768,1024]{1,0:T(8,128)(2,1)S(1)}, bf16[256,1024]{1,0:T(8,128)(2,1)S(1)}) custom-call(s32[17]{0:T(128)S(1)} %get-tuple-element.51.meta, bf16[832,256]{1,0:T(8,128)(2,1)S(1)} %pad_maximum_fusion.1.refs_0_, bf16[832,256]{1,0:T(8,128)(2,1)S(1)} %collective-permute-done.refs_0_.refs_1_, ...), custom_call_target="tpu_custom_call" | custom-call | flops 1811939328 | bytes 9437184 | tf_op jit(solution)/shard_map/pallas_call | solution.py:245
  46.8 1.5 %collective-permute-done.13.refs_4_ = bf16[2,1,256,256]{3,2,1,0:T(8,128)(2,1)S(1)} collective-permute-done((bf16[2,1,256,256]{3,2,1,0:T(8,128)(2,1)S(1)}, bf16[2,1,256,256]{3,2,1,0:T(8,128)(2,1)S(1)}, u32[]{:S(2)}, u32[]{:S(2)}) %collective-permute-start.13) | collective-permute-done | bytes 262176 | tf_op jit(solution)/shard_map/ppermute | solution.py:311
  48.4 5.4 %shard_map.89 = (f32[768,1536]{1,0:T(8,128)}, f32[768,1536]{1,0:T(8,128)S(1)}, f32[192,256]{1,0:T(8,128)S(1)}, bf16[1536,256]{1,0:T(8,128)(2,1)S(1)}, bf16[1536,...) custom-call(s32[17]{0:T(128)S(1)} %get-tuple-element.51.meta, bf16[384,256]{1,0:T(8,128)(2,1)S(1)} %collective-permute-done.11.refs_0_, ...), custom_call_target="tpu_custom_call" | custom-call | flops 1811939328 | bytes 14155776 | tf_op jit(solution)/shard_map/pallas_call | solution.py:245
  55.6 1.6 %collective-permute-start.15 = (f32[192,256]{1,0:T(8,128)S(1)}, f32[192,256]{1,0:T(8,128)S(1)}, u32[]{:S(2)}, u32[]{:S(2)}) collective-permute-start(f32[192,256]{1,0:T(8,128)S(1)} %fusion.8), channel_id=1, source_target_pairs={{0,2},{1,3},{2,0},{3,1},{4,6},{5,7},{6,4},{7,5},{8,10},{9,11},{10,... | collective-permute-start | bytes 589832 | tf_op jit(solution)/shard_map/ppermute | solution.py:416
  57.1 5.5 %collective-permute-done.15 = f32[192,256]{1,0:T(8,128)S(1)} collective-permute-done((f32[192,256]{1,0:T(8,128)S(1)}, f32[192,256]{1,0:T(8,128)S(1)}, u32[]{:S(2)}, u32[]{:S(2)}) %collective-permute-start.15) | collective-permute-done | bytes 196640 | tf_op jit(solution)/shard_map/ppermute | solution.py:416
  62.7 1.6 %collective-permute-start.16 = (f32[192,256]{1,0:T(8,128)S(1)}, f32[192,256]{1,0:T(8,128)S(1)}, u32[]{:S(2)}, u32[]{:S(2)}) collective-permute-start(f32[192,256]{1,0:T(8,128)S(1)} %fusion.11.refs_0_.refs_5_), channel_id=1, source_target_pairs={{0,8},{8,16},{16,24},{24,28},{28,20},{20,12},{12,4},{4,0},{1,9},{9... | collective-permute-start | bytes 589832 | tf_op jit(solution)/shard_map/ppermute | solution.py:65
  64.8 1.5 %collective-permute-start.24 = (f32[192,256]{1,0:T(8,128)S(1)}, f32[192,256]{1,0:T(8,128)S(1)}, u32[]{:S(2)}, u32[]{:S(2)}) collective-permute-start(f32[192,256]{1,0:T(8,128)S(1)} %fusion.11.refs_0_.refs_5_), channel_id=1, source_target_pairs={{0,2},{1,3},{2,0},{3,1},{4,6},{5,7},{6,4},{7,5},{8,10},{9,11},{10,... | collective-permute-start | bytes 589832 | tf_op jit(solution)/shard_map/ppermute | solution.py:418
  66.3 2.6 %collective-permute-done.16.refs_1_ = f32[192,256]{1,0:T(8,128)S(1)} collective-permute-done((f32[192,256]{1,0:T(8,128)S(1)}, f32[192,256]{1,0:T(8,128)S(1)}, u32[]{:S(2)}, u32[]{:S(2)}) %collective-permute-start.16) | collective-permute-done | bytes 196640 | tf_op jit(solution)/shard_map/ppermute | solution.py:65
  68.8 1.6 %collective-permute-start.17 = (f32[192,256]{1,0:T(8,128)S(1)}, f32[192,256]{1,0:T(8,128)S(1)}, u32[]{:S(2)}, u32[]{:S(2)}) collective-permute-start(f32[192,256]{1,0:T(8,128)S(1)} %collective-permute-done.16.refs_1_), channel_id=1, source_target_pairs={{0,8},{8,16},{16,24},{24,28},{28,20},{20,12},{12,4},{4,0},{1,9},{9... | collective-permute-start | bytes 589832 | tf_op jit(solution)/shard_map/ppermute | solution.py:65
  71.0 3.6 %collective-permute-done.17.refs_3_ = f32[192,256]{1,0:T(8,128)S(1)} collective-permute-done((f32[192,256]{1,0:T(8,128)S(1)}, f32[192,256]{1,0:T(8,128)S(1)}, u32[]{:S(2)}, u32[]{:S(2)}) %collective-permute-start.17) | collective-permute-done | bytes 196640 | tf_op jit(solution)/shard_map/ppermute | solution.py:65
  74.6 1.6 %collective-permute-start.20 = (f32[192,256]{1,0:T(8,128)S(1)}, f32[192,256]{1,0:T(8,128)S(1)}, u32[]{:S(2)}, u32[]{:S(2)}) collective-permute-start(f32[192,256]{1,0:T(8,128)S(1)} %collective-permute-done.17.refs_3_), channel_id=1, source_target_pairs={{0,8},{8,16},{16,24},{24,28},{28,20},{20,12},{12,4},{4,0},{1,9},{9... | collective-permute-start | bytes 589832 | tf_op jit(solution)/shard_map/ppermute | solution.py:65
  76.8 2.3 %copy-done.2 = f32[768,1536]{1,0:T(8,128)S(1)} copy-done((f32[768,1536]{1,0:T(8,128)S(1)}, f32[768,1536]{1,0:T(8,128)}, u32[]{:S(2)}) %copy-start.2) | copy-done | bytes 4718616
  80.3 1.6 %collective-permute-done.22.refs_6_ = f32[192,256]{1,0:T(8,128)S(1)} collective-permute-done((f32[192,256]{1,0:T(8,128)S(1)}, f32[192,256]{1,0:T(8,128)S(1)}, u32[]{:S(2)}, u32[]{:S(2)}) %collective-permute-start.22) | collective-permute-done | bytes 196640 | tf_op jit(solution)/shard_map/ppermute | solution.py:66
  81.9 1.6 %collective-permute-start.21 = (f32[96,256]{1,0:T(8,128)S(1)}, f32[96,256]{1,0:T(8,128)S(1)}, u32[]{:S(2)}, u32[]{:S(2)}) collective-permute-start(f32[96,256]{1,0:T(8,128)S(1)} %slice.98), channel_id=1, source_target_pairs={{0,8},{8,16},{16,24},{24,28},{28,20},{20,12},{12,4},{4,0},{1,9},{9... | collective-permute-start | bytes 294920 | tf_op jit(solution)/shard_map/ppermute | solution.py:69
  84.2 2.7 %shard_map.92 = (f32[768,256]{1,0:T(8,128)S(1)}, f32[3,256]{1,0:T(4,128)S(1)}) custom-call(s32[17]{0:T(128)S(1)} %get-tuple-element.85.meta, f32[192,256]{1,0:T(8,128)S(1)} %fusion.11.refs_0_.refs_5_, f32[192,256]{1,0:T(8,128)S(1)} %collective-permute-done.16.refs_1_, f32[192,256]{1,0:T(8,128)S(1)} %collective-permute-done.18.refs_2_, ...), custom_call_target="tpu_custom_call" | custom-call | flops 1811939328 | bytes 4718592 | tf_op jit(solution)/shard_map/pallas_call | solution.py:245
  86.9 1.4 %collective-permute-done.23.refs_1_ = f32[96,256]{1,0:T(8,128)S(1)} collective-permute-done((f32[96,256]{1,0:T(8,128)S(1)}, f32[96,256]{1,0:T(8,128)S(1)}, u32[]{:S(2)}, u32[]{:S(2)}) %collective-permute-start.23) | collective-permute-done | bytes 98336 | tf_op jit(solution)/shard_map/ppermute | solution.py:70
  88.3 2.1 %shard_map.93 = (f32[4,192,256]{2,1,0:T(8,128)S(1)}, f32[32,4,256]{2,1,0:T(4,128)}) custom-call(s32[17]{0:T(128)S(1)} %get-tuple-element.85.meta, f32[96,256]{1,0:T(8,128)S(1)} %collective-permute-done.21.refs_0_, f32[96,256]{1,0:T(8,128)S(1)} %collective-permute-done.23.refs_1_, f32[768,256]{1,0:T(8,128)S(1)} %get-tuple-element.91.refs_2_, ...), custom_call_target="tpu_custom_call" | custom-call | flops 452984832 | bytes 1179648 | tf_op jit(solution)/shard_map/pallas_call | solution.py:245
  90.5 3.7 %all-to-all-start = ((f32[32,4,256]{2,1,0:T(4,128)}), f32[32,4,256]{2,1,0:T(4,128)S(1)}, u32[]{:S(2)}, u32[]{:S(2)}) async-start(f32[32,4,256]{2,1,0:T(4,128)} %get-tuple-element.96), calls=%async_computation | async-start | bytes 262144 | tf_op jit(solution)/shard_map/all_to_all | solution.py:457
  94.2 1.8 %collective-permute-start.27 = (f32[192,256]{1,0:T(8,128)S(1)}, f32[192,256]{1,0:T(8,128)S(1)}, u32[]{:S(2)}, u32[]{:S(2)}) collective-permute-start(f32[192,256]{1,0:T(8,128)S(1)} %fusion.7), channel_id=1, source_target_pairs={{0,2},{1,3},{2,0},{3,1},{4,6},{5,7},{6,4},{7,5},{8,10},{9,11},{10,... | collective-permute-start | bytes 589832 | tf_op jit(solution)/shard_map/ppermute | solution.py:459
  96.1 6.4 %all-to-all-done = f32[32,4,256]{2,1,0:T(4,128)S(1)} async-done(((f32[32,4,256]{2,1,0:T(4,128)}), f32[32,4,256]{2,1,0:T(4,128)S(1)}, u32[]{:S(2)}, u32[]{:S(2)}) %all-to-all-start) | async-done | bytes 131104 | tf_op jit(solution)/shard_map/all_to_all | solution.py:457
  (73 shorter events, 16.0 us)
Async XLA Ops:
  2.9 12.8 %collective-permute-start = (bf16[832,256]{1,0:T(8,128)(2,1)S(1)}, bf16[832,256]{1,0:T(8,128)(2,1)S(1)}, u32[]{:S(2)}, u32[]{:S(2)}) collective-permute-start(bf16[832,256]{1,0:T(8,128)(2,1)S(1)} %pad_maximum_fusion.1.refs_0_), channel_id=1, source_target_pairs={{0,8},{8,16},{16,24},{24,28},{28,20},{20,12},{12,4},{4,0},{1,9},{9... | collective-permute-start | bytes 1277960 | tf_op jit(solution)/shard_map/ppermute | solution.py:65
  6.0 11.6 %collective-permute-start.1 = (bf16[832,256]{1,0:T(8,128)(2,1)S(1)}, bf16[832,256]{1,0:T(8,128)(2,1)S(1)}, u32[]{:S(2)}, u32[]{:S(2)}) collective-permute-start(bf16[832,256]{1,0:T(8,128)(2,1)S(1)} %pad_maximum_fusion.1.refs_0_), channel_id=1, source_target_pairs={{8,0},{16,8},{24,16},{28,24},{20,28},{12,20},{4,12},{0,4},{9,1},{1... | collective-permute-start | bytes 1277960 | tf_op jit(solution)/shard_map/ppermute | solution.py:66
  7.2 21.8 %collective-permute-start.2 = (bf16[1,256,256]{2,1,0:T(8,128)(2,1)S(1)}, bf16[1,256,256]{2,1,0:T(8,128)(2,1)S(1)}, u32[]{:S(2)}, u32[]{:S(2)}) collective-permute-start(bf16[1,256,256]{2,1,0:T(8,128)(2,1)S(1)} %maximum_bitcast_fusion.refs_7_), channel_id=1, source_target_pairs={{0,2},{1,3},{2,0},{3,1},{4,6},{5,7},{6,4},{7,5},{8,10},{9,11},{10,... | collective-permute-start | bytes 393224 | tf_op jit(solution)/shard_map/ppermute | solution.py:317
  15.8 11.0 %collective-permute-start.3 = (bf16[832,256]{1,0:T(8,128)(2,1)S(1)}, bf16[832,256]{1,0:T(8,128)(2,1)S(1)}, u32[]{:S(2)}, u32[]{:S(2)}) collective-permute-start(bf16[832,256]{1,0:T(8,128)(2,1)S(1)} %collective-permute-done.refs_0_.refs_1_), channel_id=1, source_target_pairs={{0,8},{8,16},{16,24},{24,28},{28,20},{20,12},{12,4},{4,0},{1,9},{9... | collective-permute-start | bytes 1277960 | tf_op jit(solution)/shard_map/ppermute | solution.py:65
  17.6 10.7 %collective-permute-start.4 = (bf16[832,256]{1,0:T(8,128)(2,1)S(1)}, bf16[832,256]{1,0:T(8,128)(2,1)S(1)}, u32[]{:S(2)}, u32[]{:S(2)}) collective-permute-start(bf16[832,256]{1,0:T(8,128)(2,1)S(1)} %collective-permute-done.1.refs_1_.refs_2_), channel_id=1, source_target_pairs={{8,0},{16,8},{24,16},{28,24},{20,28},{12,20},{4,12},{0,4},{9,1},{1... | collective-permute-start | bytes 1277960 | tf_op jit(solution)/shard_map/ppermute | solution.py:66
  26.8 10.1 %collective-permute-start.6 = (bf16[832,256]{1,0:T(8,128)(2,1)S(1)}, bf16[832,256]{1,0:T(8,128)(2,1)S(1)}, u32[]{:S(2)}, u32[]{:S(2)}) collective-permute-start(bf16[832,256]{1,0:T(8,128)(2,1)S(1)} %collective-permute-done.3.refs_2_.refs_3_), channel_id=1, source_target_pairs={{0,8},{8,16},{16,24},{24,28},{28,20},{20,12},{12,4},{4,0},{1,9},{9... | collective-permute-start | bytes 1277960 | tf_op jit(solution)/shard_map/ppermute | solution.py:65
  28.3 9.5 %collective-permute-start.7 = (bf16[832,256]{1,0:T(8,128)(2,1)S(1)}, bf16[832,256]{1,0:T(8,128)(2,1)S(1)}, u32[]{:S(2)}, u32[]{:S(2)}) collective-permute-start(bf16[832,256]{1,0:T(8,128)(2,1)S(1)} %collective-permute-done.4.refs_3_.refs_4_), channel_id=1, source_target_pairs={{8,0},{16,8},{24,16},{28,24},{20,28},{12,20},{4,12},{0,4},{9,1},{1... | collective-permute-start | bytes 1277960 | tf_op jit(solution)/shard_map/ppermute | solution.py:66
  29.6 8.2 %collective-permute-start.5 = (bf16[2,256,256]{2,1,0:T(8,128)(2,1)S(1)}, bf16[2,256,256]{2,1,0:T(8,128)(2,1)S(1)}, u32[]{:S(2)}, u32[]{:S(2)}) collective-permute-start(bf16[2,256,256]{2,1,0:T(8,128)(2,1)S(1)} %shard_map.85.refs_10_), channel_id=1, source_target_pairs={{0,2},{1,3},{2,0},{3,1},{4,6},{5,7},{6,4},{7,5},{8,10},{9,11},{10,... | collective-permute-start | bytes 786440 | tf_op jit(solution)/shard_map/ppermute | solution.py:317
  31.1 2.3 %copy-start.1 = (f32[4,1,1,192,1536]{4,3,2,1,0:T(8,128)S(1)}, f32[4,1,1,192,1536]{4,3,2,1,0:T(8,128)}, u32[]{:S(2)}) copy-start(f32[4,1,1,192,1536]{4,3,2,1,0:T(8,128)} %param.8) | copy-start | bytes 14155780
  37.8 5.0 %collective-permute-start.9 = (bf16[2,2,256,256]{3,2,1,0:T(8,128)(2,1)S(1)}, bf16[2,2,256,256]{3,2,1,0:T(8,128)(2,1)S(1)}, u32[]{:S(2)}, u32[]{:S(2)}) collective-permute-start(bf16[2,2,256,256]{3,2,1,0:T(8,128)(2,1)S(1)} %pad_maximum_fusion), channel_id=1, source_target_pairs={{0,1},{1,0},{2,3},{3,2},{4,5},{5,4},{6,7},{7,6},{8,9},{9,8},{10,11... | collective-permute-start | bytes 1572872 | tf_op jit(solution)/shard_map/ppermute | solution.py:311
  37.9 4.9 %collective-permute-start.8 = (bf16[2,1,256,256]{3,2,1,0:T(8,128)(2,1)S(1)}, bf16[2,1,256,256]{3,2,1,0:T(8,128)(2,1)S(1)}, u32[]{:S(2)}, u32[]{:S(2)}) collective-permute-start(bf16[2,1,256,256]{3,2,1,0:T(8,128)(2,1)S(1)} %pad_maximum_fusion.3), channel_id=1, source_target_pairs={{0,1},{1,0},{2,3},{3,2},{4,5},{5,4},{6,7},{7,6},{8,9},{9,8},{10,11... | collective-permute-start | bytes 786440 | tf_op jit(solution)/shard_map/ppermute | solution.py:311
  38.5 8.0 %collective-permute-start.11 = (bf16[384,256]{1,0:T(8,128)(2,1)S(1)}, bf16[384,256]{1,0:T(8,128)(2,1)S(1)}, u32[]{:S(2)}, u32[]{:S(2)}) collective-permute-start(bf16[384,256]{1,0:T(8,128)(2,1)S(1)} %slice.92), channel_id=1, source_target_pairs={{0,8},{8,16},{16,24},{24,28},{28,20},{20,12},{12,4},{4,0},{1,9},{9... | collective-permute-start | bytes 589832 | tf_op jit(solution)/shard_map/ppermute | solution.py:69
  40.1 6.6 %collective-permute-start.12 = (bf16[384,256]{1,0:T(8,128)(2,1)S(1)}, bf16[384,256]{1,0:T(8,128)(2,1)S(1)}, u32[]{:S(2)}, u32[]{:S(2)}) collective-permute-start(bf16[384,256]{1,0:T(8,128)(2,1)S(1)} %slice.93), channel_id=1, source_target_pairs={{8,0},{16,8},{24,16},{28,24},{20,28},{12,20},{4,12},{0,4},{9,1},{1... | collective-permute-start | bytes 589832 | tf_op jit(solution)/shard_map/ppermute | solution.py:70
  41.2 5.2 %collective-permute-start.10 = (bf16[1,256,256]{2,1,0:T(8,128)(2,1)S(1)}, bf16[1,256,256]{2,1,0:T(8,128)(2,1)S(1)}, u32[]{:S(2)}, u32[]{:S(2)}) collective-permute-start(bf16[1,256,256]{2,1,0:T(8,128)(2,1)S(1)} %shard_map.88.refs_2_), channel_id=1, source_target_pairs={{0,2},{1,3},{2,0},{3,1},{4,6},{5,7},{6,4},{7,5},{8,10},{9,11},{10,... | collective-permute-start | bytes 393224 | tf_op jit(solution)/shard_map/ppermute | solution.py:317
  46.8 1.6 %collective-permute-start.13 = (bf16[2,1,256,256]{3,2,1,0:T(8,128)(2,1)S(1)}, bf16[2,1,256,256]{3,2,1,0:T(8,128)(2,1)S(1)}, u32[]{:S(2)}, u32[]{:S(2)}) collective-permute-start(bf16[2,1,256,256]{3,2,1,0:T(8,128)(2,1)S(1)} %pad_maximum_fusion.4), channel_id=1, source_target_pairs={{0,1},{1,0},{2,3},{3,2},{4,5},{5,4},{6,7},{7,6},{8,9},{9,8},{10,11... | collective-permute-start | bytes 786440 | tf_op jit(solution)/shard_map/ppermute | solution.py:311
  53.7 8.8 %copy-start.3 = (f32[1,1,1,192]{3,2,1,0:T(1,128)S(1)}, f32[1,1,1,192]{3,2,1,0:T(1,128)}, u32[]{:S(2)}) copy-start(f32[1,1,1,192]{3,2,1,0:T(1,128)} %param.9) | copy-start | bytes 2308
  53.7 1.8 %collective-permute-start.14 = (f32[2,192,256]{2,1,0:T(8,128)S(1)}, f32[2,192,256]{2,1,0:T(8,128)S(1)}, u32[]{:S(2)}, u32[]{:S(2)}) collective-permute-start(f32[2,192,256]{2,1,0:T(8,128)S(1)} %get-tuple-element.81), channel_id=1, source_target_pairs={{0,1},{1,0},{2,3},{3,2},{4,5},{5,4},{6,7},{7,6},{8,9},{9,8},{10,11... | collective-permute-start | bytes 1179656 | tf_op jit(solution)/shard_map/ppermute | solution.py:403
  55.6 7.0 %collective-permute-start.15 = (f32[192,256]{1,0:T(8,128)S(1)}, f32[192,256]{1,0:T(8,128)S(1)}, u32[]{:S(2)}, u32[]{:S(2)}) collective-permute-start(f32[192,256]{1,0:T(8,128)S(1)} %fusion.8), channel_id=1, source_target_pairs={{0,2},{1,3},{2,0},{3,1},{4,6},{5,7},{6,4},{7,5},{8,10},{9,11},{10,... | collective-permute-start | bytes 589832 | tf_op jit(solution)/shard_map/ppermute | solution.py:416
  62.7 6.2 %collective-permute-start.16 = (f32[192,256]{1,0:T(8,128)S(1)}, f32[192,256]{1,0:T(8,128)S(1)}, u32[]{:S(2)}, u32[]{:S(2)}) collective-permute-start(f32[192,256]{1,0:T(8,128)S(1)} %fusion.11.refs_0_.refs_5_), channel_id=1, source_target_pairs={{0,8},{8,16},{16,24},{24,28},{28,20},{20,12},{12,4},{4,0},{1,9},{9... | collective-permute-start | bytes 589832 | tf_op jit(solution)/shard_map/ppermute | solution.py:65
  64.3 6.1 %collective-permute-start.18 = (f32[192,256]{1,0:T(8,128)S(1)}, f32[192,256]{1,0:T(8,128)S(1)}, u32[]{:S(2)}, u32[]{:S(2)}) collective-permute-start(f32[192,256]{1,0:T(8,128)S(1)} %fusion.11.refs_0_.refs_5_), channel_id=1, source_target_pairs={{8,0},{16,8},{24,16},{28,24},{20,28},{12,20},{4,12},{0,4},{9,1},{1... | collective-permute-start | bytes 589832 | tf_op jit(solution)/shard_map/ppermute | solution.py:66
  64.8 6.1 %collective-permute-start.24 = (f32[192,256]{1,0:T(8,128)S(1)}, f32[192,256]{1,0:T(8,128)S(1)}, u32[]{:S(2)}, u32[]{:S(2)}) collective-permute-start(f32[192,256]{1,0:T(8,128)S(1)} %fusion.11.refs_0_.refs_5_), channel_id=1, source_target_pairs={{0,2},{1,3},{2,0},{3,1},{4,6},{5,7},{6,4},{7,5},{8,10},{9,11},{10,... | collective-permute-start | bytes 589832 | tf_op jit(solution)/shard_map/ppermute | solution.py:418
  68.8 5.8 %collective-permute-start.17 = (f32[192,256]{1,0:T(8,128)S(1)}, f32[192,256]{1,0:T(8,128)S(1)}, u32[]{:S(2)}, u32[]{:S(2)}) collective-permute-start(f32[192,256]{1,0:T(8,128)S(1)} %collective-permute-done.16.refs_1_), channel_id=1, source_target_pairs={{0,8},{8,16},{16,24},{24,28},{28,20},{20,12},{12,4},{4,0},{1,9},{9... | collective-permute-start | bytes 589832 | tf_op jit(solution)/shard_map/ppermute | solution.py:65
  70.4 5.8 %collective-permute-start.19 = (f32[192,256]{1,0:T(8,128)S(1)}, f32[192,256]{1,0:T(8,128)S(1)}, u32[]{:S(2)}, u32[]{:S(2)}) collective-permute-start(f32[192,256]{1,0:T(8,128)S(1)} %collective-permute-done.18.refs_2_), channel_id=1, source_target_pairs={{8,0},{16,8},{24,16},{28,24},{20,28},{12,20},{4,12},{0,4},{9,1},{1... | collective-permute-start | bytes 589832 | tf_op jit(solution)/shard_map/ppermute | solution.py:66
  70.9 16.0 %collective-permute-start.25 = (f32[2,192,256]{2,1,0:T(8,128)S(1)}, f32[2,192,256]{2,1,0:T(8,128)S(1)}, u32[]{:S(2)}, u32[]{:S(2)}) collective-permute-start(f32[2,192,256]{2,1,0:T(8,128)S(1)} %pad_maximum_fusion.2), channel_id=1, source_target_pairs={{0,1},{1,0},{2,3},{3,2},{4,5},{5,4},{6,7},{7,6},{8,9},{9,8},{10,11... | collective-permute-start | bytes 1179656 | tf_op jit(solution)/shard_map/ppermute | solution.py:419
  74.6 5.7 %collective-permute-start.20 = (f32[192,256]{1,0:T(8,128)S(1)}, f32[192,256]{1,0:T(8,128)S(1)}, u32[]{:S(2)}, u32[]{:S(2)}) collective-permute-start(f32[192,256]{1,0:T(8,128)S(1)} %collective-permute-done.17.refs_3_), channel_id=1, source_target_pairs={{0,8},{8,16},{16,24},{24,28},{28,20},{20,12},{12,4},{4,0},{1,9},{9... | collective-permute-start | bytes 589832 | tf_op jit(solution)/shard_map/ppermute | solution.py:65
  76.2 5.7 %collective-permute-start.22 = (f32[192,256]{1,0:T(8,128)S(1)}, f32[192,256]{1,0:T(8,128)S(1)}, u32[]{:S(2)}, u32[]{:S(2)}) collective-permute-start(f32[192,256]{1,0:T(8,128)S(1)} %collective-permute-done.19.refs_4_), channel_id=1, source_target_pairs={{8,0},{16,8},{24,16},{28,24},{20,28},{12,20},{4,12},{0,4},{9,1},{1... | collective-permute-start | bytes 589832 | tf_op jit(solution)/shard_map/ppermute | solution.py:66
  76.8 2.3 %copy-start.2 = (f32[768,1536]{1,0:T(8,128)S(1)}, f32[768,1536]{1,0:T(8,128)}, u32[]{:S(2)}) copy-start(f32[768,1536]{1,0:T(8,128)} %get-tuple-element.84.gram_ref) | copy-start | bytes 14155780
  81.9 5.0 %collective-permute-start.21 = (f32[96,256]{1,0:T(8,128)S(1)}, f32[96,256]{1,0:T(8,128)S(1)}, u32[]{:S(2)}, u32[]{:S(2)}) collective-permute-start(f32[96,256]{1,0:T(8,128)S(1)} %slice.98), channel_id=1, source_target_pairs={{0,8},{8,16},{16,24},{24,28},{28,20},{20,12},{12,4},{4,0},{1,9},{9... | collective-permute-start | bytes 294920 | tf_op jit(solution)/shard_map/ppermute | solution.py:69
  83.5 4.9 %collective-permute-start.23 = (f32[96,256]{1,0:T(8,128)S(1)}, f32[96,256]{1,0:T(8,128)S(1)}, u32[]{:S(2)}, u32[]{:S(2)}) collective-permute-start(f32[96,256]{1,0:T(8,128)S(1)} %slice.99), channel_id=1, source_target_pairs={{8,0},{16,8},{24,16},{28,24},{20,28},{12,20},{4,12},{0,4},{9,1},{1... | collective-permute-start | bytes 294920 | tf_op jit(solution)/shard_map/ppermute | solution.py:70
  90.4 3.8 %collective-permute-start.26 = (f32[2,192,256]{2,1,0:T(8,128)S(1)}, f32[2,192,256]{2,1,0:T(8,128)S(1)}, u32[]{:S(2)}, u32[]{:S(2)}) collective-permute-start(f32[2,192,256]{2,1,0:T(8,128)S(1)} %slice.84), channel_id=1, source_target_pairs={{0,1},{1,0},{2,3},{3,2},{4,5},{5,4},{6,7},{7,6},{8,9},{9,8},{10,11... | collective-permute-start | bytes 1179656 | tf_op jit(solution)/shard_map/ppermute | solution.py:458
  90.5 11.9 %all-to-all-start = ((f32[32,4,256]{2,1,0:T(4,128)}), f32[32,4,256]{2,1,0:T(4,128)S(1)}, u32[]{:S(2)}, u32[]{:S(2)}) async-start(f32[32,4,256]{2,1,0:T(4,128)} %get-tuple-element.96), calls=%async_computation | async-start | bytes 262144 | tf_op jit(solution)/shard_map/all_to_all | solution.py:457
  94.2 8.4 %collective-permute-start.27 = (f32[192,256]{1,0:T(8,128)S(1)}, f32[192,256]{1,0:T(8,128)S(1)}, u32[]{:S(2)}, u32[]{:S(2)}) collective-permute-start(f32[192,256]{1,0:T(8,128)S(1)} %fusion.7), channel_id=1, source_target_pairs={{0,2},{1,3},{2,0},{3,1},{4,6},{5,7},{6,4},{7,5},{8,10},{9,11},{10,... | collective-permute-start | bytes 589832 | tf_op jit(solution)/shard_map/ppermute | solution.py:459
  (1 other events, 0.9 us)

commit v6 on v5

--- a/solution.py
+++ b/solution.py
@@ -1,4 +1,5 @@
 import functools
+import math
 
 import jax
 import jax.numpy as jnp
@@ -13,8 +14,8 @@
 VMEM = pl.BlockSpec(memory_space=pltpu.VMEM)
 HBM = pl.BlockSpec(memory_space=pltpu.HBM)
 EARLY_BYTES = 12 * 2**20
-GRAM_BYTES = 24 * 2**20
-IMAGE_BYTES = 20 * 2**20
+GRAM_BYTES = 10 * 2**20
+IMAGE_BYTES = 10 * 2**20
 
 
 def swap(count, bit):
@@ -59,16 +60,13 @@
                 self.trow[position, index] = other_trow
                 self.data[position, index] = other_data
 
-    def steps(self, value, split_rows):
-        ahead = back = value
-        for _ in range(1, self.far):
-            ahead = lax.ppermute(ahead, ("dp", "trow"), self.ahead)
-            back = lax.ppermute(back, ("dp", "trow"), self.back)
-            yield ahead, back
-        half = (split_rows // 2 + 15) // 16 * 16
-        low = lax.ppermute(ahead[:half], ("dp", "trow"), self.ahead)
-        high = lax.ppermute(back[half:split_rows], ("dp", "trow"), self.back)
-        yield low, high
+    def move(self, ahead, back):
+        axes = ("dp", "trow")
+        return [lax.ppermute(ahead, axes, self.ahead), lax.ppermute(back, axes, self.back)]
+
+    def last(self, ahead, back, rows):
+        half = (rows // 2 + 15) // 16 * 16
+        return self.move(ahead[:half], back[half:rows])
 
 
 ORDER = (1, 3, 0, 2)
@@ -88,47 +86,47 @@
     return dot(a_high, b_high, NN) + (dot(a_high, b_low, NN) + dot(a_low, b_high, NN))
 
 
-def tile_copies(whole_ref, tile_ref, me, piece, block, semaphores, outward=False):
+def tile_copies(whole_ref, tile_ref, me, piece, block, semaphores):
     copies = []
     for start in range(0, tile_ref.shape[1], block):
         lanes = pl.ds(start, block)
         for index, j in enumerate(ORDER):
             place = pl.ds(pl.multiple_of(jnp.bitwise_xor(me, j) * piece, 8), piece)
             pair = whole_ref.at[place, lanes], tile_ref.at[pl.ds(index * piece, piece), lanes]
-            if outward:
-                pair = pair[::-1]
             copies.append(pltpu.make_async_copy(*pair, semaphores.at[len(copies)]))
     return copies
 
 
 def fetch_kernel(sizes, meta, gram_ref, tile_ref, come):
-    piece, block = sizes
-    loads = tile_copies(gram_ref, tile_ref, meta[0], piece, block, come)
+    loads = tile_copies(gram_ref, tile_ref, meta[0], *sizes, come)
     for load in loads:
         load.start()
     for load in loads:
         load.wait()
 
 
+def pick_rows(out_ref, head_ref, feature_ref, data_place, data_count, piece):
+    head_part = head_ref.shape[0]
+    out_ref[:head_part, :] = head_ref[...]
+    if piece % 16 == 0:
+        out_ref[head_part:, :] = feature_ref[pl.ds(pl.multiple_of(data_place * piece, 16), piece), :]
+    else:
+        for data in range(data_count):
+
+            @pl.when(data_place == data)
+            def _():
+                out_ref[head_part:, :] = feature_ref[data * piece : (data + 1) * piece, :]
+
+
 def pick_kernel(sizes, meta, *refs):
     turns, choices, width, piece, data_count = sizes
     *shard_refs, out_ref = refs
-    head_part = shard_refs[0].shape[0] - width
     for index, turn in enumerate(turns):
         for shard_ref, choice in zip(shard_refs, choices):
 
             @pl.when(meta[turn] == choice)
             def _():
-                out_ref[index, :head_part, :] = shard_ref[width:, :]
-                if piece % 16 == 0:
-                    place = pl.ds(pl.multiple_of(meta[data_count] * piece, 16), piece)
-                    out_ref[index, head_part:, :] = shard_ref[place, :]
-                else:
-                    for data in range(data_count):
-
-                        @pl.when(meta[data_count] == data)
-                        def _():
-                            out_ref[index, head_part:, :] = shard_ref[data * piece : (data + 1) * piece, :]
+                pick_rows(out_ref.at[index], shard_ref.at[width:], shard_ref, meta[data_count], data_count, piece)
 
 
 def place_rows(round_refs, me, head_part, rows, target, turn, count):
@@ -148,7 +146,7 @@
     n, width, head_part, block, groups = sizes
     shard_refs, refs = refs[: n - 1], refs[n - 1 :]
     round_refs, refs = refs[: 3 * groups], refs[3 * groups :]
-    prior_ref, tile_ref, columns, rows, target = refs
+    prior_ref, tile_ref, side_ref, columns, rows, target = refs
     count = shard_refs[0].shape[1]
     for index in range(n - 1):
         lanes = pl.ds(pl.multiple_of(meta[index] * count, 128), count)
@@ -159,46 +157,73 @@
     scale = 1.0 / columns.shape[1]
     for start in range(0, columns.shape[0], block):
         lanes = slice(start, start + block)
-        tile_ref[:, lanes] = prior_ref[:, lanes] + dot(rows[:, :done], columns[lanes, :done], NT) * scale
-
-
-def gram_kernel(sizes, meta, *refs):
-    n, tcol_count, piece, width, head_part, block = sizes
+        column = columns[lanes, :done]
+        tile_ref[:, lanes] = prior_ref[:, lanes] + dot(rows[:, :done], column, NT) * scale
+        side_ref[lanes, :] = dot(column, target[:, :done], NT)
+
+
+def tile_rows_of(first, early_ref, last_rows, last_columns, block, scale, tile_ref, gram_ref, me, piece, stored):
+    part = pl.ds(first * piece, tile_ref.shape[0])
+    copies = []
+    for start in range(0, tile_ref.shape[1], block):
+        lanes = pl.ds(start, block)
+        tile_ref[:, lanes] = early_ref[part, lanes] + dot(last_rows[part, :], last_columns[lanes, :], NT) * scale
+        copies += store_rows(tile_ref, gram_ref, me, first, piece, lanes, stored)
+    return copies
+
+
+def store_rows(tile_ref, gram_ref, me, first, piece, lanes, stored):
+    copies = []
+    for index in range(tile_ref.shape[0] // piece):
+        place = pl.ds(pl.multiple_of(jnp.bitwise_xor(me, ORDER[first + index]) * piece, 8), piece)
+        part = tile_ref.at[pl.ds(index * piece, piece), lanes]
+        at = lanes.start // lanes.size * 2 + index
+        copies.append(pltpu.make_async_copy(part, gram_ref.at[place, lanes], stored.at[at]))
+        copies[-1].start()
+    return copies
+
+
+def send_kernel(sizes, meta, *refs):
+    n, piece, width, head_part, block = sizes
     low_ref, high_ref, *round_refs = refs[:5]
-    early_ref, columns, rows, target, gram_ref, tile_ref, right_ref, side_high, side_low, image_ref = refs[5:15]
-    last_columns, last_rows, last_target, sent = refs[15:]
-    me = meta[2 * n]
-    total_rows = columns.shape[1]
-    count = last_rows.shape[1]
-    done = total_rows - count
-    last_columns[...] = columns[:, done:]
+    early_ref, early_side, columns, sent_ref, gram_ref = refs[5:10]
+    side_high, side_low, last_columns, last_rows, last_target, tile_ref, stored = refs[10:]
+    total_rows, count = columns.shape[1], last_rows.shape[1]
+    last_columns[...] = columns[:, total_rows - count :]
     base = pl.multiple_of(meta[2 * n - 1] * width, 16)
     half = low_ref.shape[0]
     last_columns[pl.ds(base, half), :] = low_ref[...]
     last_columns[pl.ds(pl.multiple_of(base + half, 16), width - half), :] = high_ref[...]
-    place_rows(round_refs, me, head_part, last_rows, last_target, 0, count)
+    place_rows(round_refs, meta[2 * n], head_part, last_rows, last_target, 0, count)
     scale = 1.0 / total_rows
-    stores = tile_copies(gram_ref, tile_ref, me, piece, block, sent, outward=True)
-    for step in range(columns.shape[0] // block):
-        lanes = slice(step * block, (step + 1) * block)
-        last = last_columns[lanes, :]
-        tile_ref[:, lanes] = early_ref[:, lanes] + dot(last_rows[...], last, NT) * scale
-        for index in range(step * tcol_count, (step + 1) * tcol_count):
-            stores[index].start()
-        side = dot(columns[lanes, :done], target[:, :done], NT) + dot(last, last_target[...], NT)
-        side_high[lanes, :], side_low[lanes, :] = split(side * scale)
+    copies = tile_rows_of(
+        0, early_ref, last_rows, last_columns, block, scale, tile_ref, gram_ref, meta[2 * n], piece, stored
+    )
+    side = early_side[...] + dot(last_columns[...], last_target[...], NT)
+    side_high[...], side_low[...] = split(side * scale)
+    value = product(split(tile_ref[...]), (side_high[...], side_low[...]))
+    sent_ref[...] = value.reshape(sent_ref.shape)
+    for copy in copies:
+        copy.wait()
+
+
+def kept_kernel(sizes, meta, *refs):
+    piece, block = sizes
+    early_ref, last_columns, last_rows, side_high, side_low, last_target, rows, target = refs[:8]
+    _, gram_ref, right_ref, image_ref, tile_ref, stored = refs[8:]
+    total_rows, count = rows.shape[1], last_rows.shape[1]
+    done = total_rows - count
+    scale = 1.0 / total_rows
+    copies = tile_rows_of(
+        2, early_ref, last_rows, last_columns, block, scale, tile_ref, gram_ref, meta[0], piece, stored
+    )
     own = slice(2 * piece, 3 * piece)
     right = dot(rows[own, :done], target[:, :done], NT) + dot(last_rows[own, :], last_target[...], NT)
     right_ref[...] = right * scale
-    value = product(split(tile_ref[: 2 * piece, :]), (side_high[...], side_low[...]))
+    value = product(split(tile_ref[...]), (side_high[...], side_low[...]))
     image_ref[...] = value.reshape(image_ref.shape)
-    for store in stores:
-        store.wait()
-
-
-def kept_kernel(sizes, meta, tile_ref, side_high, side_low, image_ref):
-    value = product(split(tile_ref[2 * sizes :, :]), (side_high[...], side_low[...]))
-    image_ref[...] = value.reshape(image_ref.shape)
+    for copy in copies:
+        copy.wait()
 
 
 def partial_kernel(sizes, meta, *refs):
@@ -241,7 +266,7 @@
     sums_ref[...] = jnp.broadcast_to(sums[None], sums_ref.shape)
 
 
-def call(body, meta, inputs, in_specs, out_specs, out_shape, scratch, vmem, flops, read):
+def call(body, meta, inputs, in_specs, out_specs, out_shape, scratch, vmem, flops, read, aliases={}):
     return pl.pallas_call(
         body,
         grid_spec=pltpu.PrefetchScalarGridSpec(
@@ -252,6 +277,7 @@
             scratch_shapes=scratch,
         ),
         out_shape=out_shape,
+        input_output_aliases=aliases,
         compiler_params=pltpu.CompilerParams(vmem_limit_bytes=vmem),
         cost_estimate=pl.CostEstimate(flops=flops, bytes_accessed=read, transcendentals=0),
     )(meta, *inputs)
@@ -281,14 +307,15 @@
     gram_meta = jnp.concatenate([lookup[data_count : data_count + 2 * n], me_meta])
     image_meta = jnp.concatenate([lookup[data_count + 2 * n :], me_meta])
 
-    own = embeddings.reshape(row_count, width).T
+    f32, bf16 = jnp.float32, jnp.bfloat16
+    features = embeddings.reshape(row_count, width).T
     head_rows = lax.dynamic_slice_in_dim(targets, me * head_part, head_part, axis=1).T
-    payload = jnp.concatenate([own, head_rows], axis=0)
+    payload = jnp.concatenate([features, head_rows], axis=0)
 
     def pieces_of(turns):
         if turns == [0]:
-            features = lax.dynamic_slice_in_dim(own, data_place * piece, piece, axis=0)
-            return jnp.concatenate([head_rows, features], axis=0)[None]
+            own_rows = lax.dynamic_slice_in_dim(features, data_place * piece, piece, axis=0)
+            return jnp.concatenate([head_rows, own_rows], axis=0)[None]
         choices = sorted(set(ring.rounds[:, turns].ravel().tolist()))
         return call(
             functools.partial(pick_kernel, (turns, choices, width, piece, data_count)),
@@ -316,8 +343,8 @@
                 mine = pieces_of(turns)
                 waiting.append((group, mine, lax.ppermute(mine, "tcol", swap(tcol_count, 2))))
 
-    block = 384 if tile_columns % 384 == 0 else 128
-    f32, bf16 = jnp.float32, jnp.bfloat16
+    block = next(size for size in (512, 256, 128) if tile_columns % size == 0)
+    far_block = math.lcm(piece, 128)
     tile_semaphores = pltpu.SemaphoreType.DMA((tcol_count * (tile_columns // block),))
 
     def fetch(whole):
@@ -336,8 +363,12 @@
 
     prior = gram_prior.reshape(tile_rows, tile_columns)
     open_groups(0)
-    for step, arrived in enumerate(ring.steps(payload, width), 1):
-        arrived = list(arrived)
+    ahead = back = payload
+    for step in range(1, ring.far + 1):
+        if step < ring.far:
+            arrived = ahead, back = ring.move(ahead, back)
+        else:
+            arrived = ring.last(ahead, back, width)
         if step == 1:
             gram_meta, image_meta, pick_meta, *arrived = lax.optimization_barrier(
                 (gram_meta, image_meta, pick_meta, *arrived)
@@ -357,14 +388,15 @@
         gathered += arrived
         open_groups(step)
         if step == ring.far - 1:
-            early, columns, rows, target = call(
+            early, early_side, columns, rows, target = call(
                 functools.partial(early_kernel, (n, width, head_part, block, 2)),
                 gram_meta,
                 [*gathered, *groups[0], *groups[1], prior],
                 [VMEM] * (n + 6),
-                [VMEM] * 4,
+                [VMEM] * 5,
                 [
                     jax.ShapeDtypeStruct((tile_rows, tile_columns), f32),
+                    jax.ShapeDtypeStruct((tile_columns, heads), f32),
                     jax.ShapeDtypeStruct((tile_columns, total_rows), bf16),
                     jax.ShapeDtypeStruct((tile_rows, total_rows), bf16),
                     jax.ShapeDtypeStruct((heads, total_rows), bf16),
@@ -374,51 +406,56 @@
                 2 * tile_rows * tile_columns * (total_rows - row_count),
                 8 * tile_rows * tile_columns,
             )
-    half_rows = (2, piece, heads)
-    gram, gram_tile, start, side_high, side_low, sent = call(
-        functools.partial(gram_kernel, (n, tcol_count, piece, width, head_part, block)),
+    sent, gram, side_high, side_low, last_columns, last_rows, last_target = call(
+        functools.partial(send_kernel, (n, piece, width, head_part, block)),
         gram_meta,
-        [*gathered[-2:], *groups[2], early, columns, rows, target],
-        [VMEM] * 9,
-        [HBM] + [VMEM] * 5,
+        [*gathered[-2:], *groups[2], early, early_side, columns],
+        [VMEM] * 8,
+        [VMEM, HBM] + [VMEM] * 5,
+        [
+            jax.ShapeDtypeStruct((2, piece, heads), f32),
+            jax.ShapeDtypeStruct((tile_rows, tile_columns), f32),
+            jax.ShapeDtypeStruct((tile_columns, heads), bf16),
+            jax.ShapeDtypeStruct((tile_columns, heads), bf16),
+            jax.ShapeDtypeStruct((tile_columns, row_count), bf16),
+            jax.ShapeDtypeStruct((tile_rows, row_count), bf16),
+            jax.ShapeDtypeStruct((heads, row_count), bf16),
+        ],
+        [pltpu.VMEM((2 * piece, tile_columns), f32), pltpu.SemaphoreType.DMA((2 * (tile_columns // block),))],
+        GRAM_BYTES,
+        tile_rows * tile_columns * (row_count + 3 * heads),
+        4 * tile_rows * tile_columns,
+    )
+    penalty_rows = penalty.reshape(piece, 1)
+    received = lax.ppermute(sent, "tcol", swap(tcol_count, 1))
+    gram, start, kept = call(
+        functools.partial(kept_kernel, (piece, block)),
+        me_meta,
+        [early, last_columns, last_rows, side_high, side_low, last_target, rows, target, gram],
+        [VMEM] * 8 + [HBM],
+        [HBM, VMEM, VMEM],
         [
             jax.ShapeDtypeStruct((tile_rows, tile_columns), f32),
-            jax.ShapeDtypeStruct((tile_rows, tile_columns), f32),
             jax.ShapeDtypeStruct((piece, heads), f32),
-            jax.ShapeDtypeStruct((tile_columns, heads), bf16),
-            jax.ShapeDtypeStruct((tile_columns, heads), bf16),
-            jax.ShapeDtypeStruct(half_rows, f32),
+            jax.ShapeDtypeStruct((2, piece, heads), f32),
         ],
-        [
-            pltpu.VMEM((tile_columns, row_count), bf16),
-            pltpu.VMEM((tile_rows, row_count), bf16),
-            pltpu.VMEM((heads, row_count), bf16),
-            tile_semaphores,
-        ],
+        [pltpu.VMEM((2 * piece, tile_columns), f32), pltpu.SemaphoreType.DMA((2 * (tile_columns // block),))],
         GRAM_BYTES,
-        2 * tile_rows * tile_columns * (row_count + 2 * heads),
-        12 * tile_rows * tile_columns,
-    )
-    penalty_rows = penalty.reshape(piece, 1)
-    received = lax.ppermute(sent, "tcol", swap(tcol_count, 1))
-    kept = call(
-        functools.partial(kept_kernel, piece),
-        me_meta,
-        [gram_tile, side_high, side_low],
-        [VMEM] * 3,
-        VMEM,
-        jax.ShapeDtypeStruct(half_rows, f32),
-        [],
-        IMAGE_BYTES,
-        3 * tile_rows * tile_columns * heads,
-        2 * tile_rows * tile_columns,
+        tile_rows * tile_columns * (row_count + 3 * heads),
+        6 * tile_rows * tile_columns,
+        {9: 0},
     )
     image = kept[0] + received[0] + lax.ppermute(kept[1] + received[1], "tcol", swap(tcol_count, 2))
     image = image + penalty_rows * start
     far_image = lax.ppermute(image, "tcol", swap(tcol_count, 2))
     near_images = lax.ppermute(jnp.stack([image, far_image]), "tcol", swap(tcol_count, 1))
     images = [image]
-    for step, arrived in enumerate(ring.steps(image, piece), 1):
+    ahead = back = image
+    for step in range(1, ring.far + 1):
+        if step < ring.far:
+            arrived = ahead, back = ring.move(ahead, back)
+        else:
+            arrived = ring.last(ahead, back, piece)
         if step == ring.far - 2:
             *arrived, gram = lax.optimization_barrier((*arrived, gram))
             tile = fetch(gram)
@@ -439,7 +476,7 @@
     )
     axes = ("dp", "trow", "tcol")
     second, sums = call(
-        functools.partial(image_kernel, (n, data_count, piece, block)),
+        functools.partial(image_kernel, (n, data_count, piece, far_block)),
         image_meta,
         [*images[-2:], total, tile, early_sums, image, near_images, far_image, penalty_rows],
         [VMEM] * 9,
@@ -448,10 +485,10 @@
             jax.ShapeDtypeStruct((tcol_count, piece, heads), f32),
             jax.ShapeDtypeStruct((n * tcol_count, 4, heads), f32),
         ],
-        [pltpu.VMEM((block, heads), f32)],
+        [pltpu.VMEM((far_block, heads), f32)],
         IMAGE_BYTES,
-        6 * tile_rows * block * heads,
-        4 * tile_rows * block,
+        6 * tile_rows * far_block * heads,
+        4 * tile_rows * far_block,
     )
     sums, second = lax.optimization_barrier((sums, second))
     sums = lax.all_to_all(sums, axes, split_axis=0, concat_axis=0, tiled=True)

time: 104 us -> 103 us (level)
  waiting for transfers between devices: 39.7 us -> 38.6 us
  transfers between devices with their start and end apart: 29 -> 29, of which waited for: 15 -> 13; matrix products, arithmetic and copies ran while one was open for 3% -> 3% of each run, Pallas kernels for 9% -> 11%
where the time goes in v6:
time: 103 us; the launch traced here: 102 us
  waiting for transfers between devices  38.6 us (37%)
  starting transfers between devices  32.4 us (31%)
  Pallas kernels  16.6 us (16%)
  local copies, waits for them, and re-layouts  10.3 us (10%)
  between operations  2.9 us (3%)
  other arithmetic  1.38 us (1%)
    ppermute x8, waiting for transfers between devices, move(): lax.ppermute(ahead, axes, self.ahead)  22.2 us
    pallas_call x9, Pallas kernels, call(): pl.pallas_call(body, grid_spec=pltpu.PrefetchScalarGridSpec(num_scalar_pr...  16.6 us
    ppermute x8, starting transfers between devices, move(): lax.ppermute(ahead, axes, self.ahead)  14.4 us
    unnamed x10, local copies, waits for them, and re-layouts  6.83 us
    all_to_all x1, waiting for transfers between devices, shards(): sums = lax.all_to_all(sums, axes, split_axis=0, concat_axis=0, tiled=True)  6.35 us
    ppermute x1, waiting for transfers between devices, shards(): lax.ppermute(kept[1] + received[1], 'tcol', swap(tcol_count, 2))  5.68 us
    ppermute x3, starting transfers between devices, open_groups(): lax.ppermute(mine, 'tcol', swap(tcol_count, 2))  5.01 us
    all_to_all x1, starting transfers between devices, shards(): sums = lax.all_to_all(sums, axes, split_axis=0, concat_axis=0, tiled=True)  3.74 us
  transfers between devices with their start and end apart: 29, of which 13 were waited for; matrix products, arithmetic and copies ran while one was open for 3% of the time, Pallas kernels for 11%

profile of v6, /device:TPU:0, one launch (start us, length us, event | category | flops | bytes accessed | tf_op | source)
XLA Modules:
  0.0 102.1 jit_solution(6533183209355525935)
XLA Ops:
  2.9 3.1 %collective-permute-start = (bf16[832,256]{1,0:T(8,128)(2,1)S(1)}, bf16[832,256]{1,0:T(8,128)(2,1)S(1)}, u32[]{:S(2)}, u32[]{:S(2)}) collective-permute-start(bf16[832,256]{1,0:T(8,128)(2,1)S(1)} %pad_maximum_fusion.1.refs_0_), channel_id=1, source_target_pairs={{0,8},{8,16},{16,24},{24,28},{28,20},{20,12},{12,4},{4,0},{1,9},{9... | collective-permute-start | bytes 1277960 | tf_op jit(solution)/shard_map/ppermute | solution.py:65
  7.2 2.0 %collective-permute-start.2 = (bf16[1,256,256]{2,1,0:T(8,128)(2,1)S(1)}, bf16[1,256,256]{2,1,0:T(8,128)(2,1)S(1)}, u32[]{:S(2)}, u32[]{:S(2)}) collective-permute-start(bf16[1,256,256]{2,1,0:T(8,128)(2,1)S(1)} %maximum_bitcast_fusion.refs_7_), channel_id=1, source_target_pairs={{0,2},{1,3},{2,0},{3,1},{4,6},{5,7},{6,4},{7,5},{8,10},{9,11},{10,... | collective-permute-start | bytes 393224 | tf_op jit(solution)/shard_map/ppermute | solution.py:344
  13.1 2.7 %collective-permute-done.refs_0_.refs_1_ = bf16[832,256]{1,0:T(8,128)(2,1)S(1)} collective-permute-done((bf16[832,256]{1,0:T(8,128)(2,1)S(1)}, bf16[832,256]{1,0:T(8,128)(2,1)S(1)}, u32[]{:S(2)}, u32[]{:S(2)}) %collective-permute-start) | collective-permute-done | bytes 426016 | tf_op jit(solution)/shard_map/ppermute | solution.py:65
  15.8 1.8 %collective-permute-start.3 = (bf16[832,256]{1,0:T(8,128)(2,1)S(1)}, bf16[832,256]{1,0:T(8,128)(2,1)S(1)}, u32[]{:S(2)}, u32[]{:S(2)}) collective-permute-start(bf16[832,256]{1,0:T(8,128)(2,1)S(1)} %collective-permute-done.refs_0_.refs_1_), channel_id=1, source_target_pairs={{0,8},{8,16},{16,24},{24,28},{28,20},{20,12},{12,4},{4,0},{1,9},{9... | collective-permute-start | bytes 1277960 | tf_op jit(solution)/shard_map/ppermute | solution.py:65
  17.9 8.9 %collective-permute-done.3.refs_2_.refs_3_ = bf16[832,256]{1,0:T(8,128)(2,1)S(1)} collective-permute-done((bf16[832,256]{1,0:T(8,128)(2,1)S(1)}, bf16[832,256]{1,0:T(8,128)(2,1)S(1)}, u32[]{:S(2)}, u32[]{:S(2)}) %collective-permute-start.3) | collective-permute-done | bytes 426016 | tf_op jit(solution)/shard_map/ppermute | solution.py:65
  26.8 1.5 %collective-permute-start.6 = (bf16[832,256]{1,0:T(8,128)(2,1)S(1)}, bf16[832,256]{1,0:T(8,128)(2,1)S(1)}, u32[]{:S(2)}, u32[]{:S(2)}) collective-permute-start(bf16[832,256]{1,0:T(8,128)(2,1)S(1)} %collective-permute-done.3.refs_2_.refs_3_), channel_id=1, source_target_pairs={{0,8},{8,16},{16,24},{24,28},{28,20},{20,12},{12,4},{4,0},{1,9},{9... | collective-permute-start | bytes 1277960 | tf_op jit(solution)/shard_map/ppermute | solution.py:65
  29.6 1.5 %collective-permute-start.5 = (bf16[2,256,256]{2,1,0:T(8,128)(2,1)S(1)}, bf16[2,256,256]{2,1,0:T(8,128)(2,1)S(1)}, u32[]{:S(2)}, u32[]{:S(2)}) collective-permute-start(bf16[2,256,256]{2,1,0:T(8,128)(2,1)S(1)} %shard_map.85.refs_10_), channel_id=1, source_target_pairs={{0,2},{1,3},{2,0},{3,1},{4,6},{5,7},{6,4},{7,5},{8,10},{9,11},{10,... | collective-permute-start | bytes 786440 | tf_op jit(solution)/shard_map/ppermute | solution.py:344
  31.1 2.3 %copy-done.2 = f32[4,1,1,192,1536]{4,3,2,1,0:T(8,128)S(1)} copy-done((f32[4,1,1,192,1536]{4,3,2,1,0:T(8,128)S(1)}, f32[4,1,1,192,1536]{4,3,2,1,0:T(8,128)}, u32[]{:S(2)}) %copy-start.2) | copy-done | bytes 4718616
  33.9 2.9 %collective-permute-done.6.refs_5_.refs_2_ = bf16[832,256]{1,0:T(8,128)(2,1)S(1)} collective-permute-done((bf16[832,256]{1,0:T(8,128)(2,1)S(1)}, bf16[832,256]{1,0:T(8,128)(2,1)S(1)}, u32[]{:S(2)}, u32[]{:S(2)}) %collective-permute-start.6) | collective-permute-done | bytes 426016 | tf_op jit(solution)/shard_map/ppermute | solution.py:65
  38.5 1.6 %collective-permute-start.11 = (bf16[384,256]{1,0:T(8,128)(2,1)S(1)}, bf16[384,256]{1,0:T(8,128)(2,1)S(1)}, u32[]{:S(2)}, u32[]{:S(2)}) collective-permute-start(bf16[384,256]{1,0:T(8,128)(2,1)S(1)} %slice.92), channel_id=1, source_target_pairs={{0,8},{8,16},{16,24},{24,28},{28,20},{20,12},{12,4},{4,0},{1,9},{9... | collective-permute-start | bytes 589832 | tf_op jit(solution)/shard_map/ppermute | solution.py:65
  41.2 1.6 %collective-permute-start.10 = (bf16[1,256,256]{2,1,0:T(8,128)(2,1)S(1)}, bf16[1,256,256]{2,1,0:T(8,128)(2,1)S(1)}, u32[]{:S(2)}, u32[]{:S(2)}) collective-permute-start(bf16[1,256,256]{2,1,0:T(8,128)(2,1)S(1)} %shard_map.88.refs_2_), channel_id=1, source_target_pairs={{0,2},{1,3},{2,0},{3,1},{4,6},{5,7},{6,4},{7,5},{8,10},{9,11},{10,... | collective-permute-start | bytes 393224 | tf_op jit(solution)/shard_map/ppermute | solution.py:344
  42.8 3.7 %shard_map.87 = (f32[768,1536]{1,0:T(8,128)S(1)}, f32[1536,256]{1,0:T(8,128)S(1)}, bf16[1536,1024]{1,0:T(8,128)(2,1)S(1)}, bf16[768,1024]{1,0:T(8,128)(2,1)S(1)}, bf16[256,1024]{1,0:T(8,128)(2,1)S(1)}) custom-call(s32[17]{0:T(128)S(1)} %get-tuple-element.56.meta, bf16[832,256]{1,0:T(8,128)(2,1)S(1)} %pad_maximum_fusion.1.refs_0_, ...), custom_call_target="tpu_custom_call" | custom-call | flops 1811939328 | bytes 9437184 | tf_op jit(solution)/shard_map/pallas_call | solution.py:270
  46.8 1.5 %collective-permute-done.13.refs_4_ = bf16[2,1,256,256]{3,2,1,0:T(8,128)(2,1)S(1)} collective-permute-done((bf16[2,1,256,256]{3,2,1,0:T(8,128)(2,1)S(1)}, bf16[2,1,256,256]{3,2,1,0:T(8,128)(2,1)S(1)}, u32[]{:S(2)}, u32[]{:S(2)}) %collective-permute-start.13) | collective-permute-done | bytes 262176 | tf_op jit(solution)/shard_map/ppermute | solution.py:338
  48.4 3.4 %shard_map.89 = (f32[2,192,256]{2,1,0:T(8,128)S(1)}, f32[768,1536]{1,0:T(8,128)}, bf16[1536,256]{1,0:T(8,128)(2,1)S(1)}, bf16[1536,256]{1,0:T(8,128)(2,1)S(1)}, ...) custom-call(s32[17]{0:T(128)S(1)} %get-tuple-element.56.meta, ...), custom_call_target="tpu_custom_call" | custom-call | flops 1207959552 | bytes 4718592 | tf_op jit(solution)/shard_map/pallas_call | solution.py:270
  52.0 2.5 %shard_map.90 = (f32[768,1536]{1,0:T(8,128)}, f32[192,256]{1,0:T(8,128)S(1)}, f32[2,192,256]{2,1,0:T(8,128)S(1)}) custom-call(s32[1]{0:T(128)} %bitcast.meta, f32[768,1536]{1,0:T(8,128)S(1)} %get-tuple-element.75.refs_5_.refs_0_, bf16[1536,256]{1,0:T(8,128)(2,1)S(1)} %get-tuple-element.82.refs_1_, ...), custom_call_target="tpu_custom_call", output_to_operand_aliasing={{0}: (9, {})} | custom-call | flops 1207959552 | bytes 7077888 | tf_op jit(solution)/shard_map/pallas_call | solution.py:270
  54.5 1.6 %collective-permute-start.15 = (f32[192,256]{1,0:T(8,128)S(1)}, f32[192,256]{1,0:T(8,128)S(1)}, u32[]{:S(2)}, u32[]{:S(2)}) collective-permute-start(f32[192,256]{1,0:T(8,128)S(1)} %fusion.8), channel_id=1, source_target_pairs={{0,2},{1,3},{2,0},{3,1},{4,6},{5,7},{6,4},{7,5},{8,10},{9,11},{10,... | collective-permute-start | bytes 589832 | tf_op jit(solution)/shard_map/ppermute | solution.py:448
  56.1 5.7 %collective-permute-done.15 = f32[192,256]{1,0:T(8,128)S(1)} collective-permute-done((f32[192,256]{1,0:T(8,128)S(1)}, f32[192,256]{1,0:T(8,128)S(1)}, u32[]{:S(2)}, u32[]{:S(2)}) %collective-permute-start.15) | collective-permute-done | bytes 196640 | tf_op jit(solution)/shard_map/ppermute | solution.py:448
  61.9 1.6 %collective-permute-start.16 = (f32[192,256]{1,0:T(8,128)S(1)}, f32[192,256]{1,0:T(8,128)S(1)}, u32[]{:S(2)}, u32[]{:S(2)}) collective-permute-start(f32[192,256]{1,0:T(8,128)S(1)} %fusion.11.refs_0_.refs_5_), channel_id=1, source_target_pairs={{0,8},{8,16},{16,24},{24,28},{28,20},{20,12},{12,4},{4,0},{1,9},{9... | collective-permute-start | bytes 589832 | tf_op jit(solution)/shard_map/ppermute | solution.py:65
  64.0 1.5 %collective-permute-start.24 = (f32[192,256]{1,0:T(8,128)S(1)}, f32[192,256]{1,0:T(8,128)S(1)}, u32[]{:S(2)}, u32[]{:S(2)}) collective-permute-start(f32[192,256]{1,0:T(8,128)S(1)} %fusion.11.refs_0_.refs_5_), channel_id=1, source_target_pairs={{0,2},{1,3},{2,0},{3,1},{4,6},{5,7},{6,4},{7,5},{8,10},{9,11},{10,... | collective-permute-start | bytes 589832 | tf_op jit(solution)/shard_map/ppermute | solution.py:450
  65.5 2.8 %collective-permute-done.16.refs_1_ = f32[192,256]{1,0:T(8,128)S(1)} collective-permute-done((f32[192,256]{1,0:T(8,128)S(1)}, f32[192,256]{1,0:T(8,128)S(1)}, u32[]{:S(2)}, u32[]{:S(2)}) %collective-permute-start.16) | collective-permute-done | bytes 196640 | tf_op jit(solution)/shard_map/ppermute | solution.py:65
  68.3 1.6 %collective-permute-start.17 = (f32[192,256]{1,0:T(8,128)S(1)}, f32[192,256]{1,0:T(8,128)S(1)}, u32[]{:S(2)}, u32[]{:S(2)}) collective-permute-start(f32[192,256]{1,0:T(8,128)S(1)} %collective-permute-done.16.refs_1_), channel_id=1, source_target_pairs={{0,8},{8,16},{16,24},{24,28},{28,20},{20,12},{12,4},{4,0},{1,9},{9... | collective-permute-start | bytes 589832 | tf_op jit(solution)/shard_map/ppermute | solution.py:65
  70.4 3.5 %collective-permute-done.17.refs_3_ = f32[192,256]{1,0:T(8,128)S(1)} collective-permute-done((f32[192,256]{1,0:T(8,128)S(1)}, f32[192,256]{1,0:T(8,128)S(1)}, u32[]{:S(2)}, u32[]{:S(2)}) %collective-permute-start.17) | collective-permute-done | bytes 196640 | tf_op jit(solution)/shard_map/ppermute | solution.py:65
  74.0 1.6 %collective-permute-start.20 = (f32[192,256]{1,0:T(8,128)S(1)}, f32[192,256]{1,0:T(8,128)S(1)}, u32[]{:S(2)}, u32[]{:S(2)}) collective-permute-start(f32[192,256]{1,0:T(8,128)S(1)} %collective-permute-done.17.refs_3_), channel_id=1, source_target_pairs={{0,8},{8,16},{16,24},{24,28},{28,20},{20,12},{12,4},{4,0},{1,9},{9... | collective-permute-start | bytes 589832 | tf_op jit(solution)/shard_map/ppermute | solution.py:65
  76.1 2.3 %copy-done.1 = f32[768,1536]{1,0:T(8,128)S(1)} copy-done((f32[768,1536]{1,0:T(8,128)S(1)}, f32[768,1536]{1,0:T(8,128)}, u32[]{:S(2)}) %copy-start.1) | copy-done | bytes 4718616
  79.0 1.3 %collective-permute-done.20.refs_5_ = f32[192,256]{1,0:T(8,128)S(1)} collective-permute-done((f32[192,256]{1,0:T(8,128)S(1)}, f32[192,256]{1,0:T(8,128)S(1)}, u32[]{:S(2)}, u32[]{:S(2)}) %collective-permute-start.20) | collective-permute-done | bytes 196640 | tf_op jit(solution)/shard_map/ppermute | solution.py:65
  80.3 1.6 %collective-permute-start.21 = (f32[96,256]{1,0:T(8,128)S(1)}, f32[96,256]{1,0:T(8,128)S(1)}, u32[]{:S(2)}, u32[]{:S(2)}) collective-permute-start(f32[96,256]{1,0:T(8,128)S(1)} %slice.96), channel_id=1, source_target_pairs={{0,8},{8,16},{16,24},{24,28},{28,20},{20,12},{12,4},{4,0},{1,9},{9... | collective-permute-start | bytes 294920 | tf_op jit(solution)/shard_map/ppermute | solution.py:65
  82.7 2.7 %shard_map.92 = (f32[768,256]{1,0:T(8,128)S(1)}, f32[3,256]{1,0:T(4,128)S(1)}) custom-call(s32[17]{0:T(128)S(1)} %get-tuple-element.95.meta, f32[192,256]{1,0:T(8,128)S(1)} %fusion.11.refs_0_.refs_5_, f32[192,256]{1,0:T(8,128)S(1)} %collective-permute-done.16.refs_1_, f32[192,256]{1,0:T(8,128)S(1)} %collective-permute-done.18.refs_2_, ...), custom_call_target="tpu_custom_call" | custom-call | flops 1811939328 | bytes 4718592 | tf_op jit(solution)/shard_map/pallas_call | solution.py:270
  85.4 1.4 %collective-permute-done.23.refs_1_ = f32[96,256]{1,0:T(8,128)S(1)} collective-permute-done((f32[96,256]{1,0:T(8,128)S(1)}, f32[96,256]{1,0:T(8,128)S(1)}, u32[]{:S(2)}, u32[]{:S(2)}) %collective-permute-start.23) | collective-permute-done | bytes 98336 | tf_op jit(solution)/shard_map/ppermute | solution.py:65
  86.8 2.1 %shard_map.93 = (f32[4,192,256]{2,1,0:T(8,128)S(1)}, f32[32,4,256]{2,1,0:T(4,128)}) custom-call(s32[17]{0:T(128)S(1)} %get-tuple-element.95.meta, f32[96,256]{1,0:T(8,128)S(1)} %collective-permute-done.21.refs_0_, f32[96,256]{1,0:T(8,128)S(1)} %collective-permute-done.23.refs_1_, f32[768,256]{1,0:T(8,128)S(1)} %get-tuple-element.101.refs_2_, ...), custom_call_target="tpu_custom_call" | custom-call | flops 452984832 | bytes 1179648 | tf_op jit(solution)/shard_map/pallas_call | solution.py:270
  89.0 3.7 %all-to-all-start = ((f32[32,4,256]{2,1,0:T(4,128)}), f32[32,4,256]{2,1,0:T(4,128)S(1)}, u32[]{:S(2)}, u32[]{:S(2)}) async-start(f32[32,4,256]{2,1,0:T(4,128)} %get-tuple-element.106), calls=%async_computation | async-start | bytes 262144 | tf_op jit(solution)/shard_map/all_to_all | solution.py:494
  92.8 1.8 %collective-permute-start.27 = (f32[192,256]{1,0:T(8,128)S(1)}, f32[192,256]{1,0:T(8,128)S(1)}, u32[]{:S(2)}, u32[]{:S(2)}) collective-permute-start(f32[192,256]{1,0:T(8,128)S(1)} %fusion.7), channel_id=1, source_target_pairs={{0,2},{1,3},{2,0},{3,1},{4,6},{5,7},{6,4},{7,5},{8,10},{9,11},{10,... | collective-permute-start | bytes 589832 | tf_op jit(solution)/shard_map/ppermute | solution.py:496
  94.6 6.4 %all-to-all-done = f32[32,4,256]{2,1,0:T(4,128)S(1)} async-done(((f32[32,4,256]{2,1,0:T(4,128)}), f32[32,4,256]{2,1,0:T(4,128)S(1)}, u32[]{:S(2)}, u32[]{:S(2)}) %all-to-all-start) | async-done | bytes 131104 | tf_op jit(solution)/shard_map/all_to_all | solution.py:494
  (73 shorter events, 15.0 us)
Async XLA Ops:
  2.9 12.8 %collective-permute-start = (bf16[832,256]{1,0:T(8,128)(2,1)S(1)}, bf16[832,256]{1,0:T(8,128)(2,1)S(1)}, u32[]{:S(2)}, u32[]{:S(2)}) collective-permute-start(bf16[832,256]{1,0:T(8,128)(2,1)S(1)} %pad_maximum_fusion.1.refs_0_), channel_id=1, source_target_pairs={{0,8},{8,16},{16,24},{24,28},{28,20},{20,12},{12,4},{4,0},{1,9},{9... | collective-permute-start | bytes 1277960 | tf_op jit(solution)/shard_map/ppermute | solution.py:65
  6.0 11.6 %collective-permute-start.1 = (bf16[832,256]{1,0:T(8,128)(2,1)S(1)}, bf16[832,256]{1,0:T(8,128)(2,1)S(1)}, u32[]{:S(2)}, u32[]{:S(2)}) collective-permute-start(bf16[832,256]{1,0:T(8,128)(2,1)S(1)} %pad_maximum_fusion.1.refs_0_), channel_id=1, source_target_pairs={{8,0},{16,8},{24,16},{28,24},{20,28},{12,20},{4,12},{0,4},{9,1},{1... | collective-permute-start | bytes 1277960 | tf_op jit(solution)/shard_map/ppermute | solution.py:65
  7.2 21.8 %collective-permute-start.2 = (bf16[1,256,256]{2,1,0:T(8,128)(2,1)S(1)}, bf16[1,256,256]{2,1,0:T(8,128)(2,1)S(1)}, u32[]{:S(2)}, u32[]{:S(2)}) collective-permute-start(bf16[1,256,256]{2,1,0:T(8,128)(2,1)S(1)} %maximum_bitcast_fusion.refs_7_), channel_id=1, source_target_pairs={{0,2},{1,3},{2,0},{3,1},{4,6},{5,7},{6,4},{7,5},{8,10},{9,11},{10,... | collective-permute-start | bytes 393224 | tf_op jit(solution)/shard_map/ppermute | solution.py:344
  15.8 11.0 %collective-permute-start.3 = (bf16[832,256]{1,0:T(8,128)(2,1)S(1)}, bf16[832,256]{1,0:T(8,128)(2,1)S(1)}, u32[]{:S(2)}, u32[]{:S(2)}) collective-permute-start(bf16[832,256]{1,0:T(8,128)(2,1)S(1)} %collective-permute-done.refs_0_.refs_1_), channel_id=1, source_target_pairs={{0,8},{8,16},{16,24},{24,28},{28,20},{20,12},{12,4},{4,0},{1,9},{9... | collective-permute-start | bytes 1277960 | tf_op jit(solution)/shard_map/ppermute | solution.py:65
  17.6 10.7 %collective-permute-start.4 = (bf16[832,256]{1,0:T(8,128)(2,1)S(1)}, bf16[832,256]{1,0:T(8,128)(2,1)S(1)}, u32[]{:S(2)}, u32[]{:S(2)}) collective-permute-start(bf16[832,256]{1,0:T(8,128)(2,1)S(1)} %collective-permute-done.1.refs_1_.refs_2_), channel_id=1, source_target_pairs={{8,0},{16,8},{24,16},{28,24},{20,28},{12,20},{4,12},{0,4},{9,1},{1... | collective-permute-start | bytes 1277960 | tf_op jit(solution)/shard_map/ppermute | solution.py:65
  26.8 10.1 %collective-permute-start.6 = (bf16[832,256]{1,0:T(8,128)(2,1)S(1)}, bf16[832,256]{1,0:T(8,128)(2,1)S(1)}, u32[]{:S(2)}, u32[]{:S(2)}) collective-permute-start(bf16[832,256]{1,0:T(8,128)(2,1)S(1)} %collective-permute-done.3.refs_2_.refs_3_), channel_id=1, source_target_pairs={{0,8},{8,16},{16,24},{24,28},{28,20},{20,12},{12,4},{4,0},{1,9},{9... | collective-permute-start | bytes 1277960 | tf_op jit(solution)/shard_map/ppermute | solution.py:65
  28.3 9.5 %collective-permute-start.7 = (bf16[832,256]{1,0:T(8,128)(2,1)S(1)}, bf16[832,256]{1,0:T(8,128)(2,1)S(1)}, u32[]{:S(2)}, u32[]{:S(2)}) collective-permute-start(bf16[832,256]{1,0:T(8,128)(2,1)S(1)} %collective-permute-done.4.refs_3_.refs_4_), channel_id=1, source_target_pairs={{8,0},{16,8},{24,16},{28,24},{20,28},{12,20},{4,12},{0,4},{9,1},{1... | collective-permute-start | bytes 1277960 | tf_op jit(solution)/shard_map/ppermute | solution.py:65
  29.6 8.2 %collective-permute-start.5 = (bf16[2,256,256]{2,1,0:T(8,128)(2,1)S(1)}, bf16[2,256,256]{2,1,0:T(8,128)(2,1)S(1)}, u32[]{:S(2)}, u32[]{:S(2)}) collective-permute-start(bf16[2,256,256]{2,1,0:T(8,128)(2,1)S(1)} %shard_map.85.refs_10_), channel_id=1, source_target_pairs={{0,2},{1,3},{2,0},{3,1},{4,6},{5,7},{6,4},{7,5},{8,10},{9,11},{10,... | collective-permute-start | bytes 786440 | tf_op jit(solution)/shard_map/ppermute | solution.py:344
  31.1 2.3 %copy-start.2 = (f32[4,1,1,192,1536]{4,3,2,1,0:T(8,128)S(1)}, f32[4,1,1,192,1536]{4,3,2,1,0:T(8,128)}, u32[]{:S(2)}) copy-start(f32[4,1,1,192,1536]{4,3,2,1,0:T(8,128)} %param.8) | copy-start | bytes 14155780
  37.8 5.0 %collective-permute-start.9 = (bf16[2,2,256,256]{3,2,1,0:T(8,128)(2,1)S(1)}, bf16[2,2,256,256]{3,2,1,0:T(8,128)(2,1)S(1)}, u32[]{:S(2)}, u32[]{:S(2)}) collective-permute-start(bf16[2,2,256,256]{3,2,1,0:T(8,128)(2,1)S(1)} %pad_maximum_fusion), channel_id=1, source_target_pairs={{0,1},{1,0},{2,3},{3,2},{4,5},{5,4},{6,7},{7,6},{8,9},{9,8},{10,11... | collective-permute-start | bytes 1572872 | tf_op jit(solution)/shard_map/ppermute | solution.py:338
  37.9 4.9 %collective-permute-start.8 = (bf16[2,1,256,256]{3,2,1,0:T(8,128)(2,1)S(1)}, bf16[2,1,256,256]{3,2,1,0:T(8,128)(2,1)S(1)}, u32[]{:S(2)}, u32[]{:S(2)}) collective-permute-start(bf16[2,1,256,256]{3,2,1,0:T(8,128)(2,1)S(1)} %pad_maximum_fusion.3), channel_id=1, source_target_pairs={{0,1},{1,0},{2,3},{3,2},{4,5},{5,4},{6,7},{7,6},{8,9},{9,8},{10,11... | collective-permute-start | bytes 786440 | tf_op jit(solution)/shard_map/ppermute | solution.py:338
  38.5 8.0 %collective-permute-start.11 = (bf16[384,256]{1,0:T(8,128)(2,1)S(1)}, bf16[384,256]{1,0:T(8,128)(2,1)S(1)}, u32[]{:S(2)}, u32[]{:S(2)}) collective-permute-start(bf16[384,256]{1,0:T(8,128)(2,1)S(1)} %slice.92), channel_id=1, source_target_pairs={{0,8},{8,16},{16,24},{24,28},{28,20},{20,12},{12,4},{4,0},{1,9},{9... | collective-permute-start | bytes 589832 | tf_op jit(solution)/shard_map/ppermute | solution.py:65
  40.1 6.6 %collective-permute-start.12 = (bf16[384,256]{1,0:T(8,128)(2,1)S(1)}, bf16[384,256]{1,0:T(8,128)(2,1)S(1)}, u32[]{:S(2)}, u32[]{:S(2)}) collective-permute-start(bf16[384,256]{1,0:T(8,128)(2,1)S(1)} %slice.93), channel_id=1, source_target_pairs={{8,0},{16,8},{24,16},{28,24},{20,28},{12,20},{4,12},{0,4},{9,1},{1... | collective-permute-start | bytes 589832 | tf_op jit(solution)/shard_map/ppermute | solution.py:65
  41.2 5.2 %collective-permute-start.10 = (bf16[1,256,256]{2,1,0:T(8,128)(2,1)S(1)}, bf16[1,256,256]{2,1,0:T(8,128)(2,1)S(1)}, u32[]{:S(2)}, u32[]{:S(2)}) collective-permute-start(bf16[1,256,256]{2,1,0:T(8,128)(2,1)S(1)} %shard_map.88.refs_2_), channel_id=1, source_target_pairs={{0,2},{1,3},{2,0},{3,1},{4,6},{5,7},{6,4},{7,5},{8,10},{9,11},{10,... | collective-permute-start | bytes 393224 | tf_op jit(solution)/shard_map/ppermute | solution.py:344
  46.8 1.6 %collective-permute-start.13 = (bf16[2,1,256,256]{3,2,1,0:T(8,128)(2,1)S(1)}, bf16[2,1,256,256]{3,2,1,0:T(8,128)(2,1)S(1)}, u32[]{:S(2)}, u32[]{:S(2)}) collective-permute-start(bf16[2,1,256,256]{3,2,1,0:T(8,128)(2,1)S(1)} %pad_maximum_fusion.4), channel_id=1, source_target_pairs={{0,1},{1,0},{2,3},{3,2},{4,5},{5,4},{6,7},{7,6},{8,9},{9,8},{10,11... | collective-permute-start | bytes 786440 | tf_op jit(solution)/shard_map/ppermute | solution.py:338
  51.8 2.7 %collective-permute-start.14 = (f32[2,192,256]{2,1,0:T(8,128)S(1)}, f32[2,192,256]{2,1,0:T(8,128)S(1)}, u32[]{:S(2)}, u32[]{:S(2)}) collective-permute-start(f32[2,192,256]{2,1,0:T(8,128)S(1)} %get-tuple-element.91), channel_id=1, source_target_pairs={{0,1},{1,0},{2,3},{3,2},{4,5},{5,4},{6,7},{7,6},{8,9},{9,8},{10,11... | collective-permute-start | bytes 1179656 | tf_op jit(solution)/shard_map/ppermute | solution.py:430
  52.0 9.8 %copy-start.3 = (f32[1,1,1,192]{3,2,1,0:T(1,128)S(1)}, f32[1,1,1,192]{3,2,1,0:T(1,128)}, u32[]{:S(2)}) copy-start(f32[1,1,1,192]{3,2,1,0:T(1,128)} %param.9) | copy-start | bytes 2308
  54.5 7.2 %collective-permute-start.15 = (f32[192,256]{1,0:T(8,128)S(1)}, f32[192,256]{1,0:T(8,128)S(1)}, u32[]{:S(2)}, u32[]{:S(2)}) collective-permute-start(f32[192,256]{1,0:T(8,128)S(1)} %fusion.8), channel_id=1, source_target_pairs={{0,2},{1,3},{2,0},{3,1},{4,6},{5,7},{6,4},{7,5},{8,10},{9,11},{10,... | collective-permute-start | bytes 589832 | tf_op jit(solution)/shard_map/ppermute | solution.py:448
  61.9 6.4 %collective-permute-start.16 = (f32[192,256]{1,0:T(8,128)S(1)}, f32[192,256]{1,0:T(8,128)S(1)}, u32[]{:S(2)}, u32[]{:S(2)}) collective-permute-start(f32[192,256]{1,0:T(8,128)S(1)} %fusion.11.refs_0_.refs_5_), channel_id=1, source_target_pairs={{0,8},{8,16},{16,24},{24,28},{28,20},{20,12},{12,4},{4,0},{1,9},{9... | collective-permute-start | bytes 589832 | tf_op jit(solution)/shard_map/ppermute | solution.py:65
  63.5 6.4 %collective-permute-start.18 = (f32[192,256]{1,0:T(8,128)S(1)}, f32[192,256]{1,0:T(8,128)S(1)}, u32[]{:S(2)}, u32[]{:S(2)}) collective-permute-start(f32[192,256]{1,0:T(8,128)S(1)} %fusion.11.refs_0_.refs_5_), channel_id=1, source_target_pairs={{8,0},{16,8},{24,16},{28,24},{20,28},{12,20},{4,12},{0,4},{9,1},{1... | collective-permute-start | bytes 589832 | tf_op jit(solution)/shard_map/ppermute | solution.py:65
  64.0 6.4 %collective-permute-start.24 = (f32[192,256]{1,0:T(8,128)S(1)}, f32[192,256]{1,0:T(8,128)S(1)}, u32[]{:S(2)}, u32[]{:S(2)}) collective-permute-start(f32[192,256]{1,0:T(8,128)S(1)} %fusion.11.refs_0_.refs_5_), channel_id=1, source_target_pairs={{0,2},{1,3},{2,0},{3,1},{4,6},{5,7},{6,4},{7,5},{8,10},{9,11},{10,... | collective-permute-start | bytes 589832 | tf_op jit(solution)/shard_map/ppermute | solution.py:450
  68.3 5.7 %collective-permute-start.17 = (f32[192,256]{1,0:T(8,128)S(1)}, f32[192,256]{1,0:T(8,128)S(1)}, u32[]{:S(2)}, u32[]{:S(2)}) collective-permute-start(f32[192,256]{1,0:T(8,128)S(1)} %collective-permute-done.16.refs_1_), channel_id=1, source_target_pairs={{0,8},{8,16},{16,24},{24,28},{28,20},{20,12},{12,4},{4,0},{1,9},{9... | collective-permute-start | bytes 589832 | tf_op jit(solution)/shard_map/ppermute | solution.py:65
  69.9 5.7 %collective-permute-start.19 = (f32[192,256]{1,0:T(8,128)S(1)}, f32[192,256]{1,0:T(8,128)S(1)}, u32[]{:S(2)}, u32[]{:S(2)}) collective-permute-start(f32[192,256]{1,0:T(8,128)S(1)} %collective-permute-done.18.refs_2_), channel_id=1, source_target_pairs={{8,0},{16,8},{24,16},{28,24},{20,28},{12,20},{4,12},{0,4},{9,1},{1... | collective-permute-start | bytes 589832 | tf_op jit(solution)/shard_map/ppermute | solution.py:65
  70.4 15.0 %collective-permute-start.25 = (f32[2,192,256]{2,1,0:T(8,128)S(1)}, f32[2,192,256]{2,1,0:T(8,128)S(1)}, u32[]{:S(2)}, u32[]{:S(2)}) collective-permute-start(f32[2,192,256]{2,1,0:T(8,128)S(1)} %pad_maximum_fusion.2), channel_id=1, source_target_pairs={{0,1},{1,0},{2,3},{3,2},{4,5},{5,4},{6,7},{7,6},{8,9},{9,8},{10,11... | collective-permute-start | bytes 1179656 | tf_op jit(solution)/shard_map/ppermute | solution.py:451
  74.0 6.3 %collective-permute-start.20 = (f32[192,256]{1,0:T(8,128)S(1)}, f32[192,256]{1,0:T(8,128)S(1)}, u32[]{:S(2)}, u32[]{:S(2)}) collective-permute-start(f32[192,256]{1,0:T(8,128)S(1)} %collective-permute-done.17.refs_3_), channel_id=1, source_target_pairs={{0,8},{8,16},{16,24},{24,28},{28,20},{20,12},{12,4},{4,0},{1,9},{9... | collective-permute-start | bytes 589832 | tf_op jit(solution)/shard_map/ppermute | solution.py:65
  75.6 6.4 %collective-permute-start.22 = (f32[192,256]{1,0:T(8,128)S(1)}, f32[192,256]{1,0:T(8,128)S(1)}, u32[]{:S(2)}, u32[]{:S(2)}) collective-permute-start(f32[192,256]{1,0:T(8,128)S(1)} %collective-permute-done.19.refs_4_), channel_id=1, source_target_pairs={{8,0},{16,8},{24,16},{28,24},{20,28},{12,20},{4,12},{0,4},{9,1},{1... | collective-permute-start | bytes 589832 | tf_op jit(solution)/shard_map/ppermute | solution.py:65
  76.1 2.3 %copy-start.1 = (f32[768,1536]{1,0:T(8,128)S(1)}, f32[768,1536]{1,0:T(8,128)}, u32[]{:S(2)}) copy-start(f32[768,1536]{1,0:T(8,128)} %get-tuple-element.94.gram_ref) | copy-start | bytes 14155780
  80.3 5.1 %collective-permute-start.21 = (f32[96,256]{1,0:T(8,128)S(1)}, f32[96,256]{1,0:T(8,128)S(1)}, u32[]{:S(2)}, u32[]{:S(2)}) collective-permute-start(f32[96,256]{1,0:T(8,128)S(1)} %slice.96), channel_id=1, source_target_pairs={{0,8},{8,16},{16,24},{24,28},{28,20},{20,12},{12,4},{4,0},{1,9},{9... | collective-permute-start | bytes 294920 | tf_op jit(solution)/shard_map/ppermute | solution.py:65
  82.0 4.8 %collective-permute-start.23 = (f32[96,256]{1,0:T(8,128)S(1)}, f32[96,256]{1,0:T(8,128)S(1)}, u32[]{:S(2)}, u32[]{:S(2)}) collective-permute-start(f32[96,256]{1,0:T(8,128)S(1)} %slice.97), channel_id=1, source_target_pairs={{8,0},{16,8},{24,16},{28,24},{20,28},{12,20},{4,12},{0,4},{9,1},{1... | collective-permute-start | bytes 294920 | tf_op jit(solution)/shard_map/ppermute | solution.py:65
  88.9 3.8 %collective-permute-start.26 = (f32[2,192,256]{2,1,0:T(8,128)S(1)}, f32[2,192,256]{2,1,0:T(8,128)S(1)}, u32[]{:S(2)}, u32[]{:S(2)}) collective-permute-start(f32[2,192,256]{2,1,0:T(8,128)S(1)} %slice.84), channel_id=1, source_target_pairs={{0,1},{1,0},{2,3},{3,2},{4,5},{5,4},{6,7},{7,6},{8,9},{9,8},{10,11... | collective-permute-start | bytes 1179656 | tf_op jit(solution)/shard_map/ppermute | solution.py:495
  89.0 12.0 %all-to-all-start = ((f32[32,4,256]{2,1,0:T(4,128)}), f32[32,4,256]{2,1,0:T(4,128)S(1)}, u32[]{:S(2)}, u32[]{:S(2)}) async-start(f32[32,4,256]{2,1,0:T(4,128)} %get-tuple-element.106), calls=%async_computation | async-start | bytes 262144 | tf_op jit(solution)/shard_map/all_to_all | solution.py:494
  92.8 8.4 %collective-permute-start.27 = (f32[192,256]{1,0:T(8,128)S(1)}, f32[192,256]{1,0:T(8,128)S(1)}, u32[]{:S(2)}, u32[]{:S(2)}) collective-permute-start(f32[192,256]{1,0:T(8,128)S(1)} %fusion.7), channel_id=1, source_target_pairs={{0,2},{1,3},{2,0},{3,1},{4,6},{5,7},{6,4},{7,5},{8,10},{9,11},{10,... | collective-permute-start | bytes 589832 | tf_op jit(solution)/shard_map/ppermute | solution.py:496
  (1 other events, 0.9 us)

commit v7 on v6

--- a/solution.py
+++ b/solution.py
@@ -64,12 +64,12 @@
         axes = ("dp", "trow")
         return [lax.ppermute(ahead, axes, self.ahead), lax.ppermute(back, axes, self.back)]
 
-    def last(self, ahead, back, rows):
-        half = (rows // 2 + 15) // 16 * 16
+    def last(self, ahead, back, rows, more=0):
+        half = (rows // 2 + 15) // 16 * 16 + more
         return self.move(ahead[:half], back[half:rows])
 
 
-ORDER = (1, 3, 0, 2)
+ORDER = (3, 2, 1, 0)
 
 
 def split(value):
@@ -134,7 +134,7 @@
         own, far, near = round_refs[3 * group : 3 * group + 3]
         for inner in range(own.shape[0]):
             lanes = slice(turn * count, (turn + 1) * count)
-            parts = [near[0, inner], near[1, inner], own[inner], far[inner]]
+            parts = [near[1, inner], far[inner], near[0, inner], own[inner]]
             for j, part in zip(ORDER, parts):
                 at = pl.multiple_of(jnp.bitwise_xor(me, j) * head_part, 16)
                 target[pl.ds(at, head_part), lanes] = part[:head_part, :]
@@ -146,7 +146,7 @@
     n, width, head_part, block, groups = sizes
     shard_refs, refs = refs[: n - 1], refs[n - 1 :]
     round_refs, refs = refs[: 3 * groups], refs[3 * groups :]
-    prior_ref, tile_ref, side_ref, columns, rows, target = refs
+    prior_ref, now_ref, later_ref, side_ref, columns, rows, target = refs
     count = shard_refs[0].shape[1]
     for index in range(n - 1):
         lanes = pl.ds(pl.multiple_of(meta[index] * count, 128), count)
@@ -158,36 +158,30 @@
     for start in range(0, columns.shape[0], block):
         lanes = slice(start, start + block)
         column = columns[lanes, :done]
-        tile_ref[:, lanes] = prior_ref[:, lanes] + dot(rows[:, :done], column, NT) * scale
+        value = prior_ref[:, lanes] + dot(rows[:, :done], column, NT) * scale
+        now_ref[:, lanes], later_ref[:, lanes] = value[: now_ref.shape[0]], value[now_ref.shape[0] :]
         side_ref[lanes, :] = dot(column, target[:, :done], NT)
 
 
-def tile_rows_of(first, early_ref, last_rows, last_columns, block, scale, tile_ref, gram_ref, me, piece, stored):
+def tile_rows_of(first, early, last_rows, last_columns, block, scale, tile_ref, gram_ref, me, piece, stored):
     part = pl.ds(first * piece, tile_ref.shape[0])
     copies = []
     for start in range(0, tile_ref.shape[1], block):
         lanes = pl.ds(start, block)
-        tile_ref[:, lanes] = early_ref[part, lanes] + dot(last_rows[part, :], last_columns[lanes, :], NT) * scale
-        copies += store_rows(tile_ref, gram_ref, me, first, piece, lanes, stored)
+        tile_ref[:, lanes] = early[:, lanes] + dot(last_rows[part, :], last_columns[lanes, :], NT) * scale
+        for index in range(tile_ref.shape[0] // piece):
+            place = pl.ds(pl.multiple_of(jnp.bitwise_xor(me, ORDER[first + index]) * piece, 8), piece)
+            made = tile_ref.at[pl.ds(index * piece, piece), lanes]
+            copies.append(pltpu.make_async_copy(made, gram_ref.at[place, lanes], stored.at[len(copies)]))
+            copies[-1].start()
     return copies
 
 
-def store_rows(tile_ref, gram_ref, me, first, piece, lanes, stored):
-    copies = []
-    for index in range(tile_ref.shape[0] // piece):
-        place = pl.ds(pl.multiple_of(jnp.bitwise_xor(me, ORDER[first + index]) * piece, 8), piece)
-        part = tile_ref.at[pl.ds(index * piece, piece), lanes]
-        at = lanes.start // lanes.size * 2 + index
-        copies.append(pltpu.make_async_copy(part, gram_ref.at[place, lanes], stored.at[at]))
-        copies[-1].start()
-    return copies
-
-
-def send_kernel(sizes, meta, *refs):
+def first_kernel(sizes, meta, *refs):
     n, piece, width, head_part, block = sizes
     low_ref, high_ref, *round_refs = refs[:5]
-    early_ref, early_side, columns, sent_ref, gram_ref = refs[5:10]
-    side_high, side_low, last_columns, last_rows, last_target, tile_ref, stored = refs[10:]
+    early, early_side, columns, image_ref, gram_ref, tile_ref = refs[5:11]
+    side_high, side_low, last_columns, last_rows, last_target, stored = refs[11:]
     total_rows, count = columns.shape[1], last_rows.shape[1]
     last_columns[...] = columns[:, total_rows - count :]
     base = pl.multiple_of(meta[2 * n - 1] * width, 16)
@@ -196,30 +190,32 @@
     last_columns[pl.ds(pl.multiple_of(base + half, 16), width - half), :] = high_ref[...]
     place_rows(round_refs, meta[2 * n], head_part, last_rows, last_target, 0, count)
     scale = 1.0 / total_rows
-    copies = tile_rows_of(
-        0, early_ref, last_rows, last_columns, block, scale, tile_ref, gram_ref, meta[2 * n], piece, stored
-    )
+    me = meta[2 * n]
+    copies = tile_rows_of(0, early, last_rows, last_columns, block, scale, tile_ref, gram_ref, me, piece, stored)
     side = early_side[...] + dot(last_columns[...], last_target[...], NT)
     side_high[...], side_low[...] = split(side * scale)
-    value = product(split(tile_ref[...]), (side_high[...], side_low[...]))
-    sent_ref[...] = value.reshape(sent_ref.shape)
+    image_ref[...] = product(split(tile_ref[:piece, :]), (side_high[...], side_low[...]))
     for copy in copies:
         copy.wait()
 
 
-def kept_kernel(sizes, meta, *refs):
-    piece, block = sizes
-    early_ref, last_columns, last_rows, side_high, side_low, last_target, rows, target = refs[:8]
-    _, gram_ref, right_ref, image_ref, tile_ref, stored = refs[8:]
+def second_kernel(sizes, meta, *refs):
+    tile_ref, last_rows, side_high, side_low, last_target, rows, target, right_ref, image_ref = refs
+    piece = sizes
     total_rows, count = rows.shape[1], last_rows.shape[1]
     done = total_rows - count
+    image_ref[...] = product(split(tile_ref[piece:, :]), (side_high[...], side_low[...]))
+    own = slice(3 * piece, 4 * piece)
+    right = dot(rows[own, :done], target[:, :done], NT) + dot(last_rows[own, :], last_target[...], NT)
+    right_ref[...] = right * (1.0 / total_rows)
+
+
+def third_kernel(sizes, meta, *refs):
+    piece, block, total_rows = sizes
+    early, last_columns, last_rows, side_high, side_low, _, gram_ref, image_ref, tile_ref, stored = refs
     scale = 1.0 / total_rows
-    copies = tile_rows_of(
-        2, early_ref, last_rows, last_columns, block, scale, tile_ref, gram_ref, meta[0], piece, stored
-    )
-    own = slice(2 * piece, 3 * piece)
-    right = dot(rows[own, :done], target[:, :done], NT) + dot(last_rows[own, :], last_target[...], NT)
-    right_ref[...] = right * scale
+    me = meta[0]
+    copies = tile_rows_of(2, early, last_rows, last_columns, block, scale, tile_ref, gram_ref, me, piece, stored)
     value = product(split(tile_ref[...]), (side_high[...], side_low[...]))
     image_ref[...] = value.reshape(image_ref.shape)
     for copy in copies:
@@ -254,13 +250,13 @@
     side[pl.ds(pl.multiple_of(base + half, 8), piece - half), :] = high_ref[...]
     total = total_ref[...] + product(split(tile_ref[:, lanes]), split(side[...]))
     own = own_ref[...]
-    others = [near_ref[0], near_ref[1], own, far_ref[...]]
+    others = [near_ref[1], far_ref[...], near_ref[0], own]
     late = jnp.zeros((1, own.shape[1]), jnp.float32)
     for index, j in enumerate(ORDER):
         value = total[index * piece : (index + 1) * piece]
         if j == 0:
             value = value + penalty_ref[...] * own
-        out_ref[index] = value
+        out_ref[(3, 1, 2, 0).index(j)] = value
         late = late + jnp.sum(value * others[index], axis=0, keepdims=True)
     sums = jnp.concatenate([early_ref[...], late], axis=0)
     sums_ref[...] = jnp.broadcast_to(sums[None], sums_ref.shape)
@@ -388,14 +384,15 @@
         gathered += arrived
         open_groups(step)
         if step == ring.far - 1:
-            early, early_side, columns, rows, target = call(
+            early, early_later, early_side, columns, rows, target = call(
                 functools.partial(early_kernel, (n, width, head_part, block, 2)),
                 gram_meta,
                 [*gathered, *groups[0], *groups[1], prior],
                 [VMEM] * (n + 6),
-                [VMEM] * 5,
+                [VMEM] * 6,
                 [
-                    jax.ShapeDtypeStruct((tile_rows, tile_columns), f32),
+                    jax.ShapeDtypeStruct((2 * piece, tile_columns), f32),
+                    jax.ShapeDtypeStruct((2 * piece, tile_columns), f32),
                     jax.ShapeDtypeStruct((tile_columns, heads), f32),
                     jax.ShapeDtypeStruct((tile_columns, total_rows), bf16),
                     jax.ShapeDtypeStruct((tile_rows, total_rows), bf16),
@@ -406,47 +403,66 @@
                 2 * tile_rows * tile_columns * (total_rows - row_count),
                 8 * tile_rows * tile_columns,
             )
-    sent, gram, side_high, side_low, last_columns, last_rows, last_target = call(
-        functools.partial(send_kernel, (n, piece, width, head_part, block)),
+    gram_shape = jax.ShapeDtypeStruct((tile_rows, tile_columns), f32)
+    piece_shape = jax.ShapeDtypeStruct((piece, heads), f32)
+
+    def tile_scratch(pieces):
+        shape = (pieces * piece, tile_columns)
+        return [pltpu.VMEM(shape, f32), pltpu.SemaphoreType.DMA((pieces * (tile_columns // block),))]
+
+    sent, gram, first_tile, side_high, side_low, last_columns, last_rows, last_target = call(
+        functools.partial(first_kernel, (n, piece, width, head_part, block)),
         gram_meta,
         [*gathered[-2:], *groups[2], early, early_side, columns],
         [VMEM] * 8,
-        [VMEM, HBM] + [VMEM] * 5,
+        [VMEM, HBM] + [VMEM] * 6,
         [
-            jax.ShapeDtypeStruct((2, piece, heads), f32),
-            jax.ShapeDtypeStruct((tile_rows, tile_columns), f32),
+            piece_shape,
+            gram_shape,
+            jax.ShapeDtypeStruct((2 * piece, tile_columns), f32),
             jax.ShapeDtypeStruct((tile_columns, heads), bf16),
             jax.ShapeDtypeStruct((tile_columns, heads), bf16),
             jax.ShapeDtypeStruct((tile_columns, row_count), bf16),
             jax.ShapeDtypeStruct((tile_rows, row_count), bf16),
             jax.ShapeDtypeStruct((heads, row_count), bf16),
         ],
-        [pltpu.VMEM((2 * piece, tile_columns), f32), pltpu.SemaphoreType.DMA((2 * (tile_columns // block),))],
+        tile_scratch(2)[1:],
         GRAM_BYTES,
-        tile_rows * tile_columns * (row_count + 3 * heads),
-        4 * tile_rows * tile_columns,
+        2 * piece * tile_columns * (2 * row_count + 3 * heads),
+        16 * piece * tile_columns,
     )
     penalty_rows = penalty.reshape(piece, 1)
     received = lax.ppermute(sent, "tcol", swap(tcol_count, 1))
-    gram, start, kept = call(
-        functools.partial(kept_kernel, (piece, block)),
+    start, far_part = call(
+        functools.partial(second_kernel, piece),
         me_meta,
-        [early, last_columns, last_rows, side_high, side_low, last_target, rows, target, gram],
-        [VMEM] * 8 + [HBM],
-        [HBM, VMEM, VMEM],
-        [
-            jax.ShapeDtypeStruct((tile_rows, tile_columns), f32),
-            jax.ShapeDtypeStruct((piece, heads), f32),
-            jax.ShapeDtypeStruct((2, piece, heads), f32),
-        ],
-        [pltpu.VMEM((2 * piece, tile_columns), f32), pltpu.SemaphoreType.DMA((2 * (tile_columns // block),))],
+        [first_tile, last_rows, side_high, side_low, last_target, rows, target],
+        [VMEM] * 7,
+        [VMEM, VMEM],
+        [piece_shape, piece_shape],
+        [],
         GRAM_BYTES,
-        tile_rows * tile_columns * (row_count + 3 * heads),
-        6 * tile_rows * tile_columns,
-        {9: 0},
-    )
-    image = kept[0] + received[0] + lax.ppermute(kept[1] + received[1], "tcol", swap(tcol_count, 2))
-    image = image + penalty_rows * start
+        6 * piece * tile_columns * heads,
+        4 * piece * tile_columns,
+    )
+    far_part, early_later = lax.optimization_barrier((far_part + received, early_later))
+    far_sum = lax.ppermute(far_part, "tcol", swap(tcol_count, 2))
+    gram, kept = call(
+        functools.partial(third_kernel, (piece, block, total_rows)),
+        me_meta,
+        [early_later, last_columns, last_rows, side_high, side_low, gram],
+        [VMEM] * 5 + [HBM],
+        [HBM, VMEM],
+        [gram_shape, jax.ShapeDtypeStruct((2, piece, heads), f32)],
+        tile_scratch(2),
+        GRAM_BYTES,
+        4 * piece * tile_columns * (row_count + 3 * heads),
+        16 * piece * tile_columns,
+        {6: 0},
+    )
+    halves = [kept[0][: piece // 2], kept[0][piece // 2 :]]
+    near_sum = jnp.concatenate([lax.ppermute(part, "tcol", swap(tcol_count, 1)) for part in halves], axis=0)
+    image = kept[1] + near_sum + penalty_rows * start + far_sum
     far_image = lax.ppermute(image, "tcol", swap(tcol_count, 2))
     near_images = lax.ppermute(jnp.stack([image, far_image]), "tcol", swap(tcol_count, 1))
     images = [image]
@@ -455,7 +471,7 @@
         if step < ring.far:
             arrived = ahead, back = ring.move(ahead, back)
         else:
-            arrived = ring.last(ahead, back, piece)
+            arrived = ring.last(ahead, back, piece, 16 if piece > 32 else 0)
         if step == ring.far - 2:
             *arrived, gram = lax.optimization_barrier((*arrived, gram))
             tile = fetch(gram)
@@ -493,10 +509,10 @@
     sums, second = lax.optimization_barrier((sums, second))
     sums = lax.all_to_all(sums, axes, split_axis=0, concat_axis=0, tiled=True)
     received = lax.ppermute(second[:2], "tcol", swap(tcol_count, 1))
-    far_second = lax.ppermute(second[3] + received[1], "tcol", swap(tcol_count, 2))
+    far_second = lax.ppermute(second[2] + received[0], "tcol", swap(tcol_count, 2))
     far_second, sums = lax.optimization_barrier((far_second, sums))
     sums = jnp.sum(sums, axis=0)
-    second = second[2] + received[0] + far_second
+    second = second[3] + received[1] + far_second
 
     norm, curvature, image_norm, image_curvature = sums[0], sums[1], sums[2], sums[3]
     step = norm / curvature

time: 103 us -> 101 us (0.981)
  waiting for transfers between devices: 38.6 us -> 36.8 us
    ppermute x2 -> x4, waiting for transfers between devices: 5.92 us -> 2.95 us  [the longest x1 1.76 us: shards(): far_sum = lax.ppermute(far_part, 'tcol', swap(tcol_count, 2))]
    ppermute x8, waiting for transfers between devices: 2.59 us -> 4.05 us  [move(): lax.ppermute(back, axes, self.back)]
    ppermute x2 -> x4, starting transfers between devices: 3.4 us -> 3.96 us  [the longest x1 1.83 us: shards(): lax.ppermute(second[2] + received[0], 'tcol', swap(tcol_count, 2))]
    pallas_call x9 -> x10, Pallas kernels: 16.6 us -> 16.6 us  [call(): pl.pallas_call(body, grid_spec=pltpu.PrefetchScalarGridSpec(num_scalar_pr...]
  transfers between devices with their start and end apart: 29 -> 31, of which waited for: 13 -> 17; matrix products, arithmetic and copies ran while one was open for 3% -> 4% of each run, Pallas kernels for 11% -> 12%
where the time goes in v7:
time: 101 us; the launch traced here: 100 us
  waiting for transfers between devices  36.8 us (36%)
  starting transfers between devices  32.4 us (32%)
  Pallas kernels  16.6 us (16%)
  local copies, waits for them, and re-layouts  10.3 us (10%)
  between operations  2.91 us (3%)
  other arithmetic  1.38 us (1%)
    ppermute x8, waiting for transfers between devices, move(): lax.ppermute(ahead, axes, self.ahead)  21.4 us
    pallas_call x10, Pallas kernels, call(): pl.pallas_call(body, grid_spec=pltpu.PrefetchScalarGridSpec(num_scalar_pr...  16.6 us
    ppermute x8, starting transfers between devices, move(): lax.ppermute(ahead, axes, self.ahead)  14.4 us
    unnamed x10, local copies, waits for them, and re-layouts  6.83 us
    all_to_all x1, waiting for transfers between devices, shards(): sums = lax.all_to_all(sums, axes, split_axis=0, concat_axis=0, tiled=True)  6.35 us
    ppermute x3, starting transfers between devices, open_groups(): lax.ppermute(mine, 'tcol', swap(tcol_count, 2))  5.01 us
    ppermute x8, waiting for transfers between devices, move(): lax.ppermute(back, axes, self.back)  4.05 us
    all_to_all x1, starting transfers between devices, shards(): sums = lax.all_to_all(sums, axes, split_axis=0, concat_axis=0, tiled=True)  3.44 us
  transfers between devices with their start and end apart: 31, of which 17 were waited for; matrix products, arithmetic and copies ran while one was open for 4% of the time, Pallas kernels for 12%

profile of v7, /device:TPU:0, one launch (start us, length us, event | category | flops | bytes accessed | tf_op | source)
XLA Modules:
  0.0 100.4 jit_solution(6559649643866946238)
XLA Ops:
  2.9 3.1 %collective-permute-start = (bf16[832,256]{1,0:T(8,128)(2,1)S(1)}, bf16[832,256]{1,0:T(8,128)(2,1)S(1)}, u32[]{:S(2)}, u32[]{:S(2)}) collective-permute-start(bf16[832,256]{1,0:T(8,128)(2,1)S(1)} %pad_maximum_fusion.1.refs_0_), channel_id=1, source_target_pairs={{0,8},{8,16},{16,24},{24,28},{28,20},{20,12},{12,4},{4,0},{1,9},{9... | collective-permute-start | bytes 1277960 | tf_op jit(solution)/shard_map/ppermute | solution.py:65
  7.2 2.0 %collective-permute-start.2 = (bf16[1,256,256]{2,1,0:T(8,128)(2,1)S(1)}, bf16[1,256,256]{2,1,0:T(8,128)(2,1)S(1)}, u32[]{:S(2)}, u32[]{:S(2)}) collective-permute-start(bf16[1,256,256]{2,1,0:T(8,128)(2,1)S(1)} %maximum_bitcast_fusion.refs_7_), channel_id=1, source_target_pairs={{0,2},{1,3},{2,0},{3,1},{4,6},{5,7},{6,4},{7,5},{8,10},{9,11},{10,... | collective-permute-start | bytes 393224 | tf_op jit(solution)/shard_map/ppermute | solution.py:340
  13.1 2.7 %collective-permute-done.refs_0_.refs_1_ = bf16[832,256]{1,0:T(8,128)(2,1)S(1)} collective-permute-done((bf16[832,256]{1,0:T(8,128)(2,1)S(1)}, bf16[832,256]{1,0:T(8,128)(2,1)S(1)}, u32[]{:S(2)}, u32[]{:S(2)}) %collective-permute-start) | collective-permute-done | bytes 426016 | tf_op jit(solution)/shard_map/ppermute | solution.py:65
  15.8 1.8 %collective-permute-start.3 = (bf16[832,256]{1,0:T(8,128)(2,1)S(1)}, bf16[832,256]{1,0:T(8,128)(2,1)S(1)}, u32[]{:S(2)}, u32[]{:S(2)}) collective-permute-start(bf16[832,256]{1,0:T(8,128)(2,1)S(1)} %collective-permute-done.refs_0_.refs_1_), channel_id=1, source_target_pairs={{0,8},{8,16},{16,24},{24,28},{28,20},{20,12},{12,4},{4,0},{1,9},{9... | collective-permute-start | bytes 1277960 | tf_op jit(solution)/shard_map/ppermute | solution.py:65
  17.9 8.9 %collective-permute-done.3.refs_2_.refs_3_ = bf16[832,256]{1,0:T(8,128)(2,1)S(1)} collective-permute-done((bf16[832,256]{1,0:T(8,128)(2,1)S(1)}, bf16[832,256]{1,0:T(8,128)(2,1)S(1)}, u32[]{:S(2)}, u32[]{:S(2)}) %collective-permute-start.3) | collective-permute-done | bytes 426016 | tf_op jit(solution)/shard_map/ppermute | solution.py:65
  26.8 1.5 %collective-permute-start.6 = (bf16[832,256]{1,0:T(8,128)(2,1)S(1)}, bf16[832,256]{1,0:T(8,128)(2,1)S(1)}, u32[]{:S(2)}, u32[]{:S(2)}) collective-permute-start(bf16[832,256]{1,0:T(8,128)(2,1)S(1)} %collective-permute-done.3.refs_2_.refs_3_), channel_id=1, source_target_pairs={{0,8},{8,16},{16,24},{24,28},{28,20},{20,12},{12,4},{4,0},{1,9},{9... | collective-permute-start | bytes 1277960 | tf_op jit(solution)/shard_map/ppermute | solution.py:65
  29.6 1.5 %collective-permute-start.5 = (bf16[2,256,256]{2,1,0:T(8,128)(2,1)S(1)}, bf16[2,256,256]{2,1,0:T(8,128)(2,1)S(1)}, u32[]{:S(2)}, u32[]{:S(2)}) collective-permute-start(bf16[2,256,256]{2,1,0:T(8,128)(2,1)S(1)} %shard_map.85.refs_10_), channel_id=1, source_target_pairs={{0,2},{1,3},{2,0},{3,1},{4,6},{5,7},{6,4},{7,5},{8,10},{9,11},{10,... | collective-permute-start | bytes 786440 | tf_op jit(solution)/shard_map/ppermute | solution.py:340
  31.1 2.3 %copy-done.2 = f32[4,1,1,192,1536]{4,3,2,1,0:T(8,128)S(1)} copy-done((f32[4,1,1,192,1536]{4,3,2,1,0:T(8,128)S(1)}, f32[4,1,1,192,1536]{4,3,2,1,0:T(8,128)}, u32[]{:S(2)}) %copy-start.2) | copy-done | bytes 4718616
  33.9 2.9 %collective-permute-done.6.refs_5_.refs_2_ = bf16[832,256]{1,0:T(8,128)(2,1)S(1)} collective-permute-done((bf16[832,256]{1,0:T(8,128)(2,1)S(1)}, bf16[832,256]{1,0:T(8,128)(2,1)S(1)}, u32[]{:S(2)}, u32[]{:S(2)}) %collective-permute-start.6) | collective-permute-done | bytes 426016 | tf_op jit(solution)/shard_map/ppermute | solution.py:65
  38.5 1.6 %collective-permute-start.11 = (bf16[384,256]{1,0:T(8,128)(2,1)S(1)}, bf16[384,256]{1,0:T(8,128)(2,1)S(1)}, u32[]{:S(2)}, u32[]{:S(2)}) collective-permute-start(bf16[384,256]{1,0:T(8,128)(2,1)S(1)} %slice.100), channel_id=1, source_target_pairs={{0,8},{8,16},{16,24},{24,28},{28,20},{20,12},{12,4},{4,0},{1,9},{9... | collective-permute-start | bytes 589832 | tf_op jit(solution)/shard_map/ppermute | solution.py:65
  41.2 1.6 %collective-permute-start.10 = (bf16[1,256,256]{2,1,0:T(8,128)(2,1)S(1)}, bf16[1,256,256]{2,1,0:T(8,128)(2,1)S(1)}, u32[]{:S(2)}, u32[]{:S(2)}) collective-permute-start(bf16[1,256,256]{2,1,0:T(8,128)(2,1)S(1)} %shard_map.88.refs_2_), channel_id=1, source_target_pairs={{0,2},{1,3},{2,0},{3,1},{4,6},{5,7},{6,4},{7,5},{8,10},{9,11},{10,... | collective-permute-start | bytes 393224 | tf_op jit(solution)/shard_map/ppermute | solution.py:340
  42.8 3.7 %shard_map.87 = (f32[384,1536]{1,0:T(8,128)S(1)}, f32[384,1536]{1,0:T(8,128)S(1)}, f32[1536,256]{1,0:T(8,128)S(1)}, bf16[1536,1024]{1,0:T(8,128)(2,1)S(1)}, bf16...) custom-call(s32[17]{0:T(128)S(1)} %get-tuple-element.61.meta, bf16[832,256]{1,0:T(8,128)(2,1)S(1)} %pad_maximum_fusion.1.refs_0_, ...), custom_call_target="tpu_custom_call" | custom-call | flops 1811939328 | bytes 9437184 | tf_op jit(solution)/shard_map/pallas_call | solution.py:266
  46.8 1.5 %collective-permute-done.13.refs_4_ = bf16[2,1,256,256]{3,2,1,0:T(8,128)(2,1)S(1)} collective-permute-done((bf16[2,1,256,256]{3,2,1,0:T(8,128)(2,1)S(1)}, bf16[2,1,256,256]{3,2,1,0:T(8,128)(2,1)S(1)}, u32[]{:S(2)}, u32[]{:S(2)}) %collective-permute-start.13) | collective-permute-done | bytes 262176 | tf_op jit(solution)/shard_map/ppermute | solution.py:334
  48.4 3.0 %shard_map.89 = (f32[192,256]{1,0:T(8,128)S(1)}, f32[768,1536]{1,0:T(8,128)}, f32[384,1536]{1,0:T(8,128)S(1)}, bf16[1536,256]{1,0:T(8,128)(2,1)S(1)}, bf16[1536,...) custom-call(s32[17]{0:T(128)S(1)} %get-tuple-element.61.meta, ...), custom_call_target="tpu_custom_call" | custom-call | flops 754974720 | bytes 4718592 | tf_op jit(solution)/shard_map/pallas_call | solution.py:266
  52.9 1.6 %collective-permute-start.17 = (f32[192,256]{1,0:T(8,128)S(1)}, f32[192,256]{1,0:T(8,128)S(1)}, u32[]{:S(2)}, u32[]{:S(2)}) collective-permute-start(f32[192,256]{1,0:T(8,128)S(1)} %add.59), channel_id=1, source_target_pairs={{0,2},{1,3},{2,0},{3,1},{4,6},{5,7},{6,4},{7,5},{8,10},{9,11},{10,... | collective-permute-start | bytes 589832 | tf_op jit(solution)/shard_map/ppermute | solution.py:449
  54.5 2.1 %shard_map.91 = (f32[768,1536]{1,0:T(8,128)}, f32[2,192,256]{2,1,0:T(8,128)S(1)}) custom-call(s32[1]{0:T(128)} %bitcast.meta, f32[384,1536]{1,0:T(8,128)S(1)} %get-tuple-element.97.refs_0_, bf16[1536,256]{1,0:T(8,128)(2,1)S(1)} %get-tuple-element.98.refs_1_, bf16[768,256]{1,0:T(8,128)(2,1)S(1)} %get-tuple-element.88.refs_1_.refs_2_, ...), custom_call_target="tpu_custom_call", output_to_operand_aliasing={{0}: (6, {})} | custom-call | flops 1207959552 | bytes 4718592 | tf_op jit(solution)/shard_map/pallas_call | solution.py:266
  58.2 1.8 %collective-permute-done.17 = f32[192,256]{1,0:T(8,128)S(1)} collective-permute-done((f32[192,256]{1,0:T(8,128)S(1)}, f32[192,256]{1,0:T(8,128)S(1)}, u32[]{:S(2)}, u32[]{:S(2)}) %collective-permute-start.17) | collective-permute-done | bytes 196640 | tf_op jit(solution)/shard_map/ppermute | solution.py:449
  60.0 1.6 %collective-permute-start.18 = (f32[192,256]{1,0:T(8,128)S(1)}, f32[192,256]{1,0:T(8,128)S(1)}, u32[]{:S(2)}, u32[]{:S(2)}) collective-permute-start(f32[192,256]{1,0:T(8,128)S(1)} %fusion.9.refs_0_.refs_5_), channel_id=1, source_target_pairs={{0,8},{8,16},{16,24},{24,28},{28,20},{20,12},{12,4},{4,0},{1,9},{9... | collective-permute-start | bytes 589832 | tf_op jit(solution)/shard_map/ppermute | solution.py:65
  62.1 1.5 %collective-permute-start.26 = (f32[192,256]{1,0:T(8,128)S(1)}, f32[192,256]{1,0:T(8,128)S(1)}, u32[]{:S(2)}, u32[]{:S(2)}) collective-permute-start(f32[192,256]{1,0:T(8,128)S(1)} %fusion.9.refs_0_.refs_5_), channel_id=1, source_target_pairs={{0,2},{1,3},{2,0},{3,1},{4,6},{5,7},{6,4},{7,5},{8,10},{9,11},{10,... | collective-permute-start | bytes 589832 | tf_op jit(solution)/shard_map/ppermute | solution.py:466
  63.6 2.6 %collective-permute-done.18.refs_1_ = f32[192,256]{1,0:T(8,128)S(1)} collective-permute-done((f32[192,256]{1,0:T(8,128)S(1)}, f32[192,256]{1,0:T(8,128)S(1)}, u32[]{:S(2)}, u32[]{:S(2)}) %collective-permute-start.18) | collective-permute-done | bytes 196640 | tf_op jit(solution)/shard_map/ppermute | solution.py:65
  66.2 1.6 %collective-permute-start.19 = (f32[192,256]{1,0:T(8,128)S(1)}, f32[192,256]{1,0:T(8,128)S(1)}, u32[]{:S(2)}, u32[]{:S(2)}) collective-permute-start(f32[192,256]{1,0:T(8,128)S(1)} %collective-permute-done.18.refs_1_), channel_id=1, source_target_pairs={{0,8},{8,16},{16,24},{24,28},{28,20},{20,12},{12,4},{4,0},{1,9},{9... | collective-permute-start | bytes 589832 | tf_op jit(solution)/shard_map/ppermute | solution.py:65
  68.3 3.6 %collective-permute-done.19.refs_3_ = f32[192,256]{1,0:T(8,128)S(1)} collective-permute-done((f32[192,256]{1,0:T(8,128)S(1)}, f32[192,256]{1,0:T(8,128)S(1)}, u32[]{:S(2)}, u32[]{:S(2)}) %collective-permute-start.19) | collective-permute-done | bytes 196640 | tf_op jit(solution)/shard_map/ppermute | solution.py:65
  72.0 1.6 %collective-permute-start.22 = (f32[192,256]{1,0:T(8,128)S(1)}, f32[192,256]{1,0:T(8,128)S(1)}, u32[]{:S(2)}, u32[]{:S(2)}) collective-permute-start(f32[192,256]{1,0:T(8,128)S(1)} %collective-permute-done.19.refs_3_), channel_id=1, source_target_pairs={{0,8},{8,16},{16,24},{24,28},{28,20},{20,12},{12,4},{4,0},{1,9},{9... | collective-permute-start | bytes 589832 | tf_op jit(solution)/shard_map/ppermute | solution.py:65
  74.1 2.3 %copy-done.1 = f32[768,1536]{1,0:T(8,128)S(1)} copy-done((f32[768,1536]{1,0:T(8,128)S(1)}, f32[768,1536]{1,0:T(8,128)}, u32[]{:S(2)}) %copy-start.1) | copy-done | bytes 4718616
  77.6 1.6 %collective-permute-done.24.refs_6_ = f32[192,256]{1,0:T(8,128)S(1)} collective-permute-done((f32[192,256]{1,0:T(8,128)S(1)}, f32[192,256]{1,0:T(8,128)S(1)}, u32[]{:S(2)}, u32[]{:S(2)}) %collective-permute-start.24) | collective-permute-done | bytes 196640 | tf_op jit(solution)/shard_map/ppermute | solution.py:65
  79.2 1.6 %collective-permute-start.23 = (f32[112,256]{1,0:T(8,128)S(1)}, f32[112,256]{1,0:T(8,128)S(1)}, u32[]{:S(2)}, u32[]{:S(2)}) collective-permute-start(f32[112,256]{1,0:T(8,128)S(1)} %slice.102), channel_id=1, source_target_pairs={{0,8},{8,16},{16,24},{24,28},{28,20},{20,12},{12,4},{4,0},{1,9},{9... | collective-permute-start | bytes 344072 | tf_op jit(solution)/shard_map/ppermute | solution.py:65
  81.3 2.7 %shard_map.93 = (f32[768,256]{1,0:T(8,128)S(1)}, f32[3,256]{1,0:T(4,128)S(1)}) custom-call(s32[17]{0:T(128)S(1)} %get-tuple-element.105.meta, f32[192,256]{1,0:T(8,128)S(1)} %fusion.9.refs_0_.refs_5_, f32[192,256]{1,0:T(8,128)S(1)} %collective-permute-done.18.refs_1_, f32[192,256]{1,0:T(8,128)S(1)} %collective-permute-done.20.refs_2_, ...), custom_call_target="tpu_custom_call" | custom-call | flops 1811939328 | bytes 4718592 | tf_op jit(solution)/shard_map/pallas_call | solution.py:266
  84.0 1.3 %collective-permute-done.25.refs_1_ = f32[80,256]{1,0:T(8,128)S(1)} collective-permute-done((f32[80,256]{1,0:T(8,128)S(1)}, f32[80,256]{1,0:T(8,128)S(1)}, u32[]{:S(2)}, u32[]{:S(2)}) %collective-permute-start.25) | collective-permute-done | bytes 81952 | tf_op jit(solution)/shard_map/ppermute | solution.py:65
  85.4 2.1 %shard_map.94 = (f32[4,192,256]{2,1,0:T(8,128)S(1)}, f32[32,4,256]{2,1,0:T(4,128)}) custom-call(s32[17]{0:T(128)S(1)} %get-tuple-element.105.meta, f32[112,256]{1,0:T(8,128)S(1)} %collective-permute-done.23.refs_0_, f32[80,256]{1,0:T(8,128)S(1)} %collective-permute-done.25.refs_1_, f32[768,256]{1,0:T(8,128)S(1)} %get-tuple-element.111.refs_2_, ...), custom_call_target="tpu_custom_call" | custom-call | flops 452984832 | bytes 1179648 | tf_op jit(solution)/shard_map/pallas_call | solution.py:266
  87.5 3.4 %all-to-all-start = ((f32[32,4,256]{2,1,0:T(4,128)}), f32[32,4,256]{2,1,0:T(4,128)S(1)}, u32[]{:S(2)}, u32[]{:S(2)}) async-start(f32[32,4,256]{2,1,0:T(4,128)} %get-tuple-element.116), calls=%async_computation | async-start | bytes 262144 | tf_op jit(solution)/shard_map/all_to_all | solution.py:510
  91.0 1.8 %collective-permute-start.29 = (f32[192,256]{1,0:T(8,128)S(1)}, f32[192,256]{1,0:T(8,128)S(1)}, u32[]{:S(2)}, u32[]{:S(2)}) collective-permute-start(f32[192,256]{1,0:T(8,128)S(1)} %fusion.7), channel_id=1, source_target_pairs={{0,2},{1,3},{2,0},{3,1},{4,6},{5,7},{6,4},{7,5},{8,10},{9,11},{10,... | collective-permute-start | bytes 589832 | tf_op jit(solution)/shard_map/ppermute | solution.py:512
  92.9 6.4 %all-to-all-done = f32[32,4,256]{2,1,0:T(4,128)S(1)} async-done(((f32[32,4,256]{2,1,0:T(4,128)}), f32[32,4,256]{2,1,0:T(4,128)S(1)}, u32[]{:S(2)}, u32[]{:S(2)}) %all-to-all-start) | async-done | bytes 131104 | tf_op jit(solution)/shard_map/all_to_all | solution.py:510
  (79 shorter events, 18.2 us)
Async XLA Ops:
  2.9 12.8 %collective-permute-start = (bf16[832,256]{1,0:T(8,128)(2,1)S(1)}, bf16[832,256]{1,0:T(8,128)(2,1)S(1)}, u32[]{:S(2)}, u32[]{:S(2)}) collective-permute-start(bf16[832,256]{1,0:T(8,128)(2,1)S(1)} %pad_maximum_fusion.1.refs_0_), channel_id=1, source_target_pairs={{0,8},{8,16},{16,24},{24,28},{28,20},{20,12},{12,4},{4,0},{1,9},{9... | collective-permute-start | bytes 1277960 | tf_op jit(solution)/shard_map/ppermute | solution.py:65
  6.0 11.6 %collective-permute-start.1 = (bf16[832,256]{1,0:T(8,128)(2,1)S(1)}, bf16[832,256]{1,0:T(8,128)(2,1)S(1)}, u32[]{:S(2)}, u32[]{:S(2)}) collective-permute-start(bf16[832,256]{1,0:T(8,128)(2,1)S(1)} %pad_maximum_fusion.1.refs_0_), channel_id=1, source_target_pairs={{8,0},{16,8},{24,16},{28,24},{20,28},{12,20},{4,12},{0,4},{9,1},{1... | collective-permute-start | bytes 1277960 | tf_op jit(solution)/shard_map/ppermute | solution.py:65
  7.2 21.8 %collective-permute-start.2 = (bf16[1,256,256]{2,1,0:T(8,128)(2,1)S(1)}, bf16[1,256,256]{2,1,0:T(8,128)(2,1)S(1)}, u32[]{:S(2)}, u32[]{:S(2)}) collective-permute-start(bf16[1,256,256]{2,1,0:T(8,128)(2,1)S(1)} %maximum_bitcast_fusion.refs_7_), channel_id=1, source_target_pairs={{0,2},{1,3},{2,0},{3,1},{4,6},{5,7},{6,4},{7,5},{8,10},{9,11},{10,... | collective-permute-start | bytes 393224 | tf_op jit(solution)/shard_map/ppermute | solution.py:340
  15.8 11.0 %collective-permute-start.3 = (bf16[832,256]{1,0:T(8,128)(2,1)S(1)}, bf16[832,256]{1,0:T(8,128)(2,1)S(1)}, u32[]{:S(2)}, u32[]{:S(2)}) collective-permute-start(bf16[832,256]{1,0:T(8,128)(2,1)S(1)} %collective-permute-done.refs_0_.refs_1_), channel_id=1, source_target_pairs={{0,8},{8,16},{16,24},{24,28},{28,20},{20,12},{12,4},{4,0},{1,9},{9... | collective-permute-start | bytes 1277960 | tf_op jit(solution)/shard_map/ppermute | solution.py:65
  17.6 10.7 %collective-permute-start.4 = (bf16[832,256]{1,0:T(8,128)(2,1)S(1)}, bf16[832,256]{1,0:T(8,128)(2,1)S(1)}, u32[]{:S(2)}, u32[]{:S(2)}) collective-permute-start(bf16[832,256]{1,0:T(8,128)(2,1)S(1)} %collective-permute-done.1.refs_1_.refs_2_), channel_id=1, source_target_pairs={{8,0},{16,8},{24,16},{28,24},{20,28},{12,20},{4,12},{0,4},{9,1},{1... | collective-permute-start | bytes 1277960 | tf_op jit(solution)/shard_map/ppermute | solution.py:65
  26.8 10.1 %collective-permute-start.6 = (bf16[832,256]{1,0:T(8,128)(2,1)S(1)}, bf16[832,256]{1,0:T(8,128)(2,1)S(1)}, u32[]{:S(2)}, u32[]{:S(2)}) collective-permute-start(bf16[832,256]{1,0:T(8,128)(2,1)S(1)} %collective-permute-done.3.refs_2_.refs_3_), channel_id=1, source_target_pairs={{0,8},{8,16},{16,24},{24,28},{28,20},{20,12},{12,4},{4,0},{1,9},{9... | collective-permute-start | bytes 1277960 | tf_op jit(solution)/shard_map/ppermute | solution.py:65
  28.3 9.5 %collective-permute-start.7 = (bf16[832,256]{1,0:T(8,128)(2,1)S(1)}, bf16[832,256]{1,0:T(8,128)(2,1)S(1)}, u32[]{:S(2)}, u32[]{:S(2)}) collective-permute-start(bf16[832,256]{1,0:T(8,128)(2,1)S(1)} %collective-permute-done.4.refs_3_.refs_4_), channel_id=1, source_target_pairs={{8,0},{16,8},{24,16},{28,24},{20,28},{12,20},{4,12},{0,4},{9,1},{1... | collective-permute-start | bytes 1277960 | tf_op jit(solution)/shard_map/ppermute | solution.py:65
  29.6 8.2 %collective-permute-start.5 = (bf16[2,256,256]{2,1,0:T(8,128)(2,1)S(1)}, bf16[2,256,256]{2,1,0:T(8,128)(2,1)S(1)}, u32[]{:S(2)}, u32[]{:S(2)}) collective-permute-start(bf16[2,256,256]{2,1,0:T(8,128)(2,1)S(1)} %shard_map.85.refs_10_), channel_id=1, source_target_pairs={{0,2},{1,3},{2,0},{3,1},{4,6},{5,7},{6,4},{7,5},{8,10},{9,11},{10,... | collective-permute-start | bytes 786440 | tf_op jit(solution)/shard_map/ppermute | solution.py:340
  37.8 5.0 %collective-permute-start.9 = (bf16[2,2,256,256]{3,2,1,0:T(8,128)(2,1)S(1)}, bf16[2,2,256,256]{3,2,1,0:T(8,128)(2,1)S(1)}, u32[]{:S(2)}, u32[]{:S(2)}) collective-permute-start(bf16[2,2,256,256]{3,2,1,0:T(8,128)(2,1)S(1)} %pad_maximum_fusion), channel_id=1, source_target_pairs={{0,1},{1,0},{2,3},{3,2},{4,5},{5,4},{6,7},{7,6},{8,9},{9,8},{10,11... | collective-permute-start | bytes 1572872 | tf_op jit(solution)/shard_map/ppermute | solution.py:334
  37.9 4.9 %collective-permute-start.8 = (bf16[2,1,256,256]{3,2,1,0:T(8,128)(2,1)S(1)}, bf16[2,1,256,256]{3,2,1,0:T(8,128)(2,1)S(1)}, u32[]{:S(2)}, u32[]{:S(2)}) collective-permute-start(bf16[2,1,256,256]{3,2,1,0:T(8,128)(2,1)S(1)} %pad_maximum_fusion.3), channel_id=1, source_target_pairs={{0,1},{1,0},{2,3},{3,2},{4,5},{5,4},{6,7},{7,6},{8,9},{9,8},{10,11... | collective-permute-start | bytes 786440 | tf_op jit(solution)/shard_map/ppermute | solution.py:334
  38.5 8.0 %collective-permute-start.11 = (bf16[384,256]{1,0:T(8,128)(2,1)S(1)}, bf16[384,256]{1,0:T(8,128)(2,1)S(1)}, u32[]{:S(2)}, u32[]{:S(2)}) collective-permute-start(bf16[384,256]{1,0:T(8,128)(2,1)S(1)} %slice.100), channel_id=1, source_target_pairs={{0,8},{8,16},{16,24},{24,28},{28,20},{20,12},{12,4},{4,0},{1,9},{9... | collective-permute-start | bytes 589832 | tf_op jit(solution)/shard_map/ppermute | solution.py:65
  40.1 6.6 %collective-permute-start.12 = (bf16[384,256]{1,0:T(8,128)(2,1)S(1)}, bf16[384,256]{1,0:T(8,128)(2,1)S(1)}, u32[]{:S(2)}, u32[]{:S(2)}) collective-permute-start(bf16[384,256]{1,0:T(8,128)(2,1)S(1)} %slice.101), channel_id=1, source_target_pairs={{8,0},{16,8},{24,16},{28,24},{20,28},{12,20},{4,12},{0,4},{9,1},{1... | collective-permute-start | bytes 589832 | tf_op jit(solution)/shard_map/ppermute | solution.py:65
  41.2 5.2 %collective-permute-start.10 = (bf16[1,256,256]{2,1,0:T(8,128)(2,1)S(1)}, bf16[1,256,256]{2,1,0:T(8,128)(2,1)S(1)}, u32[]{:S(2)}, u32[]{:S(2)}) collective-permute-start(bf16[1,256,256]{2,1,0:T(8,128)(2,1)S(1)} %shard_map.88.refs_2_), channel_id=1, source_target_pairs={{0,2},{1,3},{2,0},{3,1},{4,6},{5,7},{6,4},{7,5},{8,10},{9,11},{10,... | collective-permute-start | bytes 393224 | tf_op jit(solution)/shard_map/ppermute | solution.py:340
  46.8 1.6 %collective-permute-start.13 = (bf16[2,1,256,256]{3,2,1,0:T(8,128)(2,1)S(1)}, bf16[2,1,256,256]{3,2,1,0:T(8,128)(2,1)S(1)}, u32[]{:S(2)}, u32[]{:S(2)}) collective-permute-start(bf16[2,1,256,256]{3,2,1,0:T(8,128)(2,1)S(1)} %pad_maximum_fusion.4), channel_id=1, source_target_pairs={{0,1},{1,0},{2,3},{3,2},{4,5},{5,4},{6,7},{7,6},{8,9},{9,8},{10,11... | collective-permute-start | bytes 786440 | tf_op jit(solution)/shard_map/ppermute | solution.py:334
  51.4 1.5 %collective-permute-start.14 = (f32[192,256]{1,0:T(8,128)S(1)}, f32[192,256]{1,0:T(8,128)S(1)}, u32[]{:S(2)}, u32[]{:S(2)}) collective-permute-start(f32[192,256]{1,0:T(8,128)S(1)} %get-tuple-element.95), channel_id=1, source_target_pairs={{0,1},{1,0},{2,3},{3,2},{4,5},{5,4},{6,7},{7,6},{8,9},{9,8},{10,11... | collective-permute-start | bytes 589832 | tf_op jit(solution)/shard_map/ppermute | solution.py:435
  52.9 7.0 %collective-permute-start.17 = (f32[192,256]{1,0:T(8,128)S(1)}, f32[192,256]{1,0:T(8,128)S(1)}, u32[]{:S(2)}, u32[]{:S(2)}) collective-permute-start(f32[192,256]{1,0:T(8,128)S(1)} %add.59), channel_id=1, source_target_pairs={{0,2},{1,3},{2,0},{3,1},{4,6},{5,7},{6,4},{7,5},{8,10},{9,11},{10,... | collective-permute-start | bytes 589832 | tf_op jit(solution)/shard_map/ppermute | solution.py:449
  54.5 5.5 %copy-start.3 = (f32[1,1,1,192]{3,2,1,0:T(1,128)S(1)}, f32[1,1,1,192]{3,2,1,0:T(1,128)}, u32[]{:S(2)}) copy-start(f32[1,1,1,192]{3,2,1,0:T(1,128)} %param.9) | copy-start | bytes 2308
  56.7 1.4 %collective-permute-start.15 = (f32[96,256]{1,0:T(8,128)S(1)}, f32[96,256]{1,0:T(8,128)S(1)}, u32[]{:S(2)}, u32[]{:S(2)}) collective-permute-start(f32[96,256]{1,0:T(8,128)S(1)} %get-tuple-element.130), channel_id=1, source_target_pairs={{0,1},{1,0},{2,3},{3,2},{4,5},{5,4},{6,7},{7,6},{8,9},{9,8},{10,11... | collective-permute-start | bytes 294920 | tf_op jit(solution)/shard_map/ppermute | solution.py:464
  56.7 1.4 %collective-permute-start.16 = (f32[96,256]{1,0:T(8,128)S(1)}, f32[96,256]{1,0:T(8,128)S(1)}, u32[]{:S(2)}, u32[]{:S(2)}) collective-permute-start(f32[96,256]{1,0:T(8,128)S(1)} %get-tuple-element.131), channel_id=1, source_target_pairs={{0,1},{1,0},{2,3},{3,2},{4,5},{5,4},{6,7},{7,6},{8,9},{9,8},{10,11... | collective-permute-start | bytes 294920 | tf_op jit(solution)/shard_map/ppermute | solution.py:464
  60.0 6.2 %collective-permute-start.18 = (f32[192,256]{1,0:T(8,128)S(1)}, f32[192,256]{1,0:T(8,128)S(1)}, u32[]{:S(2)}, u32[]{:S(2)}) collective-permute-start(f32[192,256]{1,0:T(8,128)S(1)} %fusion.9.refs_0_.refs_5_), channel_id=1, source_target_pairs={{0,8},{8,16},{16,24},{24,28},{28,20},{20,12},{12,4},{4,0},{1,9},{9... | collective-permute-start | bytes 589832 | tf_op jit(solution)/shard_map/ppermute | solution.py:65
  61.7 6.1 %collective-permute-start.20 = (f32[192,256]{1,0:T(8,128)S(1)}, f32[192,256]{1,0:T(8,128)S(1)}, u32[]{:S(2)}, u32[]{:S(2)}) collective-permute-start(f32[192,256]{1,0:T(8,128)S(1)} %fusion.9.refs_0_.refs_5_), channel_id=1, source_target_pairs={{8,0},{16,8},{24,16},{28,24},{20,28},{12,20},{4,12},{0,4},{9,1},{1... | collective-permute-start | bytes 589832 | tf_op jit(solution)/shard_map/ppermute | solution.py:65
  62.1 6.1 %collective-permute-start.26 = (f32[192,256]{1,0:T(8,128)S(1)}, f32[192,256]{1,0:T(8,128)S(1)}, u32[]{:S(2)}, u32[]{:S(2)}) collective-permute-start(f32[192,256]{1,0:T(8,128)S(1)} %fusion.9.refs_0_.refs_5_), channel_id=1, source_target_pairs={{0,2},{1,3},{2,0},{3,1},{4,6},{5,7},{6,4},{7,5},{8,10},{9,11},{10,... | collective-permute-start | bytes 589832 | tf_op jit(solution)/shard_map/ppermute | solution.py:466
  66.2 5.8 %collective-permute-start.19 = (f32[192,256]{1,0:T(8,128)S(1)}, f32[192,256]{1,0:T(8,128)S(1)}, u32[]{:S(2)}, u32[]{:S(2)}) collective-permute-start(f32[192,256]{1,0:T(8,128)S(1)} %collective-permute-done.18.refs_1_), channel_id=1, source_target_pairs={{0,8},{8,16},{16,24},{24,28},{28,20},{20,12},{12,4},{4,0},{1,9},{9... | collective-permute-start | bytes 589832 | tf_op jit(solution)/shard_map/ppermute | solution.py:65
  67.8 5.8 %collective-permute-start.21 = (f32[192,256]{1,0:T(8,128)S(1)}, f32[192,256]{1,0:T(8,128)S(1)}, u32[]{:S(2)}, u32[]{:S(2)}) collective-permute-start(f32[192,256]{1,0:T(8,128)S(1)} %collective-permute-done.20.refs_2_), channel_id=1, source_target_pairs={{8,0},{16,8},{24,16},{28,24},{20,28},{12,20},{4,12},{0,4},{9,1},{1... | collective-permute-start | bytes 589832 | tf_op jit(solution)/shard_map/ppermute | solution.py:65
  68.3 15.8 %collective-permute-start.27 = (f32[2,192,256]{2,1,0:T(8,128)S(1)}, f32[2,192,256]{2,1,0:T(8,128)S(1)}, u32[]{:S(2)}, u32[]{:S(2)}) collective-permute-start(f32[2,192,256]{2,1,0:T(8,128)S(1)} %pad_maximum_fusion.2), channel_id=1, source_target_pairs={{0,1},{1,0},{2,3},{3,2},{4,5},{5,4},{6,7},{7,6},{8,9},{9,8},{10,11... | collective-permute-start | bytes 1179656 | tf_op jit(solution)/shard_map/ppermute | solution.py:467
  72.0 5.7 %collective-permute-start.22 = (f32[192,256]{1,0:T(8,128)S(1)}, f32[192,256]{1,0:T(8,128)S(1)}, u32[]{:S(2)}, u32[]{:S(2)}) collective-permute-start(f32[192,256]{1,0:T(8,128)S(1)} %collective-permute-done.19.refs_3_), channel_id=1, source_target_pairs={{0,8},{8,16},{16,24},{24,28},{28,20},{20,12},{12,4},{4,0},{1,9},{9... | collective-permute-start | bytes 589832 | tf_op jit(solution)/shard_map/ppermute | solution.py:65
  73.6 5.7 %collective-permute-start.24 = (f32[192,256]{1,0:T(8,128)S(1)}, f32[192,256]{1,0:T(8,128)S(1)}, u32[]{:S(2)}, u32[]{:S(2)}) collective-permute-start(f32[192,256]{1,0:T(8,128)S(1)} %collective-permute-done.21.refs_4_), channel_id=1, source_target_pairs={{8,0},{16,8},{24,16},{28,24},{20,28},{12,20},{4,12},{0,4},{9,1},{1... | collective-permute-start | bytes 589832 | tf_op jit(solution)/shard_map/ppermute | solution.py:65
  79.2 6.1 %collective-permute-start.23 = (f32[112,256]{1,0:T(8,128)S(1)}, f32[112,256]{1,0:T(8,128)S(1)}, u32[]{:S(2)}, u32[]{:S(2)}) collective-permute-start(f32[112,256]{1,0:T(8,128)S(1)} %slice.102), channel_id=1, source_target_pairs={{0,8},{8,16},{16,24},{24,28},{28,20},{20,12},{12,4},{4,0},{1,9},{9... | collective-permute-start | bytes 344072 | tf_op jit(solution)/shard_map/ppermute | solution.py:65
  80.9 4.5 %collective-permute-start.25 = (f32[80,256]{1,0:T(8,128)S(1)}, f32[80,256]{1,0:T(8,128)S(1)}, u32[]{:S(2)}, u32[]{:S(2)}) collective-permute-start(f32[80,256]{1,0:T(8,128)S(1)} %slice.103), channel_id=1, source_target_pairs={{8,0},{16,8},{24,16},{28,24},{20,28},{12,20},{4,12},{0,4},{9,1},{1... | collective-permute-start | bytes 245768 | tf_op jit(solution)/shard_map/ppermute | solution.py:65
  87.5 3.5 %collective-permute-start.28 = (f32[2,192,256]{2,1,0:T(8,128)S(1)}, f32[2,192,256]{2,1,0:T(8,128)S(1)}, u32[]{:S(2)}, u32[]{:S(2)}) collective-permute-start(f32[2,192,256]{2,1,0:T(8,128)S(1)} %slice.92), channel_id=1, source_target_pairs={{0,1},{1,0},{2,3},{3,2},{4,5},{5,4},{6,7},{7,6},{8,9},{9,8},{10,11... | collective-permute-start | bytes 1179656 | tf_op jit(solution)/shard_map/ppermute | solution.py:511
  87.5 11.7 %all-to-all-start = ((f32[32,4,256]{2,1,0:T(4,128)}), f32[32,4,256]{2,1,0:T(4,128)S(1)}, u32[]{:S(2)}, u32[]{:S(2)}) async-start(f32[32,4,256]{2,1,0:T(4,128)} %get-tuple-element.116), calls=%async_computation | async-start | bytes 262144 | tf_op jit(solution)/shard_map/all_to_all | solution.py:510
  91.0 8.4 %collective-permute-start.29 = (f32[192,256]{1,0:T(8,128)S(1)}, f32[192,256]{1,0:T(8,128)S(1)}, u32[]{:S(2)}, u32[]{:S(2)}) collective-permute-start(f32[192,256]{1,0:T(8,128)S(1)} %fusion.7), channel_id=1, source_target_pairs={{0,2},{1,3},{2,0},{3,1},{4,6},{5,7},{6,4},{7,5},{8,10},{9,11},{10,... | collective-permute-start | bytes 589832 | tf_op jit(solution)/shard_map/ppermute | solution.py:512
  (3 other events, 5.6 us)

commit v8 on v7

--- a/solution.py
+++ b/solution.py
@@ -222,44 +222,48 @@
         copy.wait()
 
 
+def weighted(parts, others):
+    return sum(jnp.sum(a * b, axis=0, keepdims=True) for a, b in zip(parts, others))
+
+
 def partial_kernel(sizes, meta, *refs):
-    n, data_count, piece = sizes
+    n, data_count, piece, block = sizes
     shard_refs = refs[: n - 1]
-    tile_ref, start_ref, total_ref, sums_ref, side = refs[n - 1 :]
+    tile_ref, start_ref, near_ref, far_ref, penalty_ref, total_ref, sums_ref, far_high, far_low, side = refs[n - 1 :]
     for index in range(n - 1):
         base = pl.multiple_of((meta[n + index] * data_count + meta[index]) * piece, 8)
         side[pl.ds(base, piece), :] = shard_refs[index][...]
-    far = pl.multiple_of((meta[2 * n - 1] * data_count + meta[n - 1]) * piece, 8)
-    side[pl.ds(far, piece), :] = jnp.zeros((piece, side.shape[1]), jnp.float32)
-    total_ref[...] = product(split(tile_ref[...]), split(side[...]))
+    base = (meta[2 * n - 1] * data_count + meta[n - 1]) * piece
+    side[pl.ds(pl.multiple_of(base, 8), piece), :] = jnp.zeros((piece, side.shape[1]), jnp.float32)
+    total = product(split(tile_ref[...]), split(side[...]))
     own, start = shard_refs[0][...], start_ref[...]
-    early = [jnp.sum(a * b, axis=0, keepdims=True) for a, b in ((start, start), (start, own), (own, own))]
-    sums_ref[...] = jnp.concatenate(early, axis=0)
+    others = [near_ref[1], far_ref[...], near_ref[0], own]
+    parts = [total[index * piece : (index + 1) * piece] for index in range(len(ORDER))]
+    parts[-1] = parts[-1] + penalty_ref[...] * own
+    for index, part in enumerate(parts):
+        total_ref[index] = part
+    sums = [weighted([a], [b]) for a, b in ((start, start), (start, own), (own, own))]
+    sums_ref[...] = jnp.concatenate(sums + [weighted(parts, others)], axis=0)
+    lanes = pl.ds(pl.multiple_of(base // block * block, 128), block)
+    for place in range(block // piece):
+
+        @pl.when(base % block == place * piece)
+        def _():
+            far_high[...], far_low[...] = split(tile_ref[:, lanes][:, place * piece : (place + 1) * piece])
 
 
 def image_kernel(sizes, meta, *refs):
-    n, data_count, piece, block = sizes
-    low_ref, high_ref, total_ref, tile_ref, early_ref = refs[:5]
-    own_ref, near_ref, far_ref, penalty_ref, out_ref, sums_ref, side = refs[5:]
-    base = (meta[2 * n - 1] * data_count + meta[n - 1]) * piece
-    lanes = pl.ds(pl.multiple_of(base // block * block, 128), block)
-    base = pl.multiple_of(base % block, 8)
-    half = low_ref.shape[0]
-    side[...] = jnp.zeros_like(side)
-    side[pl.ds(base, half), :] = low_ref[...]
-    side[pl.ds(pl.multiple_of(base + half, 8), piece - half), :] = high_ref[...]
-    total = total_ref[...] + product(split(tile_ref[:, lanes]), split(side[...]))
-    own = own_ref[...]
-    others = [near_ref[1], far_ref[...], near_ref[0], own]
-    late = jnp.zeros((1, own.shape[1]), jnp.float32)
+    piece = sizes
+    low_ref, high_ref, total_ref, far_high, far_low, early_ref, own_ref, near_ref, far_ref, out_ref, sums_ref = refs
+    side = jnp.concatenate([low_ref[...], high_ref[...]], axis=0)
+    value = product((far_high[...], far_low[...]), split(side))
+    others = [near_ref[1], far_ref[...], near_ref[0], own_ref[...]]
+    parts = [value[index * piece : (index + 1) * piece] for index in range(len(ORDER))]
+    early = early_ref[...]
+    sums = jnp.concatenate([early[:3], early[3:] + weighted(parts, others)], axis=0)
+    sums_ref[...] = jnp.broadcast_to(sums[None], sums_ref.shape)
     for index, j in enumerate(ORDER):
-        value = total[index * piece : (index + 1) * piece]
-        if j == 0:
-            value = value + penalty_ref[...] * own
-        out_ref[(3, 1, 2, 0).index(j)] = value
-        late = late + jnp.sum(value * others[index], axis=0, keepdims=True)
-    sums = jnp.concatenate([early_ref[...], late], axis=0)
-    sums_ref[...] = jnp.broadcast_to(sums[None], sums_ref.shape)
+        out_ref[(3, 1, 2, 0).index(j)] = total_ref[index] + parts[index]
 
 
 def call(body, meta, inputs, in_specs, out_specs, out_shape, scratch, vmem, flops, read, aliases={}):
@@ -478,13 +482,15 @@
         if step == ring.far - 1:
             *arrived, tile = lax.optimization_barrier((*arrived, tile))
         images += arrived
-    total, early_sums = call(
-        functools.partial(partial_kernel, (n, data_count, piece)),
+    part_shape = jax.ShapeDtypeStruct((tcol_count, piece, heads), f32)
+    far_shape = jax.ShapeDtypeStruct((tile_rows, piece), bf16)
+    total, early_sums, far_high, far_low = call(
+        functools.partial(partial_kernel, (n, data_count, piece, far_block)),
         image_meta,
-        [*images[:-2], tile, start],
-        [VMEM] * (n + 1),
-        [VMEM] * 2,
-        [jax.ShapeDtypeStruct((tile_rows, heads), f32), jax.ShapeDtypeStruct((3, heads), f32)],
+        [*images[:-2], tile, start, near_images, far_image, penalty_rows],
+        [VMEM] * (n + 4),
+        [VMEM] * 4,
+        [part_shape, jax.ShapeDtypeStruct((4, heads), f32), far_shape, far_shape],
         [pltpu.VMEM((tile_columns, heads), f32)],
         IMAGE_BYTES,
         6 * tile_rows * tile_columns * heads,
@@ -492,19 +498,16 @@
     )
     axes = ("dp", "trow", "tcol")
     second, sums = call(
-        functools.partial(image_kernel, (n, data_count, piece, far_block)),
+        functools.partial(image_kernel, piece),
         image_meta,
-        [*images[-2:], total, tile, early_sums, image, near_images, far_image, penalty_rows],
+        [*images[-2:], total, far_high, far_low, early_sums, image, near_images, far_image],
         [VMEM] * 9,
         [VMEM] * 2,
-        [
-            jax.ShapeDtypeStruct((tcol_count, piece, heads), f32),
-            jax.ShapeDtypeStruct((n * tcol_count, 4, heads), f32),
-        ],
-        [pltpu.VMEM((far_block, heads), f32)],
+        [part_shape, jax.ShapeDtypeStruct((n * tcol_count, 4, heads), f32)],
+        [],
         IMAGE_BYTES,
-        6 * tile_rows * far_block * heads,
-        4 * tile_rows * far_block,
+        6 * tile_rows * piece * heads,
+        4 * tile_rows * piece,
     )
     sums, second = lax.optimization_barrier((sums, second))
     sums = lax.all_to_all(sums, axes, split_axis=0, concat_axis=0, tiled=True)

time: 101 us -> 100 us (0.990)
  no operation moved by 1% of the time
where the time goes in v8:
time: 100 us
  waiting for transfers between devices  36.5 us (36%)
  starting transfers between devices  32.4 us (32%)
  Pallas kernels  16.6 us (17%)
  local copies, waits for them, and re-layouts  10.3 us (10%)
  between operations  2.9 us (3%)
  other arithmetic  1.39 us (1%)
    ppermute x8, waiting for transfers between devices, move(): lax.ppermute(ahead, axes, self.ahead)  21.4 us
    pallas_call x10, Pallas kernels, call(): pl.pallas_call(body, grid_spec=pltpu.PrefetchScalarGridSpec(num_scalar_pr...  16.6 us
    ppermute x8, starting transfers between devices, move(): lax.ppermute(ahead, axes, self.ahead)  14.4 us
    unnamed x10, local copies, waits for them, and re-layouts  6.83 us
    all_to_all x1, waiting for transfers between devices, shards(): sums = lax.all_to_all(sums, axes, split_axis=0, concat_axis=0, tiled=True)  6.35 us
    ppermute x3, starting transfers between devices, open_groups(): lax.ppermute(mine, 'tcol', swap(tcol_count, 2))  5.01 us
    ppermute x8, waiting for transfers between devices, move(): lax.ppermute(back, axes, self.back)  3.75 us
    all_to_all x1, starting transfers between devices, shards(): sums = lax.all_to_all(sums, axes, split_axis=0, concat_axis=0, tiled=True)  3.44 us
  transfers between devices with their start and end apart: 31, of which 17 were waited for; matrix products, arithmetic and copies ran while one was open for 4% of the time, Pallas kernels for 12%

profile of v8, /device:TPU:0, one launch (start us, length us, event | category | flops | bytes accessed | tf_op | source)
XLA Modules:
  0.0 100.0 jit_solution(5065652545525357072)
XLA Ops:
  2.9 3.1 %collective-permute-start = (bf16[832,256]{1,0:T(8,128)(2,1)S(1)}, bf16[832,256]{1,0:T(8,128)(2,1)S(1)}, u32[]{:S(2)}, u32[]{:S(2)}) collective-permute-start(bf16[832,256]{1,0:T(8,128)(2,1)S(1)} %pad_maximum_fusion.1.refs_0_), channel_id=1, source_target_pairs={{0,8},{8,16},{16,24},{24,28},{28,20},{20,12},{12,4},{4,0},{1,9},{9... | collective-permute-start | bytes 1277960 | tf_op jit(solution)/shard_map/ppermute | solution.py:65
  7.2 2.0 %collective-permute-start.2 = (bf16[1,256,256]{2,1,0:T(8,128)(2,1)S(1)}, bf16[1,256,256]{2,1,0:T(8,128)(2,1)S(1)}, u32[]{:S(2)}, u32[]{:S(2)}) collective-permute-start(bf16[1,256,256]{2,1,0:T(8,128)(2,1)S(1)} %maximum_bitcast_fusion.refs_7_), channel_id=1, source_target_pairs={{0,2},{1,3},{2,0},{3,1},{4,6},{5,7},{6,4},{7,5},{8,10},{9,11},{10,... | collective-permute-start | bytes 393224 | tf_op jit(solution)/shard_map/ppermute | solution.py:344
  9.2 1.3 %dynamic_slice.12 = s32[1,1]{1,0:T(1,128)} dynamic-slice(s32[4,2]{1,0:T(4,128)} %constant.37.clone, s32[]{:T(128)S(6)} %select_n.15, s32[]{:T(128)S(6)} %select_n.16), dynamic_slice_sizes={1,1} | dynamic-slice | bytes 12 | tf_op jit(solution)/shard_map/dynamic_slice | solution.py:302
  13.1 2.7 %collective-permute-done.refs_0_.refs_1_ = bf16[832,256]{1,0:T(8,128)(2,1)S(1)} collective-permute-done((bf16[832,256]{1,0:T(8,128)(2,1)S(1)}, bf16[832,256]{1,0:T(8,128)(2,1)S(1)}, u32[]{:S(2)}, u32[]{:S(2)}) %collective-permute-start) | collective-permute-done | bytes 426016 | tf_op jit(solution)/shard_map/ppermute | solution.py:65
  15.8 1.8 %collective-permute-start.3 = (bf16[832,256]{1,0:T(8,128)(2,1)S(1)}, bf16[832,256]{1,0:T(8,128)(2,1)S(1)}, u32[]{:S(2)}, u32[]{:S(2)}) collective-permute-start(bf16[832,256]{1,0:T(8,128)(2,1)S(1)} %collective-permute-done.refs_0_.refs_1_), channel_id=1, source_target_pairs={{0,8},{8,16},{16,24},{24,28},{28,20},{20,12},{12,4},{4,0},{1,9},{9... | collective-permute-start | bytes 1277960 | tf_op jit(solution)/shard_map/ppermute | solution.py:65
  17.9 8.9 %collective-permute-done.3.refs_2_.refs_3_ = bf16[832,256]{1,0:T(8,128)(2,1)S(1)} collective-permute-done((bf16[832,256]{1,0:T(8,128)(2,1)S(1)}, bf16[832,256]{1,0:T(8,128)(2,1)S(1)}, u32[]{:S(2)}, u32[]{:S(2)}) %collective-permute-start.3) | collective-permute-done | bytes 426016 | tf_op jit(solution)/shard_map/ppermute | solution.py:65
  26.8 1.5 %collective-permute-start.6 = (bf16[832,256]{1,0:T(8,128)(2,1)S(1)}, bf16[832,256]{1,0:T(8,128)(2,1)S(1)}, u32[]{:S(2)}, u32[]{:S(2)}) collective-permute-start(bf16[832,256]{1,0:T(8,128)(2,1)S(1)} %collective-permute-done.3.refs_2_.refs_3_), channel_id=1, source_target_pairs={{0,8},{8,16},{16,24},{24,28},{28,20},{20,12},{12,4},{4,0},{1,9},{9... | collective-permute-start | bytes 1277960 | tf_op jit(solution)/shard_map/ppermute | solution.py:65
  29.6 1.5 %collective-permute-start.5 = (bf16[2,256,256]{2,1,0:T(8,128)(2,1)S(1)}, bf16[2,256,256]{2,1,0:T(8,128)(2,1)S(1)}, u32[]{:S(2)}, u32[]{:S(2)}) collective-permute-start(bf16[2,256,256]{2,1,0:T(8,128)(2,1)S(1)} %shard_map.85.refs_10_), channel_id=1, source_target_pairs={{0,2},{1,3},{2,0},{3,1},{4,6},{5,7},{6,4},{7,5},{8,10},{9,11},{10,... | collective-permute-start | bytes 786440 | tf_op jit(solution)/shard_map/ppermute | solution.py:344
  31.1 2.3 %copy-done.2 = f32[4,1,1,192,1536]{4,3,2,1,0:T(8,128)S(1)} copy-done((f32[4,1,1,192,1536]{4,3,2,1,0:T(8,128)S(1)}, f32[4,1,1,192,1536]{4,3,2,1,0:T(8,128)}, u32[]{:S(2)}) %copy-start.2) | copy-done | bytes 4718616
  33.9 2.9 %collective-permute-done.6.refs_5_.refs_2_ = bf16[832,256]{1,0:T(8,128)(2,1)S(1)} collective-permute-done((bf16[832,256]{1,0:T(8,128)(2,1)S(1)}, bf16[832,256]{1,0:T(8,128)(2,1)S(1)}, u32[]{:S(2)}, u32[]{:S(2)}) %collective-permute-start.6) | collective-permute-done | bytes 426016 | tf_op jit(solution)/shard_map/ppermute | solution.py:65
  38.5 1.6 %collective-permute-start.11 = (bf16[384,256]{1,0:T(8,128)(2,1)S(1)}, bf16[384,256]{1,0:T(8,128)(2,1)S(1)}, u32[]{:S(2)}, u32[]{:S(2)}) collective-permute-start(bf16[384,256]{1,0:T(8,128)(2,1)S(1)} %slice.100), channel_id=1, source_target_pairs={{0,8},{8,16},{16,24},{24,28},{28,20},{20,12},{12,4},{4,0},{1,9},{9... | collective-permute-start | bytes 589832 | tf_op jit(solution)/shard_map/ppermute | solution.py:65
  41.2 1.6 %collective-permute-start.10 = (bf16[1,256,256]{2,1,0:T(8,128)(2,1)S(1)}, bf16[1,256,256]{2,1,0:T(8,128)(2,1)S(1)}, u32[]{:S(2)}, u32[]{:S(2)}) collective-permute-start(bf16[1,256,256]{2,1,0:T(8,128)(2,1)S(1)} %shard_map.88.refs_2_), channel_id=1, source_target_pairs={{0,2},{1,3},{2,0},{3,1},{4,6},{5,7},{6,4},{7,5},{8,10},{9,11},{10,... | collective-permute-start | bytes 393224 | tf_op jit(solution)/shard_map/ppermute | solution.py:344
  42.8 3.7 %shard_map.87 = (f32[384,1536]{1,0:T(8,128)S(1)}, f32[384,1536]{1,0:T(8,128)S(1)}, f32[1536,256]{1,0:T(8,128)S(1)}, bf16[1536,1024]{1,0:T(8,128)(2,1)S(1)}, bf16...) custom-call(s32[17]{0:T(128)S(1)} %get-tuple-element.63.meta, bf16[832,256]{1,0:T(8,128)(2,1)S(1)} %pad_maximum_fusion.1.refs_0_, ...), custom_call_target="tpu_custom_call" | custom-call | flops 1811939328 | bytes 9437184 | tf_op jit(solution)/shard_map/pallas_call | solution.py:270
  46.8 1.5 %collective-permute-done.13.refs_4_ = bf16[2,1,256,256]{3,2,1,0:T(8,128)(2,1)S(1)} collective-permute-done((bf16[2,1,256,256]{3,2,1,0:T(8,128)(2,1)S(1)}, bf16[2,1,256,256]{3,2,1,0:T(8,128)(2,1)S(1)}, u32[]{:S(2)}, u32[]{:S(2)}) %collective-permute-start.13) | collective-permute-done | bytes 262176 | tf_op jit(solution)/shard_map/ppermute | solution.py:338
  48.4 3.0 %shard_map.89 = (f32[192,256]{1,0:T(8,128)S(1)}, f32[768,1536]{1,0:T(8,128)}, f32[384,1536]{1,0:T(8,128)S(1)}, bf16[1536,256]{1,0:T(8,128)(2,1)S(1)}, bf16[1536,...) custom-call(s32[17]{0:T(128)S(1)} %get-tuple-element.63.meta, ...), custom_call_target="tpu_custom_call" | custom-call | flops 754974720 | bytes 4718592 | tf_op jit(solution)/shard_map/pallas_call | solution.py:270
  52.9 1.6 %collective-permute-start.17 = (f32[192,256]{1,0:T(8,128)S(1)}, f32[192,256]{1,0:T(8,128)S(1)}, u32[]{:S(2)}, u32[]{:S(2)}) collective-permute-start(f32[192,256]{1,0:T(8,128)S(1)} %add.59), channel_id=1, source_target_pairs={{0,2},{1,3},{2,0},{3,1},{4,6},{5,7},{6,4},{7,5},{8,10},{9,11},{10,... | collective-permute-start | bytes 589832 | tf_op jit(solution)/shard_map/ppermute | solution.py:453
  54.5 2.1 %shard_map.91 = (f32[768,1536]{1,0:T(8,128)}, f32[2,192,256]{2,1,0:T(8,128)S(1)}) custom-call(s32[1]{0:T(128)} %bitcast.meta, f32[384,1536]{1,0:T(8,128)S(1)} %get-tuple-element.99.refs_0_, bf16[1536,256]{1,0:T(8,128)(2,1)S(1)} %get-tuple-element.100.refs_1_, ...), custom_call_target="tpu_custom_call", output_to_operand_aliasing={{0}: (6, {})} | custom-call | flops 1207959552 | bytes 4718592 | tf_op jit(solution)/shard_map/pallas_call | solution.py:270
  58.2 1.8 %collective-permute-done.17 = f32[192,256]{1,0:T(8,128)S(1)} collective-permute-done((f32[192,256]{1,0:T(8,128)S(1)}, f32[192,256]{1,0:T(8,128)S(1)}, u32[]{:S(2)}, u32[]{:S(2)}) %collective-permute-start.17) | collective-permute-done | bytes 196640 | tf_op jit(solution)/shard_map/ppermute | solution.py:453
  60.0 1.6 %collective-permute-start.18 = (f32[192,256]{1,0:T(8,128)S(1)}, f32[192,256]{1,0:T(8,128)S(1)}, u32[]{:S(2)}, u32[]{:S(2)}) collective-permute-start(f32[192,256]{1,0:T(8,128)S(1)} %fusion.9.refs_0_.refs_6_), channel_id=1, source_target_pairs={{0,8},{8,16},{16,24},{24,28},{28,20},{20,12},{12,4},{4,0},{1,9},{9... | collective-permute-start | bytes 589832 | tf_op jit(solution)/shard_map/ppermute | solution.py:65
  62.1 1.5 %collective-permute-start.26 = (f32[192,256]{1,0:T(8,128)S(1)}, f32[192,256]{1,0:T(8,128)S(1)}, u32[]{:S(2)}, u32[]{:S(2)}) collective-permute-start(f32[192,256]{1,0:T(8,128)S(1)} %fusion.9.refs_0_.refs_6_), channel_id=1, source_target_pairs={{0,2},{1,3},{2,0},{3,1},{4,6},{5,7},{6,4},{7,5},{8,10},{9,11},{10,... | collective-permute-start | bytes 589832 | tf_op jit(solution)/shard_map/ppermute | solution.py:470
  63.6 2.6 %collective-permute-done.18.refs_1_ = f32[192,256]{1,0:T(8,128)S(1)} collective-permute-done((f32[192,256]{1,0:T(8,128)S(1)}, f32[192,256]{1,0:T(8,128)S(1)}, u32[]{:S(2)}, u32[]{:S(2)}) %collective-permute-start.18) | collective-permute-done | bytes 196640 | tf_op jit(solution)/shard_map/ppermute | solution.py:65
  66.2 1.6 %collective-permute-start.19 = (f32[192,256]{1,0:T(8,128)S(1)}, f32[192,256]{1,0:T(8,128)S(1)}, u32[]{:S(2)}, u32[]{:S(2)}) collective-permute-start(f32[192,256]{1,0:T(8,128)S(1)} %collective-permute-done.18.refs_1_), channel_id=1, source_target_pairs={{0,8},{8,16},{16,24},{24,28},{28,20},{20,12},{12,4},{4,0},{1,9},{9... | collective-permute-start | bytes 589832 | tf_op jit(solution)/shard_map/ppermute | solution.py:65
  68.4 3.6 %collective-permute-done.19.refs_3_ = f32[192,256]{1,0:T(8,128)S(1)} collective-permute-done((f32[192,256]{1,0:T(8,128)S(1)}, f32[192,256]{1,0:T(8,128)S(1)}, u32[]{:S(2)}, u32[]{:S(2)}) %collective-permute-start.19) | collective-permute-done | bytes 196640 | tf_op jit(solution)/shard_map/ppermute | solution.py:65
  72.0 1.6 %collective-permute-start.22 = (f32[192,256]{1,0:T(8,128)S(1)}, f32[192,256]{1,0:T(8,128)S(1)}, u32[]{:S(2)}, u32[]{:S(2)}) collective-permute-start(f32[192,256]{1,0:T(8,128)S(1)} %collective-permute-done.19.refs_3_), channel_id=1, source_target_pairs={{0,8},{8,16},{16,24},{24,28},{28,20},{20,12},{12,4},{4,0},{1,9},{9... | collective-permute-start | bytes 589832 | tf_op jit(solution)/shard_map/ppermute | solution.py:65
  74.1 2.3 %copy-done.1 = f32[768,1536]{1,0:T(8,128)S(1)} copy-done((f32[768,1536]{1,0:T(8,128)S(1)}, f32[768,1536]{1,0:T(8,128)}, u32[]{:S(2)}) %copy-start.1) | copy-done | bytes 4718616
  77.6 1.6 %collective-permute-done.24.refs_6_ = f32[192,256]{1,0:T(8,128)S(1)} collective-permute-done((f32[192,256]{1,0:T(8,128)S(1)}, f32[192,256]{1,0:T(8,128)S(1)}, u32[]{:S(2)}, u32[]{:S(2)}) %collective-permute-start.24) | collective-permute-done | bytes 196640 | tf_op jit(solution)/shard_map/ppermute | solution.py:65
  79.2 1.6 %collective-permute-start.23 = (f32[112,256]{1,0:T(8,128)S(1)}, f32[112,256]{1,0:T(8,128)S(1)}, u32[]{:S(2)}, u32[]{:S(2)}) collective-permute-start(f32[112,256]{1,0:T(8,128)S(1)} %slice.102), channel_id=1, source_target_pairs={{0,8},{8,16},{16,24},{24,28},{28,20},{20,12},{12,4},{4,0},{1,9},{9... | collective-permute-start | bytes 344072 | tf_op jit(solution)/shard_map/ppermute | solution.py:65
  81.3 3.0 %shard_map.93 = (f32[4,192,256]{2,1,0:T(8,128)S(1)}, f32[4,256]{1,0:T(4,128)S(1)}, bf16[768,192]{1,0:T(8,128)(2,1)S(1)}, bf16[768,192]{1,0:T(8,128)(2,1)S(1)}) custom-call(s32[17]{0:T(128)S(1)} %get-tuple-element.107.meta, f32[192,256]{1,0:T(8,128)S(1)} %fusion.9.refs_0_.refs_6_, f32[192,256]{1,0:T(8,128)S(1)} %collective-permute-done.18.refs_1_, ...), custom_call_target="tpu_custom_call" | custom-call | flops 1811939328 | bytes 4718592 | tf_op jit(solution)/shard_map/pallas_call | solution.py:270
  85.4 1.7 %shard_map.94 = (f32[4,192,256]{2,1,0:T(8,128)S(1)}, f32[32,4,256]{2,1,0:T(4,128)}) custom-call(s32[17]{0:T(128)S(1)} %get-tuple-element.107.meta, f32[112,256]{1,0:T(8,128)S(1)} %collective-permute-done.23.refs_0_, f32[80,256]{1,0:T(8,128)S(1)} %collective-permute-done.25.refs_1_, f32[4,192,256]{2,1,0:T(8,128)S(1)} %get-tuple-element.113.refs_2_, ...), custom_call_target="tpu_custom_call" | custom-call | flops 226492416 | bytes 589824 | tf_op jit(solution)/shard_map/pallas_call | solution.py:270
  87.2 3.4 %all-to-all-start = ((f32[32,4,256]{2,1,0:T(4,128)}), f32[32,4,256]{2,1,0:T(4,128)S(1)}, u32[]{:S(2)}, u32[]{:S(2)}) async-start(f32[32,4,256]{2,1,0:T(4,128)} %get-tuple-element.120), calls=%async_computation | async-start | bytes 262144 | tf_op jit(solution)/shard_map/all_to_all | solution.py:513
  90.7 1.8 %collective-permute-start.29 = (f32[192,256]{1,0:T(8,128)S(1)}, f32[192,256]{1,0:T(8,128)S(1)}, u32[]{:S(2)}, u32[]{:S(2)}) collective-permute-start(f32[192,256]{1,0:T(8,128)S(1)} %fusion.7), channel_id=1, source_target_pairs={{0,2},{1,3},{2,0},{3,1},{4,6},{5,7},{6,4},{7,5},{8,10},{9,11},{10,... | collective-permute-start | bytes 589832 | tf_op jit(solution)/shard_map/ppermute | solution.py:515
  92.5 6.4 %all-to-all-done = f32[32,4,256]{2,1,0:T(4,128)S(1)} async-done(((f32[32,4,256]{2,1,0:T(4,128)}), f32[32,4,256]{2,1,0:T(4,128)S(1)}, u32[]{:S(2)}, u32[]{:S(2)}) %all-to-all-start) | async-done | bytes 131104 | tf_op jit(solution)/shard_map/all_to_all | solution.py:513
  (79 shorter events, 18.0 us)
Async XLA Ops:
  2.9 12.8 %collective-permute-start = (bf16[832,256]{1,0:T(8,128)(2,1)S(1)}, bf16[832,256]{1,0:T(8,128)(2,1)S(1)}, u32[]{:S(2)}, u32[]{:S(2)}) collective-permute-start(bf16[832,256]{1,0:T(8,128)(2,1)S(1)} %pad_maximum_fusion.1.refs_0_), channel_id=1, source_target_pairs={{0,8},{8,16},{16,24},{24,28},{28,20},{20,12},{12,4},{4,0},{1,9},{9... | collective-permute-start | bytes 1277960 | tf_op jit(solution)/shard_map/ppermute | solution.py:65
  6.0 11.6 %collective-permute-start.1 = (bf16[832,256]{1,0:T(8,128)(2,1)S(1)}, bf16[832,256]{1,0:T(8,128)(2,1)S(1)}, u32[]{:S(2)}, u32[]{:S(2)}) collective-permute-start(bf16[832,256]{1,0:T(8,128)(2,1)S(1)} %pad_maximum_fusion.1.refs_0_), channel_id=1, source_target_pairs={{8,0},{16,8},{24,16},{28,24},{20,28},{12,20},{4,12},{0,4},{9,1},{1... | collective-permute-start | bytes 1277960 | tf_op jit(solution)/shard_map/ppermute | solution.py:65
  7.2 21.8 %collective-permute-start.2 = (bf16[1,256,256]{2,1,0:T(8,128)(2,1)S(1)}, bf16[1,256,256]{2,1,0:T(8,128)(2,1)S(1)}, u32[]{:S(2)}, u32[]{:S(2)}) collective-permute-start(bf16[1,256,256]{2,1,0:T(8,128)(2,1)S(1)} %maximum_bitcast_fusion.refs_7_), channel_id=1, source_target_pairs={{0,2},{1,3},{2,0},{3,1},{4,6},{5,7},{6,4},{7,5},{8,10},{9,11},{10,... | collective-permute-start | bytes 393224 | tf_op jit(solution)/shard_map/ppermute | solution.py:344
  15.8 11.0 %collective-permute-start.3 = (bf16[832,256]{1,0:T(8,128)(2,1)S(1)}, bf16[832,256]{1,0:T(8,128)(2,1)S(1)}, u32[]{:S(2)}, u32[]{:S(2)}) collective-permute-start(bf16[832,256]{1,0:T(8,128)(2,1)S(1)} %collective-permute-done.refs_0_.refs_1_), channel_id=1, source_target_pairs={{0,8},{8,16},{16,24},{24,28},{28,20},{20,12},{12,4},{4,0},{1,9},{9... | collective-permute-start | bytes 1277960 | tf_op jit(solution)/shard_map/ppermute | solution.py:65
  17.6 10.7 %collective-permute-start.4 = (bf16[832,256]{1,0:T(8,128)(2,1)S(1)}, bf16[832,256]{1,0:T(8,128)(2,1)S(1)}, u32[]{:S(2)}, u32[]{:S(2)}) collective-permute-start(bf16[832,256]{1,0:T(8,128)(2,1)S(1)} %collective-permute-done.1.refs_1_.refs_2_), channel_id=1, source_target_pairs={{8,0},{16,8},{24,16},{28,24},{20,28},{12,20},{4,12},{0,4},{9,1},{1... | collective-permute-start | bytes 1277960 | tf_op jit(solution)/shard_map/ppermute | solution.py:65
  26.8 10.1 %collective-permute-start.6 = (bf16[832,256]{1,0:T(8,128)(2,1)S(1)}, bf16[832,256]{1,0:T(8,128)(2,1)S(1)}, u32[]{:S(2)}, u32[]{:S(2)}) collective-permute-start(bf16[832,256]{1,0:T(8,128)(2,1)S(1)} %collective-permute-done.3.refs_2_.refs_3_), channel_id=1, source_target_pairs={{0,8},{8,16},{16,24},{24,28},{28,20},{20,12},{12,4},{4,0},{1,9},{9... | collective-permute-start | bytes 1277960 | tf_op jit(solution)/shard_map/ppermute | solution.py:65
  28.3 9.5 %collective-permute-start.7 = (bf16[832,256]{1,0:T(8,128)(2,1)S(1)}, bf16[832,256]{1,0:T(8,128)(2,1)S(1)}, u32[]{:S(2)}, u32[]{:S(2)}) collective-permute-start(bf16[832,256]{1,0:T(8,128)(2,1)S(1)} %collective-permute-done.4.refs_3_.refs_4_), channel_id=1, source_target_pairs={{8,0},{16,8},{24,16},{28,24},{20,28},{12,20},{4,12},{0,4},{9,1},{1... | collective-permute-start | bytes 1277960 | tf_op jit(solution)/shard_map/ppermute | solution.py:65
  29.6 8.2 %collective-permute-start.5 = (bf16[2,256,256]{2,1,0:T(8,128)(2,1)S(1)}, bf16[2,256,256]{2,1,0:T(8,128)(2,1)S(1)}, u32[]{:S(2)}, u32[]{:S(2)}) collective-permute-start(bf16[2,256,256]{2,1,0:T(8,128)(2,1)S(1)} %shard_map.85.refs_10_), channel_id=1, source_target_pairs={{0,2},{1,3},{2,0},{3,1},{4,6},{5,7},{6,4},{7,5},{8,10},{9,11},{10,... | collective-permute-start | bytes 786440 | tf_op jit(solution)/shard_map/ppermute | solution.py:344
  37.8 5.0 %collective-permute-start.9 = (bf16[2,2,256,256]{3,2,1,0:T(8,128)(2,1)S(1)}, bf16[2,2,256,256]{3,2,1,0:T(8,128)(2,1)S(1)}, u32[]{:S(2)}, u32[]{:S(2)}) collective-permute-start(bf16[2,2,256,256]{3,2,1,0:T(8,128)(2,1)S(1)} %pad_maximum_fusion), channel_id=1, source_target_pairs={{0,1},{1,0},{2,3},{3,2},{4,5},{5,4},{6,7},{7,6},{8,9},{9,8},{10,11... | collective-permute-start | bytes 1572872 | tf_op jit(solution)/shard_map/ppermute | solution.py:338
  37.9 4.9 %collective-permute-start.8 = (bf16[2,1,256,256]{3,2,1,0:T(8,128)(2,1)S(1)}, bf16[2,1,256,256]{3,2,1,0:T(8,128)(2,1)S(1)}, u32[]{:S(2)}, u32[]{:S(2)}) collective-permute-start(bf16[2,1,256,256]{3,2,1,0:T(8,128)(2,1)S(1)} %pad_maximum_fusion.3), channel_id=1, source_target_pairs={{0,1},{1,0},{2,3},{3,2},{4,5},{5,4},{6,7},{7,6},{8,9},{9,8},{10,11... | collective-permute-start | bytes 786440 | tf_op jit(solution)/shard_map/ppermute | solution.py:338
  38.5 8.0 %collective-permute-start.11 = (bf16[384,256]{1,0:T(8,128)(2,1)S(1)}, bf16[384,256]{1,0:T(8,128)(2,1)S(1)}, u32[]{:S(2)}, u32[]{:S(2)}) collective-permute-start(bf16[384,256]{1,0:T(8,128)(2,1)S(1)} %slice.100), channel_id=1, source_target_pairs={{0,8},{8,16},{16,24},{24,28},{28,20},{20,12},{12,4},{4,0},{1,9},{9... | collective-permute-start | bytes 589832 | tf_op jit(solution)/shard_map/ppermute | solution.py:65
  40.1 6.6 %collective-permute-start.12 = (bf16[384,256]{1,0:T(8,128)(2,1)S(1)}, bf16[384,256]{1,0:T(8,128)(2,1)S(1)}, u32[]{:S(2)}, u32[]{:S(2)}) collective-permute-start(bf16[384,256]{1,0:T(8,128)(2,1)S(1)} %slice.101), channel_id=1, source_target_pairs={{8,0},{16,8},{24,16},{28,24},{20,28},{12,20},{4,12},{0,4},{9,1},{1... | collective-permute-start | bytes 589832 | tf_op jit(solution)/shard_map/ppermute | solution.py:65
  41.2 5.2 %collective-permute-start.10 = (bf16[1,256,256]{2,1,0:T(8,128)(2,1)S(1)}, bf16[1,256,256]{2,1,0:T(8,128)(2,1)S(1)}, u32[]{:S(2)}, u32[]{:S(2)}) collective-permute-start(bf16[1,256,256]{2,1,0:T(8,128)(2,1)S(1)} %shard_map.88.refs_2_), channel_id=1, source_target_pairs={{0,2},{1,3},{2,0},{3,1},{4,6},{5,7},{6,4},{7,5},{8,10},{9,11},{10,... | collective-permute-start | bytes 393224 | tf_op jit(solution)/shard_map/ppermute | solution.py:344
  46.8 1.6 %collective-permute-start.13 = (bf16[2,1,256,256]{3,2,1,0:T(8,128)(2,1)S(1)}, bf16[2,1,256,256]{3,2,1,0:T(8,128)(2,1)S(1)}, u32[]{:S(2)}, u32[]{:S(2)}) collective-permute-start(bf16[2,1,256,256]{3,2,1,0:T(8,128)(2,1)S(1)} %pad_maximum_fusion.4), channel_id=1, source_target_pairs={{0,1},{1,0},{2,3},{3,2},{4,5},{5,4},{6,7},{7,6},{8,9},{9,8},{10,11... | collective-permute-start | bytes 786440 | tf_op jit(solution)/shard_map/ppermute | solution.py:338
  51.4 1.5 %collective-permute-start.14 = (f32[192,256]{1,0:T(8,128)S(1)}, f32[192,256]{1,0:T(8,128)S(1)}, u32[]{:S(2)}, u32[]{:S(2)}) collective-permute-start(f32[192,256]{1,0:T(8,128)S(1)} %get-tuple-element.97), channel_id=1, source_target_pairs={{0,1},{1,0},{2,3},{3,2},{4,5},{5,4},{6,7},{7,6},{8,9},{9,8},{10,11... | collective-permute-start | bytes 589832 | tf_op jit(solution)/shard_map/ppermute | solution.py:439
  52.9 7.0 %collective-permute-start.17 = (f32[192,256]{1,0:T(8,128)S(1)}, f32[192,256]{1,0:T(8,128)S(1)}, u32[]{:S(2)}, u32[]{:S(2)}) collective-permute-start(f32[192,256]{1,0:T(8,128)S(1)} %add.59), channel_id=1, source_target_pairs={{0,2},{1,3},{2,0},{3,1},{4,6},{5,7},{6,4},{7,5},{8,10},{9,11},{10,... | collective-permute-start | bytes 589832 | tf_op jit(solution)/shard_map/ppermute | solution.py:453
  54.5 5.5 %copy-start.3 = (f32[1,1,1,192]{3,2,1,0:T(1,128)S(1)}, f32[1,1,1,192]{3,2,1,0:T(1,128)}, u32[]{:S(2)}) copy-start(f32[1,1,1,192]{3,2,1,0:T(1,128)} %param.9) | copy-start | bytes 2308
  56.7 1.4 %collective-permute-start.15 = (f32[96,256]{1,0:T(8,128)S(1)}, f32[96,256]{1,0:T(8,128)S(1)}, u32[]{:S(2)}, u32[]{:S(2)}) collective-permute-start(f32[96,256]{1,0:T(8,128)S(1)} %get-tuple-element.134), channel_id=1, source_target_pairs={{0,1},{1,0},{2,3},{3,2},{4,5},{5,4},{6,7},{7,6},{8,9},{9,8},{10,11... | collective-permute-start | bytes 294920 | tf_op jit(solution)/shard_map/ppermute | solution.py:468
  56.7 1.4 %collective-permute-start.16 = (f32[96,256]{1,0:T(8,128)S(1)}, f32[96,256]{1,0:T(8,128)S(1)}, u32[]{:S(2)}, u32[]{:S(2)}) collective-permute-start(f32[96,256]{1,0:T(8,128)S(1)} %get-tuple-element.135), channel_id=1, source_target_pairs={{0,1},{1,0},{2,3},{3,2},{4,5},{5,4},{6,7},{7,6},{8,9},{9,8},{10,11... | collective-permute-start | bytes 294920 | tf_op jit(solution)/shard_map/ppermute | solution.py:468
  60.0 6.2 %collective-permute-start.18 = (f32[192,256]{1,0:T(8,128)S(1)}, f32[192,256]{1,0:T(8,128)S(1)}, u32[]{:S(2)}, u32[]{:S(2)}) collective-permute-start(f32[192,256]{1,0:T(8,128)S(1)} %fusion.9.refs_0_.refs_6_), channel_id=1, source_target_pairs={{0,8},{8,16},{16,24},{24,28},{28,20},{20,12},{12,4},{4,0},{1,9},{9... | collective-permute-start | bytes 589832 | tf_op jit(solution)/shard_map/ppermute | solution.py:65
  61.7 6.1 %collective-permute-start.20 = (f32[192,256]{1,0:T(8,128)S(1)}, f32[192,256]{1,0:T(8,128)S(1)}, u32[]{:S(2)}, u32[]{:S(2)}) collective-permute-start(f32[192,256]{1,0:T(8,128)S(1)} %fusion.9.refs_0_.refs_6_), channel_id=1, source_target_pairs={{8,0},{16,8},{24,16},{28,24},{20,28},{12,20},{4,12},{0,4},{9,1},{1... | collective-permute-start | bytes 589832 | tf_op jit(solution)/shard_map/ppermute | solution.py:65
  62.1 6.1 %collective-permute-start.26 = (f32[192,256]{1,0:T(8,128)S(1)}, f32[192,256]{1,0:T(8,128)S(1)}, u32[]{:S(2)}, u32[]{:S(2)}) collective-permute-start(f32[192,256]{1,0:T(8,128)S(1)} %fusion.9.refs_0_.refs_6_), channel_id=1, source_target_pairs={{0,2},{1,3},{2,0},{3,1},{4,6},{5,7},{6,4},{7,5},{8,10},{9,11},{10,... | collective-permute-start | bytes 589832 | tf_op jit(solution)/shard_map/ppermute | solution.py:470
  66.2 5.8 %collective-permute-start.19 = (f32[192,256]{1,0:T(8,128)S(1)}, f32[192,256]{1,0:T(8,128)S(1)}, u32[]{:S(2)}, u32[]{:S(2)}) collective-permute-start(f32[192,256]{1,0:T(8,128)S(1)} %collective-permute-done.18.refs_1_), channel_id=1, source_target_pairs={{0,8},{8,16},{16,24},{24,28},{28,20},{20,12},{12,4},{4,0},{1,9},{9... | collective-permute-start | bytes 589832 | tf_op jit(solution)/shard_map/ppermute | solution.py:65
  67.8 5.8 %collective-permute-start.21 = (f32[192,256]{1,0:T(8,128)S(1)}, f32[192,256]{1,0:T(8,128)S(1)}, u32[]{:S(2)}, u32[]{:S(2)}) collective-permute-start(f32[192,256]{1,0:T(8,128)S(1)} %collective-permute-done.20.refs_2_), channel_id=1, source_target_pairs={{8,0},{16,8},{24,16},{28,24},{20,28},{12,20},{4,12},{0,4},{9,1},{1... | collective-permute-start | bytes 589832 | tf_op jit(solution)/shard_map/ppermute | solution.py:65
  68.3 13.1 %collective-permute-start.27 = (f32[2,192,256]{2,1,0:T(8,128)S(1)}, f32[2,192,256]{2,1,0:T(8,128)S(1)}, u32[]{:S(2)}, u32[]{:S(2)}) collective-permute-start(f32[2,192,256]{2,1,0:T(8,128)S(1)} %pad_maximum_fusion.2), channel_id=1, source_target_pairs={{0,1},{1,0},{2,3},{3,2},{4,5},{5,4},{6,7},{7,6},{8,9},{9,8},{10,11... | collective-permute-start | bytes 1179656 | tf_op jit(solution)/shard_map/ppermute | solution.py:471
  72.0 5.7 %collective-permute-start.22 = (f32[192,256]{1,0:T(8,128)S(1)}, f32[192,256]{1,0:T(8,128)S(1)}, u32[]{:S(2)}, u32[]{:S(2)}) collective-permute-start(f32[192,256]{1,0:T(8,128)S(1)} %collective-permute-done.19.refs_3_), channel_id=1, source_target_pairs={{0,8},{8,16},{16,24},{24,28},{28,20},{20,12},{12,4},{4,0},{1,9},{9... | collective-permute-start | bytes 589832 | tf_op jit(solution)/shard_map/ppermute | solution.py:65
  73.6 5.7 %collective-permute-start.24 = (f32[192,256]{1,0:T(8,128)S(1)}, f32[192,256]{1,0:T(8,128)S(1)}, u32[]{:S(2)}, u32[]{:S(2)}) collective-permute-start(f32[192,256]{1,0:T(8,128)S(1)} %collective-permute-done.21.refs_4_), channel_id=1, source_target_pairs={{8,0},{16,8},{24,16},{28,24},{20,28},{12,20},{4,12},{0,4},{9,1},{1... | collective-permute-start | bytes 589832 | tf_op jit(solution)/shard_map/ppermute | solution.py:65
  79.2 6.1 %collective-permute-start.23 = (f32[112,256]{1,0:T(8,128)S(1)}, f32[112,256]{1,0:T(8,128)S(1)}, u32[]{:S(2)}, u32[]{:S(2)}) collective-permute-start(f32[112,256]{1,0:T(8,128)S(1)} %slice.102), channel_id=1, source_target_pairs={{0,8},{8,16},{16,24},{24,28},{28,20},{20,12},{12,4},{4,0},{1,9},{9... | collective-permute-start | bytes 344072 | tf_op jit(solution)/shard_map/ppermute | solution.py:65
  80.9 4.5 %collective-permute-start.25 = (f32[80,256]{1,0:T(8,128)S(1)}, f32[80,256]{1,0:T(8,128)S(1)}, u32[]{:S(2)}, u32[]{:S(2)}) collective-permute-start(f32[80,256]{1,0:T(8,128)S(1)} %slice.103), channel_id=1, source_target_pairs={{8,0},{16,8},{24,16},{28,24},{20,28},{12,20},{4,12},{0,4},{9,1},{1... | collective-permute-start | bytes 245768 | tf_op jit(solution)/shard_map/ppermute | solution.py:65
  87.1 3.5 %collective-permute-start.28 = (f32[2,192,256]{2,1,0:T(8,128)S(1)}, f32[2,192,256]{2,1,0:T(8,128)S(1)}, u32[]{:S(2)}, u32[]{:S(2)}) collective-permute-start(f32[2,192,256]{2,1,0:T(8,128)S(1)} %slice.92), channel_id=1, source_target_pairs={{0,1},{1,0},{2,3},{3,2},{4,5},{5,4},{6,7},{7,6},{8,9},{9,8},{10,11... | collective-permute-start | bytes 1179656 | tf_op jit(solution)/shard_map/ppermute | solution.py:514
  87.2 11.7 %all-to-all-start = ((f32[32,4,256]{2,1,0:T(4,128)}), f32[32,4,256]{2,1,0:T(4,128)S(1)}, u32[]{:S(2)}, u32[]{:S(2)}) async-start(f32[32,4,256]{2,1,0:T(4,128)} %get-tuple-element.120), calls=%async_computation | async-start | bytes 262144 | tf_op jit(solution)/shard_map/all_to_all | solution.py:513
  90.7 8.4 %collective-permute-start.29 = (f32[192,256]{1,0:T(8,128)S(1)}, f32[192,256]{1,0:T(8,128)S(1)}, u32[]{:S(2)}, u32[]{:S(2)}) collective-permute-start(f32[192,256]{1,0:T(8,128)S(1)} %fusion.7), channel_id=1, source_target_pairs={{0,2},{1,3},{2,0},{3,1},{4,6},{5,7},{6,4},{7,5},{8,10},{9,11},{10,... | collective-permute-start | bytes 589832 | tf_op jit(solution)/shard_map/ppermute | solution.py:515
  (3 other events, 5.6 us)

commit v9 on v8

--- a/solution.py
+++ b/solution.py
@@ -475,7 +475,7 @@
         if step < ring.far:
             arrived = ahead, back = ring.move(ahead, back)
         else:
-            arrived = ring.last(ahead, back, piece, 16 if piece > 32 else 0)
+            arrived = ring.last(ahead, back, piece, piece // 6 // 16 * 16)
         if step == ring.far - 2:
             *arrived, gram = lax.optimization_barrier((*arrived, gram))
             tile = fetch(gram)

time: 100 us -> 100 us (level)
  no operation moved by 1% of the time
where the time goes in v9:
time: 100 us; the launch traced here: 99.8 us
  waiting for transfers between devices  36.2 us (36%)
  starting transfers between devices  32.4 us (32%)
  Pallas kernels  16.6 us (17%)
  local copies, waits for them, and re-layouts  10.3 us (10%)
  between operations  2.9 us (3%)
  other arithmetic  1.39 us (1%)
    ppermute x8, waiting for transfers between devices, move(): lax.ppermute(ahead, axes, self.ahead)  21.4 us
    pallas_call x10, Pallas kernels, call(): pl.pallas_call(body, grid_spec=pltpu.PrefetchScalarGridSpec(num_scalar_pr...  16.6 us
    ppermute x8, starting transfers between devices, move(): lax.ppermute(ahead, axes, self.ahead)  14.4 us
    unnamed x10, local copies, waits for them, and re-layouts  6.83 us
    all_to_all x1, waiting for transfers between devices, shards(): sums = lax.all_to_all(sums, axes, split_axis=0, concat_axis=0, tiled=True)  6.35 us
    ppermute x3, starting transfers between devices, open_groups(): lax.ppermute(mine, 'tcol', swap(tcol_count, 2))  5.01 us
    ppermute x8, waiting for transfers between devices, move(): lax.ppermute(back, axes, self.back)  3.53 us
    all_to_all x1, starting transfers between devices, shards(): sums = lax.all_to_all(sums, axes, split_axis=0, concat_axis=0, tiled=True)  3.43 us
  transfers between devices with their start and end apart: 31, of which 17 were waited for; matrix products, arithmetic and copies ran while one was open for 4% of the time, Pallas kernels for 12%

profile of v9, /device:TPU:0, one launch (start us, length us, event | category | flops | bytes accessed | tf_op | source)
XLA Modules:
  0.0 99.8 jit_solution(16824075854128715160)
XLA Ops:
  2.9 3.1 %collective-permute-start = (bf16[832,256]{1,0:T(8,128)(2,1)S(1)}, bf16[832,256]{1,0:T(8,128)(2,1)S(1)}, u32[]{:S(2)}, u32[]{:S(2)}) collective-permute-start(bf16[832,256]{1,0:T(8,128)(2,1)S(1)} %pad_maximum_fusion.1.refs_0_), channel_id=1, source_target_pairs={{0,8},{8,16},{16,24},{24,28},{28,20},{20,12},{12,4},{4,0},{1,9},{9... | collective-permute-start | bytes 1277960 | tf_op jit(solution)/shard_map/ppermute | solution.py:65
  7.2 2.0 %collective-permute-start.2 = (bf16[1,256,256]{2,1,0:T(8,128)(2,1)S(1)}, bf16[1,256,256]{2,1,0:T(8,128)(2,1)S(1)}, u32[]{:S(2)}, u32[]{:S(2)}) collective-permute-start(bf16[1,256,256]{2,1,0:T(8,128)(2,1)S(1)} %maximum_bitcast_fusion.refs_7_), channel_id=1, source_target_pairs={{0,2},{1,3},{2,0},{3,1},{4,6},{5,7},{6,4},{7,5},{8,10},{9,11},{10,... | collective-permute-start | bytes 393224 | tf_op jit(solution)/shard_map/ppermute | solution.py:344
  9.2 1.3 %dynamic_slice.12 = s32[1,1]{1,0:T(1,128)} dynamic-slice(s32[4,2]{1,0:T(4,128)} %constant.37.clone, s32[]{:T(128)S(6)} %select_n.15, s32[]{:T(128)S(6)} %select_n.16), dynamic_slice_sizes={1,1} | dynamic-slice | bytes 12 | tf_op jit(solution)/shard_map/dynamic_slice | solution.py:302
  13.1 2.7 %collective-permute-done.refs_0_.refs_1_ = bf16[832,256]{1,0:T(8,128)(2,1)S(1)} collective-permute-done((bf16[832,256]{1,0:T(8,128)(2,1)S(1)}, bf16[832,256]{1,0:T(8,128)(2,1)S(1)}, u32[]{:S(2)}, u32[]{:S(2)}) %collective-permute-start) | collective-permute-done | bytes 426016 | tf_op jit(solution)/shard_map/ppermute | solution.py:65
  15.8 1.8 %collective-permute-start.3 = (bf16[832,256]{1,0:T(8,128)(2,1)S(1)}, bf16[832,256]{1,0:T(8,128)(2,1)S(1)}, u32[]{:S(2)}, u32[]{:S(2)}) collective-permute-start(bf16[832,256]{1,0:T(8,128)(2,1)S(1)} %collective-permute-done.refs_0_.refs_1_), channel_id=1, source_target_pairs={{0,8},{8,16},{16,24},{24,28},{28,20},{20,12},{12,4},{4,0},{1,9},{9... | collective-permute-start | bytes 1277960 | tf_op jit(solution)/shard_map/ppermute | solution.py:65
  17.9 8.9 %collective-permute-done.3.refs_2_.refs_3_ = bf16[832,256]{1,0:T(8,128)(2,1)S(1)} collective-permute-done((bf16[832,256]{1,0:T(8,128)(2,1)S(1)}, bf16[832,256]{1,0:T(8,128)(2,1)S(1)}, u32[]{:S(2)}, u32[]{:S(2)}) %collective-permute-start.3) | collective-permute-done | bytes 426016 | tf_op jit(solution)/shard_map/ppermute | solution.py:65
  26.8 1.5 %collective-permute-start.6 = (bf16[832,256]{1,0:T(8,128)(2,1)S(1)}, bf16[832,256]{1,0:T(8,128)(2,1)S(1)}, u32[]{:S(2)}, u32[]{:S(2)}) collective-permute-start(bf16[832,256]{1,0:T(8,128)(2,1)S(1)} %collective-permute-done.3.refs_2_.refs_3_), channel_id=1, source_target_pairs={{0,8},{8,16},{16,24},{24,28},{28,20},{20,12},{12,4},{4,0},{1,9},{9... | collective-permute-start | bytes 1277960 | tf_op jit(solution)/shard_map/ppermute | solution.py:65
  29.6 1.5 %collective-permute-start.5 = (bf16[2,256,256]{2,1,0:T(8,128)(2,1)S(1)}, bf16[2,256,256]{2,1,0:T(8,128)(2,1)S(1)}, u32[]{:S(2)}, u32[]{:S(2)}) collective-permute-start(bf16[2,256,256]{2,1,0:T(8,128)(2,1)S(1)} %shard_map.85.refs_10_), channel_id=1, source_target_pairs={{0,2},{1,3},{2,0},{3,1},{4,6},{5,7},{6,4},{7,5},{8,10},{9,11},{10,... | collective-permute-start | bytes 786440 | tf_op jit(solution)/shard_map/ppermute | solution.py:344
  31.1 2.3 %copy-done.2 = f32[4,1,1,192,1536]{4,3,2,1,0:T(8,128)S(1)} copy-done((f32[4,1,1,192,1536]{4,3,2,1,0:T(8,128)S(1)}, f32[4,1,1,192,1536]{4,3,2,1,0:T(8,128)}, u32[]{:S(2)}) %copy-start.2) | copy-done | bytes 4718616
  33.9 2.9 %collective-permute-done.6.refs_5_.refs_2_ = bf16[832,256]{1,0:T(8,128)(2,1)S(1)} collective-permute-done((bf16[832,256]{1,0:T(8,128)(2,1)S(1)}, bf16[832,256]{1,0:T(8,128)(2,1)S(1)}, u32[]{:S(2)}, u32[]{:S(2)}) %collective-permute-start.6) | collective-permute-done | bytes 426016 | tf_op jit(solution)/shard_map/ppermute | solution.py:65
  38.5 1.6 %collective-permute-start.11 = (bf16[384,256]{1,0:T(8,128)(2,1)S(1)}, bf16[384,256]{1,0:T(8,128)(2,1)S(1)}, u32[]{:S(2)}, u32[]{:S(2)}) collective-permute-start(bf16[384,256]{1,0:T(8,128)(2,1)S(1)} %slice.100), channel_id=1, source_target_pairs={{0,8},{8,16},{16,24},{24,28},{28,20},{20,12},{12,4},{4,0},{1,9},{9... | collective-permute-start | bytes 589832 | tf_op jit(solution)/shard_map/ppermute | solution.py:65
  41.2 1.6 %collective-permute-start.10 = (bf16[1,256,256]{2,1,0:T(8,128)(2,1)S(1)}, bf16[1,256,256]{2,1,0:T(8,128)(2,1)S(1)}, u32[]{:S(2)}, u32[]{:S(2)}) collective-permute-start(bf16[1,256,256]{2,1,0:T(8,128)(2,1)S(1)} %shard_map.88.refs_2_), channel_id=1, source_target_pairs={{0,2},{1,3},{2,0},{3,1},{4,6},{5,7},{6,4},{7,5},{8,10},{9,11},{10,... | collective-permute-start | bytes 393224 | tf_op jit(solution)/shard_map/ppermute | solution.py:344
  42.8 3.7 %shard_map.87 = (f32[384,1536]{1,0:T(8,128)S(1)}, f32[384,1536]{1,0:T(8,128)S(1)}, f32[1536,256]{1,0:T(8,128)S(1)}, bf16[1536,1024]{1,0:T(8,128)(2,1)S(1)}, bf16...) custom-call(s32[17]{0:T(128)S(1)} %get-tuple-element.63.meta, bf16[832,256]{1,0:T(8,128)(2,1)S(1)} %pad_maximum_fusion.1.refs_0_, ...), custom_call_target="tpu_custom_call" | custom-call | flops 1811939328 | bytes 9437184 | tf_op jit(solution)/shard_map/pallas_call | solution.py:270
  46.8 1.5 %collective-permute-done.13.refs_4_ = bf16[2,1,256,256]{3,2,1,0:T(8,128)(2,1)S(1)} collective-permute-done((bf16[2,1,256,256]{3,2,1,0:T(8,128)(2,1)S(1)}, bf16[2,1,256,256]{3,2,1,0:T(8,128)(2,1)S(1)}, u32[]{:S(2)}, u32[]{:S(2)}) %collective-permute-start.13) | collective-permute-done | bytes 262176 | tf_op jit(solution)/shard_map/ppermute | solution.py:338
  48.4 3.0 %shard_map.89 = (f32[192,256]{1,0:T(8,128)S(1)}, f32[768,1536]{1,0:T(8,128)}, f32[384,1536]{1,0:T(8,128)S(1)}, bf16[1536,256]{1,0:T(8,128)(2,1)S(1)}, bf16[1536,...) custom-call(s32[17]{0:T(128)S(1)} %get-tuple-element.63.meta, ...), custom_call_target="tpu_custom_call" | custom-call | flops 754974720 | bytes 4718592 | tf_op jit(solution)/shard_map/pallas_call | solution.py:270
  52.9 1.6 %collective-permute-start.17 = (f32[192,256]{1,0:T(8,128)S(1)}, f32[192,256]{1,0:T(8,128)S(1)}, u32[]{:S(2)}, u32[]{:S(2)}) collective-permute-start(f32[192,256]{1,0:T(8,128)S(1)} %add.59), channel_id=1, source_target_pairs={{0,2},{1,3},{2,0},{3,1},{4,6},{5,7},{6,4},{7,5},{8,10},{9,11},{10,... | collective-permute-start | bytes 589832 | tf_op jit(solution)/shard_map/ppermute | solution.py:453
  54.5 2.1 %shard_map.91 = (f32[768,1536]{1,0:T(8,128)}, f32[2,192,256]{2,1,0:T(8,128)S(1)}) custom-call(s32[1]{0:T(128)} %bitcast.meta, f32[384,1536]{1,0:T(8,128)S(1)} %get-tuple-element.99.refs_0_, bf16[1536,256]{1,0:T(8,128)(2,1)S(1)} %get-tuple-element.100.refs_1_, ...), custom_call_target="tpu_custom_call", output_to_operand_aliasing={{0}: (6, {})} | custom-call | flops 1207959552 | bytes 4718592 | tf_op jit(solution)/shard_map/pallas_call | solution.py:270
  58.2 1.8 %collective-permute-done.17 = f32[192,256]{1,0:T(8,128)S(1)} collective-permute-done((f32[192,256]{1,0:T(8,128)S(1)}, f32[192,256]{1,0:T(8,128)S(1)}, u32[]{:S(2)}, u32[]{:S(2)}) %collective-permute-start.17) | collective-permute-done | bytes 196640 | tf_op jit(solution)/shard_map/ppermute | solution.py:453
  60.0 1.6 %collective-permute-start.18 = (f32[192,256]{1,0:T(8,128)S(1)}, f32[192,256]{1,0:T(8,128)S(1)}, u32[]{:S(2)}, u32[]{:S(2)}) collective-permute-start(f32[192,256]{1,0:T(8,128)S(1)} %fusion.9.refs_0_.refs_6_), channel_id=1, source_target_pairs={{0,8},{8,16},{16,24},{24,28},{28,20},{20,12},{12,4},{4,0},{1,9},{9... | collective-permute-start | bytes 589832 | tf_op jit(solution)/shard_map/ppermute | solution.py:65
  62.1 1.5 %collective-permute-start.26 = (f32[192,256]{1,0:T(8,128)S(1)}, f32[192,256]{1,0:T(8,128)S(1)}, u32[]{:S(2)}, u32[]{:S(2)}) collective-permute-start(f32[192,256]{1,0:T(8,128)S(1)} %fusion.9.refs_0_.refs_6_), channel_id=1, source_target_pairs={{0,2},{1,3},{2,0},{3,1},{4,6},{5,7},{6,4},{7,5},{8,10},{9,11},{10,... | collective-permute-start | bytes 589832 | tf_op jit(solution)/shard_map/ppermute | solution.py:470
  63.6 2.6 %collective-permute-done.18.refs_1_ = f32[192,256]{1,0:T(8,128)S(1)} collective-permute-done((f32[192,256]{1,0:T(8,128)S(1)}, f32[192,256]{1,0:T(8,128)S(1)}, u32[]{:S(2)}, u32[]{:S(2)}) %collective-permute-start.18) | collective-permute-done | bytes 196640 | tf_op jit(solution)/shard_map/ppermute | solution.py:65
  66.2 1.6 %collective-permute-start.19 = (f32[192,256]{1,0:T(8,128)S(1)}, f32[192,256]{1,0:T(8,128)S(1)}, u32[]{:S(2)}, u32[]{:S(2)}) collective-permute-start(f32[192,256]{1,0:T(8,128)S(1)} %collective-permute-done.18.refs_1_), channel_id=1, source_target_pairs={{0,8},{8,16},{16,24},{24,28},{28,20},{20,12},{12,4},{4,0},{1,9},{9... | collective-permute-start | bytes 589832 | tf_op jit(solution)/shard_map/ppermute | solution.py:65
  68.4 3.6 %collective-permute-done.19.refs_3_ = f32[192,256]{1,0:T(8,128)S(1)} collective-permute-done((f32[192,256]{1,0:T(8,128)S(1)}, f32[192,256]{1,0:T(8,128)S(1)}, u32[]{:S(2)}, u32[]{:S(2)}) %collective-permute-start.19) | collective-permute-done | bytes 196640 | tf_op jit(solution)/shard_map/ppermute | solution.py:65
  72.0 1.6 %collective-permute-start.22 = (f32[192,256]{1,0:T(8,128)S(1)}, f32[192,256]{1,0:T(8,128)S(1)}, u32[]{:S(2)}, u32[]{:S(2)}) collective-permute-start(f32[192,256]{1,0:T(8,128)S(1)} %collective-permute-done.19.refs_3_), channel_id=1, source_target_pairs={{0,8},{8,16},{16,24},{24,28},{28,20},{20,12},{12,4},{4,0},{1,9},{9... | collective-permute-start | bytes 589832 | tf_op jit(solution)/shard_map/ppermute | solution.py:65
  74.1 2.3 %copy-done.1 = f32[768,1536]{1,0:T(8,128)S(1)} copy-done((f32[768,1536]{1,0:T(8,128)S(1)}, f32[768,1536]{1,0:T(8,128)}, u32[]{:S(2)}) %copy-start.1) | copy-done | bytes 4718616
  77.6 1.6 %collective-permute-done.24.refs_6_ = f32[192,256]{1,0:T(8,128)S(1)} collective-permute-done((f32[192,256]{1,0:T(8,128)S(1)}, f32[192,256]{1,0:T(8,128)S(1)}, u32[]{:S(2)}, u32[]{:S(2)}) %collective-permute-start.24) | collective-permute-done | bytes 196640 | tf_op jit(solution)/shard_map/ppermute | solution.py:65
  79.2 1.6 %collective-permute-start.23 = (f32[128,256]{1,0:T(8,128)S(1)}, f32[128,256]{1,0:T(8,128)S(1)}, u32[]{:S(2)}, u32[]{:S(2)}) collective-permute-start(f32[128,256]{1,0:T(8,128)S(1)} %slice.102), channel_id=1, source_target_pairs={{0,8},{8,16},{16,24},{24,28},{28,20},{20,12},{12,4},{4,0},{1,9},{9... | collective-permute-start | bytes 393224 | tf_op jit(solution)/shard_map/ppermute | solution.py:65
  81.3 3.0 %shard_map.93 = (f32[4,192,256]{2,1,0:T(8,128)S(1)}, f32[4,256]{1,0:T(4,128)S(1)}, bf16[768,192]{1,0:T(8,128)(2,1)S(1)}, bf16[768,192]{1,0:T(8,128)(2,1)S(1)}) custom-call(s32[17]{0:T(128)S(1)} %get-tuple-element.107.meta, f32[192,256]{1,0:T(8,128)S(1)} %fusion.9.refs_0_.refs_6_, f32[192,256]{1,0:T(8,128)S(1)} %collective-permute-done.18.refs_1_, ...), custom_call_target="tpu_custom_call" | custom-call | flops 1811939328 | bytes 4718592 | tf_op jit(solution)/shard_map/pallas_call | solution.py:270
  85.2 1.7 %shard_map.94 = (f32[4,192,256]{2,1,0:T(8,128)S(1)}, f32[32,4,256]{2,1,0:T(4,128)}) custom-call(s32[17]{0:T(128)S(1)} %get-tuple-element.107.meta, f32[128,256]{1,0:T(8,128)S(1)} %collective-permute-done.23.refs_0_, f32[64,256]{1,0:T(8,128)S(1)} %collective-permute-done.25.refs_1_, f32[4,192,256]{2,1,0:T(8,128)S(1)} %get-tuple-element.113.refs_2_, ...), custom_call_target="tpu_custom_call" | custom-call | flops 226492416 | bytes 589824 | tf_op jit(solution)/shard_map/pallas_call | solution.py:270
  87.0 3.4 %all-to-all-start = ((f32[32,4,256]{2,1,0:T(4,128)}), f32[32,4,256]{2,1,0:T(4,128)S(1)}, u32[]{:S(2)}, u32[]{:S(2)}) async-start(f32[32,4,256]{2,1,0:T(4,128)} %get-tuple-element.120), calls=%async_computation | async-start | bytes 262144 | tf_op jit(solution)/shard_map/all_to_all | solution.py:513
  90.5 1.8 %collective-permute-start.29 = (f32[192,256]{1,0:T(8,128)S(1)}, f32[192,256]{1,0:T(8,128)S(1)}, u32[]{:S(2)}, u32[]{:S(2)}) collective-permute-start(f32[192,256]{1,0:T(8,128)S(1)} %fusion.7), channel_id=1, source_target_pairs={{0,2},{1,3},{2,0},{3,1},{4,6},{5,7},{6,4},{7,5},{8,10},{9,11},{10,... | collective-permute-start | bytes 589832 | tf_op jit(solution)/shard_map/ppermute | solution.py:515
  92.3 6.4 %all-to-all-done = f32[32,4,256]{2,1,0:T(4,128)S(1)} async-done(((f32[32,4,256]{2,1,0:T(4,128)}), f32[32,4,256]{2,1,0:T(4,128)S(1)}, u32[]{:S(2)}, u32[]{:S(2)}) %all-to-all-start) | async-done | bytes 131104 | tf_op jit(solution)/shard_map/all_to_all | solution.py:513
  (79 shorter events, 17.8 us)
Async XLA Ops:
  2.9 12.8 %collective-permute-start = (bf16[832,256]{1,0:T(8,128)(2,1)S(1)}, bf16[832,256]{1,0:T(8,128)(2,1)S(1)}, u32[]{:S(2)}, u32[]{:S(2)}) collective-permute-start(bf16[832,256]{1,0:T(8,128)(2,1)S(1)} %pad_maximum_fusion.1.refs_0_), channel_id=1, source_target_pairs={{0,8},{8,16},{16,24},{24,28},{28,20},{20,12},{12,4},{4,0},{1,9},{9... | collective-permute-start | bytes 1277960 | tf_op jit(solution)/shard_map/ppermute | solution.py:65
  6.0 11.6 %collective-permute-start.1 = (bf16[832,256]{1,0:T(8,128)(2,1)S(1)}, bf16[832,256]{1,0:T(8,128)(2,1)S(1)}, u32[]{:S(2)}, u32[]{:S(2)}) collective-permute-start(bf16[832,256]{1,0:T(8,128)(2,1)S(1)} %pad_maximum_fusion.1.refs_0_), channel_id=1, source_target_pairs={{8,0},{16,8},{24,16},{28,24},{20,28},{12,20},{4,12},{0,4},{9,1},{1... | collective-permute-start | bytes 1277960 | tf_op jit(solution)/shard_map/ppermute | solution.py:65
  7.2 21.8 %collective-permute-start.2 = (bf16[1,256,256]{2,1,0:T(8,128)(2,1)S(1)}, bf16[1,256,256]{2,1,0:T(8,128)(2,1)S(1)}, u32[]{:S(2)}, u32[]{:S(2)}) collective-permute-start(bf16[1,256,256]{2,1,0:T(8,128)(2,1)S(1)} %maximum_bitcast_fusion.refs_7_), channel_id=1, source_target_pairs={{0,2},{1,3},{2,0},{3,1},{4,6},{5,7},{6,4},{7,5},{8,10},{9,11},{10,... | collective-permute-start | bytes 393224 | tf_op jit(solution)/shard_map/ppermute | solution.py:344
  15.8 11.0 %collective-permute-start.3 = (bf16[832,256]{1,0:T(8,128)(2,1)S(1)}, bf16[832,256]{1,0:T(8,128)(2,1)S(1)}, u32[]{:S(2)}, u32[]{:S(2)}) collective-permute-start(bf16[832,256]{1,0:T(8,128)(2,1)S(1)} %collective-permute-done.refs_0_.refs_1_), channel_id=1, source_target_pairs={{0,8},{8,16},{16,24},{24,28},{28,20},{20,12},{12,4},{4,0},{1,9},{9... | collective-permute-start | bytes 1277960 | tf_op jit(solution)/shard_map/ppermute | solution.py:65
  17.6 10.7 %collective-permute-start.4 = (bf16[832,256]{1,0:T(8,128)(2,1)S(1)}, bf16[832,256]{1,0:T(8,128)(2,1)S(1)}, u32[]{:S(2)}, u32[]{:S(2)}) collective-permute-start(bf16[832,256]{1,0:T(8,128)(2,1)S(1)} %collective-permute-done.1.refs_1_.refs_2_), channel_id=1, source_target_pairs={{8,0},{16,8},{24,16},{28,24},{20,28},{12,20},{4,12},{0,4},{9,1},{1... | collective-permute-start | bytes 1277960 | tf_op jit(solution)/shard_map/ppermute | solution.py:65
  26.8 10.1 %collective-permute-start.6 = (bf16[832,256]{1,0:T(8,128)(2,1)S(1)}, bf16[832,256]{1,0:T(8,128)(2,1)S(1)}, u32[]{:S(2)}, u32[]{:S(2)}) collective-permute-start(bf16[832,256]{1,0:T(8,128)(2,1)S(1)} %collective-permute-done.3.refs_2_.refs_3_), channel_id=1, source_target_pairs={{0,8},{8,16},{16,24},{24,28},{28,20},{20,12},{12,4},{4,0},{1,9},{9... | collective-permute-start | bytes 1277960 | tf_op jit(solution)/shard_map/ppermute | solution.py:65
  28.3 9.5 %collective-permute-start.7 = (bf16[832,256]{1,0:T(8,128)(2,1)S(1)}, bf16[832,256]{1,0:T(8,128)(2,1)S(1)}, u32[]{:S(2)}, u32[]{:S(2)}) collective-permute-start(bf16[832,256]{1,0:T(8,128)(2,1)S(1)} %collective-permute-done.4.refs_3_.refs_4_), channel_id=1, source_target_pairs={{8,0},{16,8},{24,16},{28,24},{20,28},{12,20},{4,12},{0,4},{9,1},{1... | collective-permute-start | bytes 1277960 | tf_op jit(solution)/shard_map/ppermute | solution.py:65
  29.6 8.2 %collective-permute-start.5 = (bf16[2,256,256]{2,1,0:T(8,128)(2,1)S(1)}, bf16[2,256,256]{2,1,0:T(8,128)(2,1)S(1)}, u32[]{:S(2)}, u32[]{:S(2)}) collective-permute-start(bf16[2,256,256]{2,1,0:T(8,128)(2,1)S(1)} %shard_map.85.refs_10_), channel_id=1, source_target_pairs={{0,2},{1,3},{2,0},{3,1},{4,6},{5,7},{6,4},{7,5},{8,10},{9,11},{10,... | collective-permute-start | bytes 786440 | tf_op jit(solution)/shard_map/ppermute | solution.py:344
  37.8 5.0 %collective-permute-start.9 = (bf16[2,2,256,256]{3,2,1,0:T(8,128)(2,1)S(1)}, bf16[2,2,256,256]{3,2,1,0:T(8,128)(2,1)S(1)}, u32[]{:S(2)}, u32[]{:S(2)}) collective-permute-start(bf16[2,2,256,256]{3,2,1,0:T(8,128)(2,1)S(1)} %pad_maximum_fusion), channel_id=1, source_target_pairs={{0,1},{1,0},{2,3},{3,2},{4,5},{5,4},{6,7},{7,6},{8,9},{9,8},{10,11... | collective-permute-start | bytes 1572872 | tf_op jit(solution)/shard_map/ppermute | solution.py:338
  37.9 4.9 %collective-permute-start.8 = (bf16[2,1,256,256]{3,2,1,0:T(8,128)(2,1)S(1)}, bf16[2,1,256,256]{3,2,1,0:T(8,128)(2,1)S(1)}, u32[]{:S(2)}, u32[]{:S(2)}) collective-permute-start(bf16[2,1,256,256]{3,2,1,0:T(8,128)(2,1)S(1)} %pad_maximum_fusion.3), channel_id=1, source_target_pairs={{0,1},{1,0},{2,3},{3,2},{4,5},{5,4},{6,7},{7,6},{8,9},{9,8},{10,11... | collective-permute-start | bytes 786440 | tf_op jit(solution)/shard_map/ppermute | solution.py:338
  38.5 8.0 %collective-permute-start.11 = (bf16[384,256]{1,0:T(8,128)(2,1)S(1)}, bf16[384,256]{1,0:T(8,128)(2,1)S(1)}, u32[]{:S(2)}, u32[]{:S(2)}) collective-permute-start(bf16[384,256]{1,0:T(8,128)(2,1)S(1)} %slice.100), channel_id=1, source_target_pairs={{0,8},{8,16},{16,24},{24,28},{28,20},{20,12},{12,4},{4,0},{1,9},{9... | collective-permute-start | bytes 589832 | tf_op jit(solution)/shard_map/ppermute | solution.py:65
  40.1 6.6 %collective-permute-start.12 = (bf16[384,256]{1,0:T(8,128)(2,1)S(1)}, bf16[384,256]{1,0:T(8,128)(2,1)S(1)}, u32[]{:S(2)}, u32[]{:S(2)}) collective-permute-start(bf16[384,256]{1,0:T(8,128)(2,1)S(1)} %slice.101), channel_id=1, source_target_pairs={{8,0},{16,8},{24,16},{28,24},{20,28},{12,20},{4,12},{0,4},{9,1},{1... | collective-permute-start | bytes 589832 | tf_op jit(solution)/shard_map/ppermute | solution.py:65
  41.2 5.2 %collective-permute-start.10 = (bf16[1,256,256]{2,1,0:T(8,128)(2,1)S(1)}, bf16[1,256,256]{2,1,0:T(8,128)(2,1)S(1)}, u32[]{:S(2)}, u32[]{:S(2)}) collective-permute-start(bf16[1,256,256]{2,1,0:T(8,128)(2,1)S(1)} %shard_map.88.refs_2_), channel_id=1, source_target_pairs={{0,2},{1,3},{2,0},{3,1},{4,6},{5,7},{6,4},{7,5},{8,10},{9,11},{10,... | collective-permute-start | bytes 393224 | tf_op jit(solution)/shard_map/ppermute | solution.py:344
  46.8 1.6 %collective-permute-start.13 = (bf16[2,1,256,256]{3,2,1,0:T(8,128)(2,1)S(1)}, bf16[2,1,256,256]{3,2,1,0:T(8,128)(2,1)S(1)}, u32[]{:S(2)}, u32[]{:S(2)}) collective-permute-start(bf16[2,1,256,256]{3,2,1,0:T(8,128)(2,1)S(1)} %pad_maximum_fusion.4), channel_id=1, source_target_pairs={{0,1},{1,0},{2,3},{3,2},{4,5},{5,4},{6,7},{7,6},{8,9},{9,8},{10,11... | collective-permute-start | bytes 786440 | tf_op jit(solution)/shard_map/ppermute | solution.py:338
  51.4 1.5 %collective-permute-start.14 = (f32[192,256]{1,0:T(8,128)S(1)}, f32[192,256]{1,0:T(8,128)S(1)}, u32[]{:S(2)}, u32[]{:S(2)}) collective-permute-start(f32[192,256]{1,0:T(8,128)S(1)} %get-tuple-element.97), channel_id=1, source_target_pairs={{0,1},{1,0},{2,3},{3,2},{4,5},{5,4},{6,7},{7,6},{8,9},{9,8},{10,11... | collective-permute-start | bytes 589832 | tf_op jit(solution)/shard_map/ppermute | solution.py:439
  52.9 7.0 %collective-permute-start.17 = (f32[192,256]{1,0:T(8,128)S(1)}, f32[192,256]{1,0:T(8,128)S(1)}, u32[]{:S(2)}, u32[]{:S(2)}) collective-permute-start(f32[192,256]{1,0:T(8,128)S(1)} %add.59), channel_id=1, source_target_pairs={{0,2},{1,3},{2,0},{3,1},{4,6},{5,7},{6,4},{7,5},{8,10},{9,11},{10,... | collective-permute-start | bytes 589832 | tf_op jit(solution)/shard_map/ppermute | solution.py:453
  54.5 5.5 %copy-start.3 = (f32[1,1,1,192]{3,2,1,0:T(1,128)S(1)}, f32[1,1,1,192]{3,2,1,0:T(1,128)}, u32[]{:S(2)}) copy-start(f32[1,1,1,192]{3,2,1,0:T(1,128)} %param.9) | copy-start | bytes 2308
  56.7 1.4 %collective-permute-start.15 = (f32[96,256]{1,0:T(8,128)S(1)}, f32[96,256]{1,0:T(8,128)S(1)}, u32[]{:S(2)}, u32[]{:S(2)}) collective-permute-start(f32[96,256]{1,0:T(8,128)S(1)} %get-tuple-element.134), channel_id=1, source_target_pairs={{0,1},{1,0},{2,3},{3,2},{4,5},{5,4},{6,7},{7,6},{8,9},{9,8},{10,11... | collective-permute-start | bytes 294920 | tf_op jit(solution)/shard_map/ppermute | solution.py:468
  56.7 1.4 %collective-permute-start.16 = (f32[96,256]{1,0:T(8,128)S(1)}, f32[96,256]{1,0:T(8,128)S(1)}, u32[]{:S(2)}, u32[]{:S(2)}) collective-permute-start(f32[96,256]{1,0:T(8,128)S(1)} %get-tuple-element.135), channel_id=1, source_target_pairs={{0,1},{1,0},{2,3},{3,2},{4,5},{5,4},{6,7},{7,6},{8,9},{9,8},{10,11... | collective-permute-start | bytes 294920 | tf_op jit(solution)/shard_map/ppermute | solution.py:468
  60.0 6.2 %collective-permute-start.18 = (f32[192,256]{1,0:T(8,128)S(1)}, f32[192,256]{1,0:T(8,128)S(1)}, u32[]{:S(2)}, u32[]{:S(2)}) collective-permute-start(f32[192,256]{1,0:T(8,128)S(1)} %fusion.9.refs_0_.refs_6_), channel_id=1, source_target_pairs={{0,8},{8,16},{16,24},{24,28},{28,20},{20,12},{12,4},{4,0},{1,9},{9... | collective-permute-start | bytes 589832 | tf_op jit(solution)/shard_map/ppermute | solution.py:65
  61.7 6.1 %collective-permute-start.20 = (f32[192,256]{1,0:T(8,128)S(1)}, f32[192,256]{1,0:T(8,128)S(1)}, u32[]{:S(2)}, u32[]{:S(2)}) collective-permute-start(f32[192,256]{1,0:T(8,128)S(1)} %fusion.9.refs_0_.refs_6_), channel_id=1, source_target_pairs={{8,0},{16,8},{24,16},{28,24},{20,28},{12,20},{4,12},{0,4},{9,1},{1... | collective-permute-start | bytes 589832 | tf_op jit(solution)/shard_map/ppermute | solution.py:65
  62.1 6.1 %collective-permute-start.26 = (f32[192,256]{1,0:T(8,128)S(1)}, f32[192,256]{1,0:T(8,128)S(1)}, u32[]{:S(2)}, u32[]{:S(2)}) collective-permute-start(f32[192,256]{1,0:T(8,128)S(1)} %fusion.9.refs_0_.refs_6_), channel_id=1, source_target_pairs={{0,2},{1,3},{2,0},{3,1},{4,6},{5,7},{6,4},{7,5},{8,10},{9,11},{10,... | collective-permute-start | bytes 589832 | tf_op jit(solution)/shard_map/ppermute | solution.py:470
  66.2 5.8 %collective-permute-start.19 = (f32[192,256]{1,0:T(8,128)S(1)}, f32[192,256]{1,0:T(8,128)S(1)}, u32[]{:S(2)}, u32[]{:S(2)}) collective-permute-start(f32[192,256]{1,0:T(8,128)S(1)} %collective-permute-done.18.refs_1_), channel_id=1, source_target_pairs={{0,8},{8,16},{16,24},{24,28},{28,20},{20,12},{12,4},{4,0},{1,9},{9... | collective-permute-start | bytes 589832 | tf_op jit(solution)/shard_map/ppermute | solution.py:65
  67.8 5.8 %collective-permute-start.21 = (f32[192,256]{1,0:T(8,128)S(1)}, f32[192,256]{1,0:T(8,128)S(1)}, u32[]{:S(2)}, u32[]{:S(2)}) collective-permute-start(f32[192,256]{1,0:T(8,128)S(1)} %collective-permute-done.20.refs_2_), channel_id=1, source_target_pairs={{8,0},{16,8},{24,16},{28,24},{20,28},{12,20},{4,12},{0,4},{9,1},{1... | collective-permute-start | bytes 589832 | tf_op jit(solution)/shard_map/ppermute | solution.py:65
  68.3 13.1 %collective-permute-start.27 = (f32[2,192,256]{2,1,0:T(8,128)S(1)}, f32[2,192,256]{2,1,0:T(8,128)S(1)}, u32[]{:S(2)}, u32[]{:S(2)}) collective-permute-start(f32[2,192,256]{2,1,0:T(8,128)S(1)} %pad_maximum_fusion.2), channel_id=1, source_target_pairs={{0,1},{1,0},{2,3},{3,2},{4,5},{5,4},{6,7},{7,6},{8,9},{9,8},{10,11... | collective-permute-start | bytes 1179656 | tf_op jit(solution)/shard_map/ppermute | solution.py:471
  72.0 5.7 %collective-permute-start.22 = (f32[192,256]{1,0:T(8,128)S(1)}, f32[192,256]{1,0:T(8,128)S(1)}, u32[]{:S(2)}, u32[]{:S(2)}) collective-permute-start(f32[192,256]{1,0:T(8,128)S(1)} %collective-permute-done.19.refs_3_), channel_id=1, source_target_pairs={{0,8},{8,16},{16,24},{24,28},{28,20},{20,12},{12,4},{4,0},{1,9},{9... | collective-permute-start | bytes 589832 | tf_op jit(solution)/shard_map/ppermute | solution.py:65
  73.6 5.7 %collective-permute-start.24 = (f32[192,256]{1,0:T(8,128)S(1)}, f32[192,256]{1,0:T(8,128)S(1)}, u32[]{:S(2)}, u32[]{:S(2)}) collective-permute-start(f32[192,256]{1,0:T(8,128)S(1)} %collective-permute-done.21.refs_4_), channel_id=1, source_target_pairs={{8,0},{16,8},{24,16},{28,24},{20,28},{12,20},{4,12},{0,4},{9,1},{1... | collective-permute-start | bytes 589832 | tf_op jit(solution)/shard_map/ppermute | solution.py:65
  79.2 5.9 %collective-permute-start.23 = (f32[128,256]{1,0:T(8,128)S(1)}, f32[128,256]{1,0:T(8,128)S(1)}, u32[]{:S(2)}, u32[]{:S(2)}) collective-permute-start(f32[128,256]{1,0:T(8,128)S(1)} %slice.102), channel_id=1, source_target_pairs={{0,8},{8,16},{16,24},{24,28},{28,20},{20,12},{12,4},{4,0},{1,9},{9... | collective-permute-start | bytes 393224 | tf_op jit(solution)/shard_map/ppermute | solution.py:65
  80.9 4.3 %collective-permute-start.25 = (f32[64,256]{1,0:T(8,128)S(1)}, f32[64,256]{1,0:T(8,128)S(1)}, u32[]{:S(2)}, u32[]{:S(2)}) collective-permute-start(f32[64,256]{1,0:T(8,128)S(1)} %slice.103), channel_id=1, source_target_pairs={{8,0},{16,8},{24,16},{28,24},{20,28},{12,20},{4,12},{0,4},{9,1},{1... | collective-permute-start | bytes 196616 | tf_op jit(solution)/shard_map/ppermute | solution.py:65
  86.9 3.5 %collective-permute-start.28 = (f32[2,192,256]{2,1,0:T(8,128)S(1)}, f32[2,192,256]{2,1,0:T(8,128)S(1)}, u32[]{:S(2)}, u32[]{:S(2)}) collective-permute-start(f32[2,192,256]{2,1,0:T(8,128)S(1)} %slice.92), channel_id=1, source_target_pairs={{0,1},{1,0},{2,3},{3,2},{4,5},{5,4},{6,7},{7,6},{8,9},{9,8},{10,11... | collective-permute-start | bytes 1179656 | tf_op jit(solution)/shard_map/ppermute | solution.py:514
  87.0 11.7 %all-to-all-start = ((f32[32,4,256]{2,1,0:T(4,128)}), f32[32,4,256]{2,1,0:T(4,128)S(1)}, u32[]{:S(2)}, u32[]{:S(2)}) async-start(f32[32,4,256]{2,1,0:T(4,128)} %get-tuple-element.120), calls=%async_computation | async-start | bytes 262144 | tf_op jit(solution)/shard_map/all_to_all | solution.py:513
  90.5 8.4 %collective-permute-start.29 = (f32[192,256]{1,0:T(8,128)S(1)}, f32[192,256]{1,0:T(8,128)S(1)}, u32[]{:S(2)}, u32[]{:S(2)}) collective-permute-start(f32[192,256]{1,0:T(8,128)S(1)} %fusion.7), channel_id=1, source_target_pairs={{0,2},{1,3},{2,0},{3,1},{4,6},{5,7},{6,4},{7,5},{8,10},{9,11},{10,... | collective-permute-start | bytes 589832 | tf_op jit(solution)/shard_map/ppermute | solution.py:515
  (3 other events, 5.6 us)

commit v10 on v9

--- a/solution.py
+++ b/solution.py
@@ -146,7 +146,7 @@
     n, width, head_part, block, groups = sizes
     shard_refs, refs = refs[: n - 1], refs[n - 1 :]
     round_refs, refs = refs[: 3 * groups], refs[3 * groups :]
-    prior_ref, now_ref, later_ref, side_ref, columns, rows, target = refs
+    prior_ref, now_ref, later_ref, columns, rows, target = refs
     count = shard_refs[0].shape[1]
     for index in range(n - 1):
         lanes = pl.ds(pl.multiple_of(meta[index] * count, 128), count)
@@ -160,7 +160,19 @@
         column = columns[lanes, :done]
         value = prior_ref[:, lanes] + dot(rows[:, :done], column, NT) * scale
         now_ref[:, lanes], later_ref[:, lanes] = value[: now_ref.shape[0]], value[now_ref.shape[0] :]
-        side_ref[lanes, :] = dot(column, target[:, :done], NT)
+
+
+def rest_kernel(sizes, meta, low_ref, high_ref, columns, target, side_ref, last_columns):
+    n, width, block = sizes
+    done = columns.shape[1] - last_columns.shape[1]
+    last_columns[...] = columns[:, done:]
+    base = pl.multiple_of(meta[2 * n - 1] * width, 16)
+    half = low_ref.shape[0]
+    last_columns[pl.ds(base, half), :] = low_ref[...]
+    last_columns[pl.ds(pl.multiple_of(base + half, 16), width - half), :] = high_ref[...]
+    for start in range(0, columns.shape[0], block):
+        lanes = slice(start, start + block)
+        side_ref[lanes, :] = dot(columns[lanes, :done], target[:, :done], NT)
 
 
 def tile_rows_of(first, early, last_rows, last_columns, block, scale, tile_ref, gram_ref, me, piece, stored):
@@ -178,16 +190,11 @@
 
 
 def first_kernel(sizes, meta, *refs):
-    n, piece, width, head_part, block = sizes
-    low_ref, high_ref, *round_refs = refs[:5]
-    early, early_side, columns, image_ref, gram_ref, tile_ref = refs[5:11]
-    side_high, side_low, last_columns, last_rows, last_target, stored = refs[11:]
-    total_rows, count = columns.shape[1], last_rows.shape[1]
-    last_columns[...] = columns[:, total_rows - count :]
-    base = pl.multiple_of(meta[2 * n - 1] * width, 16)
-    half = low_ref.shape[0]
-    last_columns[pl.ds(base, half), :] = low_ref[...]
-    last_columns[pl.ds(pl.multiple_of(base + half, 16), width - half), :] = high_ref[...]
+    n, piece, total_rows, head_part, block = sizes
+    round_refs = refs[:3]
+    early, early_side, last_columns, image_ref, gram_ref, tile_ref = refs[3:9]
+    side_high, side_low, last_rows, last_target, stored = refs[9:]
+    count = last_rows.shape[1]
     place_rows(round_refs, meta[2 * n], head_part, last_rows, last_target, 0, count)
     scale = 1.0 / total_rows
     me = meta[2 * n]
@@ -388,16 +395,15 @@
         gathered += arrived
         open_groups(step)
         if step == ring.far - 1:
-            early, early_later, early_side, columns, rows, target = call(
+            early, early_later, columns, rows, target = call(
                 functools.partial(early_kernel, (n, width, head_part, block, 2)),
                 gram_meta,
                 [*gathered, *groups[0], *groups[1], prior],
                 [VMEM] * (n + 6),
-                [VMEM] * 6,
+                [VMEM] * 5,
                 [
                     jax.ShapeDtypeStruct((2 * piece, tile_columns), f32),
                     jax.ShapeDtypeStruct((2 * piece, tile_columns), f32),
-                    jax.ShapeDtypeStruct((tile_columns, heads), f32),
                     jax.ShapeDtypeStruct((tile_columns, total_rows), bf16),
                     jax.ShapeDtypeStruct((tile_rows, total_rows), bf16),
                     jax.ShapeDtypeStruct((heads, total_rows), bf16),
@@ -414,19 +420,33 @@
         shape = (pieces * piece, tile_columns)
         return [pltpu.VMEM(shape, f32), pltpu.SemaphoreType.DMA((pieces * (tile_columns // block),))]
 
-    sent, gram, first_tile, side_high, side_low, last_columns, last_rows, last_target = call(
-        functools.partial(first_kernel, (n, piece, width, head_part, block)),
+    early_side, last_columns = call(
+        functools.partial(rest_kernel, (n, width, block)),
         gram_meta,
-        [*gathered[-2:], *groups[2], early, early_side, columns],
-        [VMEM] * 8,
-        [VMEM, HBM] + [VMEM] * 6,
+        [*gathered[-2:], columns, target],
+        [VMEM] * 4,
+        [VMEM] * 2,
+        [
+            jax.ShapeDtypeStruct((tile_columns, heads), f32),
+            jax.ShapeDtypeStruct((tile_columns, row_count), bf16),
+        ],
+        [],
+        EARLY_BYTES,
+        2 * tile_columns * heads * (total_rows - row_count),
+        2 * tile_columns * total_rows,
+    )
+    sent, gram, first_tile, side_high, side_low, last_rows, last_target = call(
+        functools.partial(first_kernel, (n, piece, total_rows, head_part, block)),
+        gram_meta,
+        [*groups[2], early, early_side, last_columns],
+        [VMEM] * 6,
+        [VMEM, HBM] + [VMEM] * 5,
         [
             piece_shape,
             gram_shape,
             jax.ShapeDtypeStruct((2 * piece, tile_columns), f32),
             jax.ShapeDtypeStruct((tile_columns, heads), bf16),
             jax.ShapeDtypeStruct((tile_columns, heads), bf16),
-            jax.ShapeDtypeStruct((tile_columns, row_count), bf16),
             jax.ShapeDtypeStruct((tile_rows, row_count), bf16),
             jax.ShapeDtypeStruct((heads, row_count), bf16),
         ],

time: 100 us -> 100 us (level)
  waiting for transfers between devices: 36.2 us -> 34.6 us
    ppermute x3, waiting for transfers between devices: 1.53 us -> 0.05 us  [near_of(): lax.ppermute(jnp.stack([mine, far]), 'tcol', swap(tcol_count, 1))]
    ppermute x8, waiting for transfers between devices: 3.53 us -> 2.16 us  [move(): lax.ppermute(back, axes, self.back)]
    pallas_call x10 -> x11, Pallas kernels: 16.6 us -> 17.3 us  [call(): pl.pallas_call(body, grid_spec=pltpu.PrefetchScalarGridSpec(num_scalar_pr...]
  transfers between devices with their start and end apart: 31 -> 31, of which waited for: 17 -> 16; matrix products, arithmetic and copies ran while one was open for 4% -> 4% of each run, Pallas kernels for 12% -> 13%
where the time goes in v10:
time: 100 us; the launch traced here: 99.7 us
  waiting for transfers between devices  34.6 us (35%)
  starting transfers between devices  33.2 us (33%)
  Pallas kernels  17.3 us (17%)
  local copies, waits for them, and re-layouts  10.3 us (10%)
  between operations  2.88 us (3%)
  other arithmetic  1.39 us (1%)
    ppermute x8, waiting for transfers between devices, move(): lax.ppermute(ahead, axes, self.ahead)  22.2 us
    pallas_call x11, Pallas kernels, call(): pl.pallas_call(body, grid_spec=pltpu.PrefetchScalarGridSpec(num_scalar_pr...  17.3 us
    ppermute x8, starting transfers between devices, move(): lax.ppermute(ahead, axes, self.ahead)  14.4 us
    unnamed x10, local copies, waits for them, and re-layouts  6.83 us
    all_to_all x1, waiting for transfers between devices, shards(): sums = lax.all_to_all(sums, axes, split_axis=0, concat_axis=0, tiled=True)  6.35 us
    ppermute x3, starting transfers between devices, open_groups(): lax.ppermute(mine, 'tcol', swap(tcol_count, 2))  5.01 us
    all_to_all x1, starting transfers between devices, shards(): sums = lax.all_to_all(sums, axes, split_axis=0, concat_axis=0, tiled=True)  3.64 us
    ppermute x8, starting transfers between devices, move(): lax.ppermute(back, axes, self.back)  3.32 us
  transfers between devices with their start and end apart: 31, of which 16 were waited for; matrix products, arithmetic and copies ran while one was open for 4% of the time, Pallas kernels for 13%

profile of v10, /device:TPU:0, one launch (start us, length us, event | category | flops | bytes accessed | tf_op | source)
XLA Modules:
  0.0 99.7 jit_solution(5005741382784306542)
XLA Ops:
  2.9 3.1 %collective-permute-start = (bf16[832,256]{1,0:T(8,128)(2,1)S(1)}, bf16[832,256]{1,0:T(8,128)(2,1)S(1)}, u32[]{:S(2)}, u32[]{:S(2)}) collective-permute-start(bf16[832,256]{1,0:T(8,128)(2,1)S(1)} %pad_maximum_fusion.1.refs_0_), channel_id=1, source_target_pairs={{0,8},{8,16},{16,24},{24,28},{28,20},{20,12},{12,4},{4,0},{1,9},{9... | collective-permute-start | bytes 1277960 | tf_op jit(solution)/shard_map/ppermute | solution.py:65
  7.2 2.0 %collective-permute-start.2 = (bf16[1,256,256]{2,1,0:T(8,128)(2,1)S(1)}, bf16[1,256,256]{2,1,0:T(8,128)(2,1)S(1)}, u32[]{:S(2)}, u32[]{:S(2)}) collective-permute-start(bf16[1,256,256]{2,1,0:T(8,128)(2,1)S(1)} %maximum_bitcast_fusion.refs_7_), channel_id=1, source_target_pairs={{0,2},{1,3},{2,0},{3,1},{4,6},{5,7},{6,4},{7,5},{8,10},{9,11},{10,... | collective-permute-start | bytes 393224 | tf_op jit(solution)/shard_map/ppermute | solution.py:351
  9.2 1.3 %dynamic_slice.12 = s32[1,1]{1,0:T(1,128)} dynamic-slice(s32[4,2]{1,0:T(4,128)} %constant.37.clone, s32[]{:T(128)S(6)} %select_n.15, s32[]{:T(128)S(6)} %select_n.16), dynamic_slice_sizes={1,1} | dynamic-slice | bytes 12 | tf_op jit(solution)/shard_map/dynamic_slice | solution.py:309
  13.1 2.7 %collective-permute-done.refs_0_.refs_1_ = bf16[832,256]{1,0:T(8,128)(2,1)S(1)} collective-permute-done((bf16[832,256]{1,0:T(8,128)(2,1)S(1)}, bf16[832,256]{1,0:T(8,128)(2,1)S(1)}, u32[]{:S(2)}, u32[]{:S(2)}) %collective-permute-start) | collective-permute-done | bytes 426016 | tf_op jit(solution)/shard_map/ppermute | solution.py:65
  15.8 1.8 %collective-permute-start.3 = (bf16[832,256]{1,0:T(8,128)(2,1)S(1)}, bf16[832,256]{1,0:T(8,128)(2,1)S(1)}, u32[]{:S(2)}, u32[]{:S(2)}) collective-permute-start(bf16[832,256]{1,0:T(8,128)(2,1)S(1)} %collective-permute-done.refs_0_.refs_1_), channel_id=1, source_target_pairs={{0,8},{8,16},{16,24},{24,28},{28,20},{20,12},{12,4},{4,0},{1,9},{9... | collective-permute-start | bytes 1277960 | tf_op jit(solution)/shard_map/ppermute | solution.py:65
  17.9 8.9 %collective-permute-done.3.refs_2_.refs_3_ = bf16[832,256]{1,0:T(8,128)(2,1)S(1)} collective-permute-done((bf16[832,256]{1,0:T(8,128)(2,1)S(1)}, bf16[832,256]{1,0:T(8,128)(2,1)S(1)}, u32[]{:S(2)}, u32[]{:S(2)}) %collective-permute-start.3) | collective-permute-done | bytes 426016 | tf_op jit(solution)/shard_map/ppermute | solution.py:65
  26.8 1.5 %collective-permute-start.6 = (bf16[832,256]{1,0:T(8,128)(2,1)S(1)}, bf16[832,256]{1,0:T(8,128)(2,1)S(1)}, u32[]{:S(2)}, u32[]{:S(2)}) collective-permute-start(bf16[832,256]{1,0:T(8,128)(2,1)S(1)} %collective-permute-done.3.refs_2_.refs_3_), channel_id=1, source_target_pairs={{0,8},{8,16},{16,24},{24,28},{28,20},{20,12},{12,4},{4,0},{1,9},{9... | collective-permute-start | bytes 1277960 | tf_op jit(solution)/shard_map/ppermute | solution.py:65
  29.6 1.5 %collective-permute-start.5 = (bf16[2,256,256]{2,1,0:T(8,128)(2,1)S(1)}, bf16[2,256,256]{2,1,0:T(8,128)(2,1)S(1)}, u32[]{:S(2)}, u32[]{:S(2)}) collective-permute-start(bf16[2,256,256]{2,1,0:T(8,128)(2,1)S(1)} %shard_map.85.refs_10_), channel_id=1, source_target_pairs={{0,2},{1,3},{2,0},{3,1},{4,6},{5,7},{6,4},{7,5},{8,10},{9,11},{10,... | collective-permute-start | bytes 786440 | tf_op jit(solution)/shard_map/ppermute | solution.py:351
  31.1 2.3 %copy-done.2 = f32[4,1,1,192,1536]{4,3,2,1,0:T(8,128)S(1)} copy-done((f32[4,1,1,192,1536]{4,3,2,1,0:T(8,128)S(1)}, f32[4,1,1,192,1536]{4,3,2,1,0:T(8,128)}, u32[]{:S(2)}) %copy-start.2) | copy-done | bytes 4718616
  33.9 2.9 %collective-permute-done.6.refs_5_.refs_2_ = bf16[832,256]{1,0:T(8,128)(2,1)S(1)} collective-permute-done((bf16[832,256]{1,0:T(8,128)(2,1)S(1)}, bf16[832,256]{1,0:T(8,128)(2,1)S(1)}, u32[]{:S(2)}, u32[]{:S(2)}) %collective-permute-start.6) | collective-permute-done | bytes 426016 | tf_op jit(solution)/shard_map/ppermute | solution.py:65
  38.5 1.6 %collective-permute-start.11 = (bf16[384,256]{1,0:T(8,128)(2,1)S(1)}, bf16[384,256]{1,0:T(8,128)(2,1)S(1)}, u32[]{:S(2)}, u32[]{:S(2)}) collective-permute-start(bf16[384,256]{1,0:T(8,128)(2,1)S(1)} %slice.100), channel_id=1, source_target_pairs={{0,8},{8,16},{16,24},{24,28},{28,20},{20,12},{12,4},{4,0},{1,9},{9... | collective-permute-start | bytes 589832 | tf_op jit(solution)/shard_map/ppermute | solution.py:65
  41.2 1.6 %collective-permute-start.10 = (bf16[1,256,256]{2,1,0:T(8,128)(2,1)S(1)}, bf16[1,256,256]{2,1,0:T(8,128)(2,1)S(1)}, u32[]{:S(2)}, u32[]{:S(2)}) collective-permute-start(bf16[1,256,256]{2,1,0:T(8,128)(2,1)S(1)} %shard_map.88.refs_0_), channel_id=1, source_target_pairs={{0,2},{1,3},{2,0},{3,1},{4,6},{5,7},{6,4},{7,5},{8,10},{9,11},{10,... | collective-permute-start | bytes 393224 | tf_op jit(solution)/shard_map/ppermute | solution.py:351
  42.8 3.0 %shard_map.87 = (f32[384,1536]{1,0:T(8,128)S(1)}, f32[384,1536]{1,0:T(8,128)S(1)}, bf16[1536,1024]{1,0:T(8,128)(2,1)S(1)}, bf16[768,1024]{1,0:T(8,128)(2,1)S(1)}, bf16[256,1024]{1,0:T(8,128)(2,1)S(1)}) custom-call(s32[17]{0:T(128)S(1)} %get-tuple-element.63.meta, bf16[832,256]{1,0:T(8,128)(2,1)S(1)} %pad_maximum_fusion.1.refs_0_, ...), custom_call_target="tpu_custom_call" | custom-call | flops 1811939328 | bytes 9437184 | tf_op jit(solution)/shard_map/pallas_call | solution.py:277
  46.8 1.5 %shard_map.89 = (f32[1536,256]{1,0:T(8,128)S(1)}, bf16[1536,256]{1,0:T(8,128)(2,1)S(1)}) custom-call(s32[17]{0:T(128)S(1)} %get-tuple-element.63.meta, bf16[384,256]{1,0:T(8,128)(2,1)S(1)} %collective-permute-done.11.low_ref, bf16[384,256]{1,0:T(8,128)(2,1)S(1)} %collective-permute-done.12.high_ref, bf16[1536,1024]{1,0:T(8,128)(2,1)S(1)} %get-tuple-element.87.columns, ...), custom_call_target="tpu_custom_call" | custom-call | flops 603979776 | bytes 3145728 | tf_op jit(solution)/shard_map/pallas_call | solution.py:277
  48.4 2.9 %shard_map.90 = (f32[192,256]{1,0:T(8,128)S(1)}, f32[768,1536]{1,0:T(8,128)}, f32[384,1536]{1,0:T(8,128)S(1)}, bf16[1536,256]{1,0:T(8,128)(2,1)S(1)}, bf16[1536,...) custom-call(s32[17]{0:T(128)S(1)} %get-tuple-element.63.meta, ...), custom_call_target="tpu_custom_call" | custom-call | flops 754974720 | bytes 4718592 | tf_op jit(solution)/shard_map/pallas_call | solution.py:277
  52.9 1.6 %collective-permute-start.17 = (f32[192,256]{1,0:T(8,128)S(1)}, f32[192,256]{1,0:T(8,128)S(1)}, u32[]{:S(2)}, u32[]{:S(2)}) collective-permute-start(f32[192,256]{1,0:T(8,128)S(1)} %add.59), channel_id=1, source_target_pairs={{0,2},{1,3},{2,0},{3,1},{4,6},{5,7},{6,4},{7,5},{8,10},{9,11},{10,... | collective-permute-start | bytes 589832 | tf_op jit(solution)/shard_map/ppermute | solution.py:473
  54.5 2.1 %shard_map.92 = (f32[768,1536]{1,0:T(8,128)}, f32[2,192,256]{2,1,0:T(8,128)S(1)}) custom-call(s32[1]{0:T(128)} %bitcast.meta, f32[384,1536]{1,0:T(8,128)S(1)} %get-tuple-element.100.refs_0_, bf16[1536,256]{1,0:T(8,128)(2,1)S(1)} %get-tuple-element.90.refs_5_.refs_1_, ...), custom_call_target="tpu_custom_call", output_to_operand_aliasing={{0}: (6, {})} | custom-call | flops 1207959552 | bytes 4718592 | tf_op jit(solution)/shard_map/pallas_call | solution.py:277
  58.2 2.0 %collective-permute-done.17 = f32[192,256]{1,0:T(8,128)S(1)} collective-permute-done((f32[192,256]{1,0:T(8,128)S(1)}, f32[192,256]{1,0:T(8,128)S(1)}, u32[]{:S(2)}, u32[]{:S(2)}) %collective-permute-start.17) | collective-permute-done | bytes 196640 | tf_op jit(solution)/shard_map/ppermute | solution.py:473
  60.2 1.6 %collective-permute-start.18 = (f32[192,256]{1,0:T(8,128)S(1)}, f32[192,256]{1,0:T(8,128)S(1)}, u32[]{:S(2)}, u32[]{:S(2)}) collective-permute-start(f32[192,256]{1,0:T(8,128)S(1)} %fusion.9.refs_0_.refs_6_), channel_id=1, source_target_pairs={{0,8},{8,16},{16,24},{24,28},{28,20},{20,12},{12,4},{4,0},{1,9},{9... | collective-permute-start | bytes 589832 | tf_op jit(solution)/shard_map/ppermute | solution.py:65
  62.3 1.5 %collective-permute-start.26 = (f32[192,256]{1,0:T(8,128)S(1)}, f32[192,256]{1,0:T(8,128)S(1)}, u32[]{:S(2)}, u32[]{:S(2)}) collective-permute-start(f32[192,256]{1,0:T(8,128)S(1)} %fusion.9.refs_0_.refs_6_), channel_id=1, source_target_pairs={{0,2},{1,3},{2,0},{3,1},{4,6},{5,7},{6,4},{7,5},{8,10},{9,11},{10,... | collective-permute-start | bytes 589832 | tf_op jit(solution)/shard_map/ppermute | solution.py:490
  63.8 2.8 %collective-permute-done.18.refs_1_ = f32[192,256]{1,0:T(8,128)S(1)} collective-permute-done((f32[192,256]{1,0:T(8,128)S(1)}, f32[192,256]{1,0:T(8,128)S(1)}, u32[]{:S(2)}, u32[]{:S(2)}) %collective-permute-start.18) | collective-permute-done | bytes 196640 | tf_op jit(solution)/shard_map/ppermute | solution.py:65
  66.7 1.6 %collective-permute-start.19 = (f32[192,256]{1,0:T(8,128)S(1)}, f32[192,256]{1,0:T(8,128)S(1)}, u32[]{:S(2)}, u32[]{:S(2)}) collective-permute-start(f32[192,256]{1,0:T(8,128)S(1)} %collective-permute-done.18.refs_1_), channel_id=1, source_target_pairs={{0,8},{8,16},{16,24},{24,28},{28,20},{20,12},{12,4},{4,0},{1,9},{9... | collective-permute-start | bytes 589832 | tf_op jit(solution)/shard_map/ppermute | solution.py:65
  68.8 3.5 %collective-permute-done.19.refs_3_ = f32[192,256]{1,0:T(8,128)S(1)} collective-permute-done((f32[192,256]{1,0:T(8,128)S(1)}, f32[192,256]{1,0:T(8,128)S(1)}, u32[]{:S(2)}, u32[]{:S(2)}) %collective-permute-start.19) | collective-permute-done | bytes 196640 | tf_op jit(solution)/shard_map/ppermute | solution.py:65
  72.3 1.6 %collective-permute-start.22 = (f32[192,256]{1,0:T(8,128)S(1)}, f32[192,256]{1,0:T(8,128)S(1)}, u32[]{:S(2)}, u32[]{:S(2)}) collective-permute-start(f32[192,256]{1,0:T(8,128)S(1)} %collective-permute-done.19.refs_3_), channel_id=1, source_target_pairs={{0,8},{8,16},{16,24},{24,28},{28,20},{20,12},{12,4},{4,0},{1,9},{9... | collective-permute-start | bytes 589832 | tf_op jit(solution)/shard_map/ppermute | solution.py:65
  74.5 2.3 %copy-done.1 = f32[768,1536]{1,0:T(8,128)S(1)} copy-done((f32[768,1536]{1,0:T(8,128)S(1)}, f32[768,1536]{1,0:T(8,128)}, u32[]{:S(2)}) %copy-start.1) | copy-done | bytes 4718616
  77.4 1.3 %collective-permute-done.22.refs_5_ = f32[192,256]{1,0:T(8,128)S(1)} collective-permute-done((f32[192,256]{1,0:T(8,128)S(1)}, f32[192,256]{1,0:T(8,128)S(1)}, u32[]{:S(2)}, u32[]{:S(2)}) %collective-permute-start.22) | collective-permute-done | bytes 196640 | tf_op jit(solution)/shard_map/ppermute | solution.py:65
  78.7 1.6 %collective-permute-start.23 = (f32[128,256]{1,0:T(8,128)S(1)}, f32[128,256]{1,0:T(8,128)S(1)}, u32[]{:S(2)}, u32[]{:S(2)}) collective-permute-start(f32[128,256]{1,0:T(8,128)S(1)} %slice.102), channel_id=1, source_target_pairs={{0,8},{8,16},{16,24},{24,28},{28,20},{20,12},{12,4},{4,0},{1,9},{9... | collective-permute-start | bytes 393224 | tf_op jit(solution)/shard_map/ppermute | solution.py:65
  81.0 3.0 %shard_map.94 = (f32[4,192,256]{2,1,0:T(8,128)S(1)}, f32[4,256]{1,0:T(4,128)S(1)}, bf16[768,192]{1,0:T(8,128)(2,1)S(1)}, bf16[768,192]{1,0:T(8,128)(2,1)S(1)}) custom-call(s32[17]{0:T(128)S(1)} %get-tuple-element.107.meta, f32[192,256]{1,0:T(8,128)S(1)} %fusion.9.refs_0_.refs_6_, f32[192,256]{1,0:T(8,128)S(1)} %collective-permute-done.18.refs_1_, ...), custom_call_target="tpu_custom_call" | custom-call | flops 1811939328 | bytes 4718592 | tf_op jit(solution)/shard_map/pallas_call | solution.py:277
  84.8 1.7 %shard_map.95 = (f32[4,192,256]{2,1,0:T(8,128)S(1)}, f32[32,4,256]{2,1,0:T(4,128)}) custom-call(s32[17]{0:T(128)S(1)} %get-tuple-element.107.meta, f32[128,256]{1,0:T(8,128)S(1)} %collective-permute-done.23.refs_0_, f32[64,256]{1,0:T(8,128)S(1)} %collective-permute-done.25.refs_1_, f32[4,192,256]{2,1,0:T(8,128)S(1)} %get-tuple-element.113.refs_2_, ...), custom_call_target="tpu_custom_call" | custom-call | flops 226492416 | bytes 589824 | tf_op jit(solution)/shard_map/pallas_call | solution.py:277
  86.6 3.6 %all-to-all-start = ((f32[32,4,256]{2,1,0:T(4,128)}), f32[32,4,256]{2,1,0:T(4,128)S(1)}, u32[]{:S(2)}, u32[]{:S(2)}) async-start(f32[32,4,256]{2,1,0:T(4,128)} %get-tuple-element.120), calls=%async_computation | async-start | bytes 262144 | tf_op jit(solution)/shard_map/all_to_all | solution.py:533
  90.3 1.8 %collective-permute-start.29 = (f32[192,256]{1,0:T(8,128)S(1)}, f32[192,256]{1,0:T(8,128)S(1)}, u32[]{:S(2)}, u32[]{:S(2)}) collective-permute-start(f32[192,256]{1,0:T(8,128)S(1)} %fusion.7), channel_id=1, source_target_pairs={{0,2},{1,3},{2,0},{3,1},{4,6},{5,7},{6,4},{7,5},{8,10},{9,11},{10,... | collective-permute-start | bytes 589832 | tf_op jit(solution)/shard_map/ppermute | solution.py:535
  92.2 6.4 %all-to-all-done = f32[32,4,256]{2,1,0:T(4,128)S(1)} async-done(((f32[32,4,256]{2,1,0:T(4,128)}), f32[32,4,256]{2,1,0:T(4,128)S(1)}, u32[]{:S(2)}, u32[]{:S(2)}) %all-to-all-start) | async-done | bytes 131104 | tf_op jit(solution)/shard_map/all_to_all | solution.py:533
  (80 shorter events, 18.2 us)
Async XLA Ops:
  2.9 12.8 %collective-permute-start = (bf16[832,256]{1,0:T(8,128)(2,1)S(1)}, bf16[832,256]{1,0:T(8,128)(2,1)S(1)}, u32[]{:S(2)}, u32[]{:S(2)}) collective-permute-start(bf16[832,256]{1,0:T(8,128)(2,1)S(1)} %pad_maximum_fusion.1.refs_0_), channel_id=1, source_target_pairs={{0,8},{8,16},{16,24},{24,28},{28,20},{20,12},{12,4},{4,0},{1,9},{9... | collective-permute-start | bytes 1277960 | tf_op jit(solution)/shard_map/ppermute | solution.py:65
  6.0 11.6 %collective-permute-start.1 = (bf16[832,256]{1,0:T(8,128)(2,1)S(1)}, bf16[832,256]{1,0:T(8,128)(2,1)S(1)}, u32[]{:S(2)}, u32[]{:S(2)}) collective-permute-start(bf16[832,256]{1,0:T(8,128)(2,1)S(1)} %pad_maximum_fusion.1.refs_0_), channel_id=1, source_target_pairs={{8,0},{16,8},{24,16},{28,24},{20,28},{12,20},{4,12},{0,4},{9,1},{1... | collective-permute-start | bytes 1277960 | tf_op jit(solution)/shard_map/ppermute | solution.py:65
  7.2 21.8 %collective-permute-start.2 = (bf16[1,256,256]{2,1,0:T(8,128)(2,1)S(1)}, bf16[1,256,256]{2,1,0:T(8,128)(2,1)S(1)}, u32[]{:S(2)}, u32[]{:S(2)}) collective-permute-start(bf16[1,256,256]{2,1,0:T(8,128)(2,1)S(1)} %maximum_bitcast_fusion.refs_7_), channel_id=1, source_target_pairs={{0,2},{1,3},{2,0},{3,1},{4,6},{5,7},{6,4},{7,5},{8,10},{9,11},{10,... | collective-permute-start | bytes 393224 | tf_op jit(solution)/shard_map/ppermute | solution.py:351
  15.8 11.0 %collective-permute-start.3 = (bf16[832,256]{1,0:T(8,128)(2,1)S(1)}, bf16[832,256]{1,0:T(8,128)(2,1)S(1)}, u32[]{:S(2)}, u32[]{:S(2)}) collective-permute-start(bf16[832,256]{1,0:T(8,128)(2,1)S(1)} %collective-permute-done.refs_0_.refs_1_), channel_id=1, source_target_pairs={{0,8},{8,16},{16,24},{24,28},{28,20},{20,12},{12,4},{4,0},{1,9},{9... | collective-permute-start | bytes 1277960 | tf_op jit(solution)/shard_map/ppermute | solution.py:65
  17.6 10.7 %collective-permute-start.4 = (bf16[832,256]{1,0:T(8,128)(2,1)S(1)}, bf16[832,256]{1,0:T(8,128)(2,1)S(1)}, u32[]{:S(2)}, u32[]{:S(2)}) collective-permute-start(bf16[832,256]{1,0:T(8,128)(2,1)S(1)} %collective-permute-done.1.refs_1_.refs_2_), channel_id=1, source_target_pairs={{8,0},{16,8},{24,16},{28,24},{20,28},{12,20},{4,12},{0,4},{9,1},{1... | collective-permute-start | bytes 1277960 | tf_op jit(solution)/shard_map/ppermute | solution.py:65
  26.8 10.1 %collective-permute-start.6 = (bf16[832,256]{1,0:T(8,128)(2,1)S(1)}, bf16[832,256]{1,0:T(8,128)(2,1)S(1)}, u32[]{:S(2)}, u32[]{:S(2)}) collective-permute-start(bf16[832,256]{1,0:T(8,128)(2,1)S(1)} %collective-permute-done.3.refs_2_.refs_3_), channel_id=1, source_target_pairs={{0,8},{8,16},{16,24},{24,28},{28,20},{20,12},{12,4},{4,0},{1,9},{9... | collective-permute-start | bytes 1277960 | tf_op jit(solution)/shard_map/ppermute | solution.py:65
  28.3 9.5 %collective-permute-start.7 = (bf16[832,256]{1,0:T(8,128)(2,1)S(1)}, bf16[832,256]{1,0:T(8,128)(2,1)S(1)}, u32[]{:S(2)}, u32[]{:S(2)}) collective-permute-start(bf16[832,256]{1,0:T(8,128)(2,1)S(1)} %collective-permute-done.4.refs_3_.refs_4_), channel_id=1, source_target_pairs={{8,0},{16,8},{24,16},{28,24},{20,28},{12,20},{4,12},{0,4},{9,1},{1... | collective-permute-start | bytes 1277960 | tf_op jit(solution)/shard_map/ppermute | solution.py:65
  29.6 8.2 %collective-permute-start.5 = (bf16[2,256,256]{2,1,0:T(8,128)(2,1)S(1)}, bf16[2,256,256]{2,1,0:T(8,128)(2,1)S(1)}, u32[]{:S(2)}, u32[]{:S(2)}) collective-permute-start(bf16[2,256,256]{2,1,0:T(8,128)(2,1)S(1)} %shard_map.85.refs_10_), channel_id=1, source_target_pairs={{0,2},{1,3},{2,0},{3,1},{4,6},{5,7},{6,4},{7,5},{8,10},{9,11},{10,... | collective-permute-start | bytes 786440 | tf_op jit(solution)/shard_map/ppermute | solution.py:351
  37.8 5.0 %collective-permute-start.9 = (bf16[2,2,256,256]{3,2,1,0:T(8,128)(2,1)S(1)}, bf16[2,2,256,256]{3,2,1,0:T(8,128)(2,1)S(1)}, u32[]{:S(2)}, u32[]{:S(2)}) collective-permute-start(bf16[2,2,256,256]{3,2,1,0:T(8,128)(2,1)S(1)} %pad_maximum_fusion), channel_id=1, source_target_pairs={{0,1},{1,0},{2,3},{3,2},{4,5},{5,4},{6,7},{7,6},{8,9},{9,8},{10,11... | collective-permute-start | bytes 1572872 | tf_op jit(solution)/shard_map/ppermute | solution.py:345
  37.9 4.9 %collective-permute-start.8 = (bf16[2,1,256,256]{3,2,1,0:T(8,128)(2,1)S(1)}, bf16[2,1,256,256]{3,2,1,0:T(8,128)(2,1)S(1)}, u32[]{:S(2)}, u32[]{:S(2)}) collective-permute-start(bf16[2,1,256,256]{3,2,1,0:T(8,128)(2,1)S(1)} %pad_maximum_fusion.3), channel_id=1, source_target_pairs={{0,1},{1,0},{2,3},{3,2},{4,5},{5,4},{6,7},{7,6},{8,9},{9,8},{10,11... | collective-permute-start | bytes 786440 | tf_op jit(solution)/shard_map/ppermute | solution.py:345
  38.5 7.8 %collective-permute-start.11 = (bf16[384,256]{1,0:T(8,128)(2,1)S(1)}, bf16[384,256]{1,0:T(8,128)(2,1)S(1)}, u32[]{:S(2)}, u32[]{:S(2)}) collective-permute-start(bf16[384,256]{1,0:T(8,128)(2,1)S(1)} %slice.100), channel_id=1, source_target_pairs={{0,8},{8,16},{16,24},{24,28},{28,20},{20,12},{12,4},{4,0},{1,9},{9... | collective-permute-start | bytes 589832 | tf_op jit(solution)/shard_map/ppermute | solution.py:65
  40.1 6.6 %collective-permute-start.12 = (bf16[384,256]{1,0:T(8,128)(2,1)S(1)}, bf16[384,256]{1,0:T(8,128)(2,1)S(1)}, u32[]{:S(2)}, u32[]{:S(2)}) collective-permute-start(bf16[384,256]{1,0:T(8,128)(2,1)S(1)} %slice.101), channel_id=1, source_target_pairs={{8,0},{16,8},{24,16},{28,24},{20,28},{12,20},{4,12},{0,4},{9,1},{1... | collective-permute-start | bytes 589832 | tf_op jit(solution)/shard_map/ppermute | solution.py:65
  41.2 5.0 %collective-permute-start.10 = (bf16[1,256,256]{2,1,0:T(8,128)(2,1)S(1)}, bf16[1,256,256]{2,1,0:T(8,128)(2,1)S(1)}, u32[]{:S(2)}, u32[]{:S(2)}) collective-permute-start(bf16[1,256,256]{2,1,0:T(8,128)(2,1)S(1)} %shard_map.88.refs_0_), channel_id=1, source_target_pairs={{0,2},{1,3},{2,0},{3,1},{4,6},{5,7},{6,4},{7,5},{8,10},{9,11},{10,... | collective-permute-start | bytes 393224 | tf_op jit(solution)/shard_map/ppermute | solution.py:351
  46.8 1.6 %collective-permute-start.13 = (bf16[2,1,256,256]{3,2,1,0:T(8,128)(2,1)S(1)}, bf16[2,1,256,256]{3,2,1,0:T(8,128)(2,1)S(1)}, u32[]{:S(2)}, u32[]{:S(2)}) collective-permute-start(bf16[2,1,256,256]{3,2,1,0:T(8,128)(2,1)S(1)} %pad_maximum_fusion.4), channel_id=1, source_target_pairs={{0,1},{1,0},{2,3},{3,2},{4,5},{5,4},{6,7},{7,6},{8,9},{9,8},{10,11... | collective-permute-start | bytes 786440 | tf_op jit(solution)/shard_map/ppermute | solution.py:345
  51.3 1.6 %collective-permute-start.14 = (f32[192,256]{1,0:T(8,128)S(1)}, f32[192,256]{1,0:T(8,128)S(1)}, u32[]{:S(2)}, u32[]{:S(2)}) collective-permute-start(f32[192,256]{1,0:T(8,128)S(1)} %get-tuple-element.98), channel_id=1, source_target_pairs={{0,1},{1,0},{2,3},{3,2},{4,5},{5,4},{6,7},{7,6},{8,9},{9,8},{10,11... | collective-permute-start | bytes 589832 | tf_op jit(solution)/shard_map/ppermute | solution.py:459
  52.9 7.2 %collective-permute-start.17 = (f32[192,256]{1,0:T(8,128)S(1)}, f32[192,256]{1,0:T(8,128)S(1)}, u32[]{:S(2)}, u32[]{:S(2)}) collective-permute-start(f32[192,256]{1,0:T(8,128)S(1)} %add.59), channel_id=1, source_target_pairs={{0,2},{1,3},{2,0},{3,1},{4,6},{5,7},{6,4},{7,5},{8,10},{9,11},{10,... | collective-permute-start | bytes 589832 | tf_op jit(solution)/shard_map/ppermute | solution.py:473
  54.5 5.7 %copy-start.3 = (f32[1,1,1,192]{3,2,1,0:T(1,128)S(1)}, f32[1,1,1,192]{3,2,1,0:T(1,128)}, u32[]{:S(2)}) copy-start(f32[1,1,1,192]{3,2,1,0:T(1,128)} %param.9) | copy-start | bytes 2308
  56.6 1.4 %collective-permute-start.16 = (f32[96,256]{1,0:T(8,128)S(1)}, f32[96,256]{1,0:T(8,128)S(1)}, u32[]{:S(2)}, u32[]{:S(2)}) collective-permute-start(f32[96,256]{1,0:T(8,128)S(1)} %get-tuple-element.135), channel_id=1, source_target_pairs={{0,1},{1,0},{2,3},{3,2},{4,5},{5,4},{6,7},{7,6},{8,9},{9,8},{10,11... | collective-permute-start | bytes 294920 | tf_op jit(solution)/shard_map/ppermute | solution.py:488
  56.8 1.4 %collective-permute-start.15 = (f32[96,256]{1,0:T(8,128)S(1)}, f32[96,256]{1,0:T(8,128)S(1)}, u32[]{:S(2)}, u32[]{:S(2)}) collective-permute-start(f32[96,256]{1,0:T(8,128)S(1)} %get-tuple-element.134), channel_id=1, source_target_pairs={{0,1},{1,0},{2,3},{3,2},{4,5},{5,4},{6,7},{7,6},{8,9},{9,8},{10,11... | collective-permute-start | bytes 294920 | tf_op jit(solution)/shard_map/ppermute | solution.py:488
  60.2 6.4 %collective-permute-start.18 = (f32[192,256]{1,0:T(8,128)S(1)}, f32[192,256]{1,0:T(8,128)S(1)}, u32[]{:S(2)}, u32[]{:S(2)}) collective-permute-start(f32[192,256]{1,0:T(8,128)S(1)} %fusion.9.refs_0_.refs_6_), channel_id=1, source_target_pairs={{0,8},{8,16},{16,24},{24,28},{28,20},{20,12},{12,4},{4,0},{1,9},{9... | collective-permute-start | bytes 589832 | tf_op jit(solution)/shard_map/ppermute | solution.py:65
  61.9 6.4 %collective-permute-start.20 = (f32[192,256]{1,0:T(8,128)S(1)}, f32[192,256]{1,0:T(8,128)S(1)}, u32[]{:S(2)}, u32[]{:S(2)}) collective-permute-start(f32[192,256]{1,0:T(8,128)S(1)} %fusion.9.refs_0_.refs_6_), channel_id=1, source_target_pairs={{8,0},{16,8},{24,16},{28,24},{20,28},{12,20},{4,12},{0,4},{9,1},{1... | collective-permute-start | bytes 589832 | tf_op jit(solution)/shard_map/ppermute | solution.py:65
  62.3 6.4 %collective-permute-start.26 = (f32[192,256]{1,0:T(8,128)S(1)}, f32[192,256]{1,0:T(8,128)S(1)}, u32[]{:S(2)}, u32[]{:S(2)}) collective-permute-start(f32[192,256]{1,0:T(8,128)S(1)} %fusion.9.refs_0_.refs_6_), channel_id=1, source_target_pairs={{0,2},{1,3},{2,0},{3,1},{4,6},{5,7},{6,4},{7,5},{8,10},{9,11},{10,... | collective-permute-start | bytes 589832 | tf_op jit(solution)/shard_map/ppermute | solution.py:490
  66.7 5.7 %collective-permute-start.19 = (f32[192,256]{1,0:T(8,128)S(1)}, f32[192,256]{1,0:T(8,128)S(1)}, u32[]{:S(2)}, u32[]{:S(2)}) collective-permute-start(f32[192,256]{1,0:T(8,128)S(1)} %collective-permute-done.18.refs_1_), channel_id=1, source_target_pairs={{0,8},{8,16},{16,24},{24,28},{28,20},{20,12},{12,4},{4,0},{1,9},{9... | collective-permute-start | bytes 589832 | tf_op jit(solution)/shard_map/ppermute | solution.py:65
  68.2 5.7 %collective-permute-start.21 = (f32[192,256]{1,0:T(8,128)S(1)}, f32[192,256]{1,0:T(8,128)S(1)}, u32[]{:S(2)}, u32[]{:S(2)}) collective-permute-start(f32[192,256]{1,0:T(8,128)S(1)} %collective-permute-done.20.refs_2_), channel_id=1, source_target_pairs={{8,0},{16,8},{24,16},{28,24},{20,28},{12,20},{4,12},{0,4},{9,1},{1... | collective-permute-start | bytes 589832 | tf_op jit(solution)/shard_map/ppermute | solution.py:65
  68.7 12.3 %collective-permute-start.27 = (f32[2,192,256]{2,1,0:T(8,128)S(1)}, f32[2,192,256]{2,1,0:T(8,128)S(1)}, u32[]{:S(2)}, u32[]{:S(2)}) collective-permute-start(f32[2,192,256]{2,1,0:T(8,128)S(1)} %pad_maximum_fusion.2), channel_id=1, source_target_pairs={{0,1},{1,0},{2,3},{3,2},{4,5},{5,4},{6,7},{7,6},{8,9},{9,8},{10,11... | collective-permute-start | bytes 1179656 | tf_op jit(solution)/shard_map/ppermute | solution.py:491
  72.3 6.3 %collective-permute-start.22 = (f32[192,256]{1,0:T(8,128)S(1)}, f32[192,256]{1,0:T(8,128)S(1)}, u32[]{:S(2)}, u32[]{:S(2)}) collective-permute-start(f32[192,256]{1,0:T(8,128)S(1)} %collective-permute-done.19.refs_3_), channel_id=1, source_target_pairs={{0,8},{8,16},{16,24},{24,28},{28,20},{20,12},{12,4},{4,0},{1,9},{9... | collective-permute-start | bytes 589832 | tf_op jit(solution)/shard_map/ppermute | solution.py:65
  73.9 6.4 %collective-permute-start.24 = (f32[192,256]{1,0:T(8,128)S(1)}, f32[192,256]{1,0:T(8,128)S(1)}, u32[]{:S(2)}, u32[]{:S(2)}) collective-permute-start(f32[192,256]{1,0:T(8,128)S(1)} %collective-permute-done.21.refs_4_), channel_id=1, source_target_pairs={{8,0},{16,8},{24,16},{28,24},{20,28},{12,20},{4,12},{0,4},{9,1},{1... | collective-permute-start | bytes 589832 | tf_op jit(solution)/shard_map/ppermute | solution.py:65
  78.7 6.1 %collective-permute-start.23 = (f32[128,256]{1,0:T(8,128)S(1)}, f32[128,256]{1,0:T(8,128)S(1)}, u32[]{:S(2)}, u32[]{:S(2)}) collective-permute-start(f32[128,256]{1,0:T(8,128)S(1)} %slice.102), channel_id=1, source_target_pairs={{0,8},{8,16},{16,24},{24,28},{28,20},{20,12},{12,4},{4,0},{1,9},{9... | collective-permute-start | bytes 393224 | tf_op jit(solution)/shard_map/ppermute | solution.py:65
  80.3 4.5 %collective-permute-start.25 = (f32[64,256]{1,0:T(8,128)S(1)}, f32[64,256]{1,0:T(8,128)S(1)}, u32[]{:S(2)}, u32[]{:S(2)}) collective-permute-start(f32[64,256]{1,0:T(8,128)S(1)} %slice.103), channel_id=1, source_target_pairs={{8,0},{16,8},{24,16},{28,24},{20,28},{12,20},{4,12},{0,4},{9,1},{1... | collective-permute-start | bytes 196616 | tf_op jit(solution)/shard_map/ppermute | solution.py:65
  86.6 3.7 %collective-permute-start.28 = (f32[2,192,256]{2,1,0:T(8,128)S(1)}, f32[2,192,256]{2,1,0:T(8,128)S(1)}, u32[]{:S(2)}, u32[]{:S(2)}) collective-permute-start(f32[2,192,256]{2,1,0:T(8,128)S(1)} %slice.92), channel_id=1, source_target_pairs={{0,1},{1,0},{2,3},{3,2},{4,5},{5,4},{6,7},{7,6},{8,9},{9,8},{10,11... | collective-permute-start | bytes 1179656 | tf_op jit(solution)/shard_map/ppermute | solution.py:534
  86.6 11.9 %all-to-all-start = ((f32[32,4,256]{2,1,0:T(4,128)}), f32[32,4,256]{2,1,0:T(4,128)S(1)}, u32[]{:S(2)}, u32[]{:S(2)}) async-start(f32[32,4,256]{2,1,0:T(4,128)} %get-tuple-element.120), calls=%async_computation | async-start | bytes 262144 | tf_op jit(solution)/shard_map/all_to_all | solution.py:533
  90.3 8.4 %collective-permute-start.29 = (f32[192,256]{1,0:T(8,128)S(1)}, f32[192,256]{1,0:T(8,128)S(1)}, u32[]{:S(2)}, u32[]{:S(2)}) collective-permute-start(f32[192,256]{1,0:T(8,128)S(1)} %fusion.7), channel_id=1, source_target_pairs={{0,2},{1,3},{2,0},{3,1},{4,6},{5,7},{6,4},{7,5},{8,10},{9,11},{10,... | collective-permute-start | bytes 589832 | tf_op jit(solution)/shard_map/ppermute | solution.py:535
  (3 other events, 5.6 us)

commit v11 on v10

--- a/solution.py
+++ b/solution.py
@@ -495,7 +495,7 @@
         if step < ring.far:
             arrived = ahead, back = ring.move(ahead, back)
         else:
-            arrived = ring.last(ahead, back, piece, piece // 6 // 16 * 16)
+            arrived = ring.last(ahead, back, piece, piece // 3 // 16 * 16)
         if step == ring.far - 2:
             *arrived, gram = lax.optimization_barrier((*arrived, gram))
             tile = fetch(gram)

time: 100 us -> 100 us (level)
  no operation moved by 1% of the time
where the time goes in v11:
time: 100 us; the launch traced here: 99.8 us
  waiting for transfers between devices  34.3 us (34%)
  starting transfers between devices  33.7 us (34%)
  Pallas kernels  17.3 us (17%)
  local copies, waits for them, and re-layouts  10.3 us (10%)
  between operations  2.88 us (3%)
  other arithmetic  1.39 us (1%)
    ppermute x8, waiting for transfers between devices, move(): lax.ppermute(ahead, axes, self.ahead)  22.2 us
    pallas_call x11, Pallas kernels, call(): pl.pallas_call(body, grid_spec=pltpu.PrefetchScalarGridSpec(num_scalar_pr...  17.3 us
    ppermute x8, starting transfers between devices, move(): lax.ppermute(ahead, axes, self.ahead)  14.4 us
    unnamed x10, local copies, waits for them, and re-layouts  6.83 us
    all_to_all x1, waiting for transfers between devices, shards(): sums = lax.all_to_all(sums, axes, split_axis=0, concat_axis=0, tiled=True)  6.35 us
    ppermute x3, starting transfers between devices, open_groups(): lax.ppermute(mine, 'tcol', swap(tcol_count, 2))  5.01 us
    all_to_all x1, starting transfers between devices, shards(): sums = lax.all_to_all(sums, axes, split_axis=0, concat_axis=0, tiled=True)  4.36 us
    ppermute x8, starting transfers between devices, move(): lax.ppermute(back, axes, self.back)  3.08 us
  transfers between devices with their start and end apart: 31, of which 16 were waited for; matrix products, arithmetic and copies ran while one was open for 4% of the time, Pallas kernels for 13%

profile of v11, /device:TPU:0, one launch (start us, length us, event | category | flops | bytes accessed | tf_op | source)
XLA Modules:
  0.0 99.8 jit_solution(7721037760627261366)
XLA Ops:
  2.9 3.1 %collective-permute-start = (bf16[832,256]{1,0:T(8,128)(2,1)S(1)}, bf16[832,256]{1,0:T(8,128)(2,1)S(1)}, u32[]{:S(2)}, u32[]{:S(2)}) collective-permute-start(bf16[832,256]{1,0:T(8,128)(2,1)S(1)} %pad_maximum_fusion.1.refs_0_), channel_id=1, source_target_pairs={{0,8},{8,16},{16,24},{24,28},{28,20},{20,12},{12,4},{4,0},{1,9},{9... | collective-permute-start | bytes 1277960 | tf_op jit(solution)/shard_map/ppermute | solution.py:65
  7.2 2.0 %collective-permute-start.2 = (bf16[1,256,256]{2,1,0:T(8,128)(2,1)S(1)}, bf16[1,256,256]{2,1,0:T(8,128)(2,1)S(1)}, u32[]{:S(2)}, u32[]{:S(2)}) collective-permute-start(bf16[1,256,256]{2,1,0:T(8,128)(2,1)S(1)} %maximum_bitcast_fusion.refs_7_), channel_id=1, source_target_pairs={{0,2},{1,3},{2,0},{3,1},{4,6},{5,7},{6,4},{7,5},{8,10},{9,11},{10,... | collective-permute-start | bytes 393224 | tf_op jit(solution)/shard_map/ppermute | solution.py:351
  9.2 1.3 %dynamic_slice.12 = s32[1,1]{1,0:T(1,128)} dynamic-slice(s32[4,2]{1,0:T(4,128)} %constant.37.clone, s32[]{:T(128)S(6)} %select_n.15, s32[]{:T(128)S(6)} %select_n.16), dynamic_slice_sizes={1,1} | dynamic-slice | bytes 12 | tf_op jit(solution)/shard_map/dynamic_slice | solution.py:309
  13.1 2.7 %collective-permute-done.refs_0_.refs_1_ = bf16[832,256]{1,0:T(8,128)(2,1)S(1)} collective-permute-done((bf16[832,256]{1,0:T(8,128)(2,1)S(1)}, bf16[832,256]{1,0:T(8,128)(2,1)S(1)}, u32[]{:S(2)}, u32[]{:S(2)}) %collective-permute-start) | collective-permute-done | bytes 426016 | tf_op jit(solution)/shard_map/ppermute | solution.py:65
  15.8 1.8 %collective-permute-start.3 = (bf16[832,256]{1,0:T(8,128)(2,1)S(1)}, bf16[832,256]{1,0:T(8,128)(2,1)S(1)}, u32[]{:S(2)}, u32[]{:S(2)}) collective-permute-start(bf16[832,256]{1,0:T(8,128)(2,1)S(1)} %collective-permute-done.refs_0_.refs_1_), channel_id=1, source_target_pairs={{0,8},{8,16},{16,24},{24,28},{28,20},{20,12},{12,4},{4,0},{1,9},{9... | collective-permute-start | bytes 1277960 | tf_op jit(solution)/shard_map/ppermute | solution.py:65
  17.9 8.9 %collective-permute-done.3.refs_2_.refs_3_ = bf16[832,256]{1,0:T(8,128)(2,1)S(1)} collective-permute-done((bf16[832,256]{1,0:T(8,128)(2,1)S(1)}, bf16[832,256]{1,0:T(8,128)(2,1)S(1)}, u32[]{:S(2)}, u32[]{:S(2)}) %collective-permute-start.3) | collective-permute-done | bytes 426016 | tf_op jit(solution)/shard_map/ppermute | solution.py:65
  26.8 1.5 %collective-permute-start.6 = (bf16[832,256]{1,0:T(8,128)(2,1)S(1)}, bf16[832,256]{1,0:T(8,128)(2,1)S(1)}, u32[]{:S(2)}, u32[]{:S(2)}) collective-permute-start(bf16[832,256]{1,0:T(8,128)(2,1)S(1)} %collective-permute-done.3.refs_2_.refs_3_), channel_id=1, source_target_pairs={{0,8},{8,16},{16,24},{24,28},{28,20},{20,12},{12,4},{4,0},{1,9},{9... | collective-permute-start | bytes 1277960 | tf_op jit(solution)/shard_map/ppermute | solution.py:65
  29.6 1.5 %collective-permute-start.5 = (bf16[2,256,256]{2,1,0:T(8,128)(2,1)S(1)}, bf16[2,256,256]{2,1,0:T(8,128)(2,1)S(1)}, u32[]{:S(2)}, u32[]{:S(2)}) collective-permute-start(bf16[2,256,256]{2,1,0:T(8,128)(2,1)S(1)} %shard_map.85.refs_10_), channel_id=1, source_target_pairs={{0,2},{1,3},{2,0},{3,1},{4,6},{5,7},{6,4},{7,5},{8,10},{9,11},{10,... | collective-permute-start | bytes 786440 | tf_op jit(solution)/shard_map/ppermute | solution.py:351
  31.1 2.3 %copy-done.2 = f32[4,1,1,192,1536]{4,3,2,1,0:T(8,128)S(1)} copy-done((f32[4,1,1,192,1536]{4,3,2,1,0:T(8,128)S(1)}, f32[4,1,1,192,1536]{4,3,2,1,0:T(8,128)}, u32[]{:S(2)}) %copy-start.2) | copy-done | bytes 4718616
  33.9 2.9 %collective-permute-done.6.refs_5_.refs_2_ = bf16[832,256]{1,0:T(8,128)(2,1)S(1)} collective-permute-done((bf16[832,256]{1,0:T(8,128)(2,1)S(1)}, bf16[832,256]{1,0:T(8,128)(2,1)S(1)}, u32[]{:S(2)}, u32[]{:S(2)}) %collective-permute-start.6) | collective-permute-done | bytes 426016 | tf_op jit(solution)/shard_map/ppermute | solution.py:65
  38.5 1.6 %collective-permute-start.11 = (bf16[384,256]{1,0:T(8,128)(2,1)S(1)}, bf16[384,256]{1,0:T(8,128)(2,1)S(1)}, u32[]{:S(2)}, u32[]{:S(2)}) collective-permute-start(bf16[384,256]{1,0:T(8,128)(2,1)S(1)} %slice.100), channel_id=1, source_target_pairs={{0,8},{8,16},{16,24},{24,28},{28,20},{20,12},{12,4},{4,0},{1,9},{9... | collective-permute-start | bytes 589832 | tf_op jit(solution)/shard_map/ppermute | solution.py:65
  41.2 1.6 %collective-permute-start.10 = (bf16[1,256,256]{2,1,0:T(8,128)(2,1)S(1)}, bf16[1,256,256]{2,1,0:T(8,128)(2,1)S(1)}, u32[]{:S(2)}, u32[]{:S(2)}) collective-permute-start(bf16[1,256,256]{2,1,0:T(8,128)(2,1)S(1)} %shard_map.88.refs_0_), channel_id=1, source_target_pairs={{0,2},{1,3},{2,0},{3,1},{4,6},{5,7},{6,4},{7,5},{8,10},{9,11},{10,... | collective-permute-start | bytes 393224 | tf_op jit(solution)/shard_map/ppermute | solution.py:351
  42.8 3.0 %shard_map.87 = (f32[384,1536]{1,0:T(8,128)S(1)}, f32[384,1536]{1,0:T(8,128)S(1)}, bf16[1536,1024]{1,0:T(8,128)(2,1)S(1)}, bf16[768,1024]{1,0:T(8,128)(2,1)S(1)}, bf16[256,1024]{1,0:T(8,128)(2,1)S(1)}) custom-call(s32[17]{0:T(128)S(1)} %get-tuple-element.63.meta, bf16[832,256]{1,0:T(8,128)(2,1)S(1)} %pad_maximum_fusion.1.refs_0_, ...), custom_call_target="tpu_custom_call" | custom-call | flops 1811939328 | bytes 9437184 | tf_op jit(solution)/shard_map/pallas_call | solution.py:277
  46.8 1.5 %shard_map.89 = (f32[1536,256]{1,0:T(8,128)S(1)}, bf16[1536,256]{1,0:T(8,128)(2,1)S(1)}) custom-call(s32[17]{0:T(128)S(1)} %get-tuple-element.63.meta, bf16[384,256]{1,0:T(8,128)(2,1)S(1)} %collective-permute-done.11.low_ref, bf16[384,256]{1,0:T(8,128)(2,1)S(1)} %collective-permute-done.12.high_ref, bf16[1536,1024]{1,0:T(8,128)(2,1)S(1)} %get-tuple-element.87.columns, ...), custom_call_target="tpu_custom_call" | custom-call | flops 603979776 | bytes 3145728 | tf_op jit(solution)/shard_map/pallas_call | solution.py:277
  48.4 2.9 %shard_map.90 = (f32[192,256]{1,0:T(8,128)S(1)}, f32[768,1536]{1,0:T(8,128)}, f32[384,1536]{1,0:T(8,128)S(1)}, bf16[1536,256]{1,0:T(8,128)(2,1)S(1)}, bf16[1536,...) custom-call(s32[17]{0:T(128)S(1)} %get-tuple-element.63.meta, ...), custom_call_target="tpu_custom_call" | custom-call | flops 754974720 | bytes 4718592 | tf_op jit(solution)/shard_map/pallas_call | solution.py:277
  52.9 1.6 %collective-permute-start.17 = (f32[192,256]{1,0:T(8,128)S(1)}, f32[192,256]{1,0:T(8,128)S(1)}, u32[]{:S(2)}, u32[]{:S(2)}) collective-permute-start(f32[192,256]{1,0:T(8,128)S(1)} %add.59), channel_id=1, source_target_pairs={{0,2},{1,3},{2,0},{3,1},{4,6},{5,7},{6,4},{7,5},{8,10},{9,11},{10,... | collective-permute-start | bytes 589832 | tf_op jit(solution)/shard_map/ppermute | solution.py:473
  54.5 2.1 %shard_map.92 = (f32[768,1536]{1,0:T(8,128)}, f32[2,192,256]{2,1,0:T(8,128)S(1)}) custom-call(s32[1]{0:T(128)} %bitcast.meta, f32[384,1536]{1,0:T(8,128)S(1)} %get-tuple-element.100.refs_0_, bf16[1536,256]{1,0:T(8,128)(2,1)S(1)} %get-tuple-element.90.refs_5_.refs_1_, ...), custom_call_target="tpu_custom_call", output_to_operand_aliasing={{0}: (6, {})} | custom-call | flops 1207959552 | bytes 4718592 | tf_op jit(solution)/shard_map/pallas_call | solution.py:277
  58.2 2.0 %collective-permute-done.17 = f32[192,256]{1,0:T(8,128)S(1)} collective-permute-done((f32[192,256]{1,0:T(8,128)S(1)}, f32[192,256]{1,0:T(8,128)S(1)}, u32[]{:S(2)}, u32[]{:S(2)}) %collective-permute-start.17) | collective-permute-done | bytes 196640 | tf_op jit(solution)/shard_map/ppermute | solution.py:473
  60.2 1.6 %collective-permute-start.18 = (f32[192,256]{1,0:T(8,128)S(1)}, f32[192,256]{1,0:T(8,128)S(1)}, u32[]{:S(2)}, u32[]{:S(2)}) collective-permute-start(f32[192,256]{1,0:T(8,128)S(1)} %fusion.9.refs_0_.refs_6_), channel_id=1, source_target_pairs={{0,8},{8,16},{16,24},{24,28},{28,20},{20,12},{12,4},{4,0},{1,9},{9... | collective-permute-start | bytes 589832 | tf_op jit(solution)/shard_map/ppermute | solution.py:65
  62.3 1.5 %collective-permute-start.26 = (f32[192,256]{1,0:T(8,128)S(1)}, f32[192,256]{1,0:T(8,128)S(1)}, u32[]{:S(2)}, u32[]{:S(2)}) collective-permute-start(f32[192,256]{1,0:T(8,128)S(1)} %fusion.9.refs_0_.refs_6_), channel_id=1, source_target_pairs={{0,2},{1,3},{2,0},{3,1},{4,6},{5,7},{6,4},{7,5},{8,10},{9,11},{10,... | collective-permute-start | bytes 589832 | tf_op jit(solution)/shard_map/ppermute | solution.py:490
  63.8 2.8 %collective-permute-done.18.refs_1_ = f32[192,256]{1,0:T(8,128)S(1)} collective-permute-done((f32[192,256]{1,0:T(8,128)S(1)}, f32[192,256]{1,0:T(8,128)S(1)}, u32[]{:S(2)}, u32[]{:S(2)}) %collective-permute-start.18) | collective-permute-done | bytes 196640 | tf_op jit(solution)/shard_map/ppermute | solution.py:65
  66.7 1.6 %collective-permute-start.19 = (f32[192,256]{1,0:T(8,128)S(1)}, f32[192,256]{1,0:T(8,128)S(1)}, u32[]{:S(2)}, u32[]{:S(2)}) collective-permute-start(f32[192,256]{1,0:T(8,128)S(1)} %collective-permute-done.18.refs_1_), channel_id=1, source_target_pairs={{0,8},{8,16},{16,24},{24,28},{28,20},{20,12},{12,4},{4,0},{1,9},{9... | collective-permute-start | bytes 589832 | tf_op jit(solution)/shard_map/ppermute | solution.py:65
  68.8 3.5 %collective-permute-done.19.refs_3_ = f32[192,256]{1,0:T(8,128)S(1)} collective-permute-done((f32[192,256]{1,0:T(8,128)S(1)}, f32[192,256]{1,0:T(8,128)S(1)}, u32[]{:S(2)}, u32[]{:S(2)}) %collective-permute-start.19) | collective-permute-done | bytes 196640 | tf_op jit(solution)/shard_map/ppermute | solution.py:65
  72.3 1.6 %collective-permute-start.22 = (f32[192,256]{1,0:T(8,128)S(1)}, f32[192,256]{1,0:T(8,128)S(1)}, u32[]{:S(2)}, u32[]{:S(2)}) collective-permute-start(f32[192,256]{1,0:T(8,128)S(1)} %collective-permute-done.19.refs_3_), channel_id=1, source_target_pairs={{0,8},{8,16},{16,24},{24,28},{28,20},{20,12},{12,4},{4,0},{1,9},{9... | collective-permute-start | bytes 589832 | tf_op jit(solution)/shard_map/ppermute | solution.py:65
  74.5 2.3 %copy-done.1 = f32[768,1536]{1,0:T(8,128)S(1)} copy-done((f32[768,1536]{1,0:T(8,128)S(1)}, f32[768,1536]{1,0:T(8,128)}, u32[]{:S(2)}) %copy-start.1) | copy-done | bytes 4718616
  77.4 1.3 %collective-permute-done.22.refs_5_ = f32[192,256]{1,0:T(8,128)S(1)} collective-permute-done((f32[192,256]{1,0:T(8,128)S(1)}, f32[192,256]{1,0:T(8,128)S(1)}, u32[]{:S(2)}, u32[]{:S(2)}) %collective-permute-start.22) | collective-permute-done | bytes 196640 | tf_op jit(solution)/shard_map/ppermute | solution.py:65
  78.7 1.6 %collective-permute-start.23 = (f32[160,256]{1,0:T(8,128)S(1)}, f32[160,256]{1,0:T(8,128)S(1)}, u32[]{:S(2)}, u32[]{:S(2)}) collective-permute-start(f32[160,256]{1,0:T(8,128)S(1)} %slice.102), channel_id=1, source_target_pairs={{0,8},{8,16},{16,24},{24,28},{28,20},{20,12},{12,4},{4,0},{1,9},{9... | collective-permute-start | bytes 491528 | tf_op jit(solution)/shard_map/ppermute | solution.py:65
  80.8 3.0 %shard_map.94 = (f32[4,192,256]{2,1,0:T(8,128)S(1)}, f32[4,256]{1,0:T(4,128)S(1)}, bf16[768,192]{1,0:T(8,128)(2,1)S(1)}, bf16[768,192]{1,0:T(8,128)(2,1)S(1)}) custom-call(s32[17]{0:T(128)S(1)} %get-tuple-element.107.meta, f32[192,256]{1,0:T(8,128)S(1)} %fusion.9.refs_0_.refs_6_, f32[192,256]{1,0:T(8,128)S(1)} %collective-permute-done.18.refs_1_, ...), custom_call_target="tpu_custom_call" | custom-call | flops 1811939328 | bytes 4718592 | tf_op jit(solution)/shard_map/pallas_call | solution.py:277
  84.2 1.7 %shard_map.95 = (f32[4,192,256]{2,1,0:T(8,128)S(1)}, f32[32,4,256]{2,1,0:T(4,128)}) custom-call(s32[17]{0:T(128)S(1)} %get-tuple-element.107.meta, f32[160,256]{1,0:T(8,128)S(1)} %collective-permute-done.23.refs_0_, f32[32,256]{1,0:T(8,128)S(1)} %collective-permute-done.25.refs_1_, f32[4,192,256]{2,1,0:T(8,128)S(1)} %get-tuple-element.113.refs_2_, ...), custom_call_target="tpu_custom_call" | custom-call | flops 226492416 | bytes 589824 | tf_op jit(solution)/shard_map/pallas_call | solution.py:277
  86.0 4.4 %all-to-all-start = ((f32[32,4,256]{2,1,0:T(4,128)}), f32[32,4,256]{2,1,0:T(4,128)S(1)}, u32[]{:S(2)}, u32[]{:S(2)}) async-start(f32[32,4,256]{2,1,0:T(4,128)} %get-tuple-element.120), calls=%async_computation | async-start | bytes 262144 | tf_op jit(solution)/shard_map/all_to_all | solution.py:533
  90.5 1.8 %collective-permute-start.29 = (f32[192,256]{1,0:T(8,128)S(1)}, f32[192,256]{1,0:T(8,128)S(1)}, u32[]{:S(2)}, u32[]{:S(2)}) collective-permute-start(f32[192,256]{1,0:T(8,128)S(1)} %fusion.7), channel_id=1, source_target_pairs={{0,2},{1,3},{2,0},{3,1},{4,6},{5,7},{6,4},{7,5},{8,10},{9,11},{10,... | collective-permute-start | bytes 589832 | tf_op jit(solution)/shard_map/ppermute | solution.py:535
  92.3 6.4 %all-to-all-done = f32[32,4,256]{2,1,0:T(4,128)S(1)} async-done(((f32[32,4,256]{2,1,0:T(4,128)}), f32[32,4,256]{2,1,0:T(4,128)S(1)}, u32[]{:S(2)}, u32[]{:S(2)}) %all-to-all-start) | async-done | bytes 131104 | tf_op jit(solution)/shard_map/all_to_all | solution.py:533
  (80 shorter events, 17.6 us)
Async XLA Ops:
  2.9 12.8 %collective-permute-start = (bf16[832,256]{1,0:T(8,128)(2,1)S(1)}, bf16[832,256]{1,0:T(8,128)(2,1)S(1)}, u32[]{:S(2)}, u32[]{:S(2)}) collective-permute-start(bf16[832,256]{1,0:T(8,128)(2,1)S(1)} %pad_maximum_fusion.1.refs_0_), channel_id=1, source_target_pairs={{0,8},{8,16},{16,24},{24,28},{28,20},{20,12},{12,4},{4,0},{1,9},{9... | collective-permute-start | bytes 1277960 | tf_op jit(solution)/shard_map/ppermute | solution.py:65
  6.0 11.6 %collective-permute-start.1 = (bf16[832,256]{1,0:T(8,128)(2,1)S(1)}, bf16[832,256]{1,0:T(8,128)(2,1)S(1)}, u32[]{:S(2)}, u32[]{:S(2)}) collective-permute-start(bf16[832,256]{1,0:T(8,128)(2,1)S(1)} %pad_maximum_fusion.1.refs_0_), channel_id=1, source_target_pairs={{8,0},{16,8},{24,16},{28,24},{20,28},{12,20},{4,12},{0,4},{9,1},{1... | collective-permute-start | bytes 1277960 | tf_op jit(solution)/shard_map/ppermute | solution.py:65
  7.2 21.8 %collective-permute-start.2 = (bf16[1,256,256]{2,1,0:T(8,128)(2,1)S(1)}, bf16[1,256,256]{2,1,0:T(8,128)(2,1)S(1)}, u32[]{:S(2)}, u32[]{:S(2)}) collective-permute-start(bf16[1,256,256]{2,1,0:T(8,128)(2,1)S(1)} %maximum_bitcast_fusion.refs_7_), channel_id=1, source_target_pairs={{0,2},{1,3},{2,0},{3,1},{4,6},{5,7},{6,4},{7,5},{8,10},{9,11},{10,... | collective-permute-start | bytes 393224 | tf_op jit(solution)/shard_map/ppermute | solution.py:351
  15.8 11.0 %collective-permute-start.3 = (bf16[832,256]{1,0:T(8,128)(2,1)S(1)}, bf16[832,256]{1,0:T(8,128)(2,1)S(1)}, u32[]{:S(2)}, u32[]{:S(2)}) collective-permute-start(bf16[832,256]{1,0:T(8,128)(2,1)S(1)} %collective-permute-done.refs_0_.refs_1_), channel_id=1, source_target_pairs={{0,8},{8,16},{16,24},{24,28},{28,20},{20,12},{12,4},{4,0},{1,9},{9... | collective-permute-start | bytes 1277960 | tf_op jit(solution)/shard_map/ppermute | solution.py:65
  17.6 10.7 %collective-permute-start.4 = (bf16[832,256]{1,0:T(8,128)(2,1)S(1)}, bf16[832,256]{1,0:T(8,128)(2,1)S(1)}, u32[]{:S(2)}, u32[]{:S(2)}) collective-permute-start(bf16[832,256]{1,0:T(8,128)(2,1)S(1)} %collective-permute-done.1.refs_1_.refs_2_), channel_id=1, source_target_pairs={{8,0},{16,8},{24,16},{28,24},{20,28},{12,20},{4,12},{0,4},{9,1},{1... | collective-permute-start | bytes 1277960 | tf_op jit(solution)/shard_map/ppermute | solution.py:65
  26.8 10.1 %collective-permute-start.6 = (bf16[832,256]{1,0:T(8,128)(2,1)S(1)}, bf16[832,256]{1,0:T(8,128)(2,1)S(1)}, u32[]{:S(2)}, u32[]{:S(2)}) collective-permute-start(bf16[832,256]{1,0:T(8,128)(2,1)S(1)} %collective-permute-done.3.refs_2_.refs_3_), channel_id=1, source_target_pairs={{0,8},{8,16},{16,24},{24,28},{28,20},{20,12},{12,4},{4,0},{1,9},{9... | collective-permute-start | bytes 1277960 | tf_op jit(solution)/shard_map/ppermute | solution.py:65
  28.3 9.5 %collective-permute-start.7 = (bf16[832,256]{1,0:T(8,128)(2,1)S(1)}, bf16[832,256]{1,0:T(8,128)(2,1)S(1)}, u32[]{:S(2)}, u32[]{:S(2)}) collective-permute-start(bf16[832,256]{1,0:T(8,128)(2,1)S(1)} %collective-permute-done.4.refs_3_.refs_4_), channel_id=1, source_target_pairs={{8,0},{16,8},{24,16},{28,24},{20,28},{12,20},{4,12},{0,4},{9,1},{1... | collective-permute-start | bytes 1277960 | tf_op jit(solution)/shard_map/ppermute | solution.py:65
  29.6 8.2 %collective-permute-start.5 = (bf16[2,256,256]{2,1,0:T(8,128)(2,1)S(1)}, bf16[2,256,256]{2,1,0:T(8,128)(2,1)S(1)}, u32[]{:S(2)}, u32[]{:S(2)}) collective-permute-start(bf16[2,256,256]{2,1,0:T(8,128)(2,1)S(1)} %shard_map.85.refs_10_), channel_id=1, source_target_pairs={{0,2},{1,3},{2,0},{3,1},{4,6},{5,7},{6,4},{7,5},{8,10},{9,11},{10,... | collective-permute-start | bytes 786440 | tf_op jit(solution)/shard_map/ppermute | solution.py:351
  37.8 5.0 %collective-permute-start.9 = (bf16[2,2,256,256]{3,2,1,0:T(8,128)(2,1)S(1)}, bf16[2,2,256,256]{3,2,1,0:T(8,128)(2,1)S(1)}, u32[]{:S(2)}, u32[]{:S(2)}) collective-permute-start(bf16[2,2,256,256]{3,2,1,0:T(8,128)(2,1)S(1)} %pad_maximum_fusion), channel_id=1, source_target_pairs={{0,1},{1,0},{2,3},{3,2},{4,5},{5,4},{6,7},{7,6},{8,9},{9,8},{10,11... | collective-permute-start | bytes 1572872 | tf_op jit(solution)/shard_map/ppermute | solution.py:345
  37.9 4.9 %collective-permute-start.8 = (bf16[2,1,256,256]{3,2,1,0:T(8,128)(2,1)S(1)}, bf16[2,1,256,256]{3,2,1,0:T(8,128)(2,1)S(1)}, u32[]{:S(2)}, u32[]{:S(2)}) collective-permute-start(bf16[2,1,256,256]{3,2,1,0:T(8,128)(2,1)S(1)} %pad_maximum_fusion.3), channel_id=1, source_target_pairs={{0,1},{1,0},{2,3},{3,2},{4,5},{5,4},{6,7},{7,6},{8,9},{9,8},{10,11... | collective-permute-start | bytes 786440 | tf_op jit(solution)/shard_map/ppermute | solution.py:345
  38.5 7.8 %collective-permute-start.11 = (bf16[384,256]{1,0:T(8,128)(2,1)S(1)}, bf16[384,256]{1,0:T(8,128)(2,1)S(1)}, u32[]{:S(2)}, u32[]{:S(2)}) collective-permute-start(bf16[384,256]{1,0:T(8,128)(2,1)S(1)} %slice.100), channel_id=1, source_target_pairs={{0,8},{8,16},{16,24},{24,28},{28,20},{20,12},{12,4},{4,0},{1,9},{9... | collective-permute-start | bytes 589832 | tf_op jit(solution)/shard_map/ppermute | solution.py:65
  40.1 6.6 %collective-permute-start.12 = (bf16[384,256]{1,0:T(8,128)(2,1)S(1)}, bf16[384,256]{1,0:T(8,128)(2,1)S(1)}, u32[]{:S(2)}, u32[]{:S(2)}) collective-permute-start(bf16[384,256]{1,0:T(8,128)(2,1)S(1)} %slice.101), channel_id=1, source_target_pairs={{8,0},{16,8},{24,16},{28,24},{20,28},{12,20},{4,12},{0,4},{9,1},{1... | collective-permute-start | bytes 589832 | tf_op jit(solution)/shard_map/ppermute | solution.py:65
  41.2 5.0 %collective-permute-start.10 = (bf16[1,256,256]{2,1,0:T(8,128)(2,1)S(1)}, bf16[1,256,256]{2,1,0:T(8,128)(2,1)S(1)}, u32[]{:S(2)}, u32[]{:S(2)}) collective-permute-start(bf16[1,256,256]{2,1,0:T(8,128)(2,1)S(1)} %shard_map.88.refs_0_), channel_id=1, source_target_pairs={{0,2},{1,3},{2,0},{3,1},{4,6},{5,7},{6,4},{7,5},{8,10},{9,11},{10,... | collective-permute-start | bytes 393224 | tf_op jit(solution)/shard_map/ppermute | solution.py:351
  46.8 1.6 %collective-permute-start.13 = (bf16[2,1,256,256]{3,2,1,0:T(8,128)(2,1)S(1)}, bf16[2,1,256,256]{3,2,1,0:T(8,128)(2,1)S(1)}, u32[]{:S(2)}, u32[]{:S(2)}) collective-permute-start(bf16[2,1,256,256]{3,2,1,0:T(8,128)(2,1)S(1)} %pad_maximum_fusion.4), channel_id=1, source_target_pairs={{0,1},{1,0},{2,3},{3,2},{4,5},{5,4},{6,7},{7,6},{8,9},{9,8},{10,11... | collective-permute-start | bytes 786440 | tf_op jit(solution)/shard_map/ppermute | solution.py:345
  51.3 1.6 %collective-permute-start.14 = (f32[192,256]{1,0:T(8,128)S(1)}, f32[192,256]{1,0:T(8,128)S(1)}, u32[]{:S(2)}, u32[]{:S(2)}) collective-permute-start(f32[192,256]{1,0:T(8,128)S(1)} %get-tuple-element.98), channel_id=1, source_target_pairs={{0,1},{1,0},{2,3},{3,2},{4,5},{5,4},{6,7},{7,6},{8,9},{9,8},{10,11... | collective-permute-start | bytes 589832 | tf_op jit(solution)/shard_map/ppermute | solution.py:459
  52.9 7.2 %collective-permute-start.17 = (f32[192,256]{1,0:T(8,128)S(1)}, f32[192,256]{1,0:T(8,128)S(1)}, u32[]{:S(2)}, u32[]{:S(2)}) collective-permute-start(f32[192,256]{1,0:T(8,128)S(1)} %add.59), channel_id=1, source_target_pairs={{0,2},{1,3},{2,0},{3,1},{4,6},{5,7},{6,4},{7,5},{8,10},{9,11},{10,... | collective-permute-start | bytes 589832 | tf_op jit(solution)/shard_map/ppermute | solution.py:473
  54.5 5.7 %copy-start.3 = (f32[1,1,1,192]{3,2,1,0:T(1,128)S(1)}, f32[1,1,1,192]{3,2,1,0:T(1,128)}, u32[]{:S(2)}) copy-start(f32[1,1,1,192]{3,2,1,0:T(1,128)} %param.9) | copy-start | bytes 2308
  56.6 1.4 %collective-permute-start.16 = (f32[96,256]{1,0:T(8,128)S(1)}, f32[96,256]{1,0:T(8,128)S(1)}, u32[]{:S(2)}, u32[]{:S(2)}) collective-permute-start(f32[96,256]{1,0:T(8,128)S(1)} %get-tuple-element.135), channel_id=1, source_target_pairs={{0,1},{1,0},{2,3},{3,2},{4,5},{5,4},{6,7},{7,6},{8,9},{9,8},{10,11... | collective-permute-start | bytes 294920 | tf_op jit(solution)/shard_map/ppermute | solution.py:488
  56.8 1.4 %collective-permute-start.15 = (f32[96,256]{1,0:T(8,128)S(1)}, f32[96,256]{1,0:T(8,128)S(1)}, u32[]{:S(2)}, u32[]{:S(2)}) collective-permute-start(f32[96,256]{1,0:T(8,128)S(1)} %get-tuple-element.134), channel_id=1, source_target_pairs={{0,1},{1,0},{2,3},{3,2},{4,5},{5,4},{6,7},{7,6},{8,9},{9,8},{10,11... | collective-permute-start | bytes 294920 | tf_op jit(solution)/shard_map/ppermute | solution.py:488
  60.2 6.4 %collective-permute-start.18 = (f32[192,256]{1,0:T(8,128)S(1)}, f32[192,256]{1,0:T(8,128)S(1)}, u32[]{:S(2)}, u32[]{:S(2)}) collective-permute-start(f32[192,256]{1,0:T(8,128)S(1)} %fusion.9.refs_0_.refs_6_), channel_id=1, source_target_pairs={{0,8},{8,16},{16,24},{24,28},{28,20},{20,12},{12,4},{4,0},{1,9},{9... | collective-permute-start | bytes 589832 | tf_op jit(solution)/shard_map/ppermute | solution.py:65
  61.9 6.4 %collective-permute-start.20 = (f32[192,256]{1,0:T(8,128)S(1)}, f32[192,256]{1,0:T(8,128)S(1)}, u32[]{:S(2)}, u32[]{:S(2)}) collective-permute-start(f32[192,256]{1,0:T(8,128)S(1)} %fusion.9.refs_0_.refs_6_), channel_id=1, source_target_pairs={{8,0},{16,8},{24,16},{28,24},{20,28},{12,20},{4,12},{0,4},{9,1},{1... | collective-permute-start | bytes 589832 | tf_op jit(solution)/shard_map/ppermute | solution.py:65
  62.3 6.4 %collective-permute-start.26 = (f32[192,256]{1,0:T(8,128)S(1)}, f32[192,256]{1,0:T(8,128)S(1)}, u32[]{:S(2)}, u32[]{:S(2)}) collective-permute-start(f32[192,256]{1,0:T(8,128)S(1)} %fusion.9.refs_0_.refs_6_), channel_id=1, source_target_pairs={{0,2},{1,3},{2,0},{3,1},{4,6},{5,7},{6,4},{7,5},{8,10},{9,11},{10,... | collective-permute-start | bytes 589832 | tf_op jit(solution)/shard_map/ppermute | solution.py:490
  66.7 5.7 %collective-permute-start.19 = (f32[192,256]{1,0:T(8,128)S(1)}, f32[192,256]{1,0:T(8,128)S(1)}, u32[]{:S(2)}, u32[]{:S(2)}) collective-permute-start(f32[192,256]{1,0:T(8,128)S(1)} %collective-permute-done.18.refs_1_), channel_id=1, source_target_pairs={{0,8},{8,16},{16,24},{24,28},{28,20},{20,12},{12,4},{4,0},{1,9},{9... | collective-permute-start | bytes 589832 | tf_op jit(solution)/shard_map/ppermute | solution.py:65
  68.2 5.7 %collective-permute-start.21 = (f32[192,256]{1,0:T(8,128)S(1)}, f32[192,256]{1,0:T(8,128)S(1)}, u32[]{:S(2)}, u32[]{:S(2)}) collective-permute-start(f32[192,256]{1,0:T(8,128)S(1)} %collective-permute-done.20.refs_2_), channel_id=1, source_target_pairs={{8,0},{16,8},{24,16},{28,24},{20,28},{12,20},{4,12},{0,4},{9,1},{1... | collective-permute-start | bytes 589832 | tf_op jit(solution)/shard_map/ppermute | solution.py:65
  68.7 12.1 %collective-permute-start.27 = (f32[2,192,256]{2,1,0:T(8,128)S(1)}, f32[2,192,256]{2,1,0:T(8,128)S(1)}, u32[]{:S(2)}, u32[]{:S(2)}) collective-permute-start(f32[2,192,256]{2,1,0:T(8,128)S(1)} %pad_maximum_fusion.2), channel_id=1, source_target_pairs={{0,1},{1,0},{2,3},{3,2},{4,5},{5,4},{6,7},{7,6},{8,9},{9,8},{10,11... | collective-permute-start | bytes 1179656 | tf_op jit(solution)/shard_map/ppermute | solution.py:491
  72.3 6.3 %collective-permute-start.22 = (f32[192,256]{1,0:T(8,128)S(1)}, f32[192,256]{1,0:T(8,128)S(1)}, u32[]{:S(2)}, u32[]{:S(2)}) collective-permute-start(f32[192,256]{1,0:T(8,128)S(1)} %collective-permute-done.19.refs_3_), channel_id=1, source_target_pairs={{0,8},{8,16},{16,24},{24,28},{28,20},{20,12},{12,4},{4,0},{1,9},{9... | collective-permute-start | bytes 589832 | tf_op jit(solution)/shard_map/ppermute | solution.py:65
  73.9 6.4 %collective-permute-start.24 = (f32[192,256]{1,0:T(8,128)S(1)}, f32[192,256]{1,0:T(8,128)S(1)}, u32[]{:S(2)}, u32[]{:S(2)}) collective-permute-start(f32[192,256]{1,0:T(8,128)S(1)} %collective-permute-done.21.refs_4_), channel_id=1, source_target_pairs={{8,0},{16,8},{24,16},{28,24},{20,28},{12,20},{4,12},{0,4},{9,1},{1... | collective-permute-start | bytes 589832 | tf_op jit(solution)/shard_map/ppermute | solution.py:65
  78.7 5.6 %collective-permute-start.23 = (f32[160,256]{1,0:T(8,128)S(1)}, f32[160,256]{1,0:T(8,128)S(1)}, u32[]{:S(2)}, u32[]{:S(2)}) collective-permute-start(f32[160,256]{1,0:T(8,128)S(1)} %slice.102), channel_id=1, source_target_pairs={{0,8},{8,16},{16,24},{24,28},{28,20},{20,12},{12,4},{4,0},{1,9},{9... | collective-permute-start | bytes 491528 | tf_op jit(solution)/shard_map/ppermute | solution.py:65
  80.3 3.9 %collective-permute-start.25 = (f32[32,256]{1,0:T(8,128)S(1)}, f32[32,256]{1,0:T(8,128)S(1)}, u32[]{:S(2)}, u32[]{:S(2)}) collective-permute-start(f32[32,256]{1,0:T(8,128)S(1)} %slice.103), channel_id=1, source_target_pairs={{8,0},{16,8},{24,16},{28,24},{20,28},{12,20},{4,12},{0,4},{9,1},{1... | collective-permute-start | bytes 98312 | tf_op jit(solution)/shard_map/ppermute | solution.py:65
  86.0 4.4 %collective-permute-start.28 = (f32[2,192,256]{2,1,0:T(8,128)S(1)}, f32[2,192,256]{2,1,0:T(8,128)S(1)}, u32[]{:S(2)}, u32[]{:S(2)}) collective-permute-start(f32[2,192,256]{2,1,0:T(8,128)S(1)} %slice.92), channel_id=1, source_target_pairs={{0,1},{1,0},{2,3},{3,2},{4,5},{5,4},{6,7},{7,6},{8,9},{9,8},{10,11... | collective-permute-start | bytes 1179656 | tf_op jit(solution)/shard_map/ppermute | solution.py:534
  86.0 12.6 %all-to-all-start = ((f32[32,4,256]{2,1,0:T(4,128)}), f32[32,4,256]{2,1,0:T(4,128)S(1)}, u32[]{:S(2)}, u32[]{:S(2)}) async-start(f32[32,4,256]{2,1,0:T(4,128)} %get-tuple-element.120), calls=%async_computation | async-start | bytes 262144 | tf_op jit(solution)/shard_map/all_to_all | solution.py:533
  90.5 8.4 %collective-permute-start.29 = (f32[192,256]{1,0:T(8,128)S(1)}, f32[192,256]{1,0:T(8,128)S(1)}, u32[]{:S(2)}, u32[]{:S(2)}) collective-permute-start(f32[192,256]{1,0:T(8,128)S(1)} %fusion.7), channel_id=1, source_target_pairs={{0,2},{1,3},{2,0},{3,1},{4,6},{5,7},{6,4},{7,5},{8,10},{9,11},{10,... | collective-permute-start | bytes 589832 | tf_op jit(solution)/shard_map/ppermute | solution.py:535
  (3 other events, 5.6 us)
